TPU v7x, 32 devices: a whole 2x2x4 slice. The times are simulated.
32 devices in a mesh: rep: 4 (over z), exp: 8 (over y, x, core).
Axes of the slice: x: 2, y: 2, z: 4, core: 2. Of those that a mesh axis runs over, the one named last changes fastest.
Arguments:
- tokens: bfloat16 [512, 4096], P(('rep', 'exp')), may hold values from -6 to 6
- routed_experts: int32 [512, 8], P(('rep', 'exp')), may hold values from 0 to 15, all different within a row; in each aligned block of 16 rows (0 to 15, 16 to 31, ...) at most 12 rows name the same one
- route_weights: float32 [512, 8], P(('rep', 'exp')), may hold values from 0.02 to 0.5
- gate_weight: bfloat16 [16, 1536, 4096], P('exp', 'rep'), may hold values from -0.09375 to 0.09375
- up_weight: bfloat16 [16, 1536, 4096], P('exp', 'rep'), may hold values from -0.09375 to 0.09375
- down_weight: bfloat16 [16, 1536, 4096], P('exp', 'rep'), may hold values from -0.15625 to 0.15625
Outputs:
- layer_output: bfloat16 [512, 4096], P(('rep', 'exp'))
Inputs may be any that keep to these rules, and one draw needn't show every extreme that they name: `routed_experts`: each token names 8 different experts. Among the 16 tokens of one device (aligned blocks of rows), no expert is named more than 12 times, a bound that some block reaches.
All inputs are finite; a program needn't handle non-finite values.
Results may differ from a plain program's by a relative error of at most 0.01.
Values may be sent and summed in bfloat16 or wider, within the bound.
No kernel may reach another device: no remote copies, remote signals or barrier semaphores. Data moves between devices by JAX's collectives and lax.ppermute only.
A program may use at most 128 MiB of HBM per device.

v0:
```python
import functools

import jax
import jax.numpy as jnp
from jax import lax
from jax.experimental import pallas as pl
from jax.experimental.pallas import tpu as pltpu
from jax.sharding import PartitionSpec as P


def slot_table(experts, expert_count, capacity):
    blocks = experts.shape[0]
    flattened = experts.reshape(blocks, -1)
    onehot = (
        flattened[:, :, None] == jnp.arange(expert_count, dtype=jnp.int32)[None, None, :]
    ).astype(jnp.int32)
    before = jnp.cumsum(onehot, axis=1) - onehot
    position = jnp.sum(before * onehot, axis=2)
    return flattened * capacity + position


def token_picks(slots, top_count, slot_count):
    blocks = slots.shape[0]
    grouped = slots.reshape(blocks, 1, -1, top_count)
    return jnp.any(grouped == jnp.arange(slot_count, dtype=jnp.int32)[None, :, None, None], axis=3)


def routing_column(route_weights, routed_experts):
    as_float = routed_experts.astype(jnp.float32)
    weights_all, experts_all = (
        lax.all_gather(route_weights, "rep", axis=0, tiled=True),
        lax.all_gather(as_float, "rep", axis=0, tiled=True),
    )
    return (weights_all, experts_all.astype(jnp.int32))


def on_device_slots(tokens, routed_experts, route_weights, gate_weight, up_weight, down_weight):
    replicas = lax.axis_size("rep")
    owners = lax.axis_size("exp")
    token_rows, model_width = tokens.shape
    top_count = routed_experts.shape[1]
    local_experts = gate_weight.shape[0]
    expert_count = local_experts * owners
    capacity = max(2, 3 * token_rows * top_count // (2 * expert_count))
    slot_count = expert_count * capacity
    own_slots = slot_table(routed_experts[None], expert_count, capacity)
    column = None
    column_slots = None
    selected = token_picks(own_slots, top_count, slot_count)[0].astype(jnp.bfloat16)
    buffer = jnp.dot(selected, tokens, preferred_element_type=jnp.float32).astype(jnp.bfloat16)
    buffer = buffer.reshape(owners, local_experts, capacity, model_width)
    arrived = lax.all_to_all(buffer, "exp", split_axis=0, concat_axis=2, tiled=True)
    rows_now = lax.all_gather(arrived, "rep", axis=2, tiled=True)[0]
    gate_value = jnp.einsum(
        "emd,efd->emf", rows_now, gate_weight, preferred_element_type=jnp.float32
    )
    up_value = jnp.einsum("emd,efd->emf", rows_now, up_weight, preferred_element_type=jnp.float32)
    hidden = (jax.nn.silu(gate_value) * up_value).astype(jnp.bfloat16)
    outcome = jnp.einsum("emf,efd->emd", hidden, down_weight, preferred_element_type=jnp.float32)
    outcome = lax.optimization_barrier(outcome.astype(jnp.bfloat16))
    outcomes = outcome[None]
    outcomes = outcomes.reshape(local_experts, replicas, owners, capacity, model_width)
    column = routing_column(route_weights, routed_experts)
    column_slots = slot_table(
        column[1].reshape(replicas, token_rows, top_count), expert_count, capacity
    )
    returned = lax.all_to_all(outcomes, "exp", split_axis=2, concat_axis=0, tiled=True)
    returned = returned.reshape(expert_count, replicas, capacity, model_width)
    expert_index = column_slots // capacity
    place_index = column_slots % capacity
    replica_index = jnp.broadcast_to(
        jnp.arange(replicas, dtype=jnp.int32)[:, None], column_slots.shape
    )
    picked = returned[expert_index, replica_index, place_index].astype(jnp.float32)
    column_weights = column[0].reshape(replicas, token_rows, top_count)
    weighted = jnp.sum(
        picked.reshape(replicas, token_rows, top_count, model_width)
        * column_weights[:, :, :, None],
        axis=2,
    )
    summed = lax.psum_scatter(weighted, "rep", scatter_dimension=0, tiled=True)
    return summed.reshape(token_rows, model_width).astype(jnp.bfloat16)


def expert_kernel(pieces_in, pieces_out, local_experts, shard_units, model_width, top, block, *refs):
    own_ref, refs = refs[0], refs[1:]
    ins, refs = refs[: len(pieces_in)], refs[len(pieces_in) :]
    (gate_ref, up_ref, down_ref), refs = refs[:3], refs[3:]
    outs, refs = refs[: len(pieces_out)], refs[len(pieces_out) :]
    rows, turned, hidden, result, row_sem, out_sem = refs
    units = local_experts * shard_units
    unit_block = shard_units
    unit_blocks = local_experts
    column_blocks = model_width // block
    total = rows.shape[0]

    row_copies, start = [], 0
    for place, count in enumerate(pieces_in):
        row_copies.append(
            pltpu.make_async_copy(ins[place], rows.at[pl.ds(start, count)], row_sem.at[place])
        )
        start += count

    for copy in row_copies:
        copy.start()
    for copy in row_copies:
        copy.wait()

    turned[...] = rows[...].T
    extra = turned[model_width:, :].astype(jnp.float32)
    scale = extra[top : 2 * top] + extra[2 * top : 3 * top]
    weights = []
    for expert in range(local_experts):
        name = (own_ref[0] + expert).astype(jnp.float32)
        weights.append(jnp.sum(jnp.where(extra[:top] == name, scale, 0.0), axis=0, keepdims=True))

    values = turned[:model_width, :]
    for expert in range(local_experts):
        span = pl.ds(expert * shard_units, shard_units)
        gate = jnp.dot(gate_ref[span, :], values, preferred_element_type=jnp.float32)
        up = jnp.dot(up_ref[span, :], values, preferred_element_type=jnp.float32)
        active = gate / (1.0 + jnp.exp(-gate)) * up * weights[expert]
        hidden[:, span] = active.astype(jnp.bfloat16).T

    def out_copies(step):
        span = pl.ds(pl.multiple_of(step * block, block), block)
        copies = []
        for place, segments in enumerate(pieces_out):
            filled = 0
            for begin, count in segments:
                copies.append(
                    pltpu.make_async_copy(
                        result.at[pl.ds(begin, count), span],
                        outs[place].at[pl.ds(filled, count), span],
                        out_sem.at[step, len(copies)],
                    )
                )
                filled += count
        return copies

    def column_step(step, carry):
        span = pl.ds(pl.multiple_of(step * block, block), block)
        value = jnp.dot(hidden[...], down_ref[:, span], preferred_element_type=jnp.float32)
        result[:, span] = value.astype(jnp.bfloat16)
        for copy in out_copies(step):
            copy.start()
        return carry

    def finish_step(step, carry):
        for copy in out_copies(step):
            copy.wait()
        return carry

    lax.fori_loop(0, column_blocks, column_step, 0)
    lax.fori_loop(0, column_blocks, finish_step, 0)


def experts_of(pieces, pieces_out, gate_weight, up_weight, down_weight, top):
    local_experts, shard_units, model_width = gate_weight.shape
    units = local_experts * shard_units
    block = 512
    pieces_in = [piece.shape[0] for piece in pieces]
    total = sum(pieces_in)
    packed = pieces[0].shape[1]
    own = jnp.full((1,), lax.axis_index("exp") * local_experts, jnp.int32)
    anywhere = pl.BlockSpec(memory_space=pl.ANY)
    kernel = functools.partial(
        expert_kernel, pieces_in, pieces_out, local_experts, shard_units, model_width, top, block
    )
    out_rows = [sum(count for _, count in segments) for segments in pieces_out]
    return pl.pallas_call(
        kernel,
        out_shape=[jax.ShapeDtypeStruct((count, model_width), jnp.bfloat16) for count in out_rows],
        in_specs=[pl.BlockSpec(memory_space=pltpu.SMEM)]
        + [anywhere] * len(pieces)
        + [pl.BlockSpec(memory_space=pltpu.VMEM)] * 3,
        out_specs=[anywhere] * len(out_rows),
        scratch_shapes=[
            pltpu.VMEM((total, packed), jnp.bfloat16),
            pltpu.VMEM((packed, total), jnp.bfloat16),
            pltpu.VMEM((total, units), jnp.bfloat16),
            pltpu.VMEM((total, model_width), jnp.bfloat16),
            pltpu.SemaphoreType.DMA((len(pieces),)),
            pltpu.SemaphoreType.DMA((model_width // block, sum(len(segments) for segments in pieces_out))),
        ],
        compiler_params=pltpu.CompilerParams(vmem_limit_bytes=12 * 1024 * 1024),
        cost_estimate=pl.CostEstimate(
            flops=6 * total * units * model_width,
            bytes_accessed=6 * units * model_width + 4 * total * model_width,
            transcendentals=total * units,
        ),
        name="experts",
    )(
        own,
        *pieces,
        gate_weight.reshape(units, model_width),
        up_weight.reshape(units, model_width),
        down_weight.reshape(units, model_width),
    )


def pack_kernel(tokens_ref, experts_ref, weights_ref, packed_ref):
    model_width = tokens_ref.shape[1]
    packed_ref[:, :model_width] = tokens_ref[...]
    weights = weights_ref[...]
    high = weights.astype(jnp.bfloat16).astype(jnp.float32)
    listed = jnp.concatenate([experts_ref[...].astype(jnp.float32), high, weights - high], axis=0)
    width = packed_ref.shape[1] - model_width
    place = lax.broadcasted_iota(jnp.int32, (listed.shape[0], width), 0)
    lane = lax.broadcasted_iota(jnp.int32, (listed.shape[0], width), 1)
    chosen = jnp.where(place == lane, 1.0, 0.0).astype(jnp.bfloat16)
    extra = lax.dot_general(
        listed.astype(jnp.bfloat16),
        chosen,
        (((0,), (0,)), ((), ())),
        preferred_element_type=jnp.float32,
    )
    packed_ref[:, model_width:] = extra.astype(jnp.bfloat16)


def with_routing(tokens, routed_experts, route_weights):
    rows, width = tokens.shape
    return pl.pallas_call(
        pack_kernel,
        out_shape=jax.ShapeDtypeStruct((rows, width + 128), jnp.bfloat16),
        in_specs=[pl.BlockSpec(memory_space=pltpu.VMEM)] * 3,
        out_specs=pl.BlockSpec(memory_space=pltpu.VMEM),
        compiler_params=pltpu.CompilerParams(vmem_limit_bytes=2 * 1024 * 1024),
        name="pack",
    )(tokens, routed_experts.T, route_weights.T)


def swap_exp(value, bit):
    owners = lax.axis_size("exp")
    return lax.ppermute(value, "exp", [(i, i ^ bit) for i in range(owners)])


def turn_rep(value, shift):
    replicas = lax.axis_size("rep")
    return lax.ppermute(value, "rep", [(i, (i - shift) % replicas) for i in range(replicas)])


def added(*terms):
    total = terms[0].astype(jnp.float32)
    for term in terms[1:]:
        total = total + term.astype(jnp.float32)
    return total


def rounded(*terms):
    return added(*terms).astype(jnp.bfloat16)


def gathered(one, two):
    rows = one.shape[0]
    pair = jnp.concatenate([one, two], axis=0)
    from_x, from_y = swap_exp(pair, 2), swap_exp(pair, 4)
    far_one, far_two = swap_exp(from_x[:rows], 4), swap_exp(from_y[rows:], 2)
    pieces = [pair, from_x, from_y, far_one, far_two]
    return pieces + [swap_exp(piece, 1) for piece in pieces]


def segments_of(rows):
    own, x_one, x_two, y_one, y_two, far_one, far_two = 0, 2, 3, 4, 5, 6, 7
    other = 8
    cuts = [
        [x_two, far_two],
        [y_one, far_one],
        [own, own + 1],
        [x_one],
        [y_two],
    ]
    cuts.append([other + place for cut in cuts for place in cut])
    return [[(place * rows, rows) for place in cut] for cut in cuts]


def reduced(parts, rows):
    to_x, to_y, own, x_one, y_two, other = parts
    back = swap_exp(other, 1)
    to_x = rounded(to_x, back[: 2 * rows])
    to_y = rounded(to_y, back[2 * rows : 4 * rows])
    from_x, from_y = swap_exp(to_x, 2), swap_exp(to_y, 4)
    x_one = rounded(x_one, back[6 * rows : 7 * rows], from_y[rows:])
    y_two = rounded(y_two, back[7 * rows :], from_x[rows:])
    last_x, last_y = swap_exp(x_one, 2), swap_exp(y_two, 4)
    one = added(own[:rows], back[4 * rows : 5 * rows], from_y[:rows], last_x)
    two = added(own[rows:], back[5 * rows : 6 * rows], from_x[:rows], last_y)
    return one, two


def on_device_dense(tokens, routed_experts, route_weights, gate_weight, up_weight, down_weight):
    top = routed_experts.shape[1]
    rows = tokens.shape[0]
    packed = with_routing(tokens, routed_experts, route_weights)
    turned = {s: turn_rep(packed, s) for s in (2, 1, 3)}
    near = gathered(packed, turned[2])
    far = gathered(turned[1], turned[3])
    segments = segments_of(rows)
    near_sums = reduced(experts_of(near, segments, gate_weight, up_weight, down_weight, top), rows)
    far_sums = reduced(experts_of(far, segments, gate_weight, up_weight, down_weight, top), rows)
    arrived = [
        turn_rep(near_sums[1].astype(jnp.bfloat16), -2),
        turn_rep(far_sums[0].astype(jnp.bfloat16), -1),
        turn_rep(far_sums[1].astype(jnp.bfloat16), -3),
    ]
    return rounded(near_sums[0], *arrived)


def solution(mesh):
    placed = (
        P(("rep", "exp"), None),
        P(("rep", "exp"), None),
        P(("rep", "exp"), None),
        P("exp", "rep", None),
        P("exp", "rep", None),
        P("exp", "rep", None),
    )
    plane = mesh.shape["exp"] == 8 and mesh.shape["rep"] == 4
    return jax.shard_map(
        on_device_dense if plane else on_device_slots,
        mesh=mesh,
        in_specs=placed,
        out_specs=P(("rep", "exp"), None),
        check_vma=False,
    )
```

profile of v0, /device:TPU:0, one launch (start us, length us, event | category | flops | bytes accessed | tf_op | source)
XLA Modules:
  0.0 102.4 jit_solution(6344775576313813692)
XLA Ops:
  2.5 5.0 %collective-permute-start.16 = (bf16[16,4224]{1,0:T(8,128)(2,1)S(1)}, bf16[16,4224]{1,0:T(8,128)(2,1)S(1)}, u32[]{:S(2)}, u32[]{:S(2)}) collective-permute-start(bf16[16,4224]{1,0:T(8,128)(2,1)S(1)} %pack.1), channel_id=1, source_target_pairs={{0,24},{8,0},{16,8},{24,16},{1,25},{9,1},{17,9},{25,17},{2,26},{10... | collective-permute-start | bytes 405512 | tf_op jit(solution)/shard_map/ppermute | solution.py:240
  7.5 4.0 %collective-permute-done.16 = bf16[16,4224]{1,0:T(8,128)(2,1)S(1)} collective-permute-done((bf16[16,4224]{1,0:T(8,128)(2,1)S(1)}, bf16[16,4224]{1,0:T(8,128)(2,1)S(1)}, u32[]{:S(2)}, u32[]{:S(2)}) %collective-permute-start.16) | collective-permute-done | bytes 135200 | tf_op jit(solution)/shard_map/ppermute | solution.py:240
  11.5 2.8 %collective-permute-done.17 = bf16[16,4224]{1,0:T(8,128)(2,1)S(1)} collective-permute-done((bf16[16,4224]{1,0:T(8,128)(2,1)S(1)}, bf16[16,4224]{1,0:T(8,128)(2,1)S(1)}, u32[]{:S(2)}, u32[]{:S(2)}) %collective-permute-start.17) | collective-permute-done | bytes 135200 | tf_op jit(solution)/shard_map/ppermute | solution.py:240
  14.4 1.6 %collective-permute-start.18 = (bf16[32,4224]{1,0:T(8,128)(2,1)S(1)}, bf16[32,4224]{1,0:T(8,128)(2,1)S(1)}, u32[]{:S(2)}, u32[]{:S(2)}) collective-permute-start(bf16[32,4224]{1,0:T(8,128)(2,1)S(1)} %constant_dynamic-update-slice_fusion.refs_1_), channel_id=1, source_target_pairs={{0,2},{1,3},{2,0},{3,1},{4,6},{5,7},{6,4},{7,5},{8,10},{9,11},{10,... | collective-permute-start | bytes 811016 | tf_op jit(solution)/shard_map/ppermute | solution.py:235
  15.9 1.5 %collective-permute-start.19 = (bf16[32,4224]{1,0:T(8,128)(2,1)S(1)}, bf16[32,4224]{1,0:T(8,128)(2,1)S(1)}, u32[]{:S(2)}, u32[]{:S(2)}) collective-permute-start(bf16[32,4224]{1,0:T(8,128)(2,1)S(1)} %constant_dynamic-update-slice_fusion.refs_1_), channel_id=1, source_target_pairs={{0,4},{1,5},{2,6},{3,7},{4,0},{5,1},{6,2},{7,3},{8,12},{9,13},{10,... | collective-permute-start | bytes 811016 | tf_op jit(solution)/shard_map/ppermute | solution.py:235
  18.0 3.2 %collective-permute-done.18.refs_2_ = bf16[32,4224]{1,0:T(8,128)(2,1)S(1)} collective-permute-done((bf16[32,4224]{1,0:T(8,128)(2,1)S(1)}, bf16[32,4224]{1,0:T(8,128)(2,1)S(1)}, u32[]{:S(2)}, u32[]{:S(2)}) %collective-permute-start.18) | collective-permute-done | bytes 270368 | tf_op jit(solution)/shard_map/ppermute | solution.py:235
  21.2 1.6 %collective-permute-start.20 = (bf16[16,4224]{1,0:T(8,128)(2,1)S(1)}, bf16[16,4224]{1,0:T(8,128)(2,1)S(1)}, u32[]{:S(2)}, u32[]{:S(2)}) collective-permute-start(bf16[16,4224]{1,0:T(8,128)(2,1)S(1)} %slice.124), channel_id=1, source_target_pairs={{0,4},{1,5},{2,6},{3,7},{4,0},{5,1},{6,2},{7,3},{8,12},{9,13},{10,... | collective-permute-start | bytes 405512 | tf_op jit(solution)/shard_map/ppermute | solution.py:235
  24.9 1.4 %collective-permute-done.20.refs_4_ = bf16[16,4224]{1,0:T(8,128)(2,1)S(1)} collective-permute-done((bf16[16,4224]{1,0:T(8,128)(2,1)S(1)}, bf16[16,4224]{1,0:T(8,128)(2,1)S(1)}, u32[]{:S(2)}, u32[]{:S(2)}) %collective-permute-start.20) | collective-permute-done | bytes 135200 | tf_op jit(solution)/shard_map/ppermute | solution.py:235
  26.3 2.2 %collective-permute-done.21.refs_5_ = bf16[16,4224]{1,0:T(8,128)(2,1)S(1)} collective-permute-done((bf16[16,4224]{1,0:T(8,128)(2,1)S(1)}, bf16[16,4224]{1,0:T(8,128)(2,1)S(1)}, u32[]{:S(2)}, u32[]{:S(2)}) %collective-permute-start.21) | collective-permute-done | bytes 135200 | tf_op jit(solution)/shard_map/ppermute | solution.py:235
  30.5 2.8 %copy-done = bf16[2,384,4096]{2,1,0:T(8,128)(2,1)S(1)} copy-done((bf16[2,384,4096]{2,1,0:T(8,128)(2,1)S(1)}, bf16[2,384,4096]{2,1,0:T(8,128)(2,1)}, u32[]{:S(2)}) %copy-start) | copy-done | bytes 6291480
  33.3 2.8 %copy-done.2 = bf16[2,384,4096]{2,1,0:T(8,128)(2,1)S(1)} copy-done((bf16[2,384,4096]{2,1,0:T(8,128)(2,1)S(1)}, bf16[2,384,4096]{2,1,0:T(8,128)(2,1)}, u32[]{:S(2)}) %copy-start.2) | copy-done | bytes 6291480
  36.0 2.8 %copy-done.4 = bf16[2,384,4096]{2,1,0:T(8,128)(2,1)S(1)} copy-done((bf16[2,384,4096]{2,1,0:T(8,128)(2,1)S(1)}, bf16[2,384,4096]{2,1,0:T(8,128)(2,1)}, u32[]{:S(2)}) %copy-start.4) | copy-done | bytes 6291480
  38.8 10.4 %experts.3 = (bf16[32,4096]{1,0:T(8,128)(2,1)S(1)}, bf16[32,4096]{1,0:T(8,128)(2,1)S(1)}, bf16[32,4096]{1,0:T(8,128)(2,1)S(1)}, bf16[16,4096]{1,0:T(8,128)(2,1)S...) custom-call(s32[1]{0:T(128)} %bitcast.refs_0_, ...), custom_call_target="tpu_custom_call" | custom-call | flops 4831838208 | bytes 23068672 | tf_op jit(solution)/shard_map/experts/pallas_call | solution.py:171
  49.6 1.4 %collective-permute-start.3 = (bf16[16,4224]{1,0:T(8,128)(2,1)S(1)}, bf16[16,4224]{1,0:T(8,128)(2,1)S(1)}, u32[]{:S(2)}, u32[]{:S(2)}) collective-permute-start(bf16[16,4224]{1,0:T(8,128)(2,1)S(1)} %slice.112), channel_id=1, source_target_pairs={{0,4},{1,5},{2,6},{3,7},{4,0},{5,1},{6,2},{7,3},{8,12},{9,13},{10,... | collective-permute-start | bytes 405512 | tf_op jit(solution)/shard_map/ppermute | solution.py:235
  51.6 1.2 %collective-permute-start.4 = (bf16[16,4224]{1,0:T(8,128)(2,1)S(1)}, bf16[16,4224]{1,0:T(8,128)(2,1)S(1)}, u32[]{:S(2)}, u32[]{:S(2)}) collective-permute-start(bf16[16,4224]{1,0:T(8,128)(2,1)S(1)} %slice.113), channel_id=1, source_target_pairs={{0,2},{1,3},{2,0},{3,1},{4,6},{5,7},{6,4},{7,5},{8,10},{9,11},{10,... | collective-permute-start | bytes 405512 | tf_op jit(solution)/shard_map/ppermute | solution.py:235
  52.7 2.7 %collective-permute-done.3.refs_4_ = bf16[16,4224]{1,0:T(8,128)(2,1)S(1)} collective-permute-done((bf16[16,4224]{1,0:T(8,128)(2,1)S(1)}, bf16[16,4224]{1,0:T(8,128)(2,1)S(1)}, u32[]{:S(2)}, u32[]{:S(2)}) %collective-permute-start.3) | collective-permute-done | bytes 135200 | tf_op jit(solution)/shard_map/ppermute | solution.py:235
  55.4 1.7 %collective-permute-done.4.refs_5_ = bf16[16,4224]{1,0:T(8,128)(2,1)S(1)} collective-permute-done((bf16[16,4224]{1,0:T(8,128)(2,1)S(1)}, bf16[16,4224]{1,0:T(8,128)(2,1)S(1)}, u32[]{:S(2)}, u32[]{:S(2)}) %collective-permute-start.4) | collective-permute-done | bytes 135200 | tf_op jit(solution)/shard_map/ppermute | solution.py:235
  57.2 1.3 %collective-permute-done.9.refs_10_ = bf16[16,4224]{1,0:T(8,128)(2,1)S(1)} collective-permute-done((bf16[16,4224]{1,0:T(8,128)(2,1)S(1)}, bf16[16,4224]{1,0:T(8,128)(2,1)S(1)}, u32[]{:S(2)}, u32[]{:S(2)}) %collective-permute-start.9) | collective-permute-done | bytes 135200 | tf_op jit(solution)/shard_map/ppermute | solution.py:235
  58.5 10.4 %experts.2 = (bf16[32,4096]{1,0:T(8,128)(2,1)S(1)}, bf16[32,4096]{1,0:T(8,128)(2,1)S(1)}, bf16[32,4096]{1,0:T(8,128)(2,1)S(1)}, bf16[16,4096]{1,0:T(8,128)(2,1)S...) custom-call(s32[1]{0:T(128)} %bitcast.refs_0_, bf16[32,4224]{1,0:T(8,128)(2,1)S(1)} %pad_maximum_fusion.refs_1_, ...), custom_call_target="tpu_custom_call" | custom-call | flops 4831838208 | bytes 23068672 | tf_op jit(solution)/shard_map/experts/pallas_call | solution.py:171
  69.3 1.0 %collective-permute-start.28 = (bf16[32,4096]{1,0:T(8,128)(2,1)S(1)}, bf16[32,4096]{1,0:T(8,128)(2,1)S(1)}, u32[]{:S(2)}, u32[]{:S(2)}) collective-permute-start(bf16[32,4096]{1,0:T(8,128)(2,1)S(1)} %get-tuple-element.37), channel_id=1, source_target_pairs={{0,4},{1,5},{2,6},{3,7},{4,0},{5,1},{6,2},{7,3},{8,12},{9,13},{10,... | collective-permute-start | bytes 786440 | tf_op jit(solution)/shard_map/ppermute | solution.py:235
  70.3 1.7 %collective-permute-start.31 = (bf16[32,4096]{1,0:T(8,128)(2,1)S(1)}, bf16[32,4096]{1,0:T(8,128)(2,1)S(1)}, u32[]{:S(2)}, u32[]{:S(2)}) collective-permute-start(bf16[32,4096]{1,0:T(8,128)(2,1)S(1)} %get-tuple-element.38), channel_id=1, source_target_pairs={{0,2},{1,3},{2,0},{3,1},{4,6},{5,7},{6,4},{7,5},{8,10},{9,11},{10,... | collective-permute-start | bytes 786440 | tf_op jit(solution)/shard_map/ppermute | solution.py:235
  72.8 1.7 %collective-permute-start.13 = (bf16[32,4096]{1,0:T(8,128)(2,1)S(1)}, bf16[32,4096]{1,0:T(8,128)(2,1)S(1)}, u32[]{:S(2)}, u32[]{:S(2)}) collective-permute-start(bf16[32,4096]{1,0:T(8,128)(2,1)S(1)} %get-tuple-element.34), channel_id=1, source_target_pairs={{0,2},{1,3},{2,0},{3,1},{4,6},{5,7},{6,4},{7,5},{8,10},{9,11},{10,... | collective-permute-start | bytes 786440 | tf_op jit(solution)/shard_map/ppermute | solution.py:235
  74.5 3.9 %collective-permute-done.28 = bf16[32,4096]{1,0:T(8,128)(2,1)S(1)} collective-permute-done((bf16[32,4096]{1,0:T(8,128)(2,1)S(1)}, bf16[32,4096]{1,0:T(8,128)(2,1)S(1)}, u32[]{:S(2)}, u32[]{:S(2)}) %collective-permute-start.28) | collective-permute-done | bytes 262176 | tf_op jit(solution)/shard_map/ppermute | solution.py:235
  79.5 1.8 %collective-permute-start.29 = (bf16[16,4096]{1,0:T(8,128)(2,1)S(1)}, bf16[16,4096]{1,0:T(8,128)(2,1)S(1)}, u32[]{:S(2)}, u32[]{:S(2)}) collective-permute-start(bf16[16,4096]{1,0:T(8,128)(2,1)S(1)} %get-tuple-element.35), channel_id=1, source_target_pairs={{0,2},{1,3},{2,0},{3,1},{4,6},{5,7},{6,4},{7,5},{8,10},{9,11},{10,... | collective-permute-start | bytes 393224 | tf_op jit(solution)/shard_map/ppermute | solution.py:235
  81.9 2.2 %collective-permute-done.11 = bf16[32,4096]{1,0:T(8,128)(2,1)S(1)} collective-permute-done((bf16[32,4096]{1,0:T(8,128)(2,1)S(1)}, bf16[32,4096]{1,0:T(8,128)(2,1)S(1)}, u32[]{:S(2)}, u32[]{:S(2)}) %collective-permute-start.11) | collective-permute-done | bytes 262176 | tf_op jit(solution)/shard_map/ppermute | solution.py:235
  85.2 1.2 %collective-permute-start.14 = (bf16[16,4096]{1,0:T(8,128)(2,1)S(1)}, bf16[16,4096]{1,0:T(8,128)(2,1)S(1)}, u32[]{:S(2)}, u32[]{:S(2)}) collective-permute-start(bf16[16,4096]{1,0:T(8,128)(2,1)S(1)} %get-tuple-element.32), channel_id=1, source_target_pairs={{0,4},{1,5},{2,6},{3,7},{4,0},{5,1},{6,2},{7,3},{8,12},{9,13},{10,... | collective-permute-start | bytes 393224 | tf_op jit(solution)/shard_map/ppermute | solution.py:235
  86.3 1.2 %collective-permute-start.12 = (bf16[16,4096]{1,0:T(8,128)(2,1)S(1)}, bf16[16,4096]{1,0:T(8,128)(2,1)S(1)}, u32[]{:S(2)}, u32[]{:S(2)}) collective-permute-start(bf16[16,4096]{1,0:T(8,128)(2,1)S(1)} %get-tuple-element.31), channel_id=1, source_target_pairs={{0,2},{1,3},{2,0},{3,1},{4,6},{5,7},{6,4},{7,5},{8,10},{9,11},{10,... | collective-permute-start | bytes 393224 | tf_op jit(solution)/shard_map/ppermute | solution.py:235
  87.6 2.0 %collective-permute-start.33 = (bf16[16,4096]{1,0:T(8,128)(2,1)S(1)}, bf16[16,4096]{1,0:T(8,128)(2,1)S(1)}, u32[]{:S(2)}, u32[]{:S(2)}) collective-permute-start(bf16[16,4096]{1,0:T(8,128)(2,1)S(1)} %get-tuple-element.30), channel_id=1, source_target_pairs={{0,24},{8,0},{16,8},{24,16},{1,25},{9,1},{17,9},{25,17},{2,26},{10... | collective-permute-start | bytes 393224 | tf_op jit(solution)/shard_map/ppermute | solution.py:240
  90.3 1.2 %collective-permute-start.15 = (bf16[16,4096]{1,0:T(8,128)(2,1)S(1)}, bf16[16,4096]{1,0:T(8,128)(2,1)S(1)}, u32[]{:S(2)}, u32[]{:S(2)}) collective-permute-start(bf16[16,4096]{1,0:T(8,128)(2,1)S(1)} %add_convert_fusion.9), channel_id=1, source_target_pairs={{0,16},{8,24},{16,0},{24,8},{1,17},{9,25},{17,1},{25,9},{2,18},{10... | collective-permute-start | bytes 393224 | tf_op jit(solution)/shard_map/ppermute | solution.py:240
  91.5 3.4 %collective-permute-done.33 = bf16[16,4096]{1,0:T(8,128)(2,1)S(1)} collective-permute-done((bf16[16,4096]{1,0:T(8,128)(2,1)S(1)}, bf16[16,4096]{1,0:T(8,128)(2,1)S(1)}, u32[]{:S(2)}, u32[]{:S(2)}) %collective-permute-start.33) | collective-permute-done | bytes 131104 | tf_op jit(solution)/shard_map/ppermute | solution.py:240
  94.9 2.4 %collective-permute-done.30 = bf16[16,4096]{1,0:T(8,128)(2,1)S(1)} collective-permute-done((bf16[16,4096]{1,0:T(8,128)(2,1)S(1)}, bf16[16,4096]{1,0:T(8,128)(2,1)S(1)}, u32[]{:S(2)}, u32[]{:S(2)}) %collective-permute-start.30) | collective-permute-done | bytes 131104 | tf_op jit(solution)/shard_map/ppermute | solution.py:240
  97.2 4.3 %collective-permute-done.15 = bf16[16,4096]{1,0:T(8,128)(2,1)S(1)} collective-permute-done((bf16[16,4096]{1,0:T(8,128)(2,1)S(1)}, bf16[16,4096]{1,0:T(8,128)(2,1)S(1)}, u32[]{:S(2)}, u32[]{:S(2)}) %collective-permute-start.15) | collective-permute-done | bytes 131104 | tf_op jit(solution)/shard_map/ppermute | solution.py:240
  (71 shorter events, 13.3 us)
Async XLA Ops:
  2.5 9.0 %collective-permute-start.16 = (bf16[16,4224]{1,0:T(8,128)(2,1)S(1)}, bf16[16,4224]{1,0:T(8,128)(2,1)S(1)}, u32[]{:S(2)}, u32[]{:S(2)}) collective-permute-start(bf16[16,4224]{1,0:T(8,128)(2,1)S(1)} %pack.1), channel_id=1, source_target_pairs={{0,24},{8,0},{16,8},{24,16},{1,25},{9,1},{17,9},{25,17},{2,26},{10... | collective-permute-start | bytes 405512 | tf_op jit(solution)/shard_map/ppermute | solution.py:240
  7.5 6.8 %collective-permute-start.17 = (bf16[16,4224]{1,0:T(8,128)(2,1)S(1)}, bf16[16,4224]{1,0:T(8,128)(2,1)S(1)}, u32[]{:S(2)}, u32[]{:S(2)}) collective-permute-start(bf16[16,4224]{1,0:T(8,128)(2,1)S(1)} %pack.1), channel_id=1, source_target_pairs={{0,8},{8,16},{16,24},{24,0},{1,9},{9,17},{17,25},{25,1},{2,10},{10... | collective-permute-start | bytes 405512 | tf_op jit(solution)/shard_map/ppermute | solution.py:240
  14.4 6.8 %collective-permute-start.18 = (bf16[32,4224]{1,0:T(8,128)(2,1)S(1)}, bf16[32,4224]{1,0:T(8,128)(2,1)S(1)}, u32[]{:S(2)}, u32[]{:S(2)}) collective-permute-start(bf16[32,4224]{1,0:T(8,128)(2,1)S(1)} %constant_dynamic-update-slice_fusion.refs_1_), channel_id=1, source_target_pairs={{0,2},{1,3},{2,0},{3,1},{4,6},{5,7},{6,4},{7,5},{8,10},{9,11},{10,... | collective-permute-start | bytes 811016 | tf_op jit(solution)/shard_map/ppermute | solution.py:235
  15.9 7.5 %collective-permute-start.19 = (bf16[32,4224]{1,0:T(8,128)(2,1)S(1)}, bf16[32,4224]{1,0:T(8,128)(2,1)S(1)}, u32[]{:S(2)}, u32[]{:S(2)}) collective-permute-start(bf16[32,4224]{1,0:T(8,128)(2,1)S(1)} %constant_dynamic-update-slice_fusion.refs_1_), channel_id=1, source_target_pairs={{0,4},{1,5},{2,6},{3,7},{4,0},{5,1},{6,2},{7,3},{8,12},{9,13},{10,... | collective-permute-start | bytes 811016 | tf_op jit(solution)/shard_map/ppermute | solution.py:235
  17.4 7.4 %collective-permute-start = (bf16[16,4224]{1,0:T(8,128)(2,1)S(1)}, bf16[16,4224]{1,0:T(8,128)(2,1)S(1)}, u32[]{:S(2)}, u32[]{:S(2)}) collective-permute-start(bf16[16,4224]{1,0:T(8,128)(2,1)S(1)} %pack.1), channel_id=1, source_target_pairs={{0,16},{8,24},{16,0},{24,8},{1,17},{9,25},{17,1},{25,9},{2,18},{10... | collective-permute-start | bytes 405512 | tf_op jit(solution)/shard_map/ppermute | solution.py:240
  21.2 5.1 %collective-permute-start.20 = (bf16[16,4224]{1,0:T(8,128)(2,1)S(1)}, bf16[16,4224]{1,0:T(8,128)(2,1)S(1)}, u32[]{:S(2)}, u32[]{:S(2)}) collective-permute-start(bf16[16,4224]{1,0:T(8,128)(2,1)S(1)} %slice.124), channel_id=1, source_target_pairs={{0,4},{1,5},{2,6},{3,7},{4,0},{5,1},{6,2},{7,3},{8,12},{9,13},{10,... | collective-permute-start | bytes 405512 | tf_op jit(solution)/shard_map/ppermute | solution.py:235
  23.4 5.1 %collective-permute-start.21 = (bf16[16,4224]{1,0:T(8,128)(2,1)S(1)}, bf16[16,4224]{1,0:T(8,128)(2,1)S(1)}, u32[]{:S(2)}, u32[]{:S(2)}) collective-permute-start(bf16[16,4224]{1,0:T(8,128)(2,1)S(1)} %slice.125), channel_id=1, source_target_pairs={{0,2},{1,3},{2,0},{3,1},{4,6},{5,7},{6,4},{7,5},{8,10},{9,11},{10,... | collective-permute-start | bytes 405512 | tf_op jit(solution)/shard_map/ppermute | solution.py:235
  24.4 4.2 %collective-permute-start.22 = (bf16[32,4224]{1,0:T(8,128)(2,1)S(1)}, bf16[32,4224]{1,0:T(8,128)(2,1)S(1)}, u32[]{:S(2)}, u32[]{:S(2)}) collective-permute-start(bf16[32,4224]{1,0:T(8,128)(2,1)S(1)} %constant_dynamic-update-slice_fusion.refs_1_), channel_id=1, source_target_pairs={{0,1},{1,0},{2,3},{3,2},{4,5},{5,4},{6,7},{7,6},{8,9},{9,8},{10,11... | collective-permute-start | bytes 811016 | tf_op jit(solution)/shard_map/ppermute | solution.py:235
  24.4 5.1 %collective-permute-start.23 = (bf16[32,4224]{1,0:T(8,128)(2,1)S(1)}, bf16[32,4224]{1,0:T(8,128)(2,1)S(1)}, u32[]{:S(2)}, u32[]{:S(2)}) collective-permute-start(bf16[32,4224]{1,0:T(8,128)(2,1)S(1)} %collective-permute-done.18.refs_2_), channel_id=1, source_target_pairs={{0,1},{1,0},{2,3},{3,2},{4,5},{5,4},{6,7},{7,6},{8,9},{9,8},{10,11... | collective-permute-start | bytes 811016 | tf_op jit(solution)/shard_map/ppermute | solution.py:235
  24.9 5.4 %collective-permute-start.24 = (bf16[32,4224]{1,0:T(8,128)(2,1)S(1)}, bf16[32,4224]{1,0:T(8,128)(2,1)S(1)}, u32[]{:S(2)}, u32[]{:S(2)}) collective-permute-start(bf16[32,4224]{1,0:T(8,128)(2,1)S(1)} %collective-permute-done.19.refs_3_), channel_id=1, source_target_pairs={{0,1},{1,0},{2,3},{3,2},{4,5},{5,4},{6,7},{7,6},{8,9},{9,8},{10,11... | collective-permute-start | bytes 811016 | tf_op jit(solution)/shard_map/ppermute | solution.py:235
  26.3 4.2 %collective-permute-start.25 = (bf16[16,4224]{1,0:T(8,128)(2,1)S(1)}, bf16[16,4224]{1,0:T(8,128)(2,1)S(1)}, u32[]{:S(2)}, u32[]{:S(2)}) collective-permute-start(bf16[16,4224]{1,0:T(8,128)(2,1)S(1)} %collective-permute-done.20.refs_4_), channel_id=1, source_target_pairs={{0,1},{1,0},{2,3},{3,2},{4,5},{5,4},{6,7},{7,6},{8,9},{9,8},{10,11... | collective-permute-start | bytes 405512 | tf_op jit(solution)/shard_map/ppermute | solution.py:235
  28.5 2.0 %collective-permute-start.26 = (bf16[16,4224]{1,0:T(8,128)(2,1)S(1)}, bf16[16,4224]{1,0:T(8,128)(2,1)S(1)}, u32[]{:S(2)}, u32[]{:S(2)}) collective-permute-start(bf16[16,4224]{1,0:T(8,128)(2,1)S(1)} %collective-permute-done.21.refs_5_), channel_id=1, source_target_pairs={{0,1},{1,0},{2,3},{3,2},{4,5},{5,4},{6,7},{7,6},{8,9},{9,8},{10,11... | collective-permute-start | bytes 405512 | tf_op jit(solution)/shard_map/ppermute | solution.py:235
  28.5 21.0 %collective-permute-start.1 = (bf16[32,4224]{1,0:T(8,128)(2,1)S(1)}, bf16[32,4224]{1,0:T(8,128)(2,1)S(1)}, u32[]{:S(2)}, u32[]{:S(2)}) collective-permute-start(bf16[32,4224]{1,0:T(8,128)(2,1)S(1)} %pad_maximum_fusion.refs_1_), channel_id=1, source_target_pairs={{0,2},{1,3},{2,0},{3,1},{4,6},{5,7},{6,4},{7,5},{8,10},{9,11},{10,... | collective-permute-start | bytes 811016 | tf_op jit(solution)/shard_map/ppermute | solution.py:235
  29.5 21.5 %collective-permute-start.2 = (bf16[32,4224]{1,0:T(8,128)(2,1)S(1)}, bf16[32,4224]{1,0:T(8,128)(2,1)S(1)}, u32[]{:S(2)}, u32[]{:S(2)}) collective-permute-start(bf16[32,4224]{1,0:T(8,128)(2,1)S(1)} %pad_maximum_fusion.refs_1_), channel_id=1, source_target_pairs={{0,4},{1,5},{2,6},{3,7},{4,0},{5,1},{6,2},{7,3},{8,12},{9,13},{10,... | collective-permute-start | bytes 811016 | tf_op jit(solution)/shard_map/ppermute | solution.py:235
  30.2 21.3 %collective-permute-start.5 = (bf16[32,4224]{1,0:T(8,128)(2,1)S(1)}, bf16[32,4224]{1,0:T(8,128)(2,1)S(1)}, u32[]{:S(2)}, u32[]{:S(2)}) collective-permute-start(bf16[32,4224]{1,0:T(8,128)(2,1)S(1)} %pad_maximum_fusion.refs_1_), channel_id=1, source_target_pairs={{0,1},{1,0},{2,3},{3,2},{4,5},{5,4},{6,7},{7,6},{8,9},{9,8},{10,11... | collective-permute-start | bytes 811016 | tf_op jit(solution)/shard_map/ppermute | solution.py:235
  49.2 19.9 %collective-permute-start.27 = (bf16[128,4096]{1,0:T(8,128)(2,1)S(1)}, bf16[128,4096]{1,0:T(8,128)(2,1)S(1)}, u32[]{:S(2)}, u32[]{:S(2)}) collective-permute-start(bf16[128,4096]{1,0:T(8,128)(2,1)S(1)} %get-tuple-element.24), channel_id=1, source_target_pairs={{0,1},{1,0},{2,3},{3,2},{4,5},{5,4},{6,7},{7,6},{8,9},{9,8},{10,11... | collective-permute-start | bytes 3145736 | tf_op jit(solution)/shard_map/ppermute | solution.py:235
  49.6 5.8 %collective-permute-start.3 = (bf16[16,4224]{1,0:T(8,128)(2,1)S(1)}, bf16[16,4224]{1,0:T(8,128)(2,1)S(1)}, u32[]{:S(2)}, u32[]{:S(2)}) collective-permute-start(bf16[16,4224]{1,0:T(8,128)(2,1)S(1)} %slice.112), channel_id=1, source_target_pairs={{0,4},{1,5},{2,6},{3,7},{4,0},{5,1},{6,2},{7,3},{8,12},{9,13},{10,... | collective-permute-start | bytes 405512 | tf_op jit(solution)/shard_map/ppermute | solution.py:235
  51.0 6.2 %collective-permute-start.6 = (bf16[32,4224]{1,0:T(8,128)(2,1)S(1)}, bf16[32,4224]{1,0:T(8,128)(2,1)S(1)}, u32[]{:S(2)}, u32[]{:S(2)}) collective-permute-start(bf16[32,4224]{1,0:T(8,128)(2,1)S(1)} %collective-permute-done.1.refs_2_), channel_id=1, source_target_pairs={{0,1},{1,0},{2,3},{3,2},{4,5},{5,4},{6,7},{7,6},{8,9},{9,8},{10,11... | collective-permute-start | bytes 811016 | tf_op jit(solution)/shard_map/ppermute | solution.py:235
  51.0 6.2 %collective-permute-start.7 = (bf16[32,4224]{1,0:T(8,128)(2,1)S(1)}, bf16[32,4224]{1,0:T(8,128)(2,1)S(1)}, u32[]{:S(2)}, u32[]{:S(2)}) collective-permute-start(bf16[32,4224]{1,0:T(8,128)(2,1)S(1)} %collective-permute-done.2.refs_3_), channel_id=1, source_target_pairs={{0,1},{1,0},{2,3},{3,2},{4,5},{5,4},{6,7},{7,6},{8,9},{9,8},{10,11... | collective-permute-start | bytes 811016 | tf_op jit(solution)/shard_map/ppermute | solution.py:235
  51.6 5.6 %collective-permute-start.4 = (bf16[16,4224]{1,0:T(8,128)(2,1)S(1)}, bf16[16,4224]{1,0:T(8,128)(2,1)S(1)}, u32[]{:S(2)}, u32[]{:S(2)}) collective-permute-start(bf16[16,4224]{1,0:T(8,128)(2,1)S(1)} %slice.113), channel_id=1, source_target_pairs={{0,2},{1,3},{2,0},{3,1},{4,6},{5,7},{6,4},{7,5},{8,10},{9,11},{10,... | collective-permute-start | bytes 405512 | tf_op jit(solution)/shard_map/ppermute | solution.py:235
  68.9 3.1 %collective-permute-start.10 = (bf16[128,4096]{1,0:T(8,128)(2,1)S(1)}, bf16[128,4096]{1,0:T(8,128)(2,1)S(1)}, u32[]{:S(2)}, u32[]{:S(2)}) collective-permute-start(bf16[128,4096]{1,0:T(8,128)(2,1)S(1)} %get-tuple-element.18), channel_id=1, source_target_pairs={{0,1},{1,0},{2,3},{3,2},{4,5},{5,4},{6,7},{7,6},{8,9},{9,8},{10,11... | collective-permute-start | bytes 3145736 | tf_op jit(solution)/shard_map/ppermute | solution.py:235
  69.3 9.2 %collective-permute-start.28 = (bf16[32,4096]{1,0:T(8,128)(2,1)S(1)}, bf16[32,4096]{1,0:T(8,128)(2,1)S(1)}, u32[]{:S(2)}, u32[]{:S(2)}) collective-permute-start(bf16[32,4096]{1,0:T(8,128)(2,1)S(1)} %get-tuple-element.37), channel_id=1, source_target_pairs={{0,4},{1,5},{2,6},{3,7},{4,0},{5,1},{6,2},{7,3},{8,12},{9,13},{10,... | collective-permute-start | bytes 786440 | tf_op jit(solution)/shard_map/ppermute | solution.py:235
  70.3 9.2 %collective-permute-start.31 = (bf16[32,4096]{1,0:T(8,128)(2,1)S(1)}, bf16[32,4096]{1,0:T(8,128)(2,1)S(1)}, u32[]{:S(2)}, u32[]{:S(2)}) collective-permute-start(bf16[32,4096]{1,0:T(8,128)(2,1)S(1)} %get-tuple-element.38), channel_id=1, source_target_pairs={{0,2},{1,3},{2,0},{3,1},{4,6},{5,7},{6,4},{7,5},{8,10},{9,11},{10,... | collective-permute-start | bytes 786440 | tf_op jit(solution)/shard_map/ppermute | solution.py:235
  72.2 11.9 %collective-permute-start.11 = (bf16[32,4096]{1,0:T(8,128)(2,1)S(1)}, bf16[32,4096]{1,0:T(8,128)(2,1)S(1)}, u32[]{:S(2)}, u32[]{:S(2)}) collective-permute-start(bf16[32,4096]{1,0:T(8,128)(2,1)S(1)} %get-tuple-element.33), channel_id=1, source_target_pairs={{0,4},{1,5},{2,6},{3,7},{4,0},{5,1},{6,2},{7,3},{8,12},{9,13},{10,... | collective-permute-start | bytes 786440 | tf_op jit(solution)/shard_map/ppermute | solution.py:235
  72.8 12.3 %collective-permute-start.13 = (bf16[32,4096]{1,0:T(8,128)(2,1)S(1)}, bf16[32,4096]{1,0:T(8,128)(2,1)S(1)}, u32[]{:S(2)}, u32[]{:S(2)}) collective-permute-start(bf16[32,4096]{1,0:T(8,128)(2,1)S(1)} %get-tuple-element.34), channel_id=1, source_target_pairs={{0,2},{1,3},{2,0},{3,1},{4,6},{5,7},{6,4},{7,5},{8,10},{9,11},{10,... | collective-permute-start | bytes 786440 | tf_op jit(solution)/shard_map/ppermute | solution.py:235
  79.5 7.9 %collective-permute-start.29 = (bf16[16,4096]{1,0:T(8,128)(2,1)S(1)}, bf16[16,4096]{1,0:T(8,128)(2,1)S(1)}, u32[]{:S(2)}, u32[]{:S(2)}) collective-permute-start(bf16[16,4096]{1,0:T(8,128)(2,1)S(1)} %get-tuple-element.35), channel_id=1, source_target_pairs={{0,2},{1,3},{2,0},{3,1},{4,6},{5,7},{6,4},{7,5},{8,10},{9,11},{10,... | collective-permute-start | bytes 393224 | tf_op jit(solution)/shard_map/ppermute | solution.py:235
  81.4 6.1 %collective-permute-start.32 = (bf16[16,4096]{1,0:T(8,128)(2,1)S(1)}, bf16[16,4096]{1,0:T(8,128)(2,1)S(1)}, u32[]{:S(2)}, u32[]{:S(2)}) collective-permute-start(bf16[16,4096]{1,0:T(8,128)(2,1)S(1)} %get-tuple-element.36), channel_id=1, source_target_pairs={{0,4},{1,5},{2,6},{3,7},{4,0},{5,1},{6,2},{7,3},{8,12},{9,13},{10,... | collective-permute-start | bytes 393224 | tf_op jit(solution)/shard_map/ppermute | solution.py:235
  85.2 5.0 %collective-permute-start.14 = (bf16[16,4096]{1,0:T(8,128)(2,1)S(1)}, bf16[16,4096]{1,0:T(8,128)(2,1)S(1)}, u32[]{:S(2)}, u32[]{:S(2)}) collective-permute-start(bf16[16,4096]{1,0:T(8,128)(2,1)S(1)} %get-tuple-element.32), channel_id=1, source_target_pairs={{0,4},{1,5},{2,6},{3,7},{4,0},{5,1},{6,2},{7,3},{8,12},{9,13},{10,... | collective-permute-start | bytes 393224 | tf_op jit(solution)/shard_map/ppermute | solution.py:235
  86.3 5.2 %collective-permute-start.12 = (bf16[16,4096]{1,0:T(8,128)(2,1)S(1)}, bf16[16,4096]{1,0:T(8,128)(2,1)S(1)}, u32[]{:S(2)}, u32[]{:S(2)}) collective-permute-start(bf16[16,4096]{1,0:T(8,128)(2,1)S(1)} %get-tuple-element.31), channel_id=1, source_target_pairs={{0,2},{1,3},{2,0},{3,1},{4,6},{5,7},{6,4},{7,5},{8,10},{9,11},{10,... | collective-permute-start | bytes 393224 | tf_op jit(solution)/shard_map/ppermute | solution.py:235
  87.6 7.2 %collective-permute-start.33 = (bf16[16,4096]{1,0:T(8,128)(2,1)S(1)}, bf16[16,4096]{1,0:T(8,128)(2,1)S(1)}, u32[]{:S(2)}, u32[]{:S(2)}) collective-permute-start(bf16[16,4096]{1,0:T(8,128)(2,1)S(1)} %get-tuple-element.30), channel_id=1, source_target_pairs={{0,24},{8,0},{16,8},{24,16},{1,25},{9,1},{17,9},{25,17},{2,26},{10... | collective-permute-start | bytes 393224 | tf_op jit(solution)/shard_map/ppermute | solution.py:240
  89.6 7.6 %collective-permute-start.30 = (bf16[16,4096]{1,0:T(8,128)(2,1)S(1)}, bf16[16,4096]{1,0:T(8,128)(2,1)S(1)}, u32[]{:S(2)}, u32[]{:S(2)}) collective-permute-start(bf16[16,4096]{1,0:T(8,128)(2,1)S(1)} %get-tuple-element.29), channel_id=1, source_target_pairs={{0,8},{8,16},{16,24},{24,0},{1,9},{9,17},{17,25},{25,1},{2,10},{10... | collective-permute-start | bytes 393224 | tf_op jit(solution)/shard_map/ppermute | solution.py:240
  90.3 11.3 %collective-permute-start.15 = (bf16[16,4096]{1,0:T(8,128)(2,1)S(1)}, bf16[16,4096]{1,0:T(8,128)(2,1)S(1)}, u32[]{:S(2)}, u32[]{:S(2)}) collective-permute-start(bf16[16,4096]{1,0:T(8,128)(2,1)S(1)} %add_convert_fusion.9), channel_id=1, source_target_pairs={{0,16},{8,24},{16,0},{24,8},{1,17},{9,25},{17,1},{25,9},{2,18},{10... | collective-permute-start | bytes 393224 | tf_op jit(solution)/shard_map/ppermute | solution.py:240
  (11 other events, 72.8 us)
where the time goes:
time: 103 us; the launch traced here: 102 us
  waiting for transfers between devices  38.8 us (38%)
  starting transfers between devices  30.3 us (29%)
  Pallas kernels  21 us (20%)
  local copies, waits for them, and re-layouts  10.7 us (10%)
  other arithmetic  1.44 us (1%)
    ppermute x28, waiting for transfers between devices, swap_exp(): return lax.ppermute(value, 'exp', [(i, i ^ bit) for i in range(owners)])  21.9 us
    ppermute x28, starting transfers between devices, swap_exp(): return lax.ppermute(value, 'exp', [(i, i ^ bit) for i in range(owners)])  21.4 us
    pallas_call x2, Pallas kernels, experts_of(): pl.pallas_call(kernel, out_shape=[jax.ShapeDtypeStruct((count, model_widt...  20.8 us
    ppermute x6, waiting for transfers between devices, turn_rep(): lax.ppermute(value, 'rep', [(i, (i - shift) % replicas) for i in range(re...  16.9 us
    unnamed x19, local copies, waits for them, and re-layouts  10.6 us
    ppermute x6, starting transfers between devices, turn_rep(): lax.ppermute(value, 'rep', [(i, (i - shift) % replicas) for i in range(re...  8.89 us
  transfers between devices with their start and end apart: 34, of which 17 were waited for; matrix products, arithmetic and copies ran while one was open for 1% of the time, Pallas kernels for 20%

commit v1 on v0

--- a/solution.py
+++ b/solution.py
@@ -82,121 +82,114 @@
     return summed.reshape(token_rows, model_width).astype(jnp.bfloat16)
 
 
-def expert_kernel(pieces_in, pieces_out, local_experts, shard_units, model_width, top, block, *refs):
+def fetch_kernel(turn, source_ref, result_ref):
+    rows, width = source_ref.shape
+    block = 512
+
+    def fetch_block(step, carry):
+        span = pl.ds(pl.multiple_of(step * block, block), block)
+        if turn:
+            for part in range(0, rows, 128):
+                result_ref[span, part : part + 128] = source_ref[part : part + 128, span].T
+        else:
+            result_ref[:, span] = source_ref[:, span]
+        return carry
+
+    lax.fori_loop(0, width // block, fetch_block, 0)
+
+
+def fetched(weight, turn):
+    rows, width = weight.shape
+    return pl.pallas_call(
+        functools.partial(fetch_kernel, turn),
+        out_shape=jax.ShapeDtypeStruct((width, rows) if turn else (rows, width), jnp.bfloat16),
+        in_specs=[pl.BlockSpec(memory_space=pltpu.VMEM)],
+        out_specs=pl.BlockSpec(memory_space=pltpu.VMEM),
+        compiler_params=pltpu.CompilerParams(vmem_limit_bytes=4 * 1024 * 1024),
+        cost_estimate=pl.CostEstimate(
+            flops=0, bytes_accessed=4 * rows * width, transcendentals=0
+        ),
+        name="fetch_turned" if turn else "fetch",
+    )(weight)
+
+
+def expert_kernel(pieces_in, pieces_out, local_experts, shard_units, model_width, top, *refs):
     own_ref, refs = refs[0], refs[1:]
     ins, refs = refs[: len(pieces_in)], refs[len(pieces_in) :]
     (gate_ref, up_ref, down_ref), refs = refs[:3], refs[3:]
     outs, refs = refs[: len(pieces_out)], refs[len(pieces_out) :]
-    rows, turned, hidden, result, row_sem, out_sem = refs
+    rows, hidden = refs
     units = local_experts * shard_units
-    unit_block = shard_units
-    unit_blocks = local_experts
-    column_blocks = model_width // block
-    total = rows.shape[0]
-
-    row_copies, start = [], 0
+    unit_block = 256 if units % 256 == 0 else 128
+    block = 512
+
+    start = 0
     for place, count in enumerate(pieces_in):
-        row_copies.append(
-            pltpu.make_async_copy(ins[place], rows.at[pl.ds(start, count)], row_sem.at[place])
-        )
+        rows[start : start + count, :] = ins[place][...]
         start += count
 
-    for copy in row_copies:
-        copy.start()
-    for copy in row_copies:
-        copy.wait()
-
-    turned[...] = rows[...].T
-    extra = turned[model_width:, :].astype(jnp.float32)
-    scale = extra[top : 2 * top] + extra[2 * top : 3 * top]
+    extra = rows[:, model_width:].astype(jnp.float32)
+    width = extra.shape[1]
+    scale = pltpu.roll(extra, width - top, 1) + pltpu.roll(extra, width - 2 * top, 1)
+    lane = lax.broadcasted_iota(jnp.int32, extra.shape, 1)
     weights = []
     for expert in range(local_experts):
         name = (own_ref[0] + expert).astype(jnp.float32)
-        weights.append(jnp.sum(jnp.where(extra[:top] == name, scale, 0.0), axis=0, keepdims=True))
-
-    values = turned[:model_width, :]
-    for expert in range(local_experts):
-        span = pl.ds(expert * shard_units, shard_units)
-        gate = jnp.dot(gate_ref[span, :], values, preferred_element_type=jnp.float32)
-        up = jnp.dot(up_ref[span, :], values, preferred_element_type=jnp.float32)
-        active = gate / (1.0 + jnp.exp(-gate)) * up * weights[expert]
-        hidden[:, span] = active.astype(jnp.bfloat16).T
-
-    def out_copies(step):
-        span = pl.ds(pl.multiple_of(step * block, block), block)
-        copies = []
+        chosen = jnp.logical_and(lane < top, extra == name)
+        weights.append(jnp.sum(jnp.where(chosen, scale, 0.0), axis=1, keepdims=True))
+
+    for begin in range(0, units, unit_block):
+        span = slice(begin, begin + unit_block)
+        values = rows[:, :model_width]
+        gate = jnp.dot(values, gate_ref[:, span], preferred_element_type=jnp.float32)
+        up = jnp.dot(values, up_ref[:, span], preferred_element_type=jnp.float32)
+        unit = begin + lax.broadcasted_iota(jnp.int32, gate.shape, 1)
+        weight = weights[begin // shard_units]
+        for expert in range(begin // shard_units + 1, (begin + unit_block - 1) // shard_units + 1):
+            weight = jnp.where(unit >= expert * shard_units, weights[expert], weight)
+        active = gate / (1.0 + jnp.exp(-gate)) * up * weight
+        hidden[:, span] = active.astype(jnp.bfloat16)
+
+    for begin in range(0, model_width, block):
+        span = slice(begin, begin + block)
+        value = jnp.dot(hidden[...], down_ref[:, span], preferred_element_type=jnp.float32)
+        value = value.astype(jnp.bfloat16)
         for place, segments in enumerate(pieces_out):
             filled = 0
-            for begin, count in segments:
-                copies.append(
-                    pltpu.make_async_copy(
-                        result.at[pl.ds(begin, count), span],
-                        outs[place].at[pl.ds(filled, count), span],
-                        out_sem.at[step, len(copies)],
-                    )
-                )
+            for first, count in segments:
+                outs[place][filled : filled + count, span] = value[first : first + count]
                 filled += count
-        return copies
-
-    def column_step(step, carry):
-        span = pl.ds(pl.multiple_of(step * block, block), block)
-        value = jnp.dot(hidden[...], down_ref[:, span], preferred_element_type=jnp.float32)
-        result[:, span] = value.astype(jnp.bfloat16)
-        for copy in out_copies(step):
-            copy.start()
-        return carry
-
-    def finish_step(step, carry):
-        for copy in out_copies(step):
-            copy.wait()
-        return carry
-
-    lax.fori_loop(0, column_blocks, column_step, 0)
-    lax.fori_loop(0, column_blocks, finish_step, 0)
-
-
-def experts_of(pieces, pieces_out, gate_weight, up_weight, down_weight, top):
-    local_experts, shard_units, model_width = gate_weight.shape
-    units = local_experts * shard_units
-    block = 512
+
+
+def experts_of(pieces, pieces_out, gates, ups, downs, shard_units, top):
+    units, model_width = downs.shape
+    local_experts = units // shard_units
     pieces_in = [piece.shape[0] for piece in pieces]
     total = sum(pieces_in)
     packed = pieces[0].shape[1]
     own = jnp.full((1,), lax.axis_index("exp") * local_experts, jnp.int32)
-    anywhere = pl.BlockSpec(memory_space=pl.ANY)
+    resident = pl.BlockSpec(memory_space=pltpu.VMEM)
     kernel = functools.partial(
-        expert_kernel, pieces_in, pieces_out, local_experts, shard_units, model_width, top, block
+        expert_kernel, pieces_in, pieces_out, local_experts, shard_units, model_width, top
     )
     out_rows = [sum(count for _, count in segments) for segments in pieces_out]
     return pl.pallas_call(
         kernel,
         out_shape=[jax.ShapeDtypeStruct((count, model_width), jnp.bfloat16) for count in out_rows],
-        in_specs=[pl.BlockSpec(memory_space=pltpu.SMEM)]
-        + [anywhere] * len(pieces)
-        + [pl.BlockSpec(memory_space=pltpu.VMEM)] * 3,
-        out_specs=[anywhere] * len(out_rows),
+        in_specs=[pl.BlockSpec(memory_space=pltpu.SMEM)] + [resident] * (len(pieces) + 3),
+        out_specs=[resident] * len(out_rows),
         scratch_shapes=[
             pltpu.VMEM((total, packed), jnp.bfloat16),
-            pltpu.VMEM((packed, total), jnp.bfloat16),
             pltpu.VMEM((total, units), jnp.bfloat16),
-            pltpu.VMEM((total, model_width), jnp.bfloat16),
-            pltpu.SemaphoreType.DMA((len(pieces),)),
-            pltpu.SemaphoreType.DMA((model_width // block, sum(len(segments) for segments in pieces_out))),
         ],
         compiler_params=pltpu.CompilerParams(vmem_limit_bytes=12 * 1024 * 1024),
         cost_estimate=pl.CostEstimate(
             flops=6 * total * units * model_width,
-            bytes_accessed=6 * units * model_width + 4 * total * model_width,
+            bytes_accessed=4 * total * model_width,
             transcendentals=total * units,
         ),
         name="experts",
-    )(
-        own,
-        *pieces,
-        gate_weight.reshape(units, model_width),
-        up_weight.reshape(units, model_width),
-        down_weight.reshape(units, model_width),
-    )
+    )(own, *pieces, gates, ups, downs)
 
 
 def pack_kernel(tokens_ref, experts_ref, weights_ref, packed_ref):
@@ -225,7 +218,6 @@
         out_shape=jax.ShapeDtypeStruct((rows, width + 128), jnp.bfloat16),
         in_specs=[pl.BlockSpec(memory_space=pltpu.VMEM)] * 3,
         out_specs=pl.BlockSpec(memory_space=pltpu.VMEM),
-        compiler_params=pltpu.CompilerParams(vmem_limit_bytes=2 * 1024 * 1024),
         name="pack",
     )(tokens, routed_experts.T, route_weights.T)
 
@@ -249,15 +241,6 @@
 
 def rounded(*terms):
     return added(*terms).astype(jnp.bfloat16)
-
-
-def gathered(one, two):
-    rows = one.shape[0]
-    pair = jnp.concatenate([one, two], axis=0)
-    from_x, from_y = swap_exp(pair, 2), swap_exp(pair, 4)
-    far_one, far_two = swap_exp(from_x[:rows], 4), swap_exp(from_y[rows:], 2)
-    pieces = [pair, from_x, from_y, far_one, far_two]
-    return pieces + [swap_exp(piece, 1) for piece in pieces]
 
 
 def segments_of(rows):
@@ -274,12 +257,17 @@
     return [[(place * rows, rows) for place in cut] for cut in cuts]
 
 
-def reduced(parts, rows):
+def cores_added(parts, rows):
     to_x, to_y, own, x_one, y_two, other = parts
     back = swap_exp(other, 1)
     to_x = rounded(to_x, back[: 2 * rows])
     to_y = rounded(to_y, back[2 * rows : 4 * rows])
-    from_x, from_y = swap_exp(to_x, 2), swap_exp(to_y, 4)
+    return to_x, to_y, own, x_one, y_two, back
+
+
+def plane_halved(parts, arrived, rows):
+    to_x, to_y, own, x_one, y_two, back = parts
+    from_x, from_y = arrived
     x_one = rounded(x_one, back[6 * rows : 7 * rows], from_y[rows:])
     y_two = rounded(y_two, back[7 * rows :], from_x[rows:])
     last_x, last_y = swap_exp(x_one, 2), swap_exp(y_two, 4)
@@ -288,16 +276,56 @@
     return one, two
 
 
+def ordered(*values):
+    return lax.optimization_barrier(values)
+
+
 def on_device_dense(tokens, routed_experts, route_weights, gate_weight, up_weight, down_weight):
+    local_experts, shard_units, model_width = gate_weight.shape
+    units = local_experts * shard_units
     top = routed_experts.shape[1]
     rows = tokens.shape[0]
+    gate_weight = gate_weight.reshape(units, model_width)
+    up_weight = up_weight.reshape(units, model_width)
+    down_weight = down_weight.reshape(units, model_width)
     packed = with_routing(tokens, routed_experts, route_weights)
     turned = {s: turn_rep(packed, s) for s in (2, 1, 3)}
-    near = gathered(packed, turned[2])
-    far = gathered(turned[1], turned[3])
+
+    gates = fetched(gate_weight, True)
+    near_z, gates, up_weight = ordered(turned[2], gates, up_weight)
+    ups = fetched(up_weight, True)
+    near = jnp.concatenate([packed, near_z], axis=0)
+    near_x, near_y = swap_exp(near, 2), swap_exp(near, 4)
+    far = jnp.concatenate([turned[1], turned[3]], axis=0)
+    near_x, near_y, far, ups, down_weight = ordered(near_x, near_y, far, ups, down_weight)
+    downs = fetched(down_weight, False)
+    near_far = [swap_exp(near_x[:rows], 4), swap_exp(near_y[rows:], 2)]
+    far_x, far_y = swap_exp(far, 2), swap_exp(far, 4)
+    *near_far, downs = ordered(*near_far, downs)
+    near = [near, near_x, near_y, *near_far]
+    near = near + [swap_exp(piece, 1) for piece in near]
+
+    far_one, far_two = far_x[:rows], far_y[rows:]
+    *near, far_one, far_two = ordered(*near, far_one, far_two)
+    far = [far, far_x, far_y]
+    far_far = [swap_exp(far_one, 4), swap_exp(far_two, 2)]
+    far_other = [swap_exp(piece, 1) for piece in far]
     segments = segments_of(rows)
-    near_sums = reduced(experts_of(near, segments, gate_weight, up_weight, down_weight, top), rows)
-    far_sums = reduced(experts_of(far, segments, gate_weight, up_weight, down_weight, top), rows)
+    parts = experts_of(near, segments, gates, ups, downs, shard_units, top)
+    *parts, far_one, far_two, other_one, other_x, other_y = ordered(*parts, *far_far, *far_other)
+    far = far + [far_one, far_two, other_one, other_x, other_y]
+    far = far + [swap_exp(far_one, 1), swap_exp(far_two, 1)]
+
+    near_parts = cores_added(parts, rows)
+    arrived = [swap_exp(near_parts[0], 2), swap_exp(near_parts[1], 4)]
+    to_x, to_y, *far = ordered(near_parts[0], near_parts[1], *far)
+    near_parts = (to_x, to_y, *near_parts[2:])
+    parts = experts_of(far, segments, gates, ups, downs, shard_units, top)
+    *parts, near_x, near_y = ordered(*parts, *arrived)
+    far_parts = cores_added(parts, rows)
+    near_sums = plane_halved(near_parts, (near_x, near_y), rows)
+    arrived = [swap_exp(far_parts[0], 2), swap_exp(far_parts[1], 4)]
+    far_sums = plane_halved(far_parts, arrived, rows)
     arrived = [
         turn_rep(near_sums[1].astype(jnp.bfloat16), -2),
         turn_rep(far_sums[0].astype(jnp.bfloat16), -1),

time: 103 us -> 100 us (0.971)
  waiting for transfers between devices: 38.8 us -> 25.5 us
  local copies, waits for them, and re-layouts: 10.7 us -> 20.1 us
  starting transfers between devices: 30.3 us -> 34.5 us
  Pallas kernels: 21 us -> 18.3 us
    ppermute x6, waiting for transfers between devices: 16.9 us -> 4.59 us  [turn_rep(): lax.ppermute(value, 'rep', [(i, (i - shift) % replicas) for i in range(re...]
    pallas_call x2, Pallas kernels: 20.8 us -> 11.7 us  [experts_of(): pl.pallas_call(kernel, out_shape=[jax.ShapeDtypeStruct((count, model_widt...]
    unnamed x19 -> x26, local copies, waits for them, and re-layouts: 10.6 us -> 19.1 us
    ppermute x6, starting transfers between devices: 8.89 us -> 13.8 us  [turn_rep(): lax.ppermute(value, 'rep', [(i, (i - shift) % replicas) for i in range(re...]
    pallas_call x0 -> x3, Pallas kernels: none -> 4.88 us  [fetched(): pl.pallas_call(functools.partial(fetch_kernel, turn), out_shape=jax.Shape...]
    pallas_call x1, Pallas kernels: 0.17 us -> 1.75 us  [with_routing(): pl.pallas_call(pack_kernel, out_shape=jax.ShapeDtypeStruct((rows, width +...]
  transfers between devices with their start and end apart: 34 -> 34, of which waited for: 17 -> 14; matrix products, arithmetic and copies ran while one was open for 1% -> 1% of each run, Pallas kernels for 20% -> 17%
where the time goes in v1:
time: 100 us
  starting transfers between devices  34.5 us (34%)
  waiting for transfers between devices  25.5 us (26%)
  local copies, waits for them, and re-layouts  20.1 us (20%)
  Pallas kernels  18.3 us (18%)
  other arithmetic  1.46 us (1%)
    ppermute x28, waiting for transfers between devices, swap_exp(): return lax.ppermute(value, 'exp', [(i, i ^ bit) for i in range(owners)])  20.9 us
    ppermute x28, starting transfers between devices, swap_exp(): return lax.ppermute(value, 'exp', [(i, i ^ bit) for i in range(owners)])  20.7 us
    unnamed x26, local copies, waits for them, and re-layouts  19.1 us
    ppermute x6, starting transfers between devices, turn_rep(): lax.ppermute(value, 'rep', [(i, (i - shift) % replicas) for i in range(re...  13.8 us
    pallas_call x2, Pallas kernels, experts_of(): pl.pallas_call(kernel, out_shape=[jax.ShapeDtypeStruct((count, model_widt...  11.7 us
    pallas_call x3, Pallas kernels, fetched(): pl.pallas_call(functools.partial(fetch_kernel, turn), out_shape=jax.Shape...  4.88 us
    ppermute x6, waiting for transfers between devices, turn_rep(): lax.ppermute(value, 'rep', [(i, (i - shift) % replicas) for i in range(re...  4.59 us
  transfers between devices with their start and end apart: 34, of which 14 were waited for; matrix products, arithmetic and copies ran while one was open for 1% of the time, Pallas kernels for 17%

profile of v1, /device:TPU:0, one launch (start us, length us, event | category | flops | bytes accessed | tf_op | source)
XLA Modules:
  0.0 100.1 jit_solution(4443493242888600738)
XLA Ops:
  0.0 1.7 %pack.1 = bf16[16,4224]{1,0:T(8,128)(2,1)} custom-call(bf16[16,4096]{1,0:T(8,128)(2,1)} %tokens_ref.1, s32[8,16]{1,0:T(8,128)} %bitcast.13, f32[8,16]{1,0:T(8,128)} %bitcast.14), custom_call_target="tpu_custom_call" | custom-call | tf_op jit(solution)/shard_map/pack/pallas_call | solution.py:216
  1.7 4.0 %collective-permute-start = (bf16[16,4224]{1,0:T(8,128)(2,1)}, bf16[16,4224]{1,0:T(8,128)(2,1)S(1)}, u32[]{:S(2)}, u32[]{:S(2)}) collective-permute-start(bf16[16,4224]{1,0:T(8,128)(2,1)} %pack.1), channel_id=1, source_target_pairs={{0,16},{8,24},{16,0},{24,8},{1,17},{9,25},{17,1},{25,9},{2,18},{10... | collective-permute-start | bytes 405512 | tf_op jit(solution)/shard_map/ppermute | solution.py:232
  5.8 1.6 %collective-permute-start.4 = (bf16[16,4224]{1,0:T(8,128)(2,1)}, bf16[16,4224]{1,0:T(8,128)(2,1)S(1)}, u32[]{:S(2)}, u32[]{:S(2)}) collective-permute-start(bf16[16,4224]{1,0:T(8,128)(2,1)} %pack.1), channel_id=1, source_target_pairs={{0,8},{8,16},{16,24},{24,0},{1,9},{9,17},{17,25},{25,1},{2,10},{10... | collective-permute-start | bytes 405512 | tf_op jit(solution)/shard_map/ppermute | solution.py:232
  7.4 2.2 %collective-permute-start.3 = (bf16[16,4224]{1,0:T(8,128)(2,1)}, bf16[16,4224]{1,0:T(8,128)(2,1)S(1)}, u32[]{:S(2)}, u32[]{:S(2)}) collective-permute-start(bf16[16,4224]{1,0:T(8,128)(2,1)} %pack.1), channel_id=1, source_target_pairs={{0,24},{8,0},{16,8},{24,16},{1,25},{9,1},{17,9},{25,17},{2,26},{10... | collective-permute-start | bytes 405512 | tf_op jit(solution)/shard_map/ppermute | solution.py:232
  9.6 2.8 %copy-done.6 = bf16[2,384,4096]{2,1,0:T(8,128)(2,1)S(1)} copy-done((bf16[2,384,4096]{2,1,0:T(8,128)(2,1)S(1)}, bf16[2,384,4096]{2,1,0:T(8,128)(2,1)}, u32[]{:S(2)}) %copy-start.6) | copy-done | bytes 6291480
  12.4 2.1 %fetch_turned.2.refs_11_ = bf16[4096,768]{1,0:T(8,128)(2,1)S(1)} custom-call(bf16[768,4096]{1,0:T(8,128)(2,1)S(1)} %bitcast.8), custom_call_target="tpu_custom_call" | custom-call | bytes 12582912 | tf_op jit(solution)/shard_map/fetch_turned/pallas_call | solution.py:103
  14.5 2.7 %copy-done = bf16[4096,768]{1,0:T(8,128)(2,1)} copy-done((bf16[4096,768]{1,0:T(8,128)(2,1)}, bf16[4096,768]{1,0:T(8,128)(2,1)S(1)}, u32[]{:S(2)}) %copy-start) | copy-done | bytes 6291480
  17.2 1.6 %collective-permute-start.2 = (bf16[32,4224]{1,0:T(8,128)(2,1)S(1)}, bf16[32,4224]{1,0:T(8,128)(2,1)S(1)}, u32[]{:S(2)}, u32[]{:S(2)}) collective-permute-start(bf16[32,4224]{1,0:T(8,128)(2,1)S(1)} %pad_maximum_fusion.refs_1_), channel_id=1, source_target_pairs={{0,4},{1,5},{2,6},{3,7},{4,0},{5,1},{6,2},{7,3},{8,12},{9,13},{10,... | collective-permute-start | bytes 811016 | tf_op jit(solution)/shard_map/ppermute | solution.py:227
  18.8 1.5 %collective-permute-start.1 = (bf16[32,4224]{1,0:T(8,128)(2,1)S(1)}, bf16[32,4224]{1,0:T(8,128)(2,1)}, u32[]{:S(2)}, u32[]{:S(2)}) collective-permute-start(bf16[32,4224]{1,0:T(8,128)(2,1)S(1)} %pad_maximum_fusion.refs_1_), channel_id=1, source_target_pairs={{0,2},{1,3},{2,0},{3,1},{4,6},{5,7},{6,4},{7,5},{8,10},{9,11},{10,... | collective-permute-start | bytes 811016 | tf_op jit(solution)/shard_map/ppermute | solution.py:227
  20.3 2.1 %fetch_turned.3.refs_12_ = bf16[4096,768]{1,0:T(8,128)(2,1)S(1)} custom-call(bf16[768,4096]{1,0:T(8,128)(2,1)S(1)} %bitcast.9), custom_call_target="tpu_custom_call" | custom-call | bytes 12582912 | tf_op jit(solution)/shard_map/fetch_turned/pallas_call | solution.py:103
  22.4 2.7 %copy-done.2 = bf16[4096,768]{1,0:T(8,128)(2,1)} copy-done((bf16[4096,768]{1,0:T(8,128)(2,1)}, bf16[4096,768]{1,0:T(8,128)(2,1)S(1)}, u32[]{:S(2)}) %copy-start.2) | copy-done | bytes 6291480
  26.9 1.6 %collective-permute-start.6 = (bf16[16,4224]{1,0:T(8,128)(2,1)S(1)}, bf16[16,4224]{1,0:T(8,128)(2,1)}, u32[]{:S(2)}, u32[]{:S(2)}) collective-permute-start(bf16[16,4224]{1,0:T(8,128)(2,1)S(1)} %slice.85), channel_id=1, source_target_pairs={{0,2},{1,3},{2,0},{3,1},{4,6},{5,7},{6,4},{7,5},{8,10},{9,11},{10,... | collective-permute-start | bytes 405512 | tf_op jit(solution)/shard_map/ppermute | solution.py:227
  29.0 1.5 %collective-permute-start.5 = (bf16[16,4224]{1,0:T(8,128)(2,1)S(1)}, bf16[16,4224]{1,0:T(8,128)(2,1)}, u32[]{:S(2)}, u32[]{:S(2)}) collective-permute-start(bf16[16,4224]{1,0:T(8,128)(2,1)S(1)} %slice.84), channel_id=1, source_target_pairs={{0,4},{1,5},{2,6},{3,7},{4,0},{5,1},{6,2},{7,3},{8,12},{9,13},{10,... | collective-permute-start | bytes 405512 | tf_op jit(solution)/shard_map/ppermute | solution.py:227
  31.0 2.4 %collective-permute-done.6.refs_5_ = bf16[16,4224]{1,0:T(8,128)(2,1)} collective-permute-done((bf16[16,4224]{1,0:T(8,128)(2,1)S(1)}, bf16[16,4224]{1,0:T(8,128)(2,1)}, u32[]{:S(2)}, u32[]{:S(2)}) %collective-permute-start.6) | collective-permute-done | bytes 135200 | tf_op jit(solution)/shard_map/ppermute | solution.py:227
  33.5 3.9 %collective-permute-done.5.refs_4_ = bf16[16,4224]{1,0:T(8,128)(2,1)} collective-permute-done((bf16[16,4224]{1,0:T(8,128)(2,1)S(1)}, bf16[16,4224]{1,0:T(8,128)(2,1)}, u32[]{:S(2)}, u32[]{:S(2)}) %collective-permute-start.5) | collective-permute-done | bytes 135200 | tf_op jit(solution)/shard_map/ppermute | solution.py:227
  38.2 2.6 %copy-done.4 = bf16[768,4096]{1,0:T(8,128)(2,1)} copy-done((bf16[768,4096]{1,0:T(8,128)(2,1)}, bf16[768,4096]{1,0:T(8,128)(2,1)S(1)}, u32[]{:S(2)}) %copy-start.4) | copy-done | bytes 6291480
  44.1 2.8 %copy-done.1 = bf16[4096,768]{1,0:T(8,128)(2,1)S(1)} copy-done((bf16[4096,768]{1,0:T(8,128)(2,1)S(1)}, bf16[4096,768]{1,0:T(8,128)(2,1)}, u32[]{:S(2)}) %copy-start.1) | copy-done | bytes 6291480
  46.9 2.8 %copy-done.3 = bf16[4096,768]{1,0:T(8,128)(2,1)S(1)} copy-done((bf16[4096,768]{1,0:T(8,128)(2,1)S(1)}, bf16[4096,768]{1,0:T(8,128)(2,1)}, u32[]{:S(2)}) %copy-start.3) | copy-done | bytes 6291480
  49.6 2.8 %copy-done.5 = bf16[768,4096]{1,0:T(8,128)(2,1)S(1)} copy-done((bf16[768,4096]{1,0:T(8,128)(2,1)S(1)}, bf16[768,4096]{1,0:T(8,128)(2,1)}, u32[]{:S(2)}) %copy-start.5) | copy-done | bytes 6291480
  52.4 6.6 %experts.2 = (bf16[32,4096]{1,0:T(8,128)(2,1)S(1)}, bf16[32,4096]{1,0:T(8,128)(2,1)S(1)}, bf16[32,4096]{1,0:T(8,128)(2,1)S(1)}, bf16[16,4096]{1,0:T(8,128)(2,1)S...) custom-call(s32[1]{0:T(128)} %bitcast.refs_0_, bf16[32,4224]{1,0:T(8,128)(2,1)S(1)} %pad_maximum_fusion.refs_1_, ...), custom_call_target="tpu_custom_call" | custom-call | flops 4831838208 | bytes 4194304 | tf_op jit(solution)/shard_map/experts/pallas_call | solution.py:176
  59.7 2.1 %collective-permute-done.19 = bf16[128,4096]{1,0:T(8,128)(2,1)S(1)} collective-permute-done((bf16[128,4096]{1,0:T(8,128)(2,1)S(1)}, bf16[128,4096]{1,0:T(8,128)(2,1)S(1)}, u32[]{:S(2)}, u32[]{:S(2)}) %collective-permute-start.19) | collective-permute-done | bytes 1048608 | tf_op jit(solution)/shard_map/ppermute | solution.py:227
  61.9 1.5 %collective-permute-start.23 = (bf16[32,4096]{1,0:T(8,128)(2,1)S(1)}, bf16[32,4096]{1,0:T(8,128)(2,1)S(1)}, u32[]{:S(2)}, u32[]{:S(2)}) collective-permute-start(bf16[32,4096]{1,0:T(8,128)(2,1)S(1)} %get-tuple-element.141), channel_id=1, source_target_pairs={{0,4},{1,5},{2,6},{3,7},{4,0},{5,1},{6,2},{7,3},{8,12},{9,13},{10,... | collective-permute-start | bytes 786440 | tf_op jit(solution)/shard_map/ppermute | solution.py:227
  63.4 1.5 %collective-permute-start.22 = (bf16[32,4096]{1,0:T(8,128)(2,1)S(1)}, bf16[32,4096]{1,0:T(8,128)(2,1)S(1)}, u32[]{:S(2)}, u32[]{:S(2)}) collective-permute-start(bf16[32,4096]{1,0:T(8,128)(2,1)S(1)} %get-tuple-element.142), channel_id=1, source_target_pairs={{0,2},{1,3},{2,0},{3,1},{4,6},{5,7},{6,4},{7,5},{8,10},{9,11},{10,... | collective-permute-start | bytes 786440 | tf_op jit(solution)/shard_map/ppermute | solution.py:227
  65.0 5.1 %experts.3 = (bf16[32,4096]{1,0:T(8,128)(2,1)S(1)}, bf16[32,4096]{1,0:T(8,128)(2,1)S(1)}, bf16[32,4096]{1,0:T(8,128)(2,1)S(1)}, bf16[16,4096]{1,0:T(8,128)(2,1)S...) custom-call(s32[1]{0:T(128)} %bitcast.refs_0_, bf16[32,4224]{1,0:T(8,128)(2,1)S(1)} %pad_maximum_fusion.1.refs_1_, ...), custom_call_target="tpu_custom_call" | custom-call | flops 4831838208 | bytes 4194304 | tf_op jit(solution)/shard_map/experts/pallas_call | solution.py:176
  71.5 2.7 %collective-permute-done.27 = bf16[128,4096]{1,0:T(8,128)(2,1)S(1)} collective-permute-done((bf16[128,4096]{1,0:T(8,128)(2,1)S(1)}, bf16[128,4096]{1,0:T(8,128)(2,1)S(1)}, u32[]{:S(2)}, u32[]{:S(2)}) %collective-permute-start.27) | collective-permute-done | bytes 1048608 | tf_op jit(solution)/shard_map/ppermute | solution.py:227
  74.9 1.5 %collective-permute-start.31 = (bf16[32,4096]{1,0:T(8,128)(2,1)S(1)}, bf16[32,4096]{1,0:T(8,128)(2,1)S(1)}, u32[]{:S(2)}, u32[]{:S(2)}) collective-permute-start(bf16[32,4096]{1,0:T(8,128)(2,1)S(1)} %get-tuple-element.140), channel_id=1, source_target_pairs={{0,2},{1,3},{2,0},{3,1},{4,6},{5,7},{6,4},{7,5},{8,10},{9,11},{10,... | collective-permute-start | bytes 786440 | tf_op jit(solution)/shard_map/ppermute | solution.py:227
  78.6 4.9 %collective-permute-done.28 = bf16[32,4096]{1,0:T(8,128)(2,1)S(1)} collective-permute-done((bf16[32,4096]{1,0:T(8,128)(2,1)S(1)}, bf16[32,4096]{1,0:T(8,128)(2,1)S(1)}, u32[]{:S(2)}, u32[]{:S(2)}) %collective-permute-start.28) | collective-permute-done | bytes 262176 | tf_op jit(solution)/shard_map/ppermute | solution.py:227
  84.2 1.6 %collective-permute-start.29 = (bf16[16,4096]{1,0:T(8,128)(2,1)S(1)}, bf16[16,4096]{1,0:T(8,128)(2,1)S(1)}, u32[]{:S(2)}, u32[]{:S(2)}) collective-permute-start(bf16[16,4096]{1,0:T(8,128)(2,1)S(1)} %get-tuple-element.137), channel_id=1, source_target_pairs={{0,2},{1,3},{2,0},{3,1},{4,6},{5,7},{6,4},{7,5},{8,10},{9,11},{10,... | collective-permute-start | bytes 393224 | tf_op jit(solution)/shard_map/ppermute | solution.py:227
  85.8 1.5 %collective-permute-start.32 = (bf16[16,4096]{1,0:T(8,128)(2,1)S(1)}, bf16[16,4096]{1,0:T(8,128)(2,1)S(1)}, u32[]{:S(2)}, u32[]{:S(2)}) collective-permute-start(bf16[16,4096]{1,0:T(8,128)(2,1)S(1)} %get-tuple-element.138), channel_id=1, source_target_pairs={{0,4},{1,5},{2,6},{3,7},{4,0},{5,1},{6,2},{7,3},{8,12},{9,13},{10,... | collective-permute-start | bytes 393224 | tf_op jit(solution)/shard_map/ppermute | solution.py:227
  87.3 2.0 %collective-permute-start.26 = (bf16[16,4096]{1,0:T(8,128)(2,1)S(1)}, bf16[16,4096]{1,0:T(8,128)(2,1)S(1)}, u32[]{:S(2)}, u32[]{:S(2)}) collective-permute-start(bf16[16,4096]{1,0:T(8,128)(2,1)S(1)} %add_convert_fusion.9), channel_id=1, source_target_pairs={{0,16},{8,24},{16,0},{24,8},{1,17},{9,25},{17,1},{25,9},{2,18},{10... | collective-permute-start | bytes 393224 | tf_op jit(solution)/shard_map/ppermute | solution.py:232
  92.1 2.7 %collective-permute-start.33 = (bf16[16,4096]{1,0:T(8,128)(2,1)S(1)}, bf16[16,4096]{1,0:T(8,128)(2,1)S(1)}, u32[]{:S(2)}, u32[]{:S(2)}) collective-permute-start(bf16[16,4096]{1,0:T(8,128)(2,1)S(1)} %get-tuple-element.134), channel_id=1, source_target_pairs={{0,24},{8,0},{16,8},{24,16},{1,25},{9,1},{17,9},{25,17},{2,26},{10... | collective-permute-start | bytes 393224 | tf_op jit(solution)/shard_map/ppermute | solution.py:232
  94.8 3.6 %collective-permute-done.26 = bf16[16,4096]{1,0:T(8,128)(2,1)S(1)} collective-permute-done((bf16[16,4096]{1,0:T(8,128)(2,1)S(1)}, bf16[16,4096]{1,0:T(8,128)(2,1)S(1)}, u32[]{:S(2)}, u32[]{:S(2)}) %collective-permute-start.26) | collective-permute-done | bytes 131104 | tf_op jit(solution)/shard_map/ppermute | solution.py:232
  (83 shorter events, 17.4 us)
Async XLA Ops:
  1.7 15.4 %collective-permute-start = (bf16[16,4224]{1,0:T(8,128)(2,1)}, bf16[16,4224]{1,0:T(8,128)(2,1)S(1)}, u32[]{:S(2)}, u32[]{:S(2)}) collective-permute-start(bf16[16,4224]{1,0:T(8,128)(2,1)} %pack.1), channel_id=1, source_target_pairs={{0,16},{8,24},{16,0},{24,8},{1,17},{9,25},{17,1},{25,9},{2,18},{10... | collective-permute-start | bytes 405512 | tf_op jit(solution)/shard_map/ppermute | solution.py:232
  5.8 14.5 %collective-permute-start.4 = (bf16[16,4224]{1,0:T(8,128)(2,1)}, bf16[16,4224]{1,0:T(8,128)(2,1)S(1)}, u32[]{:S(2)}, u32[]{:S(2)}) collective-permute-start(bf16[16,4224]{1,0:T(8,128)(2,1)} %pack.1), channel_id=1, source_target_pairs={{0,8},{8,16},{16,24},{24,0},{1,9},{9,17},{17,25},{25,1},{2,10},{10... | collective-permute-start | bytes 405512 | tf_op jit(solution)/shard_map/ppermute | solution.py:232
  7.4 12.9 %collective-permute-start.3 = (bf16[16,4224]{1,0:T(8,128)(2,1)}, bf16[16,4224]{1,0:T(8,128)(2,1)S(1)}, u32[]{:S(2)}, u32[]{:S(2)}) collective-permute-start(bf16[16,4224]{1,0:T(8,128)(2,1)} %pack.1), channel_id=1, source_target_pairs={{0,24},{8,0},{16,8},{24,16},{1,25},{9,1},{17,9},{25,17},{2,26},{10... | collective-permute-start | bytes 405512 | tf_op jit(solution)/shard_map/ppermute | solution.py:232
  17.2 7.9 %collective-permute-start.2 = (bf16[32,4224]{1,0:T(8,128)(2,1)S(1)}, bf16[32,4224]{1,0:T(8,128)(2,1)S(1)}, u32[]{:S(2)}, u32[]{:S(2)}) collective-permute-start(bf16[32,4224]{1,0:T(8,128)(2,1)S(1)} %pad_maximum_fusion.refs_1_), channel_id=1, source_target_pairs={{0,4},{1,5},{2,6},{3,7},{4,0},{5,1},{6,2},{7,3},{8,12},{9,13},{10,... | collective-permute-start | bytes 811016 | tf_op jit(solution)/shard_map/ppermute | solution.py:227
  18.8 7.2 %collective-permute-start.1 = (bf16[32,4224]{1,0:T(8,128)(2,1)S(1)}, bf16[32,4224]{1,0:T(8,128)(2,1)}, u32[]{:S(2)}, u32[]{:S(2)}) collective-permute-start(bf16[32,4224]{1,0:T(8,128)(2,1)S(1)} %pad_maximum_fusion.refs_1_), channel_id=1, source_target_pairs={{0,2},{1,3},{2,0},{3,1},{4,6},{5,7},{6,4},{7,5},{8,10},{9,11},{10,... | collective-permute-start | bytes 811016 | tf_op jit(solution)/shard_map/ppermute | solution.py:227
  26.9 6.6 %collective-permute-start.6 = (bf16[16,4224]{1,0:T(8,128)(2,1)S(1)}, bf16[16,4224]{1,0:T(8,128)(2,1)}, u32[]{:S(2)}, u32[]{:S(2)}) collective-permute-start(bf16[16,4224]{1,0:T(8,128)(2,1)S(1)} %slice.85), channel_id=1, source_target_pairs={{0,2},{1,3},{2,0},{3,1},{4,6},{5,7},{6,4},{7,5},{8,10},{9,11},{10,... | collective-permute-start | bytes 405512 | tf_op jit(solution)/shard_map/ppermute | solution.py:227
  28.5 12.3 %collective-permute-start.13 = (bf16[32,4224]{1,0:T(8,128)(2,1)S(1)}, bf16[32,4224]{1,0:T(8,128)(2,1)S(1)}, u32[]{:S(2)}, u32[]{:S(2)}) collective-permute-start(bf16[32,4224]{1,0:T(8,128)(2,1)S(1)} %pad_maximum_fusion.1.refs_1_), channel_id=1, source_target_pairs={{0,4},{1,5},{2,6},{3,7},{4,0},{5,1},{6,2},{7,3},{8,12},{9,13},{10,... | collective-permute-start | bytes 811016 | tf_op jit(solution)/shard_map/ppermute | solution.py:227
  29.0 8.4 %collective-permute-start.5 = (bf16[16,4224]{1,0:T(8,128)(2,1)S(1)}, bf16[16,4224]{1,0:T(8,128)(2,1)}, u32[]{:S(2)}, u32[]{:S(2)}) collective-permute-start(bf16[16,4224]{1,0:T(8,128)(2,1)S(1)} %slice.84), channel_id=1, source_target_pairs={{0,4},{1,5},{2,6},{3,7},{4,0},{5,1},{6,2},{7,3},{8,12},{9,13},{10,... | collective-permute-start | bytes 405512 | tf_op jit(solution)/shard_map/ppermute | solution.py:227
  30.5 10.8 %collective-permute-start.12 = (bf16[32,4224]{1,0:T(8,128)(2,1)S(1)}, bf16[32,4224]{1,0:T(8,128)(2,1)S(1)}, u32[]{:S(2)}, u32[]{:S(2)}) collective-permute-start(bf16[32,4224]{1,0:T(8,128)(2,1)S(1)} %pad_maximum_fusion.1.refs_1_), channel_id=1, source_target_pairs={{0,2},{1,3},{2,0},{3,1},{4,6},{5,7},{6,4},{7,5},{8,10},{9,11},{10,... | collective-permute-start | bytes 811016 | tf_op jit(solution)/shard_map/ppermute | solution.py:227
  31.0 10.3 %collective-permute-start.7 = (bf16[32,4224]{1,0:T(8,128)(2,1)S(1)}, bf16[32,4224]{1,0:T(8,128)(2,1)}, u32[]{:S(2)}, u32[]{:S(2)}) collective-permute-start(bf16[32,4224]{1,0:T(8,128)(2,1)S(1)} %pad_maximum_fusion.refs_1_), channel_id=1, source_target_pairs={{0,1},{1,0},{2,3},{3,2},{4,5},{5,4},{6,7},{7,6},{8,9},{9,8},{10,11... | collective-permute-start | bytes 811016 | tf_op jit(solution)/shard_map/ppermute | solution.py:227
  33.5 8.4 %collective-permute-start.8 = (bf16[32,4224]{1,0:T(8,128)(2,1)}, bf16[32,4224]{1,0:T(8,128)(2,1)}, u32[]{:S(2)}, u32[]{:S(2)}) collective-permute-start(bf16[32,4224]{1,0:T(8,128)(2,1)} %collective-permute-done.1.refs_2_), channel_id=1, source_target_pairs={{0,1},{1,0},{2,3},{3,2},{4,5},{5,4},{6,7},{7,6},{8,9},{9,8},{10,11... | collective-permute-start | bytes 811016 | tf_op jit(solution)/shard_map/ppermute | solution.py:227
  37.4 4.6 %collective-permute-start.9 = (bf16[32,4224]{1,0:T(8,128)(2,1)S(1)}, bf16[32,4224]{1,0:T(8,128)(2,1)}, u32[]{:S(2)}, u32[]{:S(2)}) collective-permute-start(bf16[32,4224]{1,0:T(8,128)(2,1)S(1)} %collective-permute-done.2.refs_3_), channel_id=1, source_target_pairs={{0,1},{1,0},{2,3},{3,2},{4,5},{5,4},{6,7},{7,6},{8,9},{9,8},{10,11... | collective-permute-start | bytes 811016 | tf_op jit(solution)/shard_map/ppermute | solution.py:227
  41.4 17.6 %collective-permute-start.16 = (bf16[32,4224]{1,0:T(8,128)(2,1)S(1)}, bf16[32,4224]{1,0:T(8,128)(2,1)S(1)}, u32[]{:S(2)}, u32[]{:S(2)}) collective-permute-start(bf16[32,4224]{1,0:T(8,128)(2,1)S(1)} %pad_maximum_fusion.1.refs_1_), channel_id=1, source_target_pairs={{0,1},{1,0},{2,3},{3,2},{4,5},{5,4},{6,7},{7,6},{8,9},{9,8},{10,11... | collective-permute-start | bytes 811016 | tf_op jit(solution)/shard_map/ppermute | solution.py:227
  41.9 17.2 %collective-permute-start.18 = (bf16[32,4224]{1,0:T(8,128)(2,1)S(1)}, bf16[32,4224]{1,0:T(8,128)(2,1)S(1)}, u32[]{:S(2)}, u32[]{:S(2)}) collective-permute-start(bf16[32,4224]{1,0:T(8,128)(2,1)S(1)} %collective-permute-done.13.refs_3_), channel_id=1, source_target_pairs={{0,1},{1,0},{2,3},{3,2},{4,5},{5,4},{6,7},{7,6},{8,9},{9,8},{10,11... | collective-permute-start | bytes 811016 | tf_op jit(solution)/shard_map/ppermute | solution.py:227
  42.0 17.1 %collective-permute-start.17 = (bf16[32,4224]{1,0:T(8,128)(2,1)S(1)}, bf16[32,4224]{1,0:T(8,128)(2,1)S(1)}, u32[]{:S(2)}, u32[]{:S(2)}) collective-permute-start(bf16[32,4224]{1,0:T(8,128)(2,1)S(1)} %collective-permute-done.12.refs_2_), channel_id=1, source_target_pairs={{0,1},{1,0},{2,3},{3,2},{4,5},{5,4},{6,7},{7,6},{8,9},{9,8},{10,11... | collective-permute-start | bytes 811016 | tf_op jit(solution)/shard_map/ppermute | solution.py:227
  43.0 16.1 %collective-permute-start.14 = (bf16[16,4224]{1,0:T(8,128)(2,1)S(1)}, bf16[16,4224]{1,0:T(8,128)(2,1)S(1)}, u32[]{:S(2)}, u32[]{:S(2)}) collective-permute-start(bf16[16,4224]{1,0:T(8,128)(2,1)S(1)} %slice.112), channel_id=1, source_target_pairs={{0,4},{1,5},{2,6},{3,7},{4,0},{5,1},{6,2},{7,3},{8,12},{9,13},{10,... | collective-permute-start | bytes 405512 | tf_op jit(solution)/shard_map/ppermute | solution.py:227
  43.5 15.5 %collective-permute-start.15 = (bf16[16,4224]{1,0:T(8,128)(2,1)S(1)}, bf16[16,4224]{1,0:T(8,128)(2,1)S(1)}, u32[]{:S(2)}, u32[]{:S(2)}) collective-permute-start(bf16[16,4224]{1,0:T(8,128)(2,1)S(1)} %slice.113), channel_id=1, source_target_pairs={{0,2},{1,3},{2,0},{3,1},{4,6},{5,7},{6,4},{7,5},{8,10},{9,11},{10,... | collective-permute-start | bytes 405512 | tf_op jit(solution)/shard_map/ppermute | solution.py:227
  59.1 2.7 %collective-permute-start.19 = (bf16[128,4096]{1,0:T(8,128)(2,1)S(1)}, bf16[128,4096]{1,0:T(8,128)(2,1)S(1)}, u32[]{:S(2)}, u32[]{:S(2)}) collective-permute-start(bf16[128,4096]{1,0:T(8,128)(2,1)S(1)} %get-tuple-element.99), channel_id=1, source_target_pairs={{0,1},{1,0},{2,3},{3,2},{4,5},{5,4},{6,7},{7,6},{8,9},{9,8},{10,11... | collective-permute-start | bytes 3145736 | tf_op jit(solution)/shard_map/ppermute | solution.py:227
  59.1 5.8 %collective-permute-start.20 = (bf16[16,4224]{1,0:T(8,128)(2,1)S(1)}, bf16[16,4224]{1,0:T(8,128)(2,1)S(1)}, u32[]{:S(2)}, u32[]{:S(2)}) collective-permute-start(bf16[16,4224]{1,0:T(8,128)(2,1)S(1)} %collective-permute-done.14.refs_4_), channel_id=1, source_target_pairs={{0,1},{1,0},{2,3},{3,2},{4,5},{5,4},{6,7},{7,6},{8,9},{9,8},{10,11... | collective-permute-start | bytes 405512 | tf_op jit(solution)/shard_map/ppermute | solution.py:227
  59.6 5.3 %collective-permute-start.21 = (bf16[16,4224]{1,0:T(8,128)(2,1)S(1)}, bf16[16,4224]{1,0:T(8,128)(2,1)S(1)}, u32[]{:S(2)}, u32[]{:S(2)}) collective-permute-start(bf16[16,4224]{1,0:T(8,128)(2,1)S(1)} %collective-permute-done.15.refs_5_), channel_id=1, source_target_pairs={{0,1},{1,0},{2,3},{3,2},{4,5},{5,4},{6,7},{7,6},{8,9},{9,8},{10,11... | collective-permute-start | bytes 405512 | tf_op jit(solution)/shard_map/ppermute | solution.py:227
  61.9 8.4 %collective-permute-start.23 = (bf16[32,4096]{1,0:T(8,128)(2,1)S(1)}, bf16[32,4096]{1,0:T(8,128)(2,1)S(1)}, u32[]{:S(2)}, u32[]{:S(2)}) collective-permute-start(bf16[32,4096]{1,0:T(8,128)(2,1)S(1)} %get-tuple-element.141), channel_id=1, source_target_pairs={{0,4},{1,5},{2,6},{3,7},{4,0},{5,1},{6,2},{7,3},{8,12},{9,13},{10,... | collective-permute-start | bytes 786440 | tf_op jit(solution)/shard_map/ppermute | solution.py:227
  63.4 8.1 %collective-permute-start.22 = (bf16[32,4096]{1,0:T(8,128)(2,1)S(1)}, bf16[32,4096]{1,0:T(8,128)(2,1)S(1)}, u32[]{:S(2)}, u32[]{:S(2)}) collective-permute-start(bf16[32,4096]{1,0:T(8,128)(2,1)S(1)} %get-tuple-element.142), channel_id=1, source_target_pairs={{0,2},{1,3},{2,0},{3,1},{4,6},{5,7},{6,4},{7,5},{8,10},{9,11},{10,... | collective-permute-start | bytes 786440 | tf_op jit(solution)/shard_map/ppermute | solution.py:227
  71.5 2.7 %collective-permute-start.27 = (bf16[128,4096]{1,0:T(8,128)(2,1)S(1)}, bf16[128,4096]{1,0:T(8,128)(2,1)S(1)}, u32[]{:S(2)}, u32[]{:S(2)}) collective-permute-start(bf16[128,4096]{1,0:T(8,128)(2,1)S(1)} %get-tuple-element.128), channel_id=1, source_target_pairs={{0,1},{1,0},{2,3},{3,2},{4,5},{5,4},{6,7},{7,6},{8,9},{9,8},{10,11... | collective-permute-start | bytes 3145736 | tf_op jit(solution)/shard_map/ppermute | solution.py:227
  74.3 9.2 %collective-permute-start.28 = (bf16[32,4096]{1,0:T(8,128)(2,1)S(1)}, bf16[32,4096]{1,0:T(8,128)(2,1)S(1)}, u32[]{:S(2)}, u32[]{:S(2)}) collective-permute-start(bf16[32,4096]{1,0:T(8,128)(2,1)S(1)} %get-tuple-element.139), channel_id=1, source_target_pairs={{0,4},{1,5},{2,6},{3,7},{4,0},{5,1},{6,2},{7,3},{8,12},{9,13},{10,... | collective-permute-start | bytes 786440 | tf_op jit(solution)/shard_map/ppermute | solution.py:227
  74.9 9.2 %collective-permute-start.31 = (bf16[32,4096]{1,0:T(8,128)(2,1)S(1)}, bf16[32,4096]{1,0:T(8,128)(2,1)S(1)}, u32[]{:S(2)}, u32[]{:S(2)}) collective-permute-start(bf16[32,4096]{1,0:T(8,128)(2,1)S(1)} %get-tuple-element.140), channel_id=1, source_target_pairs={{0,2},{1,3},{2,0},{3,1},{4,6},{5,7},{6,4},{7,5},{8,10},{9,11},{10,... | collective-permute-start | bytes 786440 | tf_op jit(solution)/shard_map/ppermute | solution.py:227
  76.5 18.2 %collective-permute-start.24 = (bf16[16,4096]{1,0:T(8,128)(2,1)S(1)}, bf16[16,4096]{1,0:T(8,128)(2,1)S(1)}, u32[]{:S(2)}, u32[]{:S(2)}) collective-permute-start(bf16[16,4096]{1,0:T(8,128)(2,1)S(1)} %get-tuple-element.135), channel_id=1, source_target_pairs={{0,2},{1,3},{2,0},{3,1},{4,6},{5,7},{6,4},{7,5},{8,10},{9,11},{10,... | collective-permute-start | bytes 393224 | tf_op jit(solution)/shard_map/ppermute | solution.py:227
  77.1 10.1 %collective-permute-start.25 = (bf16[16,4096]{1,0:T(8,128)(2,1)S(1)}, bf16[16,4096]{1,0:T(8,128)(2,1)S(1)}, u32[]{:S(2)}, u32[]{:S(2)}) collective-permute-start(bf16[16,4096]{1,0:T(8,128)(2,1)S(1)} %get-tuple-element.136), channel_id=1, source_target_pairs={{0,4},{1,5},{2,6},{3,7},{4,0},{5,1},{6,2},{7,3},{8,12},{9,13},{10,... | collective-permute-start | bytes 393224 | tf_op jit(solution)/shard_map/ppermute | solution.py:227
  84.2 5.1 %collective-permute-start.29 = (bf16[16,4096]{1,0:T(8,128)(2,1)S(1)}, bf16[16,4096]{1,0:T(8,128)(2,1)S(1)}, u32[]{:S(2)}, u32[]{:S(2)}) collective-permute-start(bf16[16,4096]{1,0:T(8,128)(2,1)S(1)} %get-tuple-element.137), channel_id=1, source_target_pairs={{0,2},{1,3},{2,0},{3,1},{4,6},{5,7},{6,4},{7,5},{8,10},{9,11},{10,... | collective-permute-start | bytes 393224 | tf_op jit(solution)/shard_map/ppermute | solution.py:227
  85.8 5.0 %collective-permute-start.32 = (bf16[16,4096]{1,0:T(8,128)(2,1)S(1)}, bf16[16,4096]{1,0:T(8,128)(2,1)S(1)}, u32[]{:S(2)}, u32[]{:S(2)}) collective-permute-start(bf16[16,4096]{1,0:T(8,128)(2,1)S(1)} %get-tuple-element.138), channel_id=1, source_target_pairs={{0,4},{1,5},{2,6},{3,7},{4,0},{5,1},{6,2},{7,3},{8,12},{9,13},{10,... | collective-permute-start | bytes 393224 | tf_op jit(solution)/shard_map/ppermute | solution.py:227
  87.3 11.1 %collective-permute-start.26 = (bf16[16,4096]{1,0:T(8,128)(2,1)S(1)}, bf16[16,4096]{1,0:T(8,128)(2,1)S(1)}, u32[]{:S(2)}, u32[]{:S(2)}) collective-permute-start(bf16[16,4096]{1,0:T(8,128)(2,1)S(1)} %add_convert_fusion.9), channel_id=1, source_target_pairs={{0,16},{8,24},{16,0},{24,8},{1,17},{9,25},{17,1},{25,9},{2,18},{10... | collective-permute-start | bytes 393224 | tf_op jit(solution)/shard_map/ppermute | solution.py:232
  90.9 7.5 %collective-permute-start.30 = (bf16[16,4096]{1,0:T(8,128)(2,1)S(1)}, bf16[16,4096]{1,0:T(8,128)(2,1)S(1)}, u32[]{:S(2)}, u32[]{:S(2)}) collective-permute-start(bf16[16,4096]{1,0:T(8,128)(2,1)S(1)} %get-tuple-element.133), channel_id=1, source_target_pairs={{0,8},{8,16},{16,24},{24,0},{1,9},{9,17},{17,25},{25,1},{2,10},{10... | collective-permute-start | bytes 393224 | tf_op jit(solution)/shard_map/ppermute | solution.py:232
  92.1 7.3 %collective-permute-start.33 = (bf16[16,4096]{1,0:T(8,128)(2,1)S(1)}, bf16[16,4096]{1,0:T(8,128)(2,1)S(1)}, u32[]{:S(2)}, u32[]{:S(2)}) collective-permute-start(bf16[16,4096]{1,0:T(8,128)(2,1)S(1)} %get-tuple-element.134), channel_id=1, source_target_pairs={{0,24},{8,0},{16,8},{24,16},{1,25},{9,1},{17,9},{25,17},{2,26},{10... | collective-permute-start | bytes 393224 | tf_op jit(solution)/shard_map/ppermute | solution.py:232
  (15 other events, 109.6 us)

commit v2 on v1

--- a/solution.py
+++ b/solution.py
@@ -113,6 +113,28 @@
     )(weight)
 
 
+def gather_kernel(*refs):
+    *pieces, whole_ref = refs
+    start = 0
+    for piece_ref in pieces:
+        count = piece_ref.shape[0]
+        whole_ref[start : start + count, :] = piece_ref[...]
+        start += count
+
+
+def gathered(*pieces):
+    rows = sum(piece.shape[0] for piece in pieces)
+    resident = pl.BlockSpec(memory_space=pltpu.VMEM)
+    return pl.pallas_call(
+        gather_kernel,
+        out_shape=jax.ShapeDtypeStruct((rows, pieces[0].shape[1]), jnp.bfloat16),
+        in_specs=[resident] * len(pieces),
+        out_specs=resident,
+        compiler_params=pltpu.CompilerParams(vmem_limit_bytes=2 * 1024 * 1024),
+        name="gather",
+    )(*pieces)
+
+
 def expert_kernel(pieces_in, pieces_out, local_experts, shard_units, model_width, top, *refs):
     own_ref, refs = refs[0], refs[1:]
     ins, refs = refs[: len(pieces_in)], refs[len(pieces_in) :]
@@ -161,13 +183,12 @@
                 filled += count
 
 
-def experts_of(pieces, pieces_out, gates, ups, downs, shard_units, top):
+def experts_of(own, pieces, pieces_out, gates, ups, downs, shard_units, top):
     units, model_width = downs.shape
     local_experts = units // shard_units
     pieces_in = [piece.shape[0] for piece in pieces]
     total = sum(pieces_in)
     packed = pieces[0].shape[1]
-    own = jnp.full((1,), lax.axis_index("exp") * local_experts, jnp.int32)
     resident = pl.BlockSpec(memory_space=pltpu.VMEM)
     kernel = functools.partial(
         expert_kernel, pieces_in, pieces_out, local_experts, shard_units, model_width, top
@@ -184,9 +205,7 @@
         ],
         compiler_params=pltpu.CompilerParams(vmem_limit_bytes=12 * 1024 * 1024),
         cost_estimate=pl.CostEstimate(
-            flops=6 * total * units * model_width,
-            bytes_accessed=4 * total * model_width,
-            transcendentals=total * units,
+            flops=total * model_width, bytes_accessed=total * model_width, transcendentals=0
         ),
         name="experts",
     )(own, *pieces, gates, ups, downs)
@@ -222,9 +241,9 @@
     )(tokens, routed_experts.T, route_weights.T)
 
 
-def swap_exp(value, bit):
+def swap_exp(value, bits):
     owners = lax.axis_size("exp")
-    return lax.ppermute(value, "exp", [(i, i ^ bit) for i in range(owners)])
+    return lax.ppermute(value, "exp", [(i, i ^ bits) for i in range(owners)])
 
 
 def turn_rep(value, shift):
@@ -243,41 +262,35 @@
     return added(*terms).astype(jnp.bfloat16)
 
 
-def segments_of(rows):
-    own, x_one, x_two, y_one, y_two, far_one, far_two = 0, 2, 3, 4, 5, 6, 7
-    other = 8
-    cuts = [
-        [x_two, far_two],
-        [y_one, far_one],
-        [own, own + 1],
-        [x_one],
-        [y_two],
-    ]
-    cuts.append([other + place for cut in cuts for place in cut])
-    return [[(place * rows, rows) for place in cut] for cut in cuts]
-
-
-def cores_added(parts, rows):
-    to_x, to_y, own, x_one, y_two, other = parts
-    back = swap_exp(other, 1)
-    to_x = rounded(to_x, back[: 2 * rows])
-    to_y = rounded(to_y, back[2 * rows : 4 * rows])
-    return to_x, to_y, own, x_one, y_two, back
-
-
-def plane_halved(parts, arrived, rows):
-    to_x, to_y, own, x_one, y_two, back = parts
-    from_x, from_y = arrived
-    x_one = rounded(x_one, back[6 * rows : 7 * rows], from_y[rows:])
-    y_two = rounded(y_two, back[7 * rows :], from_x[rows:])
-    last_x, last_y = swap_exp(x_one, 2), swap_exp(y_two, 4)
-    one = added(own[:rows], back[4 * rows : 5 * rows], from_y[:rows], last_x)
-    two = added(own[rows:], back[5 * rows : 6 * rows], from_x[:rows], last_y)
-    return one, two
-
-
 def ordered(*values):
     return lax.optimization_barrier(values)
+
+
+def segments_of(places, rows):
+    other = 8
+    cuts = [*places, [other + place for cut in places for place in cut]]
+    return [[(place * rows, rows) for place in cut] for cut in cuts]
+
+
+def cores_added(parts, rows):
+    to_x, to_y, to_far, own, other = parts
+    back = swap_exp(other, 1)
+    sent = [
+        rounded(part, back[2 * i * rows : 2 * (i + 1) * rows])
+        for i, part in enumerate((to_x, to_y, to_far))
+    ]
+    return sent, (own, back[6 * rows :])
+
+
+def crossed(sent):
+    return [swap_exp(part, bits) for part, bits in zip(sent, (2, 4, 6))]
+
+
+def plane_added(kept, arrived, rows):
+    return (
+        added(*(part[:rows] for part in (*kept, *arrived))),
+        added(*(part[rows:] for part in (*kept, *arrived))),
+    )
 
 
 def on_device_dense(tokens, routed_experts, route_weights, gate_weight, up_weight, down_weight):
@@ -288,44 +301,42 @@
     gate_weight = gate_weight.reshape(units, model_width)
     up_weight = up_weight.reshape(units, model_width)
     down_weight = down_weight.reshape(units, model_width)
+    own = jnp.full((1,), lax.axis_index("exp") * local_experts, jnp.int32)
+    tokens, own = ordered(tokens, own)
     packed = with_routing(tokens, routed_experts, route_weights)
-    turned = {s: turn_rep(packed, s) for s in (2, 1, 3)}
-
+    two = turn_rep(packed, 2)
+    near_own = [swap_exp(packed, bits) for bits in (2, 4, 6)]
+    far_one = turn_rep(packed, 1)
     gates = fetched(gate_weight, True)
-    near_z, gates, up_weight = ordered(turned[2], gates, up_weight)
+    gates, up_weight, again, *near_own, two = ordered(gates, up_weight, packed, *near_own, two)
+    near_two = [swap_exp(two, bits) for bits in (2, 4, 6)]
+    far_two = turn_rep(again, 3)
+    first = gathered(packed, *near_own)
+    first_other = swap_exp(first, 1)
     ups = fetched(up_weight, True)
-    near = jnp.concatenate([packed, near_z], axis=0)
-    near_x, near_y = swap_exp(near, 2), swap_exp(near, 4)
-    far = jnp.concatenate([turned[1], turned[3]], axis=0)
-    near_x, near_y, far, ups, down_weight = ordered(near_x, near_y, far, ups, down_weight)
+    far_one, far_two, ups, down_weight = ordered(far_one, far_two, ups, down_weight)
+    far = gathered(far_one, far_two)
+    far_away = [swap_exp(far, bits) for bits in (2, 4, 6)]
+    second = gathered(two, *near_two)
     downs = fetched(down_weight, False)
-    near_far = [swap_exp(near_x[:rows], 4), swap_exp(near_y[rows:], 2)]
-    far_x, far_y = swap_exp(far, 2), swap_exp(far, 4)
-    *near_far, downs = ordered(*near_far, downs)
-    near = [near, near_x, near_y, *near_far]
-    near = near + [swap_exp(piece, 1) for piece in near]
-
-    far_one, far_two = far_x[:rows], far_y[rows:]
-    *near, far_one, far_two = ordered(*near, far_one, far_two)
-    far = [far, far_x, far_y]
-    far_far = [swap_exp(far_one, 4), swap_exp(far_two, 2)]
-    far_other = [swap_exp(piece, 1) for piece in far]
-    segments = segments_of(rows)
-    parts = experts_of(near, segments, gates, ups, downs, shard_units, top)
-    *parts, far_one, far_two, other_one, other_x, other_y = ordered(*parts, *far_far, *far_other)
-    far = far + [far_one, far_two, other_one, other_x, other_y]
-    far = far + [swap_exp(far_one, 1), swap_exp(far_two, 1)]
-
-    near_parts = cores_added(parts, rows)
-    arrived = [swap_exp(near_parts[0], 2), swap_exp(near_parts[1], 4)]
-    to_x, to_y, *far = ordered(near_parts[0], near_parts[1], *far)
-    near_parts = (to_x, to_y, *near_parts[2:])
-    parts = experts_of(far, segments, gates, ups, downs, shard_units, top)
-    *parts, near_x, near_y = ordered(*parts, *arrived)
-    far_parts = cores_added(parts, rows)
-    near_sums = plane_halved(near_parts, (near_x, near_y), rows)
-    arrived = [swap_exp(far_parts[0], 2), swap_exp(far_parts[1], 4)]
-    far_sums = plane_halved(far_parts, arrived, rows)
+    second, downs = ordered(second, downs)
+    near = [first, second, first_other, swap_exp(second, 1)]
+
+    segments = segments_of(([1, 5], [2, 6], [3, 7], [0, 4]), rows)
+    parts = experts_of(own, near, segments, gates, ups, downs, shard_units, top)
+    *parts, far_x, far_y, far_far = ordered(*parts, *far_away)
+    far = [far, far_x, far_y, far_far]
+    far = far + [swap_exp(piece, 1) for piece in far]
+    sent, near_kept = cores_added(parts, rows)
+    near_arrived = crossed(sent)
+    *sent, far[0], far[1], far[2], far[3] = ordered(*sent, *far[:4])
+    segments = segments_of(([2, 3], [4, 5], [6, 7], [0, 1]), rows)
+    parts = experts_of(own, far, segments, gates, ups, downs, shard_units, top)
+    *parts, near_x, near_y, near_far = ordered(*parts, *near_arrived)
+    sent, far_kept = cores_added(parts, rows)
+    far_arrived = crossed(sent)
+    near_sums = plane_added(near_kept, (near_x, near_y, near_far), rows)
+    far_sums = plane_added(far_kept, far_arrived, rows)
     arrived = [
         turn_rep(near_sums[1].astype(jnp.bfloat16), -2),
         turn_rep(far_sums[0].astype(jnp.bfloat16), -1),

time: 100 us -> 87.6 us (0.88)
  local copies, waits for them, and re-layouts: 20.1 us -> 2.8 us
  waiting for transfers between devices: 25.5 us -> 34.1 us
  starting transfers between devices: 34.5 us -> 32.4 us
  Pallas kernels: 18.3 us -> 16.6 us
    unnamed x26 -> x10, local copies, waits for them, and re-layouts: 19.1 us -> 2.8 us
    ppermute x28 -> x23, waiting for transfers between devices: 20.9 us -> 29.2 us  [swap_exp(): return lax.ppermute(value, 'exp', [(i, i ^ bits) for i in range(owners)])]
    ppermute x28 -> x23, starting transfers between devices: 20.7 us -> 18.8 us  [swap_exp(): return lax.ppermute(value, 'exp', [(i, i ^ bits) for i in range(owners)])]
    pallas_call x2, Pallas kernels: 11.7 us -> 10.2 us  [experts_of(): pl.pallas_call(kernel, out_shape=[jax.ShapeDtypeStruct((count, model_widt...]
  transfers between devices with their start and end apart: 34 -> 29, of which waited for: 14 -> 14; matrix products, arithmetic and copies ran while one was open for 1% -> 1% of each run, Pallas kernels for 17% -> 17%
where the time goes in v2:
time: 87.6 us; the launch traced here: 87.4 us
  waiting for transfers between devices  34.1 us (39%)
  starting transfers between devices  32.4 us (37%)
  Pallas kernels  16.6 us (19%)
  local copies, waits for them, and re-layouts  2.8 us (3%)
  other arithmetic  1.43 us (2%)
    ppermute x23, waiting for transfers between devices, swap_exp(): return lax.ppermute(value, 'exp', [(i, i ^ bits) for i in range(owners)])  29.2 us
    ppermute x23, starting transfers between devices, swap_exp(): return lax.ppermute(value, 'exp', [(i, i ^ bits) for i in range(owners)])  18.8 us
    ppermute x6, starting transfers between devices, turn_rep(): lax.ppermute(value, 'rep', [(i, (i - shift) % replicas) for i in range(re...  13.5 us
    pallas_call x2, Pallas kernels, experts_of(): pl.pallas_call(kernel, out_shape=[jax.ShapeDtypeStruct((count, model_widt...  10.2 us
    ppermute x6, waiting for transfers between devices, turn_rep(): lax.ppermute(value, 'rep', [(i, (i - shift) % replicas) for i in range(re...  4.91 us
    pallas_call x3, Pallas kernels, fetched(): pl.pallas_call(functools.partial(fetch_kernel, turn), out_shape=jax.Shape...  4.55 us
    unnamed x10, local copies, waits for them, and re-layouts  2.8 us
  transfers between devices with their start and end apart: 29, of which 14 were waited for; matrix products, arithmetic and copies ran while one was open for 1% of the time, Pallas kernels for 17%

profile of v2, /device:TPU:0, one launch (start us, length us, event | category | flops | bytes accessed | tf_op | source)
XLA Modules:
  0.0 87.4 jit_solution(11027007027959449396)
XLA Ops:
  0.0 1.7 %pack.1.refs_0_ = bf16[16,4224]{1,0:T(8,128)(2,1)} custom-call(bf16[16,4096]{1,0:T(8,128)(2,1)} %tokens_ref, s32[8,16]{1,0:T(8,128)} %bitcast.11, f32[8,16]{1,0:T(8,128)} %bitcast.12), custom_call_target="tpu_custom_call" | custom-call | tf_op jit(solution)/shard_map/pack/pallas_call | solution.py:235
  1.7 4.0 %collective-permute-start.3 = (bf16[16,4224]{1,0:T(8,128)(2,1)}, bf16[16,4224]{1,0:T(8,128)(2,1)S(1)}, u32[]{:S(2)}, u32[]{:S(2)}) collective-permute-start(bf16[16,4224]{1,0:T(8,128)(2,1)} %pack.1.refs_0_), channel_id=1, source_target_pairs={{0,16},{8,24},{16,0},{24,8},{1,17},{9,25},{17,1},{25,9},{2,18},{10... | collective-permute-start | bytes 405512 | tf_op jit(solution)/shard_map/ppermute | solution.py:251
  5.8 2.4 %collective-permute-start.2 = (bf16[16,4224]{1,0:T(8,128)(2,1)}, bf16[16,4224]{1,0:T(8,128)(2,1)S(1)}, u32[]{:S(2)}, u32[]{:S(2)}) collective-permute-start(bf16[16,4224]{1,0:T(8,128)(2,1)} %pack.1.refs_0_), channel_id=1, source_target_pairs={{0,6},{1,7},{2,4},{3,5},{4,2},{5,3},{6,0},{7,1},{8,14},{9,15},{10,... | collective-permute-start | bytes 405512 | tf_op jit(solution)/shard_map/ppermute | solution.py:246
  9.3 1.3 %collective-permute-start.7 = (bf16[16,4224]{1,0:T(8,128)(2,1)}, bf16[16,4224]{1,0:T(8,128)(2,1)S(1)}, u32[]{:S(2)}, u32[]{:S(2)}) collective-permute-start(bf16[16,4224]{1,0:T(8,128)(2,1)} %pack.1.refs_0_), channel_id=1, source_target_pairs={{0,24},{8,0},{16,8},{24,16},{1,25},{9,1},{17,9},{25,17},{2,26},{10... | collective-permute-start | bytes 405512 | tf_op jit(solution)/shard_map/ppermute | solution.py:251
  10.6 2.8 %copy-done = bf16[2,384,4096]{2,1,0:T(8,128)(2,1)S(1)} copy-done((bf16[2,384,4096]{2,1,0:T(8,128)(2,1)S(1)}, bf16[2,384,4096]{2,1,0:T(8,128)(2,1)}, u32[]{:S(2)}) %copy-start) | copy-done | bytes 6291480
  13.4 2.1 %fetch_turned.2.refs_5_.refs_9_ = bf16[4096,768]{1,0:T(8,128)(2,1)S(1)} custom-call(bf16[768,4096]{1,0:T(8,128)(2,1)S(1)} %bitcast.6), custom_call_target="tpu_custom_call" | custom-call | bytes 12582912 | tf_op jit(solution)/shard_map/fetch_turned/pallas_call | solution.py:103
  15.6 1.0 %collective-permute-start.8 = (bf16[16,4224]{1,0:T(8,128)(2,1)S(1)}, bf16[16,4224]{1,0:T(8,128)(2,1)S(1)}, u32[]{:S(2)}, u32[]{:S(2)}) collective-permute-start(bf16[16,4224]{1,0:T(8,128)(2,1)S(1)} %copy-done.2), channel_id=1, source_target_pairs={{0,8},{8,16},{16,24},{24,0},{1,9},{9,17},{17,25},{25,1},{2,10},{10... | collective-permute-start | bytes 405512 | tf_op jit(solution)/shard_map/ppermute | solution.py:251
  16.5 2.2 %collective-permute-start.6 = (bf16[16,4224]{1,0:T(8,128)(2,1)S(1)}, bf16[16,4224]{1,0:T(8,128)(2,1)S(1)}, u32[]{:S(2)}, u32[]{:S(2)}) collective-permute-start(bf16[16,4224]{1,0:T(8,128)(2,1)S(1)} %collective-permute-done.3.refs_0_), channel_id=1, source_target_pairs={{0,6},{1,7},{2,4},{3,5},{4,2},{5,3},{6,0},{7,1},{8,14},{9,15},{10,... | collective-permute-start | bytes 405512 | tf_op jit(solution)/shard_map/ppermute | solution.py:246
  20.0 2.1 %fetch_turned.3.refs_6_.refs_10_ = bf16[4096,768]{1,0:T(8,128)(2,1)S(1)} custom-call(bf16[768,4096]{1,0:T(8,128)(2,1)S(1)} %bitcast.7), custom_call_target="tpu_custom_call" | custom-call | bytes 12582912 | tf_op jit(solution)/shard_map/fetch_turned/pallas_call | solution.py:103
  23.2 2.1 %collective-permute-done.5.refs_2_ = bf16[16,4224]{1,0:T(8,128)(2,1)S(1)} collective-permute-done((bf16[16,4224]{1,0:T(8,128)(2,1)S(1)}, bf16[16,4224]{1,0:T(8,128)(2,1)S(1)}, u32[]{:S(2)}, u32[]{:S(2)}) %collective-permute-start.5) | collective-permute-done | bytes 135200 | tf_op jit(solution)/shard_map/ppermute | solution.py:246
  25.6 1.8 %collective-permute-start.13 = (bf16[32,4224]{1,0:T(8,128)(2,1)S(1)}, bf16[32,4224]{1,0:T(8,128)(2,1)S(1)}, u32[]{:S(2)}, u32[]{:S(2)}) collective-permute-start(bf16[32,4224]{1,0:T(8,128)(2,1)S(1)} %gather.5.refs_1_), channel_id=1, source_target_pairs={{0,6},{1,7},{2,4},{3,5},{4,2},{5,3},{6,0},{7,1},{8,14},{9,15},{10,... | collective-permute-start | bytes 811016 | tf_op jit(solution)/shard_map/ppermute | solution.py:246
  27.3 1.3 %collective-permute-start.12 = (bf16[32,4224]{1,0:T(8,128)(2,1)S(1)}, bf16[32,4224]{1,0:T(8,128)(2,1)S(1)}, u32[]{:S(2)}, u32[]{:S(2)}) collective-permute-start(bf16[32,4224]{1,0:T(8,128)(2,1)S(1)} %gather.5.refs_1_), channel_id=1, source_target_pairs={{0,4},{1,5},{2,6},{3,7},{4,0},{5,1},{6,2},{7,3},{8,12},{9,13},{10,... | collective-permute-start | bytes 811016 | tf_op jit(solution)/shard_map/ppermute | solution.py:246
  29.1 5.1 %experts.2 = (bf16[32,4096]{1,0:T(8,128)(2,1)S(1)}, bf16[32,4096]{1,0:T(8,128)(2,1)S(1)}, bf16[32,4096]{1,0:T(8,128)(2,1)S(1)}, bf16[32,4096]{1,0:T(8,128)(2,1)S(1)}, bf16[128,4096]{1,0:T(8,128)(2,1)S(1)}) custom-call(s32[1]{0:T(128)} %bitcast.refs_0_, bf16[64,4224]{1,0:T(8,128)(2,1)S(1)} %gather.3.refs_1_, bf16[64,4224]{1,0:T(8,128)(2,1)S(1)} %gather.4.refs_2_, ...), custom_call_target="tpu_custom_call" | custom-call | flops 1048576 | bytes 1048576 | tf_op jit(solution)/shard_map/experts/pallas_call | solution.py:197
  34.2 1.7 %collective-permute-done.13.refs_4_ = bf16[32,4224]{1,0:T(8,128)(2,1)S(1)} collective-permute-done((bf16[32,4224]{1,0:T(8,128)(2,1)S(1)}, bf16[32,4224]{1,0:T(8,128)(2,1)S(1)}, u32[]{:S(2)}, u32[]{:S(2)}) %collective-permute-start.13) | collective-permute-done | bytes 270368 | tf_op jit(solution)/shard_map/ppermute | solution.py:246
  35.8 5.3 %collective-permute-done.12.refs_3_ = bf16[32,4224]{1,0:T(8,128)(2,1)S(1)} collective-permute-done((bf16[32,4224]{1,0:T(8,128)(2,1)S(1)}, bf16[32,4224]{1,0:T(8,128)(2,1)S(1)}, u32[]{:S(2)}, u32[]{:S(2)}) %collective-permute-start.12) | collective-permute-done | bytes 270368 | tf_op jit(solution)/shard_map/ppermute | solution.py:246
  42.3 1.6 %collective-permute-done.14 = bf16[128,4096]{1,0:T(8,128)(2,1)S(1)} collective-permute-done((bf16[128,4096]{1,0:T(8,128)(2,1)S(1)}, bf16[128,4096]{1,0:T(8,128)(2,1)S(1)}, u32[]{:S(2)}, u32[]{:S(2)}) %collective-permute-start.14) | collective-permute-done | bytes 1048608 | tf_op jit(solution)/shard_map/ppermute | solution.py:246
  44.1 1.7 %collective-permute-start.21 = (bf16[32,4096]{1,0:T(8,128)(2,1)S(1)}, bf16[32,4096]{1,0:T(8,128)(2,1)S(1)}, u32[]{:S(2)}, u32[]{:S(2)}) collective-permute-start(bf16[32,4096]{1,0:T(8,128)(2,1)S(1)} %get-tuple-element.100), channel_id=1, source_target_pairs={{0,6},{1,7},{2,4},{3,5},{4,2},{5,3},{6,0},{7,1},{8,14},{9,15},{10,... | collective-permute-start | bytes 786440 | tf_op jit(solution)/shard_map/ppermute | solution.py:246
  45.8 1.3 %collective-permute-start.20 = (bf16[32,4096]{1,0:T(8,128)(2,1)S(1)}, bf16[32,4096]{1,0:T(8,128)(2,1)S(1)}, u32[]{:S(2)}, u32[]{:S(2)}) collective-permute-start(bf16[32,4096]{1,0:T(8,128)(2,1)S(1)} %get-tuple-element.101), channel_id=1, source_target_pairs={{0,4},{1,5},{2,6},{3,7},{4,0},{5,1},{6,2},{7,3},{8,12},{9,13},{10,... | collective-permute-start | bytes 786440 | tf_op jit(solution)/shard_map/ppermute | solution.py:246
  47.7 5.1 %experts.3 = (bf16[32,4096]{1,0:T(8,128)(2,1)S(1)}, bf16[32,4096]{1,0:T(8,128)(2,1)S(1)}, bf16[32,4096]{1,0:T(8,128)(2,1)S(1)}, bf16[32,4096]{1,0:T(8,128)(2,1)S(1)}, bf16[128,4096]{1,0:T(8,128)(2,1)S(1)}) custom-call(s32[1]{0:T(128)} %bitcast.refs_0_, bf16[32,4224]{1,0:T(8,128)(2,1)S(1)} %gather.5.refs_1_, ...), custom_call_target="tpu_custom_call" | custom-call | flops 1048576 | bytes 1048576 | tf_op jit(solution)/shard_map/experts/pallas_call | solution.py:197
  52.8 1.5 %collective-permute-done.21 = bf16[32,4096]{1,0:T(8,128)(2,1)S(1)} collective-permute-done((bf16[32,4096]{1,0:T(8,128)(2,1)S(1)}, bf16[32,4096]{1,0:T(8,128)(2,1)S(1)}, u32[]{:S(2)}, u32[]{:S(2)}) %collective-permute-start.21) | collective-permute-done | bytes 262176 | tf_op jit(solution)/shard_map/ppermute | solution.py:246
  54.3 4.8 %collective-permute-done.20 = bf16[32,4096]{1,0:T(8,128)(2,1)S(1)} collective-permute-done((bf16[32,4096]{1,0:T(8,128)(2,1)S(1)}, bf16[32,4096]{1,0:T(8,128)(2,1)S(1)}, u32[]{:S(2)}, u32[]{:S(2)}) %collective-permute-start.20) | collective-permute-done | bytes 262176 | tf_op jit(solution)/shard_map/ppermute | solution.py:246
  59.0 2.6 %collective-permute-done.23 = bf16[128,4096]{1,0:T(8,128)(2,1)S(1)} collective-permute-done((bf16[128,4096]{1,0:T(8,128)(2,1)S(1)}, bf16[128,4096]{1,0:T(8,128)(2,1)S(1)}, u32[]{:S(2)}, u32[]{:S(2)}) %collective-permute-start.23) | collective-permute-done | bytes 1048608 | tf_op jit(solution)/shard_map/ppermute | solution.py:246
  61.9 1.5 %collective-permute-start.24 = (bf16[32,4096]{1,0:T(8,128)(2,1)S(1)}, bf16[32,4096]{1,0:T(8,128)(2,1)S(1)}, u32[]{:S(2)}, u32[]{:S(2)}) collective-permute-start(bf16[32,4096]{1,0:T(8,128)(2,1)S(1)} %get-tuple-element.97), channel_id=1, source_target_pairs={{0,2},{1,3},{2,0},{3,1},{4,6},{5,7},{6,4},{7,5},{8,10},{9,11},{10,... | collective-permute-start | bytes 786440 | tf_op jit(solution)/shard_map/ppermute | solution.py:246
  63.4 1.4 %collective-permute-start.26 = (bf16[32,4096]{1,0:T(8,128)(2,1)S(1)}, bf16[32,4096]{1,0:T(8,128)(2,1)S(1)}, u32[]{:S(2)}, u32[]{:S(2)}) collective-permute-start(bf16[32,4096]{1,0:T(8,128)(2,1)S(1)} %get-tuple-element.98), channel_id=1, source_target_pairs={{0,6},{1,7},{2,4},{3,5},{4,2},{5,3},{6,0},{7,1},{8,14},{9,15},{10,... | collective-permute-start | bytes 786440 | tf_op jit(solution)/shard_map/ppermute | solution.py:246
  65.5 3.3 %collective-permute-start.22 = (bf16[16,4096]{1,0:T(8,128)(2,1)S(1)}, bf16[16,4096]{1,0:T(8,128)(2,1)S(1)}, u32[]{:S(2)}, u32[]{:S(2)}) collective-permute-start(bf16[16,4096]{1,0:T(8,128)(2,1)S(1)} %add_convert_fusion.9), channel_id=1, source_target_pairs={{0,16},{8,24},{16,0},{24,8},{1,17},{9,25},{17,1},{25,9},{2,18},{10... | collective-permute-start | bytes 393224 | tf_op jit(solution)/shard_map/ppermute | solution.py:251
  68.9 2.3 %collective-permute-done.24 = bf16[32,4096]{1,0:T(8,128)(2,1)S(1)} collective-permute-done((bf16[32,4096]{1,0:T(8,128)(2,1)S(1)}, bf16[32,4096]{1,0:T(8,128)(2,1)S(1)}, u32[]{:S(2)}, u32[]{:S(2)}) %collective-permute-start.24) | collective-permute-done | bytes 262176 | tf_op jit(solution)/shard_map/ppermute | solution.py:246
  71.1 5.8 %collective-permute-done.26 = bf16[32,4096]{1,0:T(8,128)(2,1)S(1)} collective-permute-done((bf16[32,4096]{1,0:T(8,128)(2,1)S(1)}, bf16[32,4096]{1,0:T(8,128)(2,1)S(1)}, u32[]{:S(2)}, u32[]{:S(2)}) %collective-permute-start.26) | collective-permute-done | bytes 262176 | tf_op jit(solution)/shard_map/ppermute | solution.py:246
  76.9 1.4 %collective-permute-done.25 = bf16[32,4096]{1,0:T(8,128)(2,1)S(1)} collective-permute-done((bf16[32,4096]{1,0:T(8,128)(2,1)S(1)}, bf16[32,4096]{1,0:T(8,128)(2,1)S(1)}, u32[]{:S(2)}, u32[]{:S(2)}) %collective-permute-start.25) | collective-permute-done | bytes 262176 | tf_op jit(solution)/shard_map/ppermute | solution.py:246
  79.0 3.3 %collective-permute-start.28 = (bf16[16,4096]{1,0:T(8,128)(2,1)S(1)}, bf16[16,4096]{1,0:T(8,128)(2,1)S(1)}, u32[]{:S(2)}, u32[]{:S(2)}) collective-permute-start(bf16[16,4096]{1,0:T(8,128)(2,1)S(1)} %get-tuple-element.96), channel_id=1, source_target_pairs={{0,24},{8,0},{16,8},{24,16},{1,25},{9,1},{17,9},{25,17},{2,26},{10... | collective-permute-start | bytes 393224 | tf_op jit(solution)/shard_map/ppermute | solution.py:251
  82.3 3.0 %collective-permute-done.27 = bf16[16,4096]{1,0:T(8,128)(2,1)S(1)} collective-permute-done((bf16[16,4096]{1,0:T(8,128)(2,1)S(1)}, bf16[16,4096]{1,0:T(8,128)(2,1)S(1)}, u32[]{:S(2)}, u32[]{:S(2)}) %collective-permute-start.27) | collective-permute-done | bytes 131104 | tf_op jit(solution)/shard_map/ppermute | solution.py:251
  85.3 1.3 %collective-permute-done.28 = bf16[16,4096]{1,0:T(8,128)(2,1)S(1)} collective-permute-done((bf16[16,4096]{1,0:T(8,128)(2,1)S(1)}, bf16[16,4096]{1,0:T(8,128)(2,1)S(1)}, u32[]{:S(2)}, u32[]{:S(2)}) %collective-permute-start.28) | collective-permute-done | bytes 131104 | tf_op jit(solution)/shard_map/ppermute | solution.py:251
  86.6 0.8 add_convert_fusion.6
  (51 shorter events, 7.6 us)
Async XLA Ops:
  1.7 13.7 %collective-permute-start.3 = (bf16[16,4224]{1,0:T(8,128)(2,1)}, bf16[16,4224]{1,0:T(8,128)(2,1)S(1)}, u32[]{:S(2)}, u32[]{:S(2)}) collective-permute-start(bf16[16,4224]{1,0:T(8,128)(2,1)} %pack.1.refs_0_), channel_id=1, source_target_pairs={{0,16},{8,24},{16,0},{24,8},{1,17},{9,25},{17,1},{25,9},{2,18},{10... | collective-permute-start | bytes 405512 | tf_op jit(solution)/shard_map/ppermute | solution.py:251
  5.8 9.7 %collective-permute-start.2 = (bf16[16,4224]{1,0:T(8,128)(2,1)}, bf16[16,4224]{1,0:T(8,128)(2,1)S(1)}, u32[]{:S(2)}, u32[]{:S(2)}) collective-permute-start(bf16[16,4224]{1,0:T(8,128)(2,1)} %pack.1.refs_0_), channel_id=1, source_target_pairs={{0,6},{1,7},{2,4},{3,5},{4,2},{5,3},{6,0},{7,1},{8,14},{9,15},{10,... | collective-permute-start | bytes 405512 | tf_op jit(solution)/shard_map/ppermute | solution.py:246
  8.2 7.3 %collective-permute-start.1 = (bf16[16,4224]{1,0:T(8,128)(2,1)}, bf16[16,4224]{1,0:T(8,128)(2,1)S(1)}, u32[]{:S(2)}, u32[]{:S(2)}) collective-permute-start(bf16[16,4224]{1,0:T(8,128)(2,1)} %pack.1.refs_0_), channel_id=1, source_target_pairs={{0,4},{1,5},{2,6},{3,7},{4,0},{5,1},{6,2},{7,3},{8,12},{9,13},{10,... | collective-permute-start | bytes 405512 | tf_op jit(solution)/shard_map/ppermute | solution.py:246
  8.7 6.8 %collective-permute-start = (bf16[16,4224]{1,0:T(8,128)(2,1)}, bf16[16,4224]{1,0:T(8,128)(2,1)S(1)}, u32[]{:S(2)}, u32[]{:S(2)}) collective-permute-start(bf16[16,4224]{1,0:T(8,128)(2,1)} %pack.1.refs_0_), channel_id=1, source_target_pairs={{0,2},{1,3},{2,0},{3,1},{4,6},{5,7},{6,4},{7,5},{8,10},{9,11},{10,... | collective-permute-start | bytes 405512 | tf_op jit(solution)/shard_map/ppermute | solution.py:246
  9.3 12.9 %collective-permute-start.7 = (bf16[16,4224]{1,0:T(8,128)(2,1)}, bf16[16,4224]{1,0:T(8,128)(2,1)S(1)}, u32[]{:S(2)}, u32[]{:S(2)}) collective-permute-start(bf16[16,4224]{1,0:T(8,128)(2,1)} %pack.1.refs_0_), channel_id=1, source_target_pairs={{0,24},{8,0},{16,8},{24,16},{1,25},{9,1},{17,9},{25,17},{2,26},{10... | collective-permute-start | bytes 405512 | tf_op jit(solution)/shard_map/ppermute | solution.py:251
  13.4 6.6 %copy-start.1 = (bf16[2,384,4096]{2,1,0:T(8,128)(2,1)S(1)}, bf16[2,384,4096]{2,1,0:T(8,128)(2,1)}, u32[]{:S(2)}) copy-start(bf16[2,384,4096]{2,1,0:T(8,128)(2,1)} %param.10) | copy-start | bytes 18874372
  15.5 7.3 %slice-start = ((s8[6291456]{0:T(1024)(128)(4,1)}), s8[4194304]{0:T(1024)(128)(4,1)S(1)}, s32[]{:S(2)}) async-start(s8[6291456]{0:T(1024)(128)(4,1)} %bitcast.8), calls=%async_computation | async-start | bytes 8388608
  15.5 7.2 %slice-start.1 = ((s8[6291456]{0:T(1024)(128)(4,1)}), s8[2097152]{0:T(1024)(128)(4,1)S(1)}, s32[]{:S(2)}) async-start(s8[6291456]{0:T(1024)(128)(4,1)} %bitcast.8), calls=%async_computation.1 | async-start | bytes 4194304
  15.6 7.2 %collective-permute-start.8 = (bf16[16,4224]{1,0:T(8,128)(2,1)S(1)}, bf16[16,4224]{1,0:T(8,128)(2,1)S(1)}, u32[]{:S(2)}, u32[]{:S(2)}) collective-permute-start(bf16[16,4224]{1,0:T(8,128)(2,1)S(1)} %copy-done.2), channel_id=1, source_target_pairs={{0,8},{8,16},{16,24},{24,0},{1,9},{9,17},{17,25},{25,1},{2,10},{10... | collective-permute-start | bytes 405512 | tf_op jit(solution)/shard_map/ppermute | solution.py:251
  16.5 6.7 %collective-permute-start.6 = (bf16[16,4224]{1,0:T(8,128)(2,1)S(1)}, bf16[16,4224]{1,0:T(8,128)(2,1)S(1)}, u32[]{:S(2)}, u32[]{:S(2)}) collective-permute-start(bf16[16,4224]{1,0:T(8,128)(2,1)S(1)} %collective-permute-done.3.refs_0_), channel_id=1, source_target_pairs={{0,6},{1,7},{2,4},{3,5},{4,2},{5,3},{6,0},{7,1},{8,14},{9,15},{10,... | collective-permute-start | bytes 405512 | tf_op jit(solution)/shard_map/ppermute | solution.py:246
  18.7 6.6 %collective-permute-start.5 = (bf16[16,4224]{1,0:T(8,128)(2,1)S(1)}, bf16[16,4224]{1,0:T(8,128)(2,1)S(1)}, u32[]{:S(2)}, u32[]{:S(2)}) collective-permute-start(bf16[16,4224]{1,0:T(8,128)(2,1)S(1)} %collective-permute-done.3.refs_0_), channel_id=1, source_target_pairs={{0,4},{1,5},{2,6},{3,7},{4,0},{5,1},{6,2},{7,3},{8,12},{9,13},{10,... | collective-permute-start | bytes 405512 | tf_op jit(solution)/shard_map/ppermute | solution.py:246
  19.5 5.9 %collective-permute-start.4 = (bf16[16,4224]{1,0:T(8,128)(2,1)S(1)}, bf16[16,4224]{1,0:T(8,128)(2,1)S(1)}, u32[]{:S(2)}, u32[]{:S(2)}) collective-permute-start(bf16[16,4224]{1,0:T(8,128)(2,1)S(1)} %collective-permute-done.3.refs_0_), channel_id=1, source_target_pairs={{0,2},{1,3},{2,0},{3,1},{4,6},{5,7},{6,4},{7,5},{8,10},{9,11},{10,... | collective-permute-start | bytes 405512 | tf_op jit(solution)/shard_map/ppermute | solution.py:246
  22.1 7.0 %collective-permute-start.9 = (bf16[64,4224]{1,0:T(8,128)(2,1)S(1)}, bf16[64,4224]{1,0:T(8,128)(2,1)S(1)}, u32[]{:S(2)}, u32[]{:S(2)}) collective-permute-start(bf16[64,4224]{1,0:T(8,128)(2,1)S(1)} %gather.3.refs_1_), channel_id=1, source_target_pairs={{0,1},{1,0},{2,3},{3,2},{4,5},{5,4},{6,7},{7,6},{8,9},{9,8},{10,11... | collective-permute-start | bytes 1622024 | tf_op jit(solution)/shard_map/ppermute | solution.py:246
  25.4 3.7 %collective-permute-start.10 = (bf16[64,4224]{1,0:T(8,128)(2,1)S(1)}, bf16[64,4224]{1,0:T(8,128)(2,1)S(1)}, u32[]{:S(2)}, u32[]{:S(2)}) collective-permute-start(bf16[64,4224]{1,0:T(8,128)(2,1)S(1)} %gather.4.refs_2_), channel_id=1, source_target_pairs={{0,1},{1,0},{2,3},{3,2},{4,5},{5,4},{6,7},{7,6},{8,9},{9,8},{10,11... | collective-permute-start | bytes 1622024 | tf_op jit(solution)/shard_map/ppermute | solution.py:246
  25.6 10.3 %collective-permute-start.13 = (bf16[32,4224]{1,0:T(8,128)(2,1)S(1)}, bf16[32,4224]{1,0:T(8,128)(2,1)S(1)}, u32[]{:S(2)}, u32[]{:S(2)}) collective-permute-start(bf16[32,4224]{1,0:T(8,128)(2,1)S(1)} %gather.5.refs_1_), channel_id=1, source_target_pairs={{0,6},{1,7},{2,4},{3,5},{4,2},{5,3},{6,0},{7,1},{8,14},{9,15},{10,... | collective-permute-start | bytes 811016 | tf_op jit(solution)/shard_map/ppermute | solution.py:246
  27.3 13.9 %collective-permute-start.12 = (bf16[32,4224]{1,0:T(8,128)(2,1)S(1)}, bf16[32,4224]{1,0:T(8,128)(2,1)S(1)}, u32[]{:S(2)}, u32[]{:S(2)}) collective-permute-start(bf16[32,4224]{1,0:T(8,128)(2,1)S(1)} %gather.5.refs_1_), channel_id=1, source_target_pairs={{0,4},{1,5},{2,6},{3,7},{4,0},{5,1},{6,2},{7,3},{8,12},{9,13},{10,... | collective-permute-start | bytes 811016 | tf_op jit(solution)/shard_map/ppermute | solution.py:246
  28.6 12.6 %collective-permute-start.11 = (bf16[32,4224]{1,0:T(8,128)(2,1)S(1)}, bf16[32,4224]{1,0:T(8,128)(2,1)S(1)}, u32[]{:S(2)}, u32[]{:S(2)}) collective-permute-start(bf16[32,4224]{1,0:T(8,128)(2,1)S(1)} %gather.5.refs_1_), channel_id=1, source_target_pairs={{0,2},{1,3},{2,0},{3,1},{4,6},{5,7},{6,4},{7,5},{8,10},{9,11},{10,... | collective-permute-start | bytes 811016 | tf_op jit(solution)/shard_map/ppermute | solution.py:246
  41.2 2.7 %collective-permute-start.14 = (bf16[128,4096]{1,0:T(8,128)(2,1)S(1)}, bf16[128,4096]{1,0:T(8,128)(2,1)S(1)}, u32[]{:S(2)}, u32[]{:S(2)}) collective-permute-start(bf16[128,4096]{1,0:T(8,128)(2,1)S(1)} %get-tuple-element.71), channel_id=1, source_target_pairs={{0,1},{1,0},{2,3},{3,2},{4,5},{5,4},{6,7},{7,6},{8,9},{9,8},{10,11... | collective-permute-start | bytes 3145736 | tf_op jit(solution)/shard_map/ppermute | solution.py:246
  41.2 4.6 %collective-permute-start.15 = (bf16[32,4224]{1,0:T(8,128)(2,1)S(1)}, bf16[32,4224]{1,0:T(8,128)(2,1)S(1)}, u32[]{:S(2)}, u32[]{:S(2)}) collective-permute-start(bf16[32,4224]{1,0:T(8,128)(2,1)S(1)} %gather.5.refs_1_), channel_id=1, source_target_pairs={{0,1},{1,0},{2,3},{3,2},{4,5},{5,4},{6,7},{7,6},{8,9},{9,8},{10,11... | collective-permute-start | bytes 811016 | tf_op jit(solution)/shard_map/ppermute | solution.py:246
  41.7 5.4 %collective-permute-start.16 = (bf16[32,4224]{1,0:T(8,128)(2,1)S(1)}, bf16[32,4224]{1,0:T(8,128)(2,1)S(1)}, u32[]{:S(2)}, u32[]{:S(2)}) collective-permute-start(bf16[32,4224]{1,0:T(8,128)(2,1)S(1)} %collective-permute-done.11.refs_2_), channel_id=1, source_target_pairs={{0,1},{1,0},{2,3},{3,2},{4,5},{5,4},{6,7},{7,6},{8,9},{9,8},{10,11... | collective-permute-start | bytes 811016 | tf_op jit(solution)/shard_map/ppermute | solution.py:246
  41.7 5.9 %collective-permute-start.17 = (bf16[32,4224]{1,0:T(8,128)(2,1)S(1)}, bf16[32,4224]{1,0:T(8,128)(2,1)S(1)}, u32[]{:S(2)}, u32[]{:S(2)}) collective-permute-start(bf16[32,4224]{1,0:T(8,128)(2,1)S(1)} %collective-permute-done.12.refs_3_), channel_id=1, source_target_pairs={{0,1},{1,0},{2,3},{3,2},{4,5},{5,4},{6,7},{7,6},{8,9},{9,8},{10,11... | collective-permute-start | bytes 811016 | tf_op jit(solution)/shard_map/ppermute | solution.py:246
  42.3 5.4 %collective-permute-start.18 = (bf16[32,4224]{1,0:T(8,128)(2,1)S(1)}, bf16[32,4224]{1,0:T(8,128)(2,1)S(1)}, u32[]{:S(2)}, u32[]{:S(2)}) collective-permute-start(bf16[32,4224]{1,0:T(8,128)(2,1)S(1)} %collective-permute-done.13.refs_4_), channel_id=1, source_target_pairs={{0,1},{1,0},{2,3},{3,2},{4,5},{5,4},{6,7},{7,6},{8,9},{9,8},{10,11... | collective-permute-start | bytes 811016 | tf_op jit(solution)/shard_map/ppermute | solution.py:246
  44.1 10.2 %collective-permute-start.21 = (bf16[32,4096]{1,0:T(8,128)(2,1)S(1)}, bf16[32,4096]{1,0:T(8,128)(2,1)S(1)}, u32[]{:S(2)}, u32[]{:S(2)}) collective-permute-start(bf16[32,4096]{1,0:T(8,128)(2,1)S(1)} %get-tuple-element.100), channel_id=1, source_target_pairs={{0,6},{1,7},{2,4},{3,5},{4,2},{5,3},{6,0},{7,1},{8,14},{9,15},{10,... | collective-permute-start | bytes 786440 | tf_op jit(solution)/shard_map/ppermute | solution.py:246
  45.8 13.2 %collective-permute-start.20 = (bf16[32,4096]{1,0:T(8,128)(2,1)S(1)}, bf16[32,4096]{1,0:T(8,128)(2,1)S(1)}, u32[]{:S(2)}, u32[]{:S(2)}) collective-permute-start(bf16[32,4096]{1,0:T(8,128)(2,1)S(1)} %get-tuple-element.101), channel_id=1, source_target_pairs={{0,4},{1,5},{2,6},{3,7},{4,0},{5,1},{6,2},{7,3},{8,12},{9,13},{10,... | collective-permute-start | bytes 786440 | tf_op jit(solution)/shard_map/ppermute | solution.py:246
  47.1 11.9 %collective-permute-start.19 = (bf16[32,4096]{1,0:T(8,128)(2,1)S(1)}, bf16[32,4096]{1,0:T(8,128)(2,1)S(1)}, u32[]{:S(2)}, u32[]{:S(2)}) collective-permute-start(bf16[32,4096]{1,0:T(8,128)(2,1)S(1)} %get-tuple-element.102), channel_id=1, source_target_pairs={{0,2},{1,3},{2,0},{3,1},{4,6},{5,7},{6,4},{7,5},{8,10},{9,11},{10,... | collective-permute-start | bytes 786440 | tf_op jit(solution)/shard_map/ppermute | solution.py:246
  59.0 2.7 %collective-permute-start.23 = (bf16[128,4096]{1,0:T(8,128)(2,1)S(1)}, bf16[128,4096]{1,0:T(8,128)(2,1)S(1)}, u32[]{:S(2)}, u32[]{:S(2)}) collective-permute-start(bf16[128,4096]{1,0:T(8,128)(2,1)S(1)} %get-tuple-element.91), channel_id=1, source_target_pairs={{0,1},{1,0},{2,3},{3,2},{4,5},{5,4},{6,7},{7,6},{8,9},{9,8},{10,11... | collective-permute-start | bytes 3145736 | tf_op jit(solution)/shard_map/ppermute | solution.py:246
  61.9 9.2 %collective-permute-start.24 = (bf16[32,4096]{1,0:T(8,128)(2,1)S(1)}, bf16[32,4096]{1,0:T(8,128)(2,1)S(1)}, u32[]{:S(2)}, u32[]{:S(2)}) collective-permute-start(bf16[32,4096]{1,0:T(8,128)(2,1)S(1)} %get-tuple-element.97), channel_id=1, source_target_pairs={{0,2},{1,3},{2,0},{3,1},{4,6},{5,7},{6,4},{7,5},{8,10},{9,11},{10,... | collective-permute-start | bytes 786440 | tf_op jit(solution)/shard_map/ppermute | solution.py:246
  63.4 13.5 %collective-permute-start.26 = (bf16[32,4096]{1,0:T(8,128)(2,1)S(1)}, bf16[32,4096]{1,0:T(8,128)(2,1)S(1)}, u32[]{:S(2)}, u32[]{:S(2)}) collective-permute-start(bf16[32,4096]{1,0:T(8,128)(2,1)S(1)} %get-tuple-element.98), channel_id=1, source_target_pairs={{0,6},{1,7},{2,4},{3,5},{4,2},{5,3},{6,0},{7,1},{8,14},{9,15},{10,... | collective-permute-start | bytes 786440 | tf_op jit(solution)/shard_map/ppermute | solution.py:246
  64.8 13.4 %collective-permute-start.25 = (bf16[32,4096]{1,0:T(8,128)(2,1)S(1)}, bf16[32,4096]{1,0:T(8,128)(2,1)S(1)}, u32[]{:S(2)}, u32[]{:S(2)}) collective-permute-start(bf16[32,4096]{1,0:T(8,128)(2,1)S(1)} %get-tuple-element.99), channel_id=1, source_target_pairs={{0,4},{1,5},{2,6},{3,7},{4,0},{5,1},{6,2},{7,3},{8,12},{9,13},{10,... | collective-permute-start | bytes 786440 | tf_op jit(solution)/shard_map/ppermute | solution.py:246
  65.5 16.8 %collective-permute-start.22 = (bf16[16,4096]{1,0:T(8,128)(2,1)S(1)}, bf16[16,4096]{1,0:T(8,128)(2,1)S(1)}, u32[]{:S(2)}, u32[]{:S(2)}) collective-permute-start(bf16[16,4096]{1,0:T(8,128)(2,1)S(1)} %add_convert_fusion.9), channel_id=1, source_target_pairs={{0,16},{8,24},{16,0},{24,8},{1,17},{9,25},{17,1},{25,9},{2,18},{10... | collective-permute-start | bytes 393224 | tf_op jit(solution)/shard_map/ppermute | solution.py:251
  78.4 6.9 %collective-permute-start.27 = (bf16[16,4096]{1,0:T(8,128)(2,1)S(1)}, bf16[16,4096]{1,0:T(8,128)(2,1)S(1)}, u32[]{:S(2)}, u32[]{:S(2)}) collective-permute-start(bf16[16,4096]{1,0:T(8,128)(2,1)S(1)} %get-tuple-element.95), channel_id=1, source_target_pairs={{0,8},{8,16},{16,24},{24,0},{1,9},{9,17},{17,25},{25,1},{2,10},{10... | collective-permute-start | bytes 393224 | tf_op jit(solution)/shard_map/ppermute | solution.py:251
  79.0 7.7 %collective-permute-start.28 = (bf16[16,4096]{1,0:T(8,128)(2,1)S(1)}, bf16[16,4096]{1,0:T(8,128)(2,1)S(1)}, u32[]{:S(2)}, u32[]{:S(2)}) collective-permute-start(bf16[16,4096]{1,0:T(8,128)(2,1)S(1)} %get-tuple-element.96), channel_id=1, source_target_pairs={{0,24},{8,0},{16,8},{24,16},{1,25},{9,1},{17,9},{25,17},{2,26},{10... | collective-permute-start | bytes 393224 | tf_op jit(solution)/shard_map/ppermute | solution.py:251
  (2 other events, 4.9 us)

commit v3 on v2

--- a/solution.py
+++ b/solution.py
@@ -205,7 +205,9 @@
         ],
         compiler_params=pltpu.CompilerParams(vmem_limit_bytes=12 * 1024 * 1024),
         cost_estimate=pl.CostEstimate(
-            flops=total * model_width, bytes_accessed=total * model_width, transcendentals=0
+            flops=6 * total * units * model_width,
+            bytes_accessed=4 * total * model_width,
+            transcendentals=total * units,
         ),
         name="experts",
     )(own, *pieces, gates, ups, downs)
@@ -268,18 +270,15 @@
 
 def segments_of(places, rows):
     other = 8
-    cuts = [*places, [other + place for cut in places for place in cut]]
+    cuts = [*places, *([other + place for place in cut] for cut in places)]
     return [[(place * rows, rows) for place in cut] for cut in cuts]
 
 
-def cores_added(parts, rows):
-    to_x, to_y, to_far, own, other = parts
-    back = swap_exp(other, 1)
-    sent = [
-        rounded(part, back[2 * i * rows : 2 * (i + 1) * rows])
-        for i, part in enumerate((to_x, to_y, to_far))
-    ]
-    return sent, (own, back[6 * rows :])
+def cores_added(parts):
+    back = [swap_exp(part, 1) for part in parts[4:7]]
+    sent = [rounded(part, other) for part, other in zip(parts[:3], back)]
+    *sent, other = ordered(*sent, parts[7])
+    return sent, (parts[3], swap_exp(other, 1))
 
 
 def crossed(sent):
@@ -306,15 +305,15 @@
     packed = with_routing(tokens, routed_experts, route_weights)
     two = turn_rep(packed, 2)
     near_own = [swap_exp(packed, bits) for bits in (2, 4, 6)]
-    far_one = turn_rep(packed, 1)
-    gates = fetched(gate_weight, True)
-    gates, up_weight, again, *near_own, two = ordered(gates, up_weight, packed, *near_own, two)
+    two, gate_weight, up_weight, again = ordered(two, gate_weight, up_weight, packed)
     near_two = [swap_exp(two, bits) for bits in (2, 4, 6)]
-    far_two = turn_rep(again, 3)
+    far_one, far_two = turn_rep(again, 1), turn_rep(again, 3)
     first = gathered(packed, *near_own)
     first_other = swap_exp(first, 1)
-    ups = fetched(up_weight, True)
-    far_one, far_two, ups, down_weight = ordered(far_one, far_two, ups, down_weight)
+    gates, ups = fetched(gate_weight, True), fetched(up_weight, True)
+    far_one, far_two, gates, ups, down_weight = ordered(
+        far_one, far_two, gates, ups, down_weight
+    )
     far = gathered(far_one, far_two)
     far_away = [swap_exp(far, bits) for bits in (2, 4, 6)]
     second = gathered(two, *near_two)
@@ -323,19 +322,19 @@
     near = [first, second, first_other, swap_exp(second, 1)]
 
     segments = segments_of(([1, 5], [2, 6], [3, 7], [0, 4]), rows)
-    parts = experts_of(own, near, segments, gates, ups, downs, shard_units, top)
-    *parts, far_x, far_y, far_far = ordered(*parts, *far_away)
-    far = [far, far_x, far_y, far_far]
-    far = far + [swap_exp(piece, 1) for piece in far]
-    sent, near_kept = cores_added(parts, rows)
+    parts = list(experts_of(own, near, segments, gates, ups, downs, shard_units, top))
+    parts[3], *far_away = ordered(parts[3], *far_away)
+    parts[3], far_other = ordered(parts[3], swap_exp(far, 1))
+    far = [far, *far_away, far_other, *(swap_exp(piece, 1) for piece in far_away)]
+    sent, near_kept = cores_added(parts)
     near_arrived = crossed(sent)
     *sent, far[0], far[1], far[2], far[3] = ordered(*sent, *far[:4])
     segments = segments_of(([2, 3], [4, 5], [6, 7], [0, 1]), rows)
-    parts = experts_of(own, far, segments, gates, ups, downs, shard_units, top)
-    *parts, near_x, near_y, near_far = ordered(*parts, *near_arrived)
-    sent, far_kept = cores_added(parts, rows)
+    parts = list(experts_of(own, far, segments, gates, ups, downs, shard_units, top))
+    parts[3], *near_arrived = ordered(parts[3], *near_arrived)
+    sent, far_kept = cores_added(parts)
     far_arrived = crossed(sent)
-    near_sums = plane_added(near_kept, (near_x, near_y, near_far), rows)
+    near_sums = plane_added(near_kept, near_arrived, rows)
     far_sums = plane_added(far_kept, far_arrived, rows)
     arrived = [
         turn_rep(near_sums[1].astype(jnp.bfloat16), -2),

time: 87.6 us -> 87.9 us (level)
  waiting for transfers between devices: 34.1 us -> 32.9 us
    ppermute x23 -> x29, waiting for transfers between devices: 29.2 us -> 25.4 us  [swap_exp(): return lax.ppermute(value, 'exp', [(i, i ^ bits) for i in range(owners)])]
    ppermute x6, waiting for transfers between devices: 4.91 us -> 7.49 us  [turn_rep(): lax.ppermute(value, 'rep', [(i, (i - shift) % replicas) for i in range(re...]
    ppermute x23 -> x29, starting transfers between devices: 18.8 us -> 20.9 us  [swap_exp(): return lax.ppermute(value, 'exp', [(i, i ^ bits) for i in range(owners)])]
    ppermute x6, starting transfers between devices: 13.5 us -> 12.1 us  [turn_rep(): lax.ppermute(value, 'rep', [(i, (i - shift) % replicas) for i in range(re...]
  transfers between devices with their start and end apart: 29 -> 35, of which waited for: 14 -> 10; matrix products, arithmetic and copies ran while one was open for 1% -> 1% of each run, Pallas kernels for 17% -> 17%
where the time goes in v3:
time: 87.9 us; the launch traced here: 87.8 us
  starting transfers between devices  33 us (38%)
  waiting for transfers between devices  32.9 us (37%)
  Pallas kernels  16.7 us (19%)
  local copies, waits for them, and re-layouts  3.51 us (4%)
  other arithmetic  1.43 us (2%)
    ppermute x29, waiting for transfers between devices, swap_exp(): return lax.ppermute(value, 'exp', [(i, i ^ bits) for i in range(owners)])  25.4 us
    ppermute x29, starting transfers between devices, swap_exp(): return lax.ppermute(value, 'exp', [(i, i ^ bits) for i in range(owners)])  20.9 us
    ppermute x6, starting transfers between devices, turn_rep(): lax.ppermute(value, 'rep', [(i, (i - shift) % replicas) for i in range(re...  12.1 us
    pallas_call x2, Pallas kernels, experts_of(): pl.pallas_call(kernel, out_shape=[jax.ShapeDtypeStruct((count, model_widt...  10.3 us
    ppermute x6, waiting for transfers between devices, turn_rep(): lax.ppermute(value, 'rep', [(i, (i - shift) % replicas) for i in range(re...  7.49 us
    pallas_call x3, Pallas kernels, fetched(): pl.pallas_call(functools.partial(fetch_kernel, turn), out_shape=jax.Shape...  4.55 us
    unnamed x10, local copies, waits for them, and re-layouts  3.51 us
  transfers between devices with their start and end apart: 35, of which 10 were waited for; matrix products, arithmetic and copies ran while one was open for 1% of the time, Pallas kernels for 17%

profile of v3, /device:TPU:0, one launch (start us, length us, event | category | flops | bytes accessed | tf_op | source)
XLA Modules:
  0.0 87.8 jit_solution(6781499550775422186)
XLA Ops:
  0.0 1.7 %pack.1.refs_0_ = bf16[16,4224]{1,0:T(8,128)(2,1)} custom-call(bf16[16,4096]{1,0:T(8,128)(2,1)} %tokens_ref, s32[8,16]{1,0:T(8,128)} %bitcast.11, f32[8,16]{1,0:T(8,128)} %bitcast.12), custom_call_target="tpu_custom_call" | custom-call | tf_op jit(solution)/shard_map/pack/pallas_call | solution.py:237
  1.7 4.0 %collective-permute-start.3 = (bf16[16,4224]{1,0:T(8,128)(2,1)}, bf16[16,4224]{1,0:T(8,128)(2,1)S(1)}, u32[]{:S(2)}, u32[]{:S(2)}) collective-permute-start(bf16[16,4224]{1,0:T(8,128)(2,1)} %pack.1.refs_0_), channel_id=1, source_target_pairs={{0,16},{8,24},{16,0},{24,8},{1,17},{9,25},{17,1},{25,9},{2,18},{10... | collective-permute-start | bytes 405512 | tf_op jit(solution)/shard_map/ppermute | solution.py:253
  5.8 1.5 %collective-permute-start = (bf16[16,4224]{1,0:T(8,128)(2,1)}, bf16[16,4224]{1,0:T(8,128)(2,1)S(1)}, u32[]{:S(2)}, u32[]{:S(2)}) collective-permute-start(bf16[16,4224]{1,0:T(8,128)(2,1)} %pack.1.refs_0_), channel_id=1, source_target_pairs={{0,2},{1,3},{2,0},{3,1},{4,6},{5,7},{6,4},{7,5},{8,10},{9,11},{10,... | collective-permute-start | bytes 405512 | tf_op jit(solution)/shard_map/ppermute | solution.py:248
  7.3 1.5 %collective-permute-start.1 = (bf16[16,4224]{1,0:T(8,128)(2,1)}, bf16[16,4224]{1,0:T(8,128)(2,1)S(1)}, u32[]{:S(2)}, u32[]{:S(2)}) collective-permute-start(bf16[16,4224]{1,0:T(8,128)(2,1)} %pack.1.refs_0_), channel_id=1, source_target_pairs={{0,4},{1,5},{2,6},{3,7},{4,0},{5,1},{6,2},{7,3},{8,12},{9,13},{10,... | collective-permute-start | bytes 405512 | tf_op jit(solution)/shard_map/ppermute | solution.py:248
  9.3 3.2 %collective-permute-done.3.refs_0_ = bf16[16,4224]{1,0:T(8,128)(2,1)S(1)} collective-permute-done((bf16[16,4224]{1,0:T(8,128)(2,1)}, bf16[16,4224]{1,0:T(8,128)(2,1)S(1)}, u32[]{:S(2)}, u32[]{:S(2)}) %collective-permute-start.3) | collective-permute-done | bytes 135200 | tf_op jit(solution)/shard_map/ppermute | solution.py:253
  12.5 3.5 %collective-permute-start.7 = (bf16[16,4224]{1,0:T(8,128)(2,1)}, bf16[16,4224]{1,0:T(8,128)(2,1)S(1)}, u32[]{:S(2)}, u32[]{:S(2)}) collective-permute-start(bf16[16,4224]{1,0:T(8,128)(2,1)} %pack.1.refs_0_), channel_id=1, source_target_pairs={{0,24},{8,0},{16,8},{24,16},{1,25},{9,1},{17,9},{25,17},{2,26},{10... | collective-permute-start | bytes 405512 | tf_op jit(solution)/shard_map/ppermute | solution.py:253
  16.0 1.5 %collective-permute-start.4 = (bf16[16,4224]{1,0:T(8,128)(2,1)S(1)}, bf16[16,4224]{1,0:T(8,128)(2,1)S(1)}, u32[]{:S(2)}, u32[]{:S(2)}) collective-permute-start(bf16[16,4224]{1,0:T(8,128)(2,1)S(1)} %collective-permute-done.3.refs_0_), channel_id=1, source_target_pairs={{0,2},{1,3},{2,0},{3,1},{4,6},{5,7},{6,4},{7,5},{8,10},{9,11},{10,... | collective-permute-start | bytes 405512 | tf_op jit(solution)/shard_map/ppermute | solution.py:248
  17.5 1.5 %collective-permute-start.5 = (bf16[16,4224]{1,0:T(8,128)(2,1)S(1)}, bf16[16,4224]{1,0:T(8,128)(2,1)S(1)}, u32[]{:S(2)}, u32[]{:S(2)}) collective-permute-start(bf16[16,4224]{1,0:T(8,128)(2,1)S(1)} %collective-permute-done.3.refs_0_), channel_id=1, source_target_pairs={{0,4},{1,5},{2,6},{3,7},{4,0},{5,1},{6,2},{7,3},{8,12},{9,13},{10,... | collective-permute-start | bytes 405512 | tf_op jit(solution)/shard_map/ppermute | solution.py:248
  19.5 2.8 %copy-done = bf16[2,384,4096]{2,1,0:T(8,128)(2,1)S(1)} copy-done((bf16[2,384,4096]{2,1,0:T(8,128)(2,1)S(1)}, bf16[2,384,4096]{2,1,0:T(8,128)(2,1)}, u32[]{:S(2)}) %copy-start) | copy-done | bytes 6291480
  22.3 2.1 %fetch_turned.2.refs_5_.refs_9_ = bf16[4096,768]{1,0:T(8,128)(2,1)S(1)} custom-call(bf16[768,4096]{1,0:T(8,128)(2,1)S(1)} %bitcast.6), custom_call_target="tpu_custom_call" | custom-call | bytes 12582912 | tf_op jit(solution)/shard_map/fetch_turned/pallas_call | solution.py:103
  24.4 0.7 copy-done.1
  25.1 2.1 %fetch_turned.3.refs_6_.refs_10_ = bf16[4096,768]{1,0:T(8,128)(2,1)S(1)} custom-call(bf16[768,4096]{1,0:T(8,128)(2,1)S(1)} %bitcast.7), custom_call_target="tpu_custom_call" | custom-call | bytes 12582912 | tf_op jit(solution)/shard_map/fetch_turned/pallas_call | solution.py:103
  28.4 1.6 %collective-permute-start.11 = (bf16[32,4224]{1,0:T(8,128)(2,1)S(1)}, bf16[32,4224]{1,0:T(8,128)(2,1)S(1)}, u32[]{:S(2)}, u32[]{:S(2)}) collective-permute-start(bf16[32,4224]{1,0:T(8,128)(2,1)S(1)} %gather.5.refs_1_), channel_id=1, source_target_pairs={{0,2},{1,3},{2,0},{3,1},{4,6},{5,7},{6,4},{7,5},{8,10},{9,11},{10,... | collective-permute-start | bytes 811016 | tf_op jit(solution)/shard_map/ppermute | solution.py:248
  30.0 1.5 %collective-permute-start.12 = (bf16[32,4224]{1,0:T(8,128)(2,1)S(1)}, bf16[32,4224]{1,0:T(8,128)(2,1)S(1)}, u32[]{:S(2)}, u32[]{:S(2)}) collective-permute-start(bf16[32,4224]{1,0:T(8,128)(2,1)S(1)} %gather.5.refs_1_), channel_id=1, source_target_pairs={{0,4},{1,5},{2,6},{3,7},{4,0},{5,1},{6,2},{7,3},{8,12},{9,13},{10,... | collective-permute-start | bytes 811016 | tf_op jit(solution)/shard_map/ppermute | solution.py:248
  32.0 5.1 %experts.2 = (bf16[32,4096]{1,0:T(8,128)(2,1)S(1)}, bf16[32,4096]{1,0:T(8,128)(2,1)S(1)}, bf16[32,4096]{1,0:T(8,128)(2,1)S(1)}, bf16[32,4096]{1,0:T(8,128)(2,1)S...) custom-call(s32[1]{0:T(128)} %bitcast.refs_0_, ...), custom_call_target="tpu_custom_call" | custom-call | flops 4831838208 | bytes 4194304 | tf_op jit(solution)/shard_map/experts/pallas_call | solution.py:197
  37.1 0.6 collective-permute-start.17
  37.8 6.1 %collective-permute-done.12.refs_3_ = bf16[32,4224]{1,0:T(8,128)(2,1)S(1)} collective-permute-done((bf16[32,4224]{1,0:T(8,128)(2,1)S(1)}, bf16[32,4224]{1,0:T(8,128)(2,1)S(1)}, u32[]{:S(2)}, u32[]{:S(2)}) %collective-permute-start.12) | collective-permute-done | bytes 270368 | tf_op jit(solution)/shard_map/ppermute | solution.py:248
  45.1 1.5 %collective-permute-done.16 = bf16[32,4096]{1,0:T(8,128)(2,1)S(1)} collective-permute-done((bf16[32,4096]{1,0:T(8,128)(2,1)S(1)}, bf16[32,4096]{1,0:T(8,128)(2,1)S(1)}, u32[]{:S(2)}, u32[]{:S(2)}) %collective-permute-start.16) | collective-permute-done | bytes 262176 | tf_op jit(solution)/shard_map/ppermute | solution.py:248
  47.1 1.3 %collective-permute-start.22 = (bf16[32,4096]{1,0:T(8,128)(2,1)S(1)}, bf16[32,4096]{1,0:T(8,128)(2,1)S(1)}, u32[]{:S(2)}, u32[]{:S(2)}) collective-permute-start(bf16[32,4096]{1,0:T(8,128)(2,1)S(1)} %add_convert_fusion.5), channel_id=1, source_target_pairs={{0,2},{1,3},{2,0},{3,1},{4,6},{5,7},{6,4},{7,5},{8,10},{9,11},{10,... | collective-permute-start | bytes 786440 | tf_op jit(solution)/shard_map/ppermute | solution.py:248
  48.4 0.8 collective-permute-start.23
  49.2 1.4 %collective-permute-start.24 = (bf16[32,4096]{1,0:T(8,128)(2,1)S(1)}, bf16[32,4096]{1,0:T(8,128)(2,1)S(1)}, u32[]{:S(2)}, u32[]{:S(2)}) collective-permute-start(bf16[32,4096]{1,0:T(8,128)(2,1)S(1)} %add_convert_fusion.3), channel_id=1, source_target_pairs={{0,6},{1,7},{2,4},{3,5},{4,2},{5,3},{6,0},{7,1},{8,14},{9,15},{10,... | collective-permute-start | bytes 786440 | tf_op jit(solution)/shard_map/ppermute | solution.py:248
  50.6 5.1 %experts.3 = (bf16[32,4096]{1,0:T(8,128)(2,1)S(1)}, bf16[32,4096]{1,0:T(8,128)(2,1)S(1)}, bf16[32,4096]{1,0:T(8,128)(2,1)S(1)}, bf16[32,4096]{1,0:T(8,128)(2,1)S...) custom-call(s32[1]{0:T(128)} %bitcast.refs_0_, ...), custom_call_target="tpu_custom_call" | custom-call | flops 4831838208 | bytes 4194304 | tf_op jit(solution)/shard_map/experts/pallas_call | solution.py:197
  56.4 4.0 %collective-permute-done.23 = bf16[32,4096]{1,0:T(8,128)(2,1)S(1)} collective-permute-done((bf16[32,4096]{1,0:T(8,128)(2,1)S(1)}, bf16[32,4096]{1,0:T(8,128)(2,1)S(1)}, u32[]{:S(2)}, u32[]{:S(2)}) %collective-permute-start.23) | collective-permute-done | bytes 262176 | tf_op jit(solution)/shard_map/ppermute | solution.py:248
  60.4 1.6 %collective-permute-done.24 = bf16[32,4096]{1,0:T(8,128)(2,1)S(1)} collective-permute-done((bf16[32,4096]{1,0:T(8,128)(2,1)S(1)}, bf16[32,4096]{1,0:T(8,128)(2,1)S(1)}, u32[]{:S(2)}, u32[]{:S(2)}) %collective-permute-start.24) | collective-permute-done | bytes 262176 | tf_op jit(solution)/shard_map/ppermute | solution.py:248
  62.4 2.3 %collective-permute-start.30 = (bf16[32,4096]{1,0:T(8,128)(2,1)S(1)}, bf16[32,4096]{1,0:T(8,128)(2,1)S(1)}, u32[]{:S(2)}, u32[]{:S(2)}) collective-permute-start(bf16[32,4096]{1,0:T(8,128)(2,1)S(1)} %add_convert_fusion.2), channel_id=1, source_target_pairs={{0,2},{1,3},{2,0},{3,1},{4,6},{5,7},{6,4},{7,5},{8,10},{9,11},{10,... | collective-permute-start | bytes 786440 | tf_op jit(solution)/shard_map/ppermute | solution.py:248
  64.7 1.5 %collective-permute-start.31 = (bf16[32,4096]{1,0:T(8,128)(2,1)S(1)}, bf16[32,4096]{1,0:T(8,128)(2,1)S(1)}, u32[]{:S(2)}, u32[]{:S(2)}) collective-permute-start(bf16[32,4096]{1,0:T(8,128)(2,1)S(1)} %add_convert_fusion.1), channel_id=1, source_target_pairs={{0,4},{1,5},{2,6},{3,7},{4,0},{5,1},{6,2},{7,3},{8,12},{9,13},{10,... | collective-permute-start | bytes 786440 | tf_op jit(solution)/shard_map/ppermute | solution.py:248
  66.3 0.6 collective-permute-start.25
  66.9 4.9 %collective-permute-done.30 = bf16[32,4096]{1,0:T(8,128)(2,1)S(1)} collective-permute-done((bf16[32,4096]{1,0:T(8,128)(2,1)S(1)}, bf16[32,4096]{1,0:T(8,128)(2,1)S(1)}, u32[]{:S(2)}, u32[]{:S(2)}) %collective-permute-start.30) | collective-permute-done | bytes 262176 | tf_op jit(solution)/shard_map/ppermute | solution.py:248
  71.8 6.8 %collective-permute-done.31 = bf16[32,4096]{1,0:T(8,128)(2,1)S(1)} collective-permute-done((bf16[32,4096]{1,0:T(8,128)(2,1)S(1)}, bf16[32,4096]{1,0:T(8,128)(2,1)S(1)}, u32[]{:S(2)}, u32[]{:S(2)}) %collective-permute-start.31) | collective-permute-done | bytes 262176 | tf_op jit(solution)/shard_map/ppermute | solution.py:248
  78.8 3.9 %collective-permute-start.34 = (bf16[16,4096]{1,0:T(8,128)(2,1)S(1)}, bf16[16,4096]{1,0:T(8,128)(2,1)S(1)}, u32[]{:S(2)}, u32[]{:S(2)}) collective-permute-start(bf16[16,4096]{1,0:T(8,128)(2,1)S(1)} %get-tuple-element.108), channel_id=1, source_target_pairs={{0,24},{8,0},{16,8},{24,16},{1,25},{9,1},{17,9},{25,17},{2,26},{10... | collective-permute-start | bytes 393224 | tf_op jit(solution)/shard_map/ppermute | solution.py:253
  82.7 4.3 %collective-permute-done.33 = bf16[16,4096]{1,0:T(8,128)(2,1)S(1)} collective-permute-done((bf16[16,4096]{1,0:T(8,128)(2,1)S(1)}, bf16[16,4096]{1,0:T(8,128)(2,1)S(1)}, u32[]{:S(2)}, u32[]{:S(2)}) %collective-permute-start.33) | collective-permute-done | bytes 131104 | tf_op jit(solution)/shard_map/ppermute | solution.py:253
  87.0 0.8 add_convert_fusion.6
  (67 shorter events, 5.6 us)
Async XLA Ops:
  1.7 10.7 %collective-permute-start.3 = (bf16[16,4224]{1,0:T(8,128)(2,1)}, bf16[16,4224]{1,0:T(8,128)(2,1)S(1)}, u32[]{:S(2)}, u32[]{:S(2)}) collective-permute-start(bf16[16,4224]{1,0:T(8,128)(2,1)} %pack.1.refs_0_), channel_id=1, source_target_pairs={{0,16},{8,24},{16,0},{24,8},{1,17},{9,25},{17,1},{25,9},{2,18},{10... | collective-permute-start | bytes 405512 | tf_op jit(solution)/shard_map/ppermute | solution.py:253
  5.8 10.2 %collective-permute-start = (bf16[16,4224]{1,0:T(8,128)(2,1)}, bf16[16,4224]{1,0:T(8,128)(2,1)S(1)}, u32[]{:S(2)}, u32[]{:S(2)}) collective-permute-start(bf16[16,4224]{1,0:T(8,128)(2,1)} %pack.1.refs_0_), channel_id=1, source_target_pairs={{0,2},{1,3},{2,0},{3,1},{4,6},{5,7},{6,4},{7,5},{8,10},{9,11},{10,... | collective-permute-start | bytes 405512 | tf_op jit(solution)/shard_map/ppermute | solution.py:248
  7.3 10.2 %collective-permute-start.1 = (bf16[16,4224]{1,0:T(8,128)(2,1)}, bf16[16,4224]{1,0:T(8,128)(2,1)S(1)}, u32[]{:S(2)}, u32[]{:S(2)}) collective-permute-start(bf16[16,4224]{1,0:T(8,128)(2,1)} %pack.1.refs_0_), channel_id=1, source_target_pairs={{0,4},{1,5},{2,6},{3,7},{4,0},{5,1},{6,2},{7,3},{8,12},{9,13},{10,... | collective-permute-start | bytes 405512 | tf_op jit(solution)/shard_map/ppermute | solution.py:248
  8.8 10.2 %collective-permute-start.2 = (bf16[16,4224]{1,0:T(8,128)(2,1)}, bf16[16,4224]{1,0:T(8,128)(2,1)S(1)}, u32[]{:S(2)}, u32[]{:S(2)}) collective-permute-start(bf16[16,4224]{1,0:T(8,128)(2,1)} %pack.1.refs_0_), channel_id=1, source_target_pairs={{0,6},{1,7},{2,4},{3,5},{4,2},{5,3},{6,0},{7,1},{8,14},{9,15},{10,... | collective-permute-start | bytes 405512 | tf_op jit(solution)/shard_map/ppermute | solution.py:248
  12.5 14.7 %collective-permute-start.7 = (bf16[16,4224]{1,0:T(8,128)(2,1)}, bf16[16,4224]{1,0:T(8,128)(2,1)S(1)}, u32[]{:S(2)}, u32[]{:S(2)}) collective-permute-start(bf16[16,4224]{1,0:T(8,128)(2,1)} %pack.1.refs_0_), channel_id=1, source_target_pairs={{0,24},{8,0},{16,8},{24,16},{1,25},{9,1},{17,9},{25,17},{2,26},{10... | collective-permute-start | bytes 405512 | tf_op jit(solution)/shard_map/ppermute | solution.py:253
  16.0 11.3 %collective-permute-start.8 = (bf16[16,4224]{1,0:T(8,128)(2,1)}, bf16[16,4224]{1,0:T(8,128)(2,1)S(1)}, u32[]{:S(2)}, u32[]{:S(2)}) collective-permute-start(bf16[16,4224]{1,0:T(8,128)(2,1)} %pack.1.refs_0_), channel_id=1, source_target_pairs={{0,8},{8,16},{16,24},{24,0},{1,9},{9,17},{17,25},{25,1},{2,10},{10... | collective-permute-start | bytes 405512 | tf_op jit(solution)/shard_map/ppermute | solution.py:253
  16.0 11.8 %collective-permute-start.4 = (bf16[16,4224]{1,0:T(8,128)(2,1)S(1)}, bf16[16,4224]{1,0:T(8,128)(2,1)S(1)}, u32[]{:S(2)}, u32[]{:S(2)}) collective-permute-start(bf16[16,4224]{1,0:T(8,128)(2,1)S(1)} %collective-permute-done.3.refs_0_), channel_id=1, source_target_pairs={{0,2},{1,3},{2,0},{3,1},{4,6},{5,7},{6,4},{7,5},{8,10},{9,11},{10,... | collective-permute-start | bytes 405512 | tf_op jit(solution)/shard_map/ppermute | solution.py:248
  17.5 10.3 %collective-permute-start.5 = (bf16[16,4224]{1,0:T(8,128)(2,1)S(1)}, bf16[16,4224]{1,0:T(8,128)(2,1)S(1)}, u32[]{:S(2)}, u32[]{:S(2)}) collective-permute-start(bf16[16,4224]{1,0:T(8,128)(2,1)S(1)} %collective-permute-done.3.refs_0_), channel_id=1, source_target_pairs={{0,4},{1,5},{2,6},{3,7},{4,0},{5,1},{6,2},{7,3},{8,12},{9,13},{10,... | collective-permute-start | bytes 405512 | tf_op jit(solution)/shard_map/ppermute | solution.py:248
  19.0 8.8 %collective-permute-start.6 = (bf16[16,4224]{1,0:T(8,128)(2,1)S(1)}, bf16[16,4224]{1,0:T(8,128)(2,1)S(1)}, u32[]{:S(2)}, u32[]{:S(2)}) collective-permute-start(bf16[16,4224]{1,0:T(8,128)(2,1)S(1)} %collective-permute-done.3.refs_0_), channel_id=1, source_target_pairs={{0,6},{1,7},{2,4},{3,5},{4,2},{5,3},{6,0},{7,1},{8,14},{9,15},{10,... | collective-permute-start | bytes 405512 | tf_op jit(solution)/shard_map/ppermute | solution.py:248
  27.2 4.8 %collective-permute-start.9 = (bf16[64,4224]{1,0:T(8,128)(2,1)S(1)}, bf16[64,4224]{1,0:T(8,128)(2,1)S(1)}, u32[]{:S(2)}, u32[]{:S(2)}) collective-permute-start(bf16[64,4224]{1,0:T(8,128)(2,1)S(1)} %gather.3.refs_1_), channel_id=1, source_target_pairs={{0,1},{1,0},{2,3},{3,2},{4,5},{5,4},{6,7},{7,6},{8,9},{9,8},{10,11... | collective-permute-start | bytes 1622024 | tf_op jit(solution)/shard_map/ppermute | solution.py:248
  27.9 4.1 %collective-permute-start.10 = (bf16[64,4224]{1,0:T(8,128)(2,1)S(1)}, bf16[64,4224]{1,0:T(8,128)(2,1)S(1)}, u32[]{:S(2)}, u32[]{:S(2)}) collective-permute-start(bf16[64,4224]{1,0:T(8,128)(2,1)S(1)} %gather.4.refs_2_), channel_id=1, source_target_pairs={{0,1},{1,0},{2,3},{3,2},{4,5},{5,4},{6,7},{7,6},{8,9},{9,8},{10,11... | collective-permute-start | bytes 1622024 | tf_op jit(solution)/shard_map/ppermute | solution.py:248
  28.4 9.4 %collective-permute-start.11 = (bf16[32,4224]{1,0:T(8,128)(2,1)S(1)}, bf16[32,4224]{1,0:T(8,128)(2,1)S(1)}, u32[]{:S(2)}, u32[]{:S(2)}) collective-permute-start(bf16[32,4224]{1,0:T(8,128)(2,1)S(1)} %gather.5.refs_1_), channel_id=1, source_target_pairs={{0,2},{1,3},{2,0},{3,1},{4,6},{5,7},{6,4},{7,5},{8,10},{9,11},{10,... | collective-permute-start | bytes 811016 | tf_op jit(solution)/shard_map/ppermute | solution.py:248
  30.0 13.9 %collective-permute-start.12 = (bf16[32,4224]{1,0:T(8,128)(2,1)S(1)}, bf16[32,4224]{1,0:T(8,128)(2,1)S(1)}, u32[]{:S(2)}, u32[]{:S(2)}) collective-permute-start(bf16[32,4224]{1,0:T(8,128)(2,1)S(1)} %gather.5.refs_1_), channel_id=1, source_target_pairs={{0,4},{1,5},{2,6},{3,7},{4,0},{5,1},{6,2},{7,3},{8,12},{9,13},{10,... | collective-permute-start | bytes 811016 | tf_op jit(solution)/shard_map/ppermute | solution.py:248
  31.5 12.4 %collective-permute-start.13 = (bf16[32,4224]{1,0:T(8,128)(2,1)S(1)}, bf16[32,4224]{1,0:T(8,128)(2,1)S(1)}, u32[]{:S(2)}, u32[]{:S(2)}) collective-permute-start(bf16[32,4224]{1,0:T(8,128)(2,1)S(1)} %gather.5.refs_1_), channel_id=1, source_target_pairs={{0,6},{1,7},{2,4},{3,5},{4,2},{5,3},{6,0},{7,1},{8,14},{9,15},{10,... | collective-permute-start | bytes 811016 | tf_op jit(solution)/shard_map/ppermute | solution.py:248
  32.0 11.9 %collective-permute-start.14 = (bf16[32,4224]{1,0:T(8,128)(2,1)S(1)}, bf16[32,4224]{1,0:T(8,128)(2,1)S(1)}, u32[]{:S(2)}, u32[]{:S(2)}) collective-permute-start(bf16[32,4224]{1,0:T(8,128)(2,1)S(1)} %gather.5.refs_1_), channel_id=1, source_target_pairs={{0,1},{1,0},{2,3},{3,2},{4,5},{5,4},{6,7},{7,6},{8,9},{9,8},{10,11... | collective-permute-start | bytes 811016 | tf_op jit(solution)/shard_map/ppermute | solution.py:248
  37.1 7.8 %collective-permute-start.17 = (bf16[32,4096]{1,0:T(8,128)(2,1)S(1)}, bf16[32,4096]{1,0:T(8,128)(2,1)S(1)}, u32[]{:S(2)}, u32[]{:S(2)}) collective-permute-start(bf16[32,4096]{1,0:T(8,128)(2,1)S(1)} %get-tuple-element.77), channel_id=1, source_target_pairs={{0,1},{1,0},{2,3},{3,2},{4,5},{5,4},{6,7},{7,6},{8,9},{9,8},{10,11... | collective-permute-start | bytes 786440 | tf_op jit(solution)/shard_map/ppermute | solution.py:248
  43.9 5.3 %collective-permute-start.19 = (bf16[32,4224]{1,0:T(8,128)(2,1)S(1)}, bf16[32,4224]{1,0:T(8,128)(2,1)S(1)}, u32[]{:S(2)}, u32[]{:S(2)}) collective-permute-start(bf16[32,4224]{1,0:T(8,128)(2,1)S(1)} %collective-permute-done.11.refs_2_), channel_id=1, source_target_pairs={{0,1},{1,0},{2,3},{3,2},{4,5},{5,4},{6,7},{7,6},{8,9},{9,8},{10,11... | collective-permute-start | bytes 811016 | tf_op jit(solution)/shard_map/ppermute | solution.py:248
  43.9 6.7 %collective-permute-start.20 = (bf16[32,4224]{1,0:T(8,128)(2,1)S(1)}, bf16[32,4224]{1,0:T(8,128)(2,1)S(1)}, u32[]{:S(2)}, u32[]{:S(2)}) collective-permute-start(bf16[32,4224]{1,0:T(8,128)(2,1)S(1)} %collective-permute-done.12.refs_3_), channel_id=1, source_target_pairs={{0,1},{1,0},{2,3},{3,2},{4,5},{5,4},{6,7},{7,6},{8,9},{9,8},{10,11... | collective-permute-start | bytes 811016 | tf_op jit(solution)/shard_map/ppermute | solution.py:248
  44.4 6.2 %collective-permute-start.21 = (bf16[32,4224]{1,0:T(8,128)(2,1)S(1)}, bf16[32,4224]{1,0:T(8,128)(2,1)S(1)}, u32[]{:S(2)}, u32[]{:S(2)}) collective-permute-start(bf16[32,4224]{1,0:T(8,128)(2,1)S(1)} %collective-permute-done.13.refs_4_), channel_id=1, source_target_pairs={{0,1},{1,0},{2,3},{3,2},{4,5},{5,4},{6,7},{7,6},{8,9},{9,8},{10,11... | collective-permute-start | bytes 811016 | tf_op jit(solution)/shard_map/ppermute | solution.py:248
  47.1 9.3 %collective-permute-start.22 = (bf16[32,4096]{1,0:T(8,128)(2,1)S(1)}, bf16[32,4096]{1,0:T(8,128)(2,1)S(1)}, u32[]{:S(2)}, u32[]{:S(2)}) collective-permute-start(bf16[32,4096]{1,0:T(8,128)(2,1)S(1)} %add_convert_fusion.5), channel_id=1, source_target_pairs={{0,2},{1,3},{2,0},{3,1},{4,6},{5,7},{6,4},{7,5},{8,10},{9,11},{10,... | collective-permute-start | bytes 786440 | tf_op jit(solution)/shard_map/ppermute | solution.py:248
  48.4 12.1 %collective-permute-start.23 = (bf16[32,4096]{1,0:T(8,128)(2,1)S(1)}, bf16[32,4096]{1,0:T(8,128)(2,1)S(1)}, u32[]{:S(2)}, u32[]{:S(2)}) collective-permute-start(bf16[32,4096]{1,0:T(8,128)(2,1)S(1)} %add_convert_fusion.4), channel_id=1, source_target_pairs={{0,4},{1,5},{2,6},{3,7},{4,0},{5,1},{6,2},{7,3},{8,12},{9,13},{10,... | collective-permute-start | bytes 786440 | tf_op jit(solution)/shard_map/ppermute | solution.py:248
  49.2 12.9 %collective-permute-start.24 = (bf16[32,4096]{1,0:T(8,128)(2,1)S(1)}, bf16[32,4096]{1,0:T(8,128)(2,1)S(1)}, u32[]{:S(2)}, u32[]{:S(2)}) collective-permute-start(bf16[32,4096]{1,0:T(8,128)(2,1)S(1)} %add_convert_fusion.3), channel_id=1, source_target_pairs={{0,6},{1,7},{2,4},{3,5},{4,2},{5,3},{6,0},{7,1},{8,14},{9,15},{10,... | collective-permute-start | bytes 786440 | tf_op jit(solution)/shard_map/ppermute | solution.py:248
  55.8 6.3 %collective-permute-start.28 = (bf16[32,4096]{1,0:T(8,128)(2,1)S(1)}, bf16[32,4096]{1,0:T(8,128)(2,1)S(1)}, u32[]{:S(2)}, u32[]{:S(2)}) collective-permute-start(bf16[32,4096]{1,0:T(8,128)(2,1)S(1)} %get-tuple-element.101), channel_id=1, source_target_pairs={{0,1},{1,0},{2,3},{3,2},{4,5},{5,4},{6,7},{7,6},{8,9},{9,8},{10,11... | collective-permute-start | bytes 786440 | tf_op jit(solution)/shard_map/ppermute | solution.py:248
  55.8 10.3 %collective-permute-start.18 = (bf16[32,4096]{1,0:T(8,128)(2,1)S(1)}, bf16[32,4096]{1,0:T(8,128)(2,1)S(1)}, u32[]{:S(2)}, u32[]{:S(2)}) collective-permute-start(bf16[32,4096]{1,0:T(8,128)(2,1)S(1)} %get-tuple-element.79), channel_id=1, source_target_pairs={{0,1},{1,0},{2,3},{3,2},{4,5},{5,4},{6,7},{7,6},{8,9},{9,8},{10,11... | collective-permute-start | bytes 786440 | tf_op jit(solution)/shard_map/ppermute | solution.py:248
  56.3 5.8 %collective-permute-start.27 = (bf16[32,4096]{1,0:T(8,128)(2,1)S(1)}, bf16[32,4096]{1,0:T(8,128)(2,1)S(1)}, u32[]{:S(2)}, u32[]{:S(2)}) collective-permute-start(bf16[32,4096]{1,0:T(8,128)(2,1)S(1)} %get-tuple-element.99), channel_id=1, source_target_pairs={{0,1},{1,0},{2,3},{3,2},{4,5},{5,4},{6,7},{7,6},{8,9},{9,8},{10,11... | collective-permute-start | bytes 786440 | tf_op jit(solution)/shard_map/ppermute | solution.py:248
  62.3 4.6 %collective-permute-start.29 = (bf16[32,4096]{1,0:T(8,128)(2,1)S(1)}, bf16[32,4096]{1,0:T(8,128)(2,1)S(1)}, u32[]{:S(2)}, u32[]{:S(2)}) collective-permute-start(bf16[32,4096]{1,0:T(8,128)(2,1)S(1)} %get-tuple-element.103), channel_id=1, source_target_pairs={{0,1},{1,0},{2,3},{3,2},{4,5},{5,4},{6,7},{7,6},{8,9},{9,8},{10,11... | collective-permute-start | bytes 786440 | tf_op jit(solution)/shard_map/ppermute | solution.py:248
  62.4 9.4 %collective-permute-start.30 = (bf16[32,4096]{1,0:T(8,128)(2,1)S(1)}, bf16[32,4096]{1,0:T(8,128)(2,1)S(1)}, u32[]{:S(2)}, u32[]{:S(2)}) collective-permute-start(bf16[32,4096]{1,0:T(8,128)(2,1)S(1)} %add_convert_fusion.2), channel_id=1, source_target_pairs={{0,2},{1,3},{2,0},{3,1},{4,6},{5,7},{6,4},{7,5},{8,10},{9,11},{10,... | collective-permute-start | bytes 786440 | tf_op jit(solution)/shard_map/ppermute | solution.py:248
  64.7 13.9 %collective-permute-start.31 = (bf16[32,4096]{1,0:T(8,128)(2,1)S(1)}, bf16[32,4096]{1,0:T(8,128)(2,1)S(1)}, u32[]{:S(2)}, u32[]{:S(2)}) collective-permute-start(bf16[32,4096]{1,0:T(8,128)(2,1)S(1)} %add_convert_fusion.1), channel_id=1, source_target_pairs={{0,4},{1,5},{2,6},{3,7},{4,0},{5,1},{6,2},{7,3},{8,12},{9,13},{10,... | collective-permute-start | bytes 786440 | tf_op jit(solution)/shard_map/ppermute | solution.py:248
  66.2 12.4 %collective-permute-start.32 = (bf16[32,4096]{1,0:T(8,128)(2,1)S(1)}, bf16[32,4096]{1,0:T(8,128)(2,1)S(1)}, u32[]{:S(2)}, u32[]{:S(2)}) collective-permute-start(bf16[32,4096]{1,0:T(8,128)(2,1)S(1)} %add_convert_fusion), channel_id=1, source_target_pairs={{0,6},{1,7},{2,4},{3,5},{4,2},{5,3},{6,0},{7,1},{8,14},{9,15},{10,... | collective-permute-start | bytes 786440 | tf_op jit(solution)/shard_map/ppermute | solution.py:248
  66.3 16.4 %collective-permute-start.25 = (bf16[16,4096]{1,0:T(8,128)(2,1)S(1)}, bf16[16,4096]{1,0:T(8,128)(2,1)S(1)}, u32[]{:S(2)}, u32[]{:S(2)}) collective-permute-start(bf16[16,4096]{1,0:T(8,128)(2,1)S(1)} %add_convert_fusion.9), channel_id=1, source_target_pairs={{0,16},{8,24},{16,0},{24,8},{1,17},{9,25},{17,1},{25,9},{2,18},{10... | collective-permute-start | bytes 393224 | tf_op jit(solution)/shard_map/ppermute | solution.py:253
  78.7 8.2 %collective-permute-start.33 = (bf16[16,4096]{1,0:T(8,128)(2,1)S(1)}, bf16[16,4096]{1,0:T(8,128)(2,1)S(1)}, u32[]{:S(2)}, u32[]{:S(2)}) collective-permute-start(bf16[16,4096]{1,0:T(8,128)(2,1)S(1)} %get-tuple-element.107), channel_id=1, source_target_pairs={{0,8},{8,16},{16,24},{24,0},{1,9},{9,17},{17,25},{25,1},{2,10},{10... | collective-permute-start | bytes 393224 | tf_op jit(solution)/shard_map/ppermute | solution.py:253
  78.8 8.2 %collective-permute-start.34 = (bf16[16,4096]{1,0:T(8,128)(2,1)S(1)}, bf16[16,4096]{1,0:T(8,128)(2,1)S(1)}, u32[]{:S(2)}, u32[]{:S(2)}) collective-permute-start(bf16[16,4096]{1,0:T(8,128)(2,1)S(1)} %get-tuple-element.108), channel_id=1, source_target_pairs={{0,24},{8,0},{16,8},{24,16},{1,25},{9,1},{17,9},{25,17},{2,26},{10... | collective-permute-start | bytes 393224 | tf_op jit(solution)/shard_map/ppermute | solution.py:253
  (8 other events, 20.8 us)

commit v4 on v3

--- a/solution.py
+++ b/solution.py
@@ -268,28 +268,8 @@
     return lax.optimization_barrier(values)
 
 
-def segments_of(places, rows):
-    other = 8
-    cuts = [*places, *([other + place for place in cut] for cut in places)]
-    return [[(place * rows, rows) for place in cut] for cut in cuts]
-
-
-def cores_added(parts):
-    back = [swap_exp(part, 1) for part in parts[4:7]]
-    sent = [rounded(part, other) for part, other in zip(parts[:3], back)]
-    *sent, other = ordered(*sent, parts[7])
-    return sent, (parts[3], swap_exp(other, 1))
-
-
-def crossed(sent):
-    return [swap_exp(part, bits) for part, bits in zip(sent, (2, 4, 6))]
-
-
-def plane_added(kept, arrived, rows):
-    return (
-        added(*(part[:rows] for part in (*kept, *arrived))),
-        added(*(part[rows:] for part in (*kept, *arrived))),
-    )
+def row_groups(places, rows):
+    return [[(place * rows, rows) for place in group] for group in places]
 
 
 def on_device_dense(tokens, routed_experts, route_weights, gate_weight, up_weight, down_weight):
@@ -303,45 +283,63 @@
     own = jnp.full((1,), lax.axis_index("exp") * local_experts, jnp.int32)
     tokens, own = ordered(tokens, own)
     packed = with_routing(tokens, routed_experts, route_weights)
+
     two = turn_rep(packed, 2)
-    near_own = [swap_exp(packed, bits) for bits in (2, 4, 6)]
-    two, gate_weight, up_weight, again = ordered(two, gate_weight, up_weight, packed)
-    near_two = [swap_exp(two, bits) for bits in (2, 4, 6)]
-    far_one, far_two = turn_rep(again, 1), turn_rep(again, 3)
-    first = gathered(packed, *near_own)
+    x_own, y_own, far_own = [swap_exp(packed, bits) for bits in (2, 4, 6)]
+    one, three = turn_rep(packed, 1), turn_rep(packed, 3)
+    gates = fetched(gate_weight, True)
+    two, far_own, y_own, x_own, gates, up_weight = ordered(
+        two, far_own, y_own, x_own, gates, up_weight
+    )
+    x_two, y_two, far_two = [swap_exp(two, bits) for bits in (2, 4, 6)]
+    far_one, far_three = turn_rep(far_own, 1), turn_rep(far_own, 3)
+    first = gathered(packed, x_own, y_own, far_own)
     first_other = swap_exp(first, 1)
-    gates, ups = fetched(gate_weight, True), fetched(up_weight, True)
-    far_one, far_two, gates, ups, down_weight = ordered(
-        far_one, far_two, gates, ups, down_weight
-    )
-    far = gathered(far_one, far_two)
-    far_away = [swap_exp(far, bits) for bits in (2, 4, 6)]
-    second = gathered(two, *near_two)
+    ups = fetched(up_weight, True)
+    one, three, ups, down_weight = ordered(one, three, ups, down_weight)
+    pair = gathered(one, three)
+    x_pair, y_pair = swap_exp(pair, 2), swap_exp(pair, 4)
+    second = gathered(two, x_two, y_two, far_two)
     downs = fetched(down_weight, False)
-    second, downs = ordered(second, downs)
+    second, downs, far_one, far_three = ordered(second, downs, far_one, far_three)
+
     near = [first, second, first_other, swap_exp(second, 1)]
-
-    segments = segments_of(([1, 5], [2, 6], [3, 7], [0, 4]), rows)
-    parts = list(experts_of(own, near, segments, gates, ups, downs, shard_units, top))
-    parts[3], *far_away = ordered(parts[3], *far_away)
-    parts[3], far_other = ordered(parts[3], swap_exp(far, 1))
-    far = [far, *far_away, far_other, *(swap_exp(piece, 1) for piece in far_away)]
-    sent, near_kept = cores_added(parts)
-    near_arrived = crossed(sent)
-    *sent, far[0], far[1], far[2], far[3] = ordered(*sent, *far[:4])
-    segments = segments_of(([2, 3], [4, 5], [6, 7], [0, 1]), rows)
-    parts = list(experts_of(own, far, segments, gates, ups, downs, shard_units, top))
-    parts[3], *near_arrived = ordered(parts[3], *near_arrived)
-    sent, far_kept = cores_added(parts)
-    far_arrived = crossed(sent)
-    near_sums = plane_added(near_kept, near_arrived, rows)
-    far_sums = plane_added(far_kept, far_arrived, rows)
-    arrived = [
-        turn_rep(near_sums[1].astype(jnp.bfloat16), -2),
-        turn_rep(far_sums[0].astype(jnp.bfloat16), -1),
-        turn_rep(far_sums[1].astype(jnp.bfloat16), -3),
-    ]
-    return rounded(near_sums[0], *arrived)
+    groups = row_groups([[5, 1], [6, 2], [7], [13, 9, 14, 10, 15], [4, 0, 3], [12, 8, 11]], rows)
+    parts = experts_of(own, near, groups, gates, ups, downs, shard_units, top)
+    *parts, x_pair, y_pair = ordered(*parts, x_pair, y_pair)
+    to_x, to_y, to_far, other, near_kept, near_other = parts
+    back = swap_exp(other, 1)
+    to_x = rounded(to_x, back[: 2 * rows])
+    to_y = rounded(to_y, back[2 * rows : 4 * rows])
+    to_far = rounded(to_far, back[4 * rows :])
+    to_x, to_y, to_far, near_other = ordered(to_x, to_y, to_far, near_other)
+    near_x, near_y, near_far = swap_exp(to_x, 2), swap_exp(to_y, 4), swap_exp(to_far, 6)
+    near_back = swap_exp(near_other, 1)
+
+    far = [pair, x_pair, y_pair, far_one, far_three]
+    far = far + [swap_exp(piece, 1) for piece in far]
+    to_x, to_y, to_far, *far = ordered(to_x, to_y, to_far, *far)
+    groups = row_groups([[6], [7], [2, 3], [4, 5], [14, 15, 10, 11, 12, 13, 8, 9], [0, 1]], rows)
+    parts = experts_of(own, far, groups, gates, ups, downs, shard_units, top)
+    to_one, to_three, to_x, to_y, other, far_kept = parts
+    far_kept, near_x, near_y, near_far = ordered(far_kept, near_x, near_y, near_far)
+    back = swap_exp(other, 1)
+    to_one, to_three = rounded(to_one, back[:rows]), rounded(to_three, back[rows : 2 * rows])
+    to_x = rounded(to_x, back[2 * rows : 4 * rows])
+    to_y = rounded(to_y, back[4 * rows : 6 * rows])
+    kept = added(near_kept, near_back)
+    to_two = rounded(kept[:rows], near_x[:rows], near_y[:rows], near_far)
+    to_two, to_one, to_three = ordered(to_two, to_one, to_three)
+    from_two = turn_rep(to_two, -2)
+    from_one, from_three = turn_rep(to_one, -1), turn_rep(to_three, -3)
+    far_x, far_y = swap_exp(to_x, 2), swap_exp(to_y, 4)
+
+    own_sum = kept[rows : 2 * rows] + added(near_x[rows:], near_y[rows:])
+    to_far = (kept[2 * rows :] + added(from_one, from_three)).astype(jnp.bfloat16)
+    from_far = swap_exp(to_far, 6)
+    sums = added(far_kept, back[6 * rows :], far_x, far_y).astype(jnp.bfloat16)
+    arrived = [turn_rep(sums[:rows], -1), turn_rep(sums[rows:], -3)]
+    return rounded(own_sum, from_two, from_far, *arrived)
 
 
 def solution(mesh):

time: 87.9 us -> 83.3 us (0.948)
  waiting for transfers between devices: 32.9 us -> 24.9 us
  starting transfers between devices: 33 us -> 36.7 us
    ppermute x29 -> x24, waiting for transfers between devices: 25.4 us -> 6.91 us  [swap_exp(): return lax.ppermute(value, 'exp', [(i, i ^ bits) for i in range(owners)])]
    ppermute x6 -> x10, waiting for transfers between devices: 7.49 us -> 18 us  [turn_rep(): lax.ppermute(value, 'rep', [(i, (i - shift) % replicas) for i in range(re...]
    ppermute x6 -> x10, starting transfers between devices: 12.1 us -> 17.5 us  [turn_rep(): lax.ppermute(value, 'rep', [(i, (i - shift) % replicas) for i in range(re...]
    ppermute x29 -> x24, starting transfers between devices: 20.9 us -> 19.2 us  [swap_exp(): return lax.ppermute(value, 'exp', [(i, i ^ bits) for i in range(owners)])]
  transfers between devices with their start and end apart: 35 -> 34, of which waited for: 10 -> 13; matrix products, arithmetic and copies ran while one was open for 1% -> 1% of each run, Pallas kernels for 17% -> 18%
where the time goes in v4:
time: 83.3 us; the launch traced here: 83.1 us
  starting transfers between devices  36.7 us (44%)
  waiting for transfers between devices  24.9 us (30%)
  Pallas kernels  16.8 us (20%)
  local copies, waits for them, and re-layouts  2.96 us (4%)
  other arithmetic  1.45 us (2%)
    ppermute x24, starting transfers between devices, swap_exp(): return lax.ppermute(value, 'exp', [(i, i ^ bits) for i in range(owners)])  19.2 us
    ppermute x10, waiting for transfers between devices, turn_rep(): lax.ppermute(value, 'rep', [(i, (i - shift) % replicas) for i in range(re...  18 us
    ppermute x10, starting transfers between devices, turn_rep(): lax.ppermute(value, 'rep', [(i, (i - shift) % replicas) for i in range(re...  17.5 us
    pallas_call x2, Pallas kernels, experts_of(): pl.pallas_call(kernel, out_shape=[jax.ShapeDtypeStruct((count, model_widt...  10.1 us
    ppermute x24, waiting for transfers between devices, swap_exp(): return lax.ppermute(value, 'exp', [(i, i ^ bits) for i in range(owners)])  6.91 us
    pallas_call x3, Pallas kernels, fetched(): pl.pallas_call(functools.partial(fetch_kernel, turn), out_shape=jax.Shape...  4.88 us
    unnamed x10, local copies, waits for them, and re-layouts  2.94 us
    pallas_call x1, Pallas kernels, with_routing(): pl.pallas_call(pack_kernel, out_shape=jax.ShapeDtypeStruct((rows, width +...  1.74 us
  transfers between devices with their start and end apart: 34, of which 13 were waited for; matrix products, arithmetic and copies ran while one was open for 1% of the time, Pallas kernels for 18%

profile of v4, /device:TPU:0, one launch (start us, length us, event | category | flops | bytes accessed | tf_op | source)
XLA Modules:
  0.0 83.1 jit_solution(5203854901679807603)
XLA Ops:
  0.0 1.7 %pack.1.refs_0_ = bf16[16,4224]{1,0:T(8,128)(2,1)} custom-call(bf16[16,4096]{1,0:T(8,128)(2,1)} %tokens_ref, s32[8,16]{1,0:T(8,128)} %bitcast.11, f32[8,16]{1,0:T(8,128)} %bitcast.12), custom_call_target="tpu_custom_call" | custom-call | tf_op jit(solution)/shard_map/pack/pallas_call | solution.py:237
  1.7 4.0 %collective-permute-start = (bf16[16,4224]{1,0:T(8,128)(2,1)}, bf16[16,4224]{1,0:T(8,128)(2,1)S(1)}, u32[]{:S(2)}, u32[]{:S(2)}) collective-permute-start(bf16[16,4224]{1,0:T(8,128)(2,1)} %pack.1.refs_0_), channel_id=1, source_target_pairs={{0,16},{8,24},{16,0},{24,8},{1,17},{9,25},{17,1},{25,9},{2,18},{10... | collective-permute-start | bytes 405512 | tf_op jit(solution)/shard_map/ppermute | solution.py:253
  5.8 2.4 %collective-permute-start.1 = (bf16[16,4224]{1,0:T(8,128)(2,1)}, bf16[16,4224]{1,0:T(8,128)(2,1)S(1)}, u32[]{:S(2)}, u32[]{:S(2)}) collective-permute-start(bf16[16,4224]{1,0:T(8,128)(2,1)} %pack.1.refs_0_), channel_id=1, source_target_pairs={{0,6},{1,7},{2,4},{3,5},{4,2},{5,3},{6,0},{7,1},{8,14},{9,15},{10,... | collective-permute-start | bytes 405512 | tf_op jit(solution)/shard_map/ppermute | solution.py:248
  9.3 1.3 %collective-permute-start.7 = (bf16[16,4224]{1,0:T(8,128)(2,1)}, bf16[16,4224]{1,0:T(8,128)(2,1)S(1)}, u32[]{:S(2)}, u32[]{:S(2)}) collective-permute-start(bf16[16,4224]{1,0:T(8,128)(2,1)} %pack.1.refs_0_), channel_id=1, source_target_pairs={{0,24},{8,0},{16,8},{24,16},{1,25},{9,1},{17,9},{25,17},{2,26},{10... | collective-permute-start | bytes 405512 | tf_op jit(solution)/shard_map/ppermute | solution.py:253
  10.6 2.5 %collective-permute-done.refs_0_ = bf16[16,4224]{1,0:T(8,128)(2,1)S(1)} collective-permute-done((bf16[16,4224]{1,0:T(8,128)(2,1)}, bf16[16,4224]{1,0:T(8,128)(2,1)S(1)}, u32[]{:S(2)}, u32[]{:S(2)}) %collective-permute-start) | collective-permute-done | bytes 135200 | tf_op jit(solution)/shard_map/ppermute | solution.py:253
  13.2 3.0 %collective-permute-start.8 = (bf16[16,4224]{1,0:T(8,128)(2,1)}, bf16[16,4224]{1,0:T(8,128)(2,1)S(1)}, u32[]{:S(2)}, u32[]{:S(2)}) collective-permute-start(bf16[16,4224]{1,0:T(8,128)(2,1)} %pack.1.refs_0_), channel_id=1, source_target_pairs={{0,8},{8,16},{16,24},{24,0},{1,9},{9,17},{17,25},{25,1},{2,10},{10... | collective-permute-start | bytes 405512 | tf_op jit(solution)/shard_map/ppermute | solution.py:253
  16.2 2.8 %copy-done = bf16[2,384,4096]{2,1,0:T(8,128)(2,1)S(1)} copy-done((bf16[2,384,4096]{2,1,0:T(8,128)(2,1)S(1)}, bf16[2,384,4096]{2,1,0:T(8,128)(2,1)}, u32[]{:S(2)}) %copy-start) | copy-done | bytes 6291480
  19.0 2.1 %fetch_turned.2.refs_5_.refs_11_ = bf16[4096,768]{1,0:T(8,128)(2,1)S(1)} custom-call(bf16[768,4096]{1,0:T(8,128)(2,1)S(1)} %bitcast.6), custom_call_target="tpu_custom_call" | custom-call | bytes 12582912 | tf_op jit(solution)/shard_map/fetch_turned/pallas_call | solution.py:103
  21.1 1.6 %collective-permute-start.4 = (bf16[16,4224]{1,0:T(8,128)(2,1)S(1)}, bf16[16,4224]{1,0:T(8,128)(2,1)S(1)}, u32[]{:S(2)}, u32[]{:S(2)}) collective-permute-start(bf16[16,4224]{1,0:T(8,128)(2,1)S(1)} %collective-permute-done.refs_0_), channel_id=1, source_target_pairs={{0,2},{1,3},{2,0},{3,1},{4,6},{5,7},{6,4},{7,5},{8,10},{9,11},{10,... | collective-permute-start | bytes 405512 | tf_op jit(solution)/shard_map/ppermute | solution.py:248
  22.7 1.5 %collective-permute-start.5 = (bf16[16,4224]{1,0:T(8,128)(2,1)S(1)}, bf16[16,4224]{1,0:T(8,128)(2,1)S(1)}, u32[]{:S(2)}, u32[]{:S(2)}) collective-permute-start(bf16[16,4224]{1,0:T(8,128)(2,1)S(1)} %collective-permute-done.refs_0_), channel_id=1, source_target_pairs={{0,4},{1,5},{2,6},{3,7},{4,0},{5,1},{6,2},{7,3},{8,12},{9,13},{10,... | collective-permute-start | bytes 405512 | tf_op jit(solution)/shard_map/ppermute | solution.py:248
  24.7 2.7 %collective-permute-start.9 = (bf16[16,4224]{1,0:T(8,128)(2,1)S(1)}, bf16[16,4224]{1,0:T(8,128)(2,1)S(1)}, u32[]{:S(2)}, u32[]{:S(2)}) collective-permute-start(bf16[16,4224]{1,0:T(8,128)(2,1)S(1)} %collective-permute-done.1.refs_3_), channel_id=1, source_target_pairs={{0,24},{8,0},{16,8},{24,16},{1,25},{9,1},{17,9},{25,17},{2,26},{10... | collective-permute-start | bytes 405512 | tf_op jit(solution)/shard_map/ppermute | solution.py:253
  27.4 2.1 %fetch_turned.3.refs_6_.refs_12_ = bf16[4096,768]{1,0:T(8,128)(2,1)S(1)} custom-call(bf16[768,4096]{1,0:T(8,128)(2,1)S(1)} %bitcast.7), custom_call_target="tpu_custom_call" | custom-call | bytes 12582912 | tf_op jit(solution)/shard_map/fetch_turned/pallas_call | solution.py:103
  31.1 4.0 %collective-permute-done.10.refs_5_ = bf16[16,4224]{1,0:T(8,128)(2,1)S(1)} collective-permute-done((bf16[16,4224]{1,0:T(8,128)(2,1)S(1)}, bf16[16,4224]{1,0:T(8,128)(2,1)S(1)}, u32[]{:S(2)}, u32[]{:S(2)}) %collective-permute-start.10) | collective-permute-done | bytes 135200 | tf_op jit(solution)/shard_map/ppermute | solution.py:253
  35.0 1.6 %collective-permute-start.13 = (bf16[32,4224]{1,0:T(8,128)(2,1)S(1)}, bf16[32,4224]{1,0:T(8,128)(2,1)S(1)}, u32[]{:S(2)}, u32[]{:S(2)}) collective-permute-start(bf16[32,4224]{1,0:T(8,128)(2,1)S(1)} %gather.5.refs_1_), channel_id=1, source_target_pairs={{0,2},{1,3},{2,0},{3,1},{4,6},{5,7},{6,4},{7,5},{8,10},{9,11},{10,... | collective-permute-start | bytes 811016 | tf_op jit(solution)/shard_map/ppermute | solution.py:248
  36.6 1.5 %collective-permute-start.14 = (bf16[32,4224]{1,0:T(8,128)(2,1)S(1)}, bf16[32,4224]{1,0:T(8,128)(2,1)S(1)}, u32[]{:S(2)}, u32[]{:S(2)}) collective-permute-start(bf16[32,4224]{1,0:T(8,128)(2,1)S(1)} %gather.5.refs_1_), channel_id=1, source_target_pairs={{0,4},{1,5},{2,6},{3,7},{4,0},{5,1},{6,2},{7,3},{8,12},{9,13},{10,... | collective-permute-start | bytes 811016 | tf_op jit(solution)/shard_map/ppermute | solution.py:248
  38.1 5.1 %experts.2 = (bf16[32,4096]{1,0:T(8,128)(2,1)S(1)}, bf16[32,4096]{1,0:T(8,128)(2,1)S(1)}, bf16[16,4096]{1,0:T(8,128)(2,1)S(1)}, bf16[80,4096]{1,0:T(8,128)(2,1)S...) custom-call(s32[1]{0:T(128)} %bitcast.refs_0_, bf16[64,4224]{1,0:T(8,128)(2,1)S(1)} %gather.3.refs_1_, ...), custom_call_target="tpu_custom_call" | custom-call | flops 4831838208 | bytes 4194304 | tf_op jit(solution)/shard_map/experts/pallas_call | solution.py:197
  43.2 0.8 collective-permute-done.13.refs_2_
  44.0 1.2 %collective-permute-done.14.refs_3_ = bf16[32,4224]{1,0:T(8,128)(2,1)S(1)} collective-permute-done((bf16[32,4224]{1,0:T(8,128)(2,1)S(1)}, bf16[32,4224]{1,0:T(8,128)(2,1)S(1)}, u32[]{:S(2)}, u32[]{:S(2)}) %collective-permute-start.14) | collective-permute-done | bytes 270368 | tf_op jit(solution)/shard_map/ppermute | solution.py:248
  46.2 1.1 %collective-permute-done.15 = bf16[80,4096]{1,0:T(8,128)(2,1)S(1)} collective-permute-done((bf16[80,4096]{1,0:T(8,128)(2,1)S(1)}, bf16[80,4096]{1,0:T(8,128)(2,1)S(1)}, u32[]{:S(2)}, u32[]{:S(2)}) %collective-permute-start.15) | collective-permute-done | bytes 655392 | tf_op jit(solution)/shard_map/ppermute | solution.py:248
  48.6 1.5 %collective-permute-start.23 = (bf16[32,4096]{1,0:T(8,128)(2,1)S(1)}, bf16[32,4096]{1,0:T(8,128)(2,1)S(1)}, u32[]{:S(2)}, u32[]{:S(2)}) collective-permute-start(bf16[32,4096]{1,0:T(8,128)(2,1)S(1)} %get-tuple-element.90), channel_id=1, source_target_pairs={{0,4},{1,5},{2,6},{3,7},{4,0},{5,1},{6,2},{7,3},{8,12},{9,13},{10,... | collective-permute-start | bytes 786440 | tf_op jit(solution)/shard_map/ppermute | solution.py:248
  50.1 1.4 %collective-permute-start.24 = (bf16[16,4096]{1,0:T(8,128)(2,1)S(1)}, bf16[16,4096]{1,0:T(8,128)(2,1)S(1)}, u32[]{:S(2)}, u32[]{:S(2)}) collective-permute-start(bf16[16,4096]{1,0:T(8,128)(2,1)S(1)} %add_convert_fusion.7), channel_id=1, source_target_pairs={{0,6},{1,7},{2,4},{3,5},{4,2},{5,3},{6,0},{7,1},{8,14},{9,15},{10,... | collective-permute-start | bytes 393224 | tf_op jit(solution)/shard_map/ppermute | solution.py:248
  51.6 5.1 %experts.3 = (bf16[16,4096]{1,0:T(8,128)(2,1)S(1)}, bf16[16,4096]{1,0:T(8,128)(2,1)S(1)}, bf16[32,4096]{1,0:T(8,128)(2,1)S(1)}, bf16[32,4096]{1,0:T(8,128)(2,1)S...) custom-call(s32[1]{0:T(128)} %bitcast.refs_0_, bf16[32,4224]{1,0:T(8,128)(2,1)S(1)} %gather.5.refs_1_, ...), custom_call_target="tpu_custom_call" | custom-call | flops 4831838208 | bytes 4194304 | tf_op jit(solution)/shard_map/experts/pallas_call | solution.py:197
  56.7 3.5 %collective-permute-done.24 = bf16[16,4096]{1,0:T(8,128)(2,1)S(1)} collective-permute-done((bf16[16,4096]{1,0:T(8,128)(2,1)S(1)}, bf16[16,4096]{1,0:T(8,128)(2,1)S(1)}, u32[]{:S(2)}, u32[]{:S(2)}) %collective-permute-start.24) | collective-permute-done | bytes 131104 | tf_op jit(solution)/shard_map/ppermute | solution.py:248
  60.4 1.4 %collective-permute-start.28 = (bf16[16,4096]{1,0:T(8,128)(2,1)S(1)}, bf16[16,4096]{1,0:T(8,128)(2,1)S(1)}, u32[]{:S(2)}, u32[]{:S(2)}) collective-permute-start(bf16[16,4096]{1,0:T(8,128)(2,1)S(1)} %get-tuple-element.115), channel_id=1, source_target_pairs={{0,24},{8,0},{16,8},{24,16},{1,25},{9,1},{17,9},{25,17},{2,26},{10... | collective-permute-start | bytes 393224 | tf_op jit(solution)/shard_map/ppermute | solution.py:253
  62.7 0.9 %collective-permute-start.31 = (bf16[32,4096]{1,0:T(8,128)(2,1)S(1)}, bf16[32,4096]{1,0:T(8,128)(2,1)S(1)}, u32[]{:S(2)}, u32[]{:S(2)}) collective-permute-start(bf16[32,4096]{1,0:T(8,128)(2,1)S(1)} %get-tuple-element.122), channel_id=1, source_target_pairs={{0,4},{1,5},{2,6},{3,7},{4,0},{5,1},{6,2},{7,3},{8,12},{9,13},{10,... | collective-permute-start | bytes 786440 | tf_op jit(solution)/shard_map/ppermute | solution.py:248
  63.5 1.5 %collective-permute-start.30 = (bf16[32,4096]{1,0:T(8,128)(2,1)S(1)}, bf16[32,4096]{1,0:T(8,128)(2,1)S(1)}, u32[]{:S(2)}, u32[]{:S(2)}) collective-permute-start(bf16[32,4096]{1,0:T(8,128)(2,1)S(1)} %get-tuple-element.121), channel_id=1, source_target_pairs={{0,2},{1,3},{2,0},{3,1},{4,6},{5,7},{6,4},{7,5},{8,10},{9,11},{10,... | collective-permute-start | bytes 786440 | tf_op jit(solution)/shard_map/ppermute | solution.py:248
  65.3 1.8 %collective-permute-done.28 = bf16[16,4096]{1,0:T(8,128)(2,1)S(1)} collective-permute-done((bf16[16,4096]{1,0:T(8,128)(2,1)S(1)}, bf16[16,4096]{1,0:T(8,128)(2,1)S(1)}, u32[]{:S(2)}, u32[]{:S(2)}) %collective-permute-start.28) | collective-permute-done | bytes 131104 | tf_op jit(solution)/shard_map/ppermute | solution.py:253
  67.0 2.7 %collective-permute-done.27 = bf16[16,4096]{1,0:T(8,128)(2,1)S(1)} collective-permute-done((bf16[16,4096]{1,0:T(8,128)(2,1)S(1)}, bf16[16,4096]{1,0:T(8,128)(2,1)S(1)}, u32[]{:S(2)}, u32[]{:S(2)}) %collective-permute-start.27) | collective-permute-done | bytes 131104 | tf_op jit(solution)/shard_map/ppermute | solution.py:253
  69.8 1.6 %collective-permute-start.29 = (bf16[16,4096]{1,0:T(8,128)(2,1)S(1)}, bf16[16,4096]{1,0:T(8,128)(2,1)S(1)}, u32[]{:S(2)}, u32[]{:S(2)}) collective-permute-start(bf16[16,4096]{1,0:T(8,128)(2,1)S(1)} %fusion), channel_id=1, source_target_pairs={{0,6},{1,7},{2,4},{3,5},{4,2},{5,3},{6,0},{7,1},{8,14},{9,15},{10,... | collective-permute-start | bytes 393224 | tf_op jit(solution)/shard_map/ppermute | solution.py:248
  71.6 4.0 %collective-permute-start.33 = (bf16[16,4096]{1,0:T(8,128)(2,1)S(1)}, bf16[16,4096]{1,0:T(8,128)(2,1)S(1)}, u32[]{:S(2)}, u32[]{:S(2)}) collective-permute-start(bf16[16,4096]{1,0:T(8,128)(2,1)S(1)} %get-tuple-element.126), channel_id=1, source_target_pairs={{0,24},{8,0},{16,8},{24,16},{1,25},{9,1},{17,9},{25,17},{2,26},{10... | collective-permute-start | bytes 393224 | tf_op jit(solution)/shard_map/ppermute | solution.py:253
  75.7 2.3 %collective-permute-done.33 = bf16[16,4096]{1,0:T(8,128)(2,1)S(1)} collective-permute-done((bf16[16,4096]{1,0:T(8,128)(2,1)S(1)}, bf16[16,4096]{1,0:T(8,128)(2,1)S(1)}, u32[]{:S(2)}, u32[]{:S(2)}) %collective-permute-start.33) | collective-permute-done | bytes 131104 | tf_op jit(solution)/shard_map/ppermute | solution.py:253
  78.1 4.2 %collective-permute-done.32 = bf16[16,4096]{1,0:T(8,128)(2,1)S(1)} collective-permute-done((bf16[16,4096]{1,0:T(8,128)(2,1)S(1)}, bf16[16,4096]{1,0:T(8,128)(2,1)S(1)}, u32[]{:S(2)}, u32[]{:S(2)}) %collective-permute-start.32) | collective-permute-done | bytes 131104 | tf_op jit(solution)/shard_map/ppermute | solution.py:253
  (66 shorter events, 7.9 us)
Async XLA Ops:
  1.7 11.4 %collective-permute-start = (bf16[16,4224]{1,0:T(8,128)(2,1)}, bf16[16,4224]{1,0:T(8,128)(2,1)S(1)}, u32[]{:S(2)}, u32[]{:S(2)}) collective-permute-start(bf16[16,4224]{1,0:T(8,128)(2,1)} %pack.1.refs_0_), channel_id=1, source_target_pairs={{0,16},{8,24},{16,0},{24,8},{1,17},{9,25},{17,1},{25,9},{2,18},{10... | collective-permute-start | bytes 405512 | tf_op jit(solution)/shard_map/ppermute | solution.py:253
  5.8 15.3 %collective-permute-start.1 = (bf16[16,4224]{1,0:T(8,128)(2,1)}, bf16[16,4224]{1,0:T(8,128)(2,1)S(1)}, u32[]{:S(2)}, u32[]{:S(2)}) collective-permute-start(bf16[16,4224]{1,0:T(8,128)(2,1)} %pack.1.refs_0_), channel_id=1, source_target_pairs={{0,6},{1,7},{2,4},{3,5},{4,2},{5,3},{6,0},{7,1},{8,14},{9,15},{10,... | collective-permute-start | bytes 405512 | tf_op jit(solution)/shard_map/ppermute | solution.py:248
  8.2 12.8 %collective-permute-start.2 = (bf16[16,4224]{1,0:T(8,128)(2,1)}, bf16[16,4224]{1,0:T(8,128)(2,1)S(1)}, u32[]{:S(2)}, u32[]{:S(2)}) collective-permute-start(bf16[16,4224]{1,0:T(8,128)(2,1)} %pack.1.refs_0_), channel_id=1, source_target_pairs={{0,4},{1,5},{2,6},{3,7},{4,0},{5,1},{6,2},{7,3},{8,12},{9,13},{10,... | collective-permute-start | bytes 405512 | tf_op jit(solution)/shard_map/ppermute | solution.py:248
  8.7 12.3 %collective-permute-start.3 = (bf16[16,4224]{1,0:T(8,128)(2,1)}, bf16[16,4224]{1,0:T(8,128)(2,1)S(1)}, u32[]{:S(2)}, u32[]{:S(2)}) collective-permute-start(bf16[16,4224]{1,0:T(8,128)(2,1)} %pack.1.refs_0_), channel_id=1, source_target_pairs={{0,2},{1,3},{2,0},{3,1},{4,6},{5,7},{6,4},{7,5},{8,10},{9,11},{10,... | collective-permute-start | bytes 405512 | tf_op jit(solution)/shard_map/ppermute | solution.py:248
  9.3 15.4 %collective-permute-start.7 = (bf16[16,4224]{1,0:T(8,128)(2,1)}, bf16[16,4224]{1,0:T(8,128)(2,1)S(1)}, u32[]{:S(2)}, u32[]{:S(2)}) collective-permute-start(bf16[16,4224]{1,0:T(8,128)(2,1)} %pack.1.refs_0_), channel_id=1, source_target_pairs={{0,24},{8,0},{16,8},{24,16},{1,25},{9,1},{17,9},{25,17},{2,26},{10... | collective-permute-start | bytes 405512 | tf_op jit(solution)/shard_map/ppermute | solution.py:253
  13.2 14.2 %collective-permute-start.8 = (bf16[16,4224]{1,0:T(8,128)(2,1)}, bf16[16,4224]{1,0:T(8,128)(2,1)S(1)}, u32[]{:S(2)}, u32[]{:S(2)}) collective-permute-start(bf16[16,4224]{1,0:T(8,128)(2,1)} %pack.1.refs_0_), channel_id=1, source_target_pairs={{0,8},{8,16},{16,24},{24,0},{1,9},{9,17},{17,25},{25,1},{2,10},{10... | collective-permute-start | bytes 405512 | tf_op jit(solution)/shard_map/ppermute | solution.py:253
  21.1 9.3 %collective-permute-start.4 = (bf16[16,4224]{1,0:T(8,128)(2,1)S(1)}, bf16[16,4224]{1,0:T(8,128)(2,1)S(1)}, u32[]{:S(2)}, u32[]{:S(2)}) collective-permute-start(bf16[16,4224]{1,0:T(8,128)(2,1)S(1)} %collective-permute-done.refs_0_), channel_id=1, source_target_pairs={{0,2},{1,3},{2,0},{3,1},{4,6},{5,7},{6,4},{7,5},{8,10},{9,11},{10,... | collective-permute-start | bytes 405512 | tf_op jit(solution)/shard_map/ppermute | solution.py:248
  22.7 7.9 %collective-permute-start.5 = (bf16[16,4224]{1,0:T(8,128)(2,1)S(1)}, bf16[16,4224]{1,0:T(8,128)(2,1)S(1)}, u32[]{:S(2)}, u32[]{:S(2)}) collective-permute-start(bf16[16,4224]{1,0:T(8,128)(2,1)S(1)} %collective-permute-done.refs_0_), channel_id=1, source_target_pairs={{0,4},{1,5},{2,6},{3,7},{4,0},{5,1},{6,2},{7,3},{8,12},{9,13},{10,... | collective-permute-start | bytes 405512 | tf_op jit(solution)/shard_map/ppermute | solution.py:248
  24.2 6.4 %collective-permute-start.6 = (bf16[16,4224]{1,0:T(8,128)(2,1)S(1)}, bf16[16,4224]{1,0:T(8,128)(2,1)S(1)}, u32[]{:S(2)}, u32[]{:S(2)}) collective-permute-start(bf16[16,4224]{1,0:T(8,128)(2,1)S(1)} %collective-permute-done.refs_0_), channel_id=1, source_target_pairs={{0,6},{1,7},{2,4},{3,5},{4,2},{5,3},{6,0},{7,1},{8,14},{9,15},{10,... | collective-permute-start | bytes 405512 | tf_op jit(solution)/shard_map/ppermute | solution.py:248
  24.7 6.4 %collective-permute-start.9 = (bf16[16,4224]{1,0:T(8,128)(2,1)S(1)}, bf16[16,4224]{1,0:T(8,128)(2,1)S(1)}, u32[]{:S(2)}, u32[]{:S(2)}) collective-permute-start(bf16[16,4224]{1,0:T(8,128)(2,1)S(1)} %collective-permute-done.1.refs_3_), channel_id=1, source_target_pairs={{0,24},{8,0},{16,8},{24,16},{1,25},{9,1},{17,9},{25,17},{2,26},{10... | collective-permute-start | bytes 405512 | tf_op jit(solution)/shard_map/ppermute | solution.py:253
  27.4 7.6 %collective-permute-start.10 = (bf16[16,4224]{1,0:T(8,128)(2,1)S(1)}, bf16[16,4224]{1,0:T(8,128)(2,1)S(1)}, u32[]{:S(2)}, u32[]{:S(2)}) collective-permute-start(bf16[16,4224]{1,0:T(8,128)(2,1)S(1)} %collective-permute-done.1.refs_3_), channel_id=1, source_target_pairs={{0,8},{8,16},{16,24},{24,0},{1,9},{9,17},{17,25},{25,1},{2,10},{10... | collective-permute-start | bytes 405512 | tf_op jit(solution)/shard_map/ppermute | solution.py:253
  30.5 7.7 %collective-permute-start.11 = (bf16[64,4224]{1,0:T(8,128)(2,1)S(1)}, bf16[64,4224]{1,0:T(8,128)(2,1)S(1)}, u32[]{:S(2)}, u32[]{:S(2)}) collective-permute-start(bf16[64,4224]{1,0:T(8,128)(2,1)S(1)} %gather.3.refs_1_), channel_id=1, source_target_pairs={{0,1},{1,0},{2,3},{3,2},{4,5},{5,4},{6,7},{7,6},{8,9},{9,8},{10,11... | collective-permute-start | bytes 1622024 | tf_op jit(solution)/shard_map/ppermute | solution.py:248
  35.0 3.1 %collective-permute-start.12 = (bf16[64,4224]{1,0:T(8,128)(2,1)S(1)}, bf16[64,4224]{1,0:T(8,128)(2,1)S(1)}, u32[]{:S(2)}, u32[]{:S(2)}) collective-permute-start(bf16[64,4224]{1,0:T(8,128)(2,1)S(1)} %gather.4.refs_2_), channel_id=1, source_target_pairs={{0,1},{1,0},{2,3},{3,2},{4,5},{5,4},{6,7},{7,6},{8,9},{9,8},{10,11... | collective-permute-start | bytes 1622024 | tf_op jit(solution)/shard_map/ppermute | solution.py:248
  35.0 9.0 %collective-permute-start.13 = (bf16[32,4224]{1,0:T(8,128)(2,1)S(1)}, bf16[32,4224]{1,0:T(8,128)(2,1)S(1)}, u32[]{:S(2)}, u32[]{:S(2)}) collective-permute-start(bf16[32,4224]{1,0:T(8,128)(2,1)S(1)} %gather.5.refs_1_), channel_id=1, source_target_pairs={{0,2},{1,3},{2,0},{3,1},{4,6},{5,7},{6,4},{7,5},{8,10},{9,11},{10,... | collective-permute-start | bytes 811016 | tf_op jit(solution)/shard_map/ppermute | solution.py:248
  36.6 8.6 %collective-permute-start.14 = (bf16[32,4224]{1,0:T(8,128)(2,1)S(1)}, bf16[32,4224]{1,0:T(8,128)(2,1)S(1)}, u32[]{:S(2)}, u32[]{:S(2)}) collective-permute-start(bf16[32,4224]{1,0:T(8,128)(2,1)S(1)} %gather.5.refs_1_), channel_id=1, source_target_pairs={{0,4},{1,5},{2,6},{3,7},{4,0},{5,1},{6,2},{7,3},{8,12},{9,13},{10,... | collective-permute-start | bytes 811016 | tf_op jit(solution)/shard_map/ppermute | solution.py:248
  45.2 2.5 %collective-permute-start.17 = (bf16[32,4224]{1,0:T(8,128)(2,1)S(1)}, bf16[32,4224]{1,0:T(8,128)(2,1)S(1)}, u32[]{:S(2)}, u32[]{:S(2)}) collective-permute-start(bf16[32,4224]{1,0:T(8,128)(2,1)S(1)} %gather.5.refs_1_), channel_id=1, source_target_pairs={{0,1},{1,0},{2,3},{3,2},{4,5},{5,4},{6,7},{7,6},{8,9},{9,8},{10,11... | collective-permute-start | bytes 811016 | tf_op jit(solution)/shard_map/ppermute | solution.py:248
  45.7 2.9 %collective-permute-start.21 = (bf16[16,4224]{1,0:T(8,128)(2,1)S(1)}, bf16[16,4224]{1,0:T(8,128)(2,1)S(1)}, u32[]{:S(2)}, u32[]{:S(2)}) collective-permute-start(bf16[16,4224]{1,0:T(8,128)(2,1)S(1)} %collective-permute-done.10.refs_5_), channel_id=1, source_target_pairs={{0,1},{1,0},{2,3},{3,2},{4,5},{5,4},{6,7},{7,6},{8,9},{9,8},{10,11... | collective-permute-start | bytes 405512 | tf_op jit(solution)/shard_map/ppermute | solution.py:248
  46.2 3.9 %collective-permute-start.18 = (bf16[32,4224]{1,0:T(8,128)(2,1)S(1)}, bf16[32,4224]{1,0:T(8,128)(2,1)S(1)}, u32[]{:S(2)}, u32[]{:S(2)}) collective-permute-start(bf16[32,4224]{1,0:T(8,128)(2,1)S(1)} %collective-permute-done.13.refs_2_), channel_id=1, source_target_pairs={{0,1},{1,0},{2,3},{3,2},{4,5},{5,4},{6,7},{7,6},{8,9},{9,8},{10,11... | collective-permute-start | bytes 811016 | tf_op jit(solution)/shard_map/ppermute | solution.py:248
  47.3 4.3 %collective-permute-start.19 = (bf16[32,4224]{1,0:T(8,128)(2,1)S(1)}, bf16[32,4224]{1,0:T(8,128)(2,1)S(1)}, u32[]{:S(2)}, u32[]{:S(2)}) collective-permute-start(bf16[32,4224]{1,0:T(8,128)(2,1)S(1)} %collective-permute-done.14.refs_3_), channel_id=1, source_target_pairs={{0,1},{1,0},{2,3},{3,2},{4,5},{5,4},{6,7},{7,6},{8,9},{9,8},{10,11... | collective-permute-start | bytes 811016 | tf_op jit(solution)/shard_map/ppermute | solution.py:248
  47.7 12.5 %collective-permute-start.16 = (bf16[48,4096]{1,0:T(8,128)(2,1)S(1)}, bf16[48,4096]{1,0:T(8,128)(2,1)S(1)}, u32[]{:S(2)}, u32[]{:S(2)}) collective-permute-start(bf16[48,4096]{1,0:T(8,128)(2,1)S(1)} %get-tuple-element.88), channel_id=1, source_target_pairs={{0,1},{1,0},{2,3},{3,2},{4,5},{5,4},{6,7},{7,6},{8,9},{9,8},{10,11... | collective-permute-start | bytes 1179656 | tf_op jit(solution)/shard_map/ppermute | solution.py:248
  48.1 12.1 %collective-permute-start.22 = (bf16[32,4096]{1,0:T(8,128)(2,1)S(1)}, bf16[32,4096]{1,0:T(8,128)(2,1)S(1)}, u32[]{:S(2)}, u32[]{:S(2)}) collective-permute-start(bf16[32,4096]{1,0:T(8,128)(2,1)S(1)} %get-tuple-element.89), channel_id=1, source_target_pairs={{0,2},{1,3},{2,0},{3,1},{4,6},{5,7},{6,4},{7,5},{8,10},{9,11},{10,... | collective-permute-start | bytes 786440 | tf_op jit(solution)/shard_map/ppermute | solution.py:248
  48.6 11.6 %collective-permute-start.23 = (bf16[32,4096]{1,0:T(8,128)(2,1)S(1)}, bf16[32,4096]{1,0:T(8,128)(2,1)S(1)}, u32[]{:S(2)}, u32[]{:S(2)}) collective-permute-start(bf16[32,4096]{1,0:T(8,128)(2,1)S(1)} %get-tuple-element.90), channel_id=1, source_target_pairs={{0,4},{1,5},{2,6},{3,7},{4,0},{5,1},{6,2},{7,3},{8,12},{9,13},{10,... | collective-permute-start | bytes 786440 | tf_op jit(solution)/shard_map/ppermute | solution.py:248
  50.1 10.1 %collective-permute-start.24 = (bf16[16,4096]{1,0:T(8,128)(2,1)S(1)}, bf16[16,4096]{1,0:T(8,128)(2,1)S(1)}, u32[]{:S(2)}, u32[]{:S(2)}) collective-permute-start(bf16[16,4096]{1,0:T(8,128)(2,1)S(1)} %add_convert_fusion.7), channel_id=1, source_target_pairs={{0,6},{1,7},{2,4},{3,5},{4,2},{5,3},{6,0},{7,1},{8,14},{9,15},{10,... | collective-permute-start | bytes 393224 | tf_op jit(solution)/shard_map/ppermute | solution.py:248
  56.6 3.7 %collective-permute-start.25 = (bf16[128,4096]{1,0:T(8,128)(2,1)S(1)}, bf16[128,4096]{1,0:T(8,128)(2,1)S(1)}, u32[]{:S(2)}, u32[]{:S(2)}) collective-permute-start(bf16[128,4096]{1,0:T(8,128)(2,1)S(1)} %get-tuple-element.111), channel_id=1, source_target_pairs={{0,1},{1,0},{2,3},{3,2},{4,5},{5,4},{6,7},{7,6},{8,9},{9,8},{10,11... | collective-permute-start | bytes 3145736 | tf_op jit(solution)/shard_map/ppermute | solution.py:248
  60.4 6.6 %collective-permute-start.28 = (bf16[16,4096]{1,0:T(8,128)(2,1)S(1)}, bf16[16,4096]{1,0:T(8,128)(2,1)S(1)}, u32[]{:S(2)}, u32[]{:S(2)}) collective-permute-start(bf16[16,4096]{1,0:T(8,128)(2,1)S(1)} %get-tuple-element.115), channel_id=1, source_target_pairs={{0,24},{8,0},{16,8},{24,16},{1,25},{9,1},{17,9},{25,17},{2,26},{10... | collective-permute-start | bytes 393224 | tf_op jit(solution)/shard_map/ppermute | solution.py:253
  61.9 7.9 %collective-permute-start.27 = (bf16[16,4096]{1,0:T(8,128)(2,1)S(1)}, bf16[16,4096]{1,0:T(8,128)(2,1)S(1)}, u32[]{:S(2)}, u32[]{:S(2)}) collective-permute-start(bf16[16,4096]{1,0:T(8,128)(2,1)S(1)} %get-tuple-element.114), channel_id=1, source_target_pairs={{0,8},{8,16},{16,24},{24,0},{1,9},{9,17},{17,25},{25,1},{2,10},{10... | collective-permute-start | bytes 393224 | tf_op jit(solution)/shard_map/ppermute | solution.py:253
  62.7 8.7 %collective-permute-start.31 = (bf16[32,4096]{1,0:T(8,128)(2,1)S(1)}, bf16[32,4096]{1,0:T(8,128)(2,1)S(1)}, u32[]{:S(2)}, u32[]{:S(2)}) collective-permute-start(bf16[32,4096]{1,0:T(8,128)(2,1)S(1)} %get-tuple-element.122), channel_id=1, source_target_pairs={{0,4},{1,5},{2,6},{3,7},{4,0},{5,1},{6,2},{7,3},{8,12},{9,13},{10,... | collective-permute-start | bytes 786440 | tf_op jit(solution)/shard_map/ppermute | solution.py:248
  63.5 7.9 %collective-permute-start.30 = (bf16[32,4096]{1,0:T(8,128)(2,1)S(1)}, bf16[32,4096]{1,0:T(8,128)(2,1)S(1)}, u32[]{:S(2)}, u32[]{:S(2)}) collective-permute-start(bf16[32,4096]{1,0:T(8,128)(2,1)S(1)} %get-tuple-element.121), channel_id=1, source_target_pairs={{0,2},{1,3},{2,0},{3,1},{4,6},{5,7},{6,4},{7,5},{8,10},{9,11},{10,... | collective-permute-start | bytes 786440 | tf_op jit(solution)/shard_map/ppermute | solution.py:248
  65.0 10.5 %collective-permute-start.26 = (bf16[16,4096]{1,0:T(8,128)(2,1)S(1)}, bf16[16,4096]{1,0:T(8,128)(2,1)S(1)}, u32[]{:S(2)}, u32[]{:S(2)}) collective-permute-start(bf16[16,4096]{1,0:T(8,128)(2,1)S(1)} %fusion.3), channel_id=1, source_target_pairs={{0,16},{8,24},{16,0},{24,8},{1,17},{9,25},{17,1},{25,9},{2,18},{10... | collective-permute-start | bytes 393224 | tf_op jit(solution)/shard_map/ppermute | solution.py:253
  69.8 5.9 %collective-permute-start.29 = (bf16[16,4096]{1,0:T(8,128)(2,1)S(1)}, bf16[16,4096]{1,0:T(8,128)(2,1)S(1)}, u32[]{:S(2)}, u32[]{:S(2)}) collective-permute-start(bf16[16,4096]{1,0:T(8,128)(2,1)S(1)} %fusion), channel_id=1, source_target_pairs={{0,6},{1,7},{2,4},{3,5},{4,2},{5,3},{6,0},{7,1},{8,14},{9,15},{10,... | collective-permute-start | bytes 393224 | tf_op jit(solution)/shard_map/ppermute | solution.py:248
  71.6 6.5 %collective-permute-start.33 = (bf16[16,4096]{1,0:T(8,128)(2,1)S(1)}, bf16[16,4096]{1,0:T(8,128)(2,1)S(1)}, u32[]{:S(2)}, u32[]{:S(2)}) collective-permute-start(bf16[16,4096]{1,0:T(8,128)(2,1)S(1)} %get-tuple-element.126), channel_id=1, source_target_pairs={{0,24},{8,0},{16,8},{24,16},{1,25},{9,1},{17,9},{25,17},{2,26},{10... | collective-permute-start | bytes 393224 | tf_op jit(solution)/shard_map/ppermute | solution.py:253
  75.5 6.8 %collective-permute-start.32 = (bf16[16,4096]{1,0:T(8,128)(2,1)S(1)}, bf16[16,4096]{1,0:T(8,128)(2,1)S(1)}, u32[]{:S(2)}, u32[]{:S(2)}) collective-permute-start(bf16[16,4096]{1,0:T(8,128)(2,1)S(1)} %get-tuple-element.125), channel_id=1, source_target_pairs={{0,8},{8,16},{16,24},{24,0},{1,9},{9,17},{17,25},{25,1},{2,10},{10... | collective-permute-start | bytes 393224 | tf_op jit(solution)/shard_map/ppermute | solution.py:253
  (7 other events, 33.3 us)

commit v5 on v4

--- a/solution.py
+++ b/solution.py
@@ -213,12 +213,22 @@
     )(own, *pieces, gates, ups, downs)
 
 
-def pack_kernel(tokens_ref, experts_ref, weights_ref, packed_ref):
+def pack_kernel(
+    tokens_ref, experts_ref, weights_ref, packed_ref, experts, weights, sems
+):
     model_width = tokens_ref.shape[1]
-    packed_ref[:, :model_width] = tokens_ref[...]
-    weights = weights_ref[...]
-    high = weights.astype(jnp.bfloat16).astype(jnp.float32)
-    listed = jnp.concatenate([experts_ref[...].astype(jnp.float32), high, weights - high], axis=0)
+    copies = [
+        pltpu.make_async_copy(experts_ref, experts, sems.at[0]),
+        pltpu.make_async_copy(weights_ref, weights, sems.at[1]),
+        pltpu.make_async_copy(tokens_ref, packed_ref.at[:, pl.ds(0, model_width)], sems.at[2]),
+    ]
+    for copy in copies:
+        copy.start()
+    copies[0].wait()
+    copies[1].wait()
+    values = weights[...]
+    high = values.astype(jnp.bfloat16).astype(jnp.float32)
+    listed = jnp.concatenate([experts[...].astype(jnp.float32), high, values - high], axis=0)
     width = packed_ref.shape[1] - model_width
     place = lax.broadcasted_iota(jnp.int32, (listed.shape[0], width), 0)
     lane = lax.broadcasted_iota(jnp.int32, (listed.shape[0], width), 1)
@@ -230,17 +240,41 @@
         preferred_element_type=jnp.float32,
     )
     packed_ref[:, model_width:] = extra.astype(jnp.bfloat16)
+    copies[2].wait()
 
 
 def with_routing(tokens, routed_experts, route_weights):
     rows, width = tokens.shape
+    top = routed_experts.shape[1]
     return pl.pallas_call(
         pack_kernel,
         out_shape=jax.ShapeDtypeStruct((rows, width + 128), jnp.bfloat16),
-        in_specs=[pl.BlockSpec(memory_space=pltpu.VMEM)] * 3,
+        in_specs=[pl.BlockSpec(memory_space=pl.ANY)] * 3,
         out_specs=pl.BlockSpec(memory_space=pltpu.VMEM),
+        scratch_shapes=[
+            pltpu.VMEM((top, rows), jnp.int32),
+            pltpu.VMEM((top, rows), jnp.float32),
+            pltpu.SemaphoreType.DMA((3,)),
+        ],
+        compiler_params=pltpu.CompilerParams(vmem_limit_bytes=2 * 1024 * 1024),
         name="pack",
     )(tokens, routed_experts.T, route_weights.T)
+
+
+def begin_kernel(own_ref, gate_ref, up_ref, down_ref, index_ref):
+    index_ref[0] = own_ref[0]
+
+
+def begun(own, *weights):
+    scalar = pl.BlockSpec(memory_space=pltpu.SMEM)
+    return pl.pallas_call(
+        begin_kernel,
+        out_shape=jax.ShapeDtypeStruct((1,), jnp.int32),
+        in_specs=[scalar] + [pl.BlockSpec(memory_space=pl.ANY)] * 3,
+        out_specs=scalar,
+        compiler_params=pltpu.CompilerParams(vmem_limit_bytes=50 * 1024 * 1024),
+        name="begin",
+    )(own, *weights)
 
 
 def swap_exp(value, bits):
@@ -281,16 +315,17 @@
     up_weight = up_weight.reshape(units, model_width)
     down_weight = down_weight.reshape(units, model_width)
     own = jnp.full((1,), lax.axis_index("exp") * local_experts, jnp.int32)
+    own = begun(own, gate_weight, up_weight, down_weight)
     tokens, own = ordered(tokens, own)
     packed = with_routing(tokens, routed_experts, route_weights)
 
     two = turn_rep(packed, 2)
     x_own, y_own, far_own = [swap_exp(packed, bits) for bits in (2, 4, 6)]
-    one, three = turn_rep(packed, 1), turn_rep(packed, 3)
     gates = fetched(gate_weight, True)
-    two, far_own, y_own, x_own, gates, up_weight = ordered(
-        two, far_own, y_own, x_own, gates, up_weight
-    )
+    x_own, y_own, far_own, two, gates, up_weight, again = ordered(
+        x_own, y_own, far_own, two, gates, up_weight, packed
+    )
+    one, three = turn_rep(again, 1), turn_rep(again, 3)
     x_two, y_two, far_two = [swap_exp(two, bits) for bits in (2, 4, 6)]
     far_one, far_three = turn_rep(far_own, 1), turn_rep(far_own, 3)
     first = gathered(packed, x_own, y_own, far_own)
@@ -301,12 +336,14 @@
     x_pair, y_pair = swap_exp(pair, 2), swap_exp(pair, 4)
     second = gathered(two, x_two, y_two, far_two)
     downs = fetched(down_weight, False)
-    second, downs, far_one, far_three = ordered(second, downs, far_one, far_three)
+    second, downs = ordered(second, downs)
 
     near = [first, second, first_other, swap_exp(second, 1)]
     groups = row_groups([[5, 1], [6, 2], [7], [13, 9, 14, 10, 15], [4, 0, 3], [12, 8, 11]], rows)
     parts = experts_of(own, near, groups, gates, ups, downs, shard_units, top)
-    *parts, x_pair, y_pair = ordered(*parts, x_pair, y_pair)
+    *parts, x_pair, y_pair, far_one, far_three = ordered(
+        *parts, x_pair, y_pair, far_one, far_three
+    )
     to_x, to_y, to_far, other, near_kept, near_other = parts
     back = swap_exp(other, 1)
     to_x = rounded(to_x, back[: 2 * rows])
@@ -329,7 +366,7 @@
     to_y = rounded(to_y, back[4 * rows : 6 * rows])
     kept = added(near_kept, near_back)
     to_two = rounded(kept[:rows], near_x[:rows], near_y[:rows], near_far)
-    to_two, to_one, to_three = ordered(to_two, to_one, to_three)
+    to_two, to_one, to_three, to_x, to_y = ordered(to_two, to_one, to_three, to_x, to_y)
     from_two = turn_rep(to_two, -2)
     from_one, from_three = turn_rep(to_one, -1), turn_rep(to_three, -3)
     far_x, far_y = swap_exp(to_x, 2), swap_exp(to_y, 4)

time: 83.3 us -> 77.3 us (0.928)
  waiting for transfers between devices: 24.9 us -> 20.2 us
  local copies, waits for them, and re-layouts: 2.96 us -> 0.43 us
    ppermute x10, waiting for transfers between devices: 18 us -> 9.59 us  [turn_rep(): lax.ppermute(value, 'rep', [(i, (i - shift) % replicas) for i in range(re...]
    ppermute x24, waiting for transfers between devices: 6.91 us -> 10.6 us  [swap_exp(): return lax.ppermute(value, 'exp', [(i, i ^ bits) for i in range(owners)])]
    unnamed x10 -> x16, local copies, waits for them, and re-layouts: 2.94 us -> 0.41 us
    ppermute x10, starting transfers between devices: 17.5 us -> 19.5 us  [turn_rep(): lax.ppermute(value, 'rep', [(i, (i - shift) % replicas) for i in range(re...]
    pallas_call x1, Pallas kernels: 1.74 us -> 0.29 us  [with_routing(): pl.pallas_call(pack_kernel, out_shape=jax.ShapeDtypeStruct((rows, width +...]
    pallas_call x2, Pallas kernels: 10.1 us -> 11.5 us  [experts_of(): pl.pallas_call(kernel, out_shape=[jax.ShapeDtypeStruct((count, model_widt...]
    ppermute x24, starting transfers between devices: 19.2 us -> 18 us  [swap_exp(): return lax.ppermute(value, 'exp', [(i, i ^ bits) for i in range(owners)])]
  transfers between devices with their start and end apart: 34 -> 34, of which waited for: 13 -> 18; matrix products, arithmetic and copies ran while one was open for 1% -> 1% of each run, Pallas kernels for 18% -> 21%
where the time goes in v5:
time: 77.3 us; the launch traced here: 77.2 us
  starting transfers between devices  37.5 us (49%)
  waiting for transfers between devices  20.2 us (26%)
  Pallas kernels  17.3 us (22%)
  other arithmetic  1.49 us (2%)
    ppermute x10, starting transfers between devices, turn_rep(): lax.ppermute(value, 'rep', [(i, (i - shift) % replicas) for i in range(re...  19.5 us
    ppermute x24, starting transfers between devices, swap_exp(): return lax.ppermute(value, 'exp', [(i, i ^ bits) for i in range(owners)])  18 us
    pallas_call x2, Pallas kernels, experts_of(): pl.pallas_call(kernel, out_shape=[jax.ShapeDtypeStruct((count, model_widt...  11.5 us
    ppermute x24, waiting for transfers between devices, swap_exp(): return lax.ppermute(value, 'exp', [(i, i ^ bits) for i in range(owners)])  10.6 us
    ppermute x10, waiting for transfers between devices, turn_rep(): lax.ppermute(value, 'rep', [(i, (i - shift) % replicas) for i in range(re...  9.59 us
    pallas_call x3, Pallas kernels, fetched(): pl.pallas_call(functools.partial(fetch_kernel, turn), out_shape=jax.Shape...  4.88 us
  transfers between devices with their start and end apart: 34, of which 18 were waited for; matrix products, arithmetic and copies ran while one was open for 1% of the time, Pallas kernels for 21%

profile of v5, /device:TPU:0, one launch (start us, length us, event | category | flops | bytes accessed | tf_op | source)
XLA Modules:
  0.0 77.2 jit_solution(2657643521762798451)
XLA Ops:
  1.2 4.1 %collective-permute-start.3 = (bf16[16,4224]{1,0:T(8,128)(2,1)S(1)}, bf16[16,4224]{1,0:T(8,128)(2,1)S(1)}, u32[]{:S(2)}, u32[]{:S(2)}) collective-permute-start(bf16[16,4224]{1,0:T(8,128)(2,1)S(1)} %pack.1.refs_0_), channel_id=1, source_target_pairs={{0,16},{8,24},{16,0},{24,8},{1,17},{9,25},{17,1},{25,9},{2,18},{10... | collective-permute-start | bytes 405512 | tf_op jit(solution)/shard_map/ppermute | solution.py:287
  5.3 2.4 %collective-permute-start.2 = (bf16[16,4224]{1,0:T(8,128)(2,1)S(1)}, bf16[16,4224]{1,0:T(8,128)(2,1)S(1)}, u32[]{:S(2)}, u32[]{:S(2)}) collective-permute-start(bf16[16,4224]{1,0:T(8,128)(2,1)S(1)} %pack.1.refs_0_), channel_id=1, source_target_pairs={{0,6},{1,7},{2,4},{3,5},{4,2},{5,3},{6,0},{7,1},{8,14},{9,15},{10,... | collective-permute-start | bytes 405512 | tf_op jit(solution)/shard_map/ppermute | solution.py:282
  8.8 2.1 %fetch_turned.2.refs_5_.refs_11_ = bf16[4096,768]{1,0:T(8,128)(2,1)S(1)} custom-call(bf16[768,4096]{1,0:T(8,128)(2,1)S(1)} %bitcast.7), custom_call_target="tpu_custom_call" | custom-call | bytes 12582912 | tf_op jit(solution)/shard_map/fetch_turned/pallas_call | solution.py:103
  10.9 0.9 %collective-permute-done.3.refs_0_ = bf16[16,4224]{1,0:T(8,128)(2,1)S(1)} collective-permute-done((bf16[16,4224]{1,0:T(8,128)(2,1)S(1)}, bf16[16,4224]{1,0:T(8,128)(2,1)S(1)}, u32[]{:S(2)}, u32[]{:S(2)}) %collective-permute-start.3) | collective-permute-done | bytes 135200 | tf_op jit(solution)/shard_map/ppermute | solution.py:287
  11.8 2.4 %collective-permute-done.1.refs_2_ = bf16[16,4224]{1,0:T(8,128)(2,1)S(1)} collective-permute-done((bf16[16,4224]{1,0:T(8,128)(2,1)S(1)}, bf16[16,4224]{1,0:T(8,128)(2,1)S(1)}, u32[]{:S(2)}, u32[]{:S(2)}) %collective-permute-start.1) | collective-permute-done | bytes 135200 | tf_op jit(solution)/shard_map/ppermute | solution.py:282
  14.2 1.6 %collective-permute-start.8 = (bf16[16,4224]{1,0:T(8,128)(2,1)S(1)}, bf16[16,4224]{1,0:T(8,128)(2,1)S(1)}, u32[]{:S(2)}, u32[]{:S(2)}) collective-permute-start(bf16[16,4224]{1,0:T(8,128)(2,1)S(1)} %pack.1.refs_0_), channel_id=1, source_target_pairs={{0,8},{8,16},{16,24},{24,0},{1,9},{9,17},{17,25},{25,1},{2,10},{10... | collective-permute-start | bytes 405512 | tf_op jit(solution)/shard_map/ppermute | solution.py:287
  15.8 2.2 %collective-permute-start.7 = (bf16[16,4224]{1,0:T(8,128)(2,1)S(1)}, bf16[16,4224]{1,0:T(8,128)(2,1)S(1)}, u32[]{:S(2)}, u32[]{:S(2)}) collective-permute-start(bf16[16,4224]{1,0:T(8,128)(2,1)S(1)} %pack.1.refs_0_), channel_id=1, source_target_pairs={{0,24},{8,0},{16,8},{24,16},{1,25},{9,1},{17,9},{25,17},{2,26},{10... | collective-permute-start | bytes 405512 | tf_op jit(solution)/shard_map/ppermute | solution.py:287
  18.1 1.7 %collective-permute-start.6 = (bf16[16,4224]{1,0:T(8,128)(2,1)S(1)}, bf16[16,4224]{1,0:T(8,128)(2,1)S(1)}, u32[]{:S(2)}, u32[]{:S(2)}) collective-permute-start(bf16[16,4224]{1,0:T(8,128)(2,1)S(1)} %collective-permute-done.3.refs_0_), channel_id=1, source_target_pairs={{0,6},{1,7},{2,4},{3,5},{4,2},{5,3},{6,0},{7,1},{8,14},{9,15},{10,... | collective-permute-start | bytes 405512 | tf_op jit(solution)/shard_map/ppermute | solution.py:282
  19.7 1.3 %collective-permute-start.5 = (bf16[16,4224]{1,0:T(8,128)(2,1)S(1)}, bf16[16,4224]{1,0:T(8,128)(2,1)S(1)}, u32[]{:S(2)}, u32[]{:S(2)}) collective-permute-start(bf16[16,4224]{1,0:T(8,128)(2,1)S(1)} %collective-permute-done.3.refs_0_), channel_id=1, source_target_pairs={{0,4},{1,5},{2,6},{3,7},{4,0},{5,1},{6,2},{7,3},{8,12},{9,13},{10,... | collective-permute-start | bytes 405512 | tf_op jit(solution)/shard_map/ppermute | solution.py:282
  21.5 2.1 %fetch_turned.3.refs_6_.refs_12_ = bf16[4096,768]{1,0:T(8,128)(2,1)S(1)} custom-call(bf16[768,4096]{1,0:T(8,128)(2,1)S(1)} %bitcast.11), custom_call_target="tpu_custom_call" | custom-call | bytes 12582912 | tf_op jit(solution)/shard_map/fetch_turned/pallas_call | solution.py:103
  23.8 0.8 fetch.1.refs_7_.refs_13_
  25.2 1.4 %collective-permute-done.5.refs_2_ = bf16[16,4224]{1,0:T(8,128)(2,1)S(1)} collective-permute-done((bf16[16,4224]{1,0:T(8,128)(2,1)S(1)}, bf16[16,4224]{1,0:T(8,128)(2,1)S(1)}, u32[]{:S(2)}, u32[]{:S(2)}) %collective-permute-start.5) | collective-permute-done | bytes 135200 | tf_op jit(solution)/shard_map/ppermute | solution.py:282
  26.8 3.8 %collective-permute-start.13 = (bf16[16,4224]{1,0:T(8,128)(2,1)S(1)}, bf16[16,4224]{1,0:T(8,128)(2,1)S(1)}, u32[]{:S(2)}, u32[]{:S(2)}) collective-permute-start(bf16[16,4224]{1,0:T(8,128)(2,1)S(1)} %collective-permute-done.2.refs_3_), channel_id=1, source_target_pairs={{0,24},{8,0},{16,8},{24,16},{1,25},{9,1},{17,9},{25,17},{2,26},{10... | collective-permute-start | bytes 405512 | tf_op jit(solution)/shard_map/ppermute | solution.py:287
  30.7 1.5 %collective-permute-start.12 = (bf16[32,4224]{1,0:T(8,128)(2,1)S(1)}, bf16[32,4224]{1,0:T(8,128)(2,1)S(1)}, u32[]{:S(2)}, u32[]{:S(2)}) collective-permute-start(bf16[32,4224]{1,0:T(8,128)(2,1)S(1)} %gather.5.refs_1_), channel_id=1, source_target_pairs={{0,4},{1,5},{2,6},{3,7},{4,0},{5,1},{6,2},{7,3},{8,12},{9,13},{10,... | collective-permute-start | bytes 811016 | tf_op jit(solution)/shard_map/ppermute | solution.py:282
  32.8 5.7 %experts.2 = (bf16[32,4096]{1,0:T(8,128)(2,1)S(1)}, bf16[32,4096]{1,0:T(8,128)(2,1)S(1)}, bf16[16,4096]{1,0:T(8,128)(2,1)S(1)}, bf16[80,4096]{1,0:T(8,128)(2,1)S...) custom-call(s32[1]{0:T(128)} %begin.1.refs_0_, bf16[64,4224]{1,0:T(8,128)(2,1)S(1)} %gather.3.refs_1_, ...), custom_call_target="tpu_custom_call" | custom-call | flops 4831838208 | bytes 4194304 | tf_op jit(solution)/shard_map/experts/pallas_call | solution.py:197
  39.0 1.2 %collective-permute-done.11.refs_2_ = bf16[32,4224]{1,0:T(8,128)(2,1)S(1)} collective-permute-done((bf16[32,4224]{1,0:T(8,128)(2,1)S(1)}, bf16[32,4224]{1,0:T(8,128)(2,1)S(1)}, u32[]{:S(2)}, u32[]{:S(2)}) %collective-permute-start.11) | collective-permute-done | bytes 270368 | tf_op jit(solution)/shard_map/ppermute | solution.py:282
  41.2 1.1 %collective-permute-done.15 = bf16[80,4096]{1,0:T(8,128)(2,1)S(1)} collective-permute-done((bf16[80,4096]{1,0:T(8,128)(2,1)S(1)}, bf16[80,4096]{1,0:T(8,128)(2,1)S(1)}, u32[]{:S(2)}, u32[]{:S(2)}) %collective-permute-start.15) | collective-permute-done | bytes 655392 | tf_op jit(solution)/shard_map/ppermute | solution.py:282
  42.7 1.5 %collective-permute-start.24 = (bf16[16,4096]{1,0:T(8,128)(2,1)S(1)}, bf16[16,4096]{1,0:T(8,128)(2,1)S(1)}, u32[]{:S(2)}, u32[]{:S(2)}) collective-permute-start(bf16[16,4096]{1,0:T(8,128)(2,1)S(1)} %add_convert_fusion.7), channel_id=1, source_target_pairs={{0,6},{1,7},{2,4},{3,5},{4,2},{5,3},{6,0},{7,1},{8,14},{9,15},{10,... | collective-permute-start | bytes 393224 | tf_op jit(solution)/shard_map/ppermute | solution.py:282
  44.7 1.5 %collective-permute-start.23 = (bf16[32,4096]{1,0:T(8,128)(2,1)S(1)}, bf16[32,4096]{1,0:T(8,128)(2,1)S(1)}, u32[]{:S(2)}, u32[]{:S(2)}) collective-permute-start(bf16[32,4096]{1,0:T(8,128)(2,1)S(1)} %get-tuple-element.94), channel_id=1, source_target_pairs={{0,4},{1,5},{2,6},{3,7},{4,0},{5,1},{6,2},{7,3},{8,12},{9,13},{10,... | collective-permute-start | bytes 786440 | tf_op jit(solution)/shard_map/ppermute | solution.py:282
  46.2 5.7 %experts.3 = (bf16[16,4096]{1,0:T(8,128)(2,1)S(1)}, bf16[16,4096]{1,0:T(8,128)(2,1)S(1)}, bf16[32,4096]{1,0:T(8,128)(2,1)S(1)}, bf16[32,4096]{1,0:T(8,128)(2,1)S...) custom-call(s32[1]{0:T(128)} %begin.1.refs_0_, bf16[32,4224]{1,0:T(8,128)(2,1)S(1)} %gather.5.refs_1_, ...), custom_call_target="tpu_custom_call" | custom-call | flops 4831838208 | bytes 4194304 | tf_op jit(solution)/shard_map/experts/pallas_call | solution.py:197
  52.5 1.5 %collective-permute-done.22 = bf16[32,4096]{1,0:T(8,128)(2,1)S(1)} collective-permute-done((bf16[32,4096]{1,0:T(8,128)(2,1)S(1)}, bf16[32,4096]{1,0:T(8,128)(2,1)S(1)}, u32[]{:S(2)}, u32[]{:S(2)}) %collective-permute-start.22) | collective-permute-done | bytes 262176 | tf_op jit(solution)/shard_map/ppermute | solution.py:282
  54.1 0.9 %collective-permute-done.23 = bf16[32,4096]{1,0:T(8,128)(2,1)S(1)} collective-permute-done((bf16[32,4096]{1,0:T(8,128)(2,1)S(1)}, bf16[32,4096]{1,0:T(8,128)(2,1)S(1)}, u32[]{:S(2)}, u32[]{:S(2)}) %collective-permute-start.23) | collective-permute-done | bytes 262176 | tf_op jit(solution)/shard_map/ppermute | solution.py:282
  55.4 3.8 %collective-permute-start.28 = (bf16[16,4096]{1,0:T(8,128)(2,1)S(1)}, bf16[16,4096]{1,0:T(8,128)(2,1)S(1)}, u32[]{:S(2)}, u32[]{:S(2)}) collective-permute-start(bf16[16,4096]{1,0:T(8,128)(2,1)S(1)} %get-tuple-element.121), channel_id=1, source_target_pairs={{0,24},{8,0},{16,8},{24,16},{1,25},{9,1},{17,9},{25,17},{2,26},{10... | collective-permute-start | bytes 393224 | tf_op jit(solution)/shard_map/ppermute | solution.py:287
  59.8 1.4 %collective-permute-start.31 = (bf16[32,4096]{1,0:T(8,128)(2,1)S(1)}, bf16[32,4096]{1,0:T(8,128)(2,1)S(1)}, u32[]{:S(2)}, u32[]{:S(2)}) collective-permute-start(bf16[32,4096]{1,0:T(8,128)(2,1)S(1)} %get-tuple-element.124), channel_id=1, source_target_pairs={{0,4},{1,5},{2,6},{3,7},{4,0},{5,1},{6,2},{7,3},{8,12},{9,13},{10,... | collective-permute-start | bytes 786440 | tf_op jit(solution)/shard_map/ppermute | solution.py:282
  61.2 2.4 %collective-permute-done.27 = bf16[16,4096]{1,0:T(8,128)(2,1)S(1)} collective-permute-done((bf16[16,4096]{1,0:T(8,128)(2,1)S(1)}, bf16[16,4096]{1,0:T(8,128)(2,1)S(1)}, u32[]{:S(2)}, u32[]{:S(2)}) %collective-permute-start.27) | collective-permute-done | bytes 131104 | tf_op jit(solution)/shard_map/ppermute | solution.py:287
  63.6 2.6 %collective-permute-done.28 = bf16[16,4096]{1,0:T(8,128)(2,1)S(1)} collective-permute-done((bf16[16,4096]{1,0:T(8,128)(2,1)S(1)}, bf16[16,4096]{1,0:T(8,128)(2,1)S(1)}, u32[]{:S(2)}, u32[]{:S(2)}) %collective-permute-start.28) | collective-permute-done | bytes 131104 | tf_op jit(solution)/shard_map/ppermute | solution.py:287
  66.2 1.5 %collective-permute-start.29 = (bf16[16,4096]{1,0:T(8,128)(2,1)S(1)}, bf16[16,4096]{1,0:T(8,128)(2,1)S(1)}, u32[]{:S(2)}, u32[]{:S(2)}) collective-permute-start(bf16[16,4096]{1,0:T(8,128)(2,1)S(1)} %fusion), channel_id=1, source_target_pairs={{0,6},{1,7},{2,4},{3,5},{4,2},{5,3},{6,0},{7,1},{8,14},{9,15},{10,... | collective-permute-start | bytes 393224 | tf_op jit(solution)/shard_map/ppermute | solution.py:282
  68.8 0.6 collective-permute-start.32
  69.4 3.3 %collective-permute-start.33 = (bf16[16,4096]{1,0:T(8,128)(2,1)S(1)}, bf16[16,4096]{1,0:T(8,128)(2,1)S(1)}, u32[]{:S(2)}, u32[]{:S(2)}) collective-permute-start(bf16[16,4096]{1,0:T(8,128)(2,1)S(1)} %get-tuple-element.132), channel_id=1, source_target_pairs={{0,24},{8,0},{16,8},{24,16},{1,25},{9,1},{17,9},{25,17},{2,26},{10... | collective-permute-start | bytes 393224 | tf_op jit(solution)/shard_map/ppermute | solution.py:287
  72.7 3.1 %collective-permute-done.32 = bf16[16,4096]{1,0:T(8,128)(2,1)S(1)} collective-permute-done((bf16[16,4096]{1,0:T(8,128)(2,1)S(1)}, bf16[16,4096]{1,0:T(8,128)(2,1)S(1)}, u32[]{:S(2)}, u32[]{:S(2)}) %collective-permute-start.32) | collective-permute-done | bytes 131104 | tf_op jit(solution)/shard_map/ppermute | solution.py:287
  75.7 0.6 collective-permute-done.33
  76.4 0.8 %fusion.8 = bf16[16,4096]{1,0:T(8,128)(2,1)} fusion(f32[48,4096]{1,0:T(8,128)S(1)} %convert_add_fusion, bf16[16,4096]{1,0:T(8,128)(2,1)S(1)} %collective-permute-done.33, bf16[16,4096]{1,0:T(8,128)(2,1)S(1)} %collective-permute-done.32, bf16[16,4096]{1,0:T(8,128)(2,1)S(1)} %collective-permute-done.29, bf16[16,4096]{1,0:T(8,128)(2,1)S(1)} %collective-permute-done.26, ...), kind=kLoop, calls=%fused_computation.17 | loop fusion | flops 851968 | bytes 1179648 | tf_op jit(solution)/shard_map/convert_element_type | solution.py:298
  (74 shorter events, 9.5 us)
Async XLA Ops:
  1.2 10.6 %collective-permute-start.3 = (bf16[16,4224]{1,0:T(8,128)(2,1)S(1)}, bf16[16,4224]{1,0:T(8,128)(2,1)S(1)}, u32[]{:S(2)}, u32[]{:S(2)}) collective-permute-start(bf16[16,4224]{1,0:T(8,128)(2,1)S(1)} %pack.1.refs_0_), channel_id=1, source_target_pairs={{0,16},{8,24},{16,0},{24,8},{1,17},{9,25},{17,1},{25,9},{2,18},{10... | collective-permute-start | bytes 405512 | tf_op jit(solution)/shard_map/ppermute | solution.py:287
  5.3 6.5 %collective-permute-start.2 = (bf16[16,4224]{1,0:T(8,128)(2,1)S(1)}, bf16[16,4224]{1,0:T(8,128)(2,1)S(1)}, u32[]{:S(2)}, u32[]{:S(2)}) collective-permute-start(bf16[16,4224]{1,0:T(8,128)(2,1)S(1)} %pack.1.refs_0_), channel_id=1, source_target_pairs={{0,6},{1,7},{2,4},{3,5},{4,2},{5,3},{6,0},{7,1},{8,14},{9,15},{10,... | collective-permute-start | bytes 405512 | tf_op jit(solution)/shard_map/ppermute | solution.py:282
  7.8 6.4 %collective-permute-start.1 = (bf16[16,4224]{1,0:T(8,128)(2,1)S(1)}, bf16[16,4224]{1,0:T(8,128)(2,1)S(1)}, u32[]{:S(2)}, u32[]{:S(2)}) collective-permute-start(bf16[16,4224]{1,0:T(8,128)(2,1)S(1)} %pack.1.refs_0_), channel_id=1, source_target_pairs={{0,4},{1,5},{2,6},{3,7},{4,0},{5,1},{6,2},{7,3},{8,12},{9,13},{10,... | collective-permute-start | bytes 405512 | tf_op jit(solution)/shard_map/ppermute | solution.py:282
  8.3 5.9 %collective-permute-start = (bf16[16,4224]{1,0:T(8,128)(2,1)S(1)}, bf16[16,4224]{1,0:T(8,128)(2,1)S(1)}, u32[]{:S(2)}, u32[]{:S(2)}) collective-permute-start(bf16[16,4224]{1,0:T(8,128)(2,1)S(1)} %pack.1.refs_0_), channel_id=1, source_target_pairs={{0,2},{1,3},{2,0},{3,1},{4,6},{5,7},{6,4},{7,5},{8,10},{9,11},{10,... | collective-permute-start | bytes 405512 | tf_op jit(solution)/shard_map/ppermute | solution.py:282
  14.2 9.4 %collective-permute-start.8 = (bf16[16,4224]{1,0:T(8,128)(2,1)S(1)}, bf16[16,4224]{1,0:T(8,128)(2,1)S(1)}, u32[]{:S(2)}, u32[]{:S(2)}) collective-permute-start(bf16[16,4224]{1,0:T(8,128)(2,1)S(1)} %pack.1.refs_0_), channel_id=1, source_target_pairs={{0,8},{8,16},{16,24},{24,0},{1,9},{9,17},{17,25},{25,1},{2,10},{10... | collective-permute-start | bytes 405512 | tf_op jit(solution)/shard_map/ppermute | solution.py:287
  15.8 8.0 %collective-permute-start.7 = (bf16[16,4224]{1,0:T(8,128)(2,1)S(1)}, bf16[16,4224]{1,0:T(8,128)(2,1)S(1)}, u32[]{:S(2)}, u32[]{:S(2)}) collective-permute-start(bf16[16,4224]{1,0:T(8,128)(2,1)S(1)} %pack.1.refs_0_), channel_id=1, source_target_pairs={{0,24},{8,0},{16,8},{24,16},{1,25},{9,1},{17,9},{25,17},{2,26},{10... | collective-permute-start | bytes 405512 | tf_op jit(solution)/shard_map/ppermute | solution.py:287
  18.1 7.1 %collective-permute-start.6 = (bf16[16,4224]{1,0:T(8,128)(2,1)S(1)}, bf16[16,4224]{1,0:T(8,128)(2,1)S(1)}, u32[]{:S(2)}, u32[]{:S(2)}) collective-permute-start(bf16[16,4224]{1,0:T(8,128)(2,1)S(1)} %collective-permute-done.3.refs_0_), channel_id=1, source_target_pairs={{0,6},{1,7},{2,4},{3,5},{4,2},{5,3},{6,0},{7,1},{8,14},{9,15},{10,... | collective-permute-start | bytes 405512 | tf_op jit(solution)/shard_map/ppermute | solution.py:282
  19.7 6.8 %collective-permute-start.5 = (bf16[16,4224]{1,0:T(8,128)(2,1)S(1)}, bf16[16,4224]{1,0:T(8,128)(2,1)S(1)}, u32[]{:S(2)}, u32[]{:S(2)}) collective-permute-start(bf16[16,4224]{1,0:T(8,128)(2,1)S(1)} %collective-permute-done.3.refs_0_), channel_id=1, source_target_pairs={{0,4},{1,5},{2,6},{3,7},{4,0},{5,1},{6,2},{7,3},{8,12},{9,13},{10,... | collective-permute-start | bytes 405512 | tf_op jit(solution)/shard_map/ppermute | solution.py:282
  21.1 5.6 %collective-permute-start.4 = (bf16[16,4224]{1,0:T(8,128)(2,1)S(1)}, bf16[16,4224]{1,0:T(8,128)(2,1)S(1)}, u32[]{:S(2)}, u32[]{:S(2)}) collective-permute-start(bf16[16,4224]{1,0:T(8,128)(2,1)S(1)} %collective-permute-done.3.refs_0_), channel_id=1, source_target_pairs={{0,2},{1,3},{2,0},{3,1},{4,6},{5,7},{6,4},{7,5},{8,10},{9,11},{10,... | collective-permute-start | bytes 405512 | tf_op jit(solution)/shard_map/ppermute | solution.py:282
  23.7 8.5 %collective-permute-start.9 = (bf16[64,4224]{1,0:T(8,128)(2,1)S(1)}, bf16[64,4224]{1,0:T(8,128)(2,1)S(1)}, u32[]{:S(2)}, u32[]{:S(2)}) collective-permute-start(bf16[64,4224]{1,0:T(8,128)(2,1)S(1)} %gather.3.refs_1_), channel_id=1, source_target_pairs={{0,1},{1,0},{2,3},{3,2},{4,5},{5,4},{6,7},{7,6},{8,9},{9,8},{10,11... | collective-permute-start | bytes 1622024 | tf_op jit(solution)/shard_map/ppermute | solution.py:282
  26.7 6.1 %collective-permute-start.10 = (bf16[64,4224]{1,0:T(8,128)(2,1)S(1)}, bf16[64,4224]{1,0:T(8,128)(2,1)S(1)}, u32[]{:S(2)}, u32[]{:S(2)}) collective-permute-start(bf16[64,4224]{1,0:T(8,128)(2,1)S(1)} %gather.4.refs_2_), channel_id=1, source_target_pairs={{0,1},{1,0},{2,3},{3,2},{4,5},{5,4},{6,7},{7,6},{8,9},{9,8},{10,11... | collective-permute-start | bytes 1622024 | tf_op jit(solution)/shard_map/ppermute | solution.py:282
  26.8 11.8 %collective-permute-start.14 = (bf16[16,4224]{1,0:T(8,128)(2,1)S(1)}, bf16[16,4224]{1,0:T(8,128)(2,1)S(1)}, u32[]{:S(2)}, u32[]{:S(2)}) collective-permute-start(bf16[16,4224]{1,0:T(8,128)(2,1)S(1)} %collective-permute-done.2.refs_3_), channel_id=1, source_target_pairs={{0,8},{8,16},{16,24},{24,0},{1,9},{9,17},{17,25},{25,1},{2,10},{10... | collective-permute-start | bytes 405512 | tf_op jit(solution)/shard_map/ppermute | solution.py:287
  26.8 11.7 %collective-permute-start.13 = (bf16[16,4224]{1,0:T(8,128)(2,1)S(1)}, bf16[16,4224]{1,0:T(8,128)(2,1)S(1)}, u32[]{:S(2)}, u32[]{:S(2)}) collective-permute-start(bf16[16,4224]{1,0:T(8,128)(2,1)S(1)} %collective-permute-done.2.refs_3_), channel_id=1, source_target_pairs={{0,24},{8,0},{16,8},{24,16},{1,25},{9,1},{17,9},{25,17},{2,26},{10... | collective-permute-start | bytes 405512 | tf_op jit(solution)/shard_map/ppermute | solution.py:287
  30.7 8.3 %collective-permute-start.12 = (bf16[32,4224]{1,0:T(8,128)(2,1)S(1)}, bf16[32,4224]{1,0:T(8,128)(2,1)S(1)}, u32[]{:S(2)}, u32[]{:S(2)}) collective-permute-start(bf16[32,4224]{1,0:T(8,128)(2,1)S(1)} %gather.5.refs_1_), channel_id=1, source_target_pairs={{0,4},{1,5},{2,6},{3,7},{4,0},{5,1},{6,2},{7,3},{8,12},{9,13},{10,... | collective-permute-start | bytes 811016 | tf_op jit(solution)/shard_map/ppermute | solution.py:282
  32.2 8.0 %collective-permute-start.11 = (bf16[32,4224]{1,0:T(8,128)(2,1)S(1)}, bf16[32,4224]{1,0:T(8,128)(2,1)S(1)}, u32[]{:S(2)}, u32[]{:S(2)}) collective-permute-start(bf16[32,4224]{1,0:T(8,128)(2,1)S(1)} %gather.5.refs_1_), channel_id=1, source_target_pairs={{0,2},{1,3},{2,0},{3,1},{4,6},{5,7},{6,4},{7,5},{8,10},{9,11},{10,... | collective-permute-start | bytes 811016 | tf_op jit(solution)/shard_map/ppermute | solution.py:282
  40.7 3.4 %collective-permute-start.20 = (bf16[16,4224]{1,0:T(8,128)(2,1)S(1)}, bf16[16,4224]{1,0:T(8,128)(2,1)S(1)}, u32[]{:S(2)}, u32[]{:S(2)}) collective-permute-start(bf16[16,4224]{1,0:T(8,128)(2,1)S(1)} %collective-permute-done.13.refs_4_), channel_id=1, source_target_pairs={{0,1},{1,0},{2,3},{3,2},{4,5},{5,4},{6,7},{7,6},{8,9},{9,8},{10,11... | collective-permute-start | bytes 405512 | tf_op jit(solution)/shard_map/ppermute | solution.py:282
  40.7 4.0 %collective-permute-start.21 = (bf16[16,4224]{1,0:T(8,128)(2,1)S(1)}, bf16[16,4224]{1,0:T(8,128)(2,1)S(1)}, u32[]{:S(2)}, u32[]{:S(2)}) collective-permute-start(bf16[16,4224]{1,0:T(8,128)(2,1)S(1)} %collective-permute-done.14.refs_5_), channel_id=1, source_target_pairs={{0,1},{1,0},{2,3},{3,2},{4,5},{5,4},{6,7},{7,6},{8,9},{9,8},{10,11... | collective-permute-start | bytes 405512 | tf_op jit(solution)/shard_map/ppermute | solution.py:282
  41.2 5.0 %collective-permute-start.18 = (bf16[32,4224]{1,0:T(8,128)(2,1)S(1)}, bf16[32,4224]{1,0:T(8,128)(2,1)S(1)}, u32[]{:S(2)}, u32[]{:S(2)}) collective-permute-start(bf16[32,4224]{1,0:T(8,128)(2,1)S(1)} %collective-permute-done.11.refs_2_), channel_id=1, source_target_pairs={{0,1},{1,0},{2,3},{3,2},{4,5},{5,4},{6,7},{7,6},{8,9},{9,8},{10,11... | collective-permute-start | bytes 811016 | tf_op jit(solution)/shard_map/ppermute | solution.py:282
  42.3 3.9 %collective-permute-start.19 = (bf16[32,4224]{1,0:T(8,128)(2,1)S(1)}, bf16[32,4224]{1,0:T(8,128)(2,1)S(1)}, u32[]{:S(2)}, u32[]{:S(2)}) collective-permute-start(bf16[32,4224]{1,0:T(8,128)(2,1)S(1)} %collective-permute-done.12.refs_3_), channel_id=1, source_target_pairs={{0,1},{1,0},{2,3},{3,2},{4,5},{5,4},{6,7},{7,6},{8,9},{9,8},{10,11... | collective-permute-start | bytes 811016 | tf_op jit(solution)/shard_map/ppermute | solution.py:282
  42.7 9.9 %collective-permute-start.24 = (bf16[16,4096]{1,0:T(8,128)(2,1)S(1)}, bf16[16,4096]{1,0:T(8,128)(2,1)S(1)}, u32[]{:S(2)}, u32[]{:S(2)}) collective-permute-start(bf16[16,4096]{1,0:T(8,128)(2,1)S(1)} %add_convert_fusion.7), channel_id=1, source_target_pairs={{0,6},{1,7},{2,4},{3,5},{4,2},{5,3},{6,0},{7,1},{8,14},{9,15},{10,... | collective-permute-start | bytes 393224 | tf_op jit(solution)/shard_map/ppermute | solution.py:282
  44.1 9.9 %collective-permute-start.22 = (bf16[32,4096]{1,0:T(8,128)(2,1)S(1)}, bf16[32,4096]{1,0:T(8,128)(2,1)S(1)}, u32[]{:S(2)}, u32[]{:S(2)}) collective-permute-start(bf16[32,4096]{1,0:T(8,128)(2,1)S(1)} %get-tuple-element.93), channel_id=1, source_target_pairs={{0,2},{1,3},{2,0},{3,1},{4,6},{5,7},{6,4},{7,5},{8,10},{9,11},{10,... | collective-permute-start | bytes 786440 | tf_op jit(solution)/shard_map/ppermute | solution.py:282
  44.7 10.2 %collective-permute-start.23 = (bf16[32,4096]{1,0:T(8,128)(2,1)S(1)}, bf16[32,4096]{1,0:T(8,128)(2,1)S(1)}, u32[]{:S(2)}, u32[]{:S(2)}) collective-permute-start(bf16[32,4096]{1,0:T(8,128)(2,1)S(1)} %get-tuple-element.94), channel_id=1, source_target_pairs={{0,4},{1,5},{2,6},{3,7},{4,0},{5,1},{6,2},{7,3},{8,12},{9,13},{10,... | collective-permute-start | bytes 786440 | tf_op jit(solution)/shard_map/ppermute | solution.py:282
  46.2 8.8 %collective-permute-start.16 = (bf16[48,4096]{1,0:T(8,128)(2,1)S(1)}, bf16[48,4096]{1,0:T(8,128)(2,1)S(1)}, u32[]{:S(2)}, u32[]{:S(2)}) collective-permute-start(bf16[48,4096]{1,0:T(8,128)(2,1)S(1)} %get-tuple-element.92), channel_id=1, source_target_pairs={{0,1},{1,0},{2,3},{3,2},{4,5},{5,4},{6,7},{7,6},{8,9},{9,8},{10,11... | collective-permute-start | bytes 1179656 | tf_op jit(solution)/shard_map/ppermute | solution.py:282
  51.9 3.2 %collective-permute-start.25 = (bf16[128,4096]{1,0:T(8,128)(2,1)S(1)}, bf16[128,4096]{1,0:T(8,128)(2,1)S(1)}, u32[]{:S(2)}, u32[]{:S(2)}) collective-permute-start(bf16[128,4096]{1,0:T(8,128)(2,1)S(1)} %get-tuple-element.115), channel_id=1, source_target_pairs={{0,1},{1,0},{2,3},{3,2},{4,5},{5,4},{6,7},{7,6},{8,9},{9,8},{10,11... | collective-permute-start | bytes 3145736 | tf_op jit(solution)/shard_map/ppermute | solution.py:282
  55.3 8.3 %collective-permute-start.27 = (bf16[16,4096]{1,0:T(8,128)(2,1)S(1)}, bf16[16,4096]{1,0:T(8,128)(2,1)S(1)}, u32[]{:S(2)}, u32[]{:S(2)}) collective-permute-start(bf16[16,4096]{1,0:T(8,128)(2,1)S(1)} %get-tuple-element.120), channel_id=1, source_target_pairs={{0,8},{8,16},{16,24},{24,0},{1,9},{9,17},{17,25},{25,1},{2,10},{10... | collective-permute-start | bytes 393224 | tf_op jit(solution)/shard_map/ppermute | solution.py:287
  55.4 10.8 %collective-permute-start.28 = (bf16[16,4096]{1,0:T(8,128)(2,1)S(1)}, bf16[16,4096]{1,0:T(8,128)(2,1)S(1)}, u32[]{:S(2)}, u32[]{:S(2)}) collective-permute-start(bf16[16,4096]{1,0:T(8,128)(2,1)S(1)} %get-tuple-element.121), channel_id=1, source_target_pairs={{0,24},{8,0},{16,8},{24,16},{1,25},{9,1},{17,9},{25,17},{2,26},{10... | collective-permute-start | bytes 393224 | tf_op jit(solution)/shard_map/ppermute | solution.py:287
  59.2 13.4 %collective-permute-start.26 = (bf16[16,4096]{1,0:T(8,128)(2,1)S(1)}, bf16[16,4096]{1,0:T(8,128)(2,1)S(1)}, u32[]{:S(2)}, u32[]{:S(2)}) collective-permute-start(bf16[16,4096]{1,0:T(8,128)(2,1)S(1)} %fusion.3), channel_id=1, source_target_pairs={{0,16},{8,24},{16,0},{24,8},{1,17},{9,25},{17,1},{25,9},{2,18},{10... | collective-permute-start | bytes 393224 | tf_op jit(solution)/shard_map/ppermute | solution.py:287
  59.2 9.1 %collective-permute-start.30 = (bf16[32,4096]{1,0:T(8,128)(2,1)S(1)}, bf16[32,4096]{1,0:T(8,128)(2,1)S(1)}, u32[]{:S(2)}, u32[]{:S(2)}) collective-permute-start(bf16[32,4096]{1,0:T(8,128)(2,1)S(1)} %get-tuple-element.123), channel_id=1, source_target_pairs={{0,2},{1,3},{2,0},{3,1},{4,6},{5,7},{6,4},{7,5},{8,10},{9,11},{10,... | collective-permute-start | bytes 786440 | tf_op jit(solution)/shard_map/ppermute | solution.py:282
  59.8 8.8 %collective-permute-start.31 = (bf16[32,4096]{1,0:T(8,128)(2,1)S(1)}, bf16[32,4096]{1,0:T(8,128)(2,1)S(1)}, u32[]{:S(2)}, u32[]{:S(2)}) collective-permute-start(bf16[32,4096]{1,0:T(8,128)(2,1)S(1)} %get-tuple-element.124), channel_id=1, source_target_pairs={{0,4},{1,5},{2,6},{3,7},{4,0},{5,1},{6,2},{7,3},{8,12},{9,13},{10,... | collective-permute-start | bytes 786440 | tf_op jit(solution)/shard_map/ppermute | solution.py:282
  66.2 6.4 %collective-permute-start.29 = (bf16[16,4096]{1,0:T(8,128)(2,1)S(1)}, bf16[16,4096]{1,0:T(8,128)(2,1)S(1)}, u32[]{:S(2)}, u32[]{:S(2)}) collective-permute-start(bf16[16,4096]{1,0:T(8,128)(2,1)S(1)} %fusion), channel_id=1, source_target_pairs={{0,6},{1,7},{2,4},{3,5},{4,2},{5,3},{6,0},{7,1},{8,14},{9,15},{10,... | collective-permute-start | bytes 393224 | tf_op jit(solution)/shard_map/ppermute | solution.py:282
  68.8 7.0 %collective-permute-start.32 = (bf16[16,4096]{1,0:T(8,128)(2,1)S(1)}, bf16[16,4096]{1,0:T(8,128)(2,1)S(1)}, u32[]{:S(2)}, u32[]{:S(2)}) collective-permute-start(bf16[16,4096]{1,0:T(8,128)(2,1)S(1)} %get-tuple-element.131), channel_id=1, source_target_pairs={{0,8},{8,16},{16,24},{24,0},{1,9},{9,17},{17,25},{25,1},{2,10},{10... | collective-permute-start | bytes 393224 | tf_op jit(solution)/shard_map/ppermute | solution.py:287
  69.4 7.0 %collective-permute-start.33 = (bf16[16,4096]{1,0:T(8,128)(2,1)S(1)}, bf16[16,4096]{1,0:T(8,128)(2,1)S(1)}, u32[]{:S(2)}, u32[]{:S(2)}) collective-permute-start(bf16[16,4096]{1,0:T(8,128)(2,1)S(1)} %get-tuple-element.132), channel_id=1, source_target_pairs={{0,24},{8,0},{16,8},{24,16},{1,25},{9,1},{17,9},{25,17},{2,26},{10... | collective-permute-start | bytes 393224 | tf_op jit(solution)/shard_map/ppermute | solution.py:287
  (10 other events, 84.9 us)

commit v6 on v5

--- a/solution.py
+++ b/solution.py
@@ -321,22 +321,20 @@
 
     two = turn_rep(packed, 2)
     x_own, y_own, far_own = [swap_exp(packed, bits) for bits in (2, 4, 6)]
-    gates = fetched(gate_weight, True)
-    x_own, y_own, far_own, two, gates, up_weight, again = ordered(
-        x_own, y_own, far_own, two, gates, up_weight, packed
+    gates, ups = fetched(gate_weight, True), fetched(up_weight, True)
+    x_own, y_own, far_own, two, gates, ups, again = ordered(
+        x_own, y_own, far_own, two, gates, ups, packed
     )
     one, three = turn_rep(again, 1), turn_rep(again, 3)
     x_two, y_two, far_two = [swap_exp(two, bits) for bits in (2, 4, 6)]
     far_one, far_three = turn_rep(far_own, 1), turn_rep(far_own, 3)
     first = gathered(packed, x_own, y_own, far_own)
     first_other = swap_exp(first, 1)
-    ups = fetched(up_weight, True)
-    one, three, ups, down_weight = ordered(one, three, ups, down_weight)
+    second = gathered(two, x_two, y_two, far_two)
+    downs = fetched(down_weight, False)
+    second, downs, one, three = ordered(second, downs, one, three)
     pair = gathered(one, three)
     x_pair, y_pair = swap_exp(pair, 2), swap_exp(pair, 4)
-    second = gathered(two, x_two, y_two, far_two)
-    downs = fetched(down_weight, False)
-    second, downs = ordered(second, downs)
 
     near = [first, second, first_other, swap_exp(second, 1)]
     groups = row_groups([[5, 1], [6, 2], [7], [13, 9, 14, 10, 15], [4, 0, 3], [12, 8, 11]], rows)

time: 77.3 us -> 76.8 us (level)
    ppermute x24, waiting for transfers between devices: 10.6 us -> 8.57 us  [swap_exp(): return lax.ppermute(value, 'exp', [(i, i ^ bits) for i in range(owners)])]
    ppermute x10, waiting for transfers between devices: 9.59 us -> 11.5 us  [turn_rep(): lax.ppermute(value, 'rep', [(i, (i - shift) % replicas) for i in range(re...]
where the time goes in v6:
time: 76.8 us; the launch traced here: 76.6 us
  starting transfers between devices  37.1 us (48%)
  waiting for transfers between devices  20.1 us (26%)
  Pallas kernels  17.3 us (23%)
  other arithmetic  1.49 us (2%)
    ppermute x10, starting transfers between devices, turn_rep(): lax.ppermute(value, 'rep', [(i, (i - shift) % replicas) for i in range(re...  19.5 us
    ppermute x24, starting transfers between devices, swap_exp(): return lax.ppermute(value, 'exp', [(i, i ^ bits) for i in range(owners)])  17.6 us
    pallas_call x2, Pallas kernels, experts_of(): pl.pallas_call(kernel, out_shape=[jax.ShapeDtypeStruct((count, model_widt...  11.5 us
    ppermute x10, waiting for transfers between devices, turn_rep(): lax.ppermute(value, 'rep', [(i, (i - shift) % replicas) for i in range(re...  11.5 us
    ppermute x24, waiting for transfers between devices, swap_exp(): return lax.ppermute(value, 'exp', [(i, i ^ bits) for i in range(owners)])  8.57 us
    pallas_call x3, Pallas kernels, fetched(): pl.pallas_call(functools.partial(fetch_kernel, turn), out_shape=jax.Shape...  4.88 us
  transfers between devices with their start and end apart: 34, of which 18 were waited for; matrix products, arithmetic and copies ran while one was open for 1% of the time, Pallas kernels for 21%

profile of v6, /device:TPU:0, one launch (start us, length us, event | category | flops | bytes accessed | tf_op | source)
XLA Modules:
  0.0 76.6 jit_solution(378490733864496073)
XLA Ops:
  1.2 4.1 %collective-permute-start.3 = (bf16[16,4224]{1,0:T(8,128)(2,1)S(1)}, bf16[16,4224]{1,0:T(8,128)(2,1)S(1)}, u32[]{:S(2)}, u32[]{:S(2)}) collective-permute-start(bf16[16,4224]{1,0:T(8,128)(2,1)S(1)} %pack.1.refs_0_), channel_id=1, source_target_pairs={{0,16},{8,24},{16,0},{24,8},{1,17},{9,25},{17,1},{25,9},{2,18},{10... | collective-permute-start | bytes 405512 | tf_op jit(solution)/shard_map/ppermute | solution.py:287
  5.3 2.4 %collective-permute-start.2 = (bf16[16,4224]{1,0:T(8,128)(2,1)S(1)}, bf16[16,4224]{1,0:T(8,128)(2,1)S(1)}, u32[]{:S(2)}, u32[]{:S(2)}) collective-permute-start(bf16[16,4224]{1,0:T(8,128)(2,1)S(1)} %pack.1.refs_0_), channel_id=1, source_target_pairs={{0,6},{1,7},{2,4},{3,5},{4,2},{5,3},{6,0},{7,1},{8,14},{9,15},{10,... | collective-permute-start | bytes 405512 | tf_op jit(solution)/shard_map/ppermute | solution.py:282
  8.8 2.1 %fetch_turned.2.refs_5_.refs_11_ = bf16[4096,768]{1,0:T(8,128)(2,1)S(1)} custom-call(bf16[768,4096]{1,0:T(8,128)(2,1)S(1)} %bitcast.7), custom_call_target="tpu_custom_call" | custom-call | bytes 12582912 | tf_op jit(solution)/shard_map/fetch_turned/pallas_call | solution.py:103
  10.9 2.1 %fetch_turned.3.refs_6_.refs_12_ = bf16[4096,768]{1,0:T(8,128)(2,1)S(1)} custom-call(bf16[768,4096]{1,0:T(8,128)(2,1)S(1)} %bitcast.11), custom_call_target="tpu_custom_call" | custom-call | bytes 12582912 | tf_op jit(solution)/shard_map/fetch_turned/pallas_call | solution.py:103
  13.0 1.1 %collective-permute-done.1.refs_2_ = bf16[16,4224]{1,0:T(8,128)(2,1)S(1)} collective-permute-done((bf16[16,4224]{1,0:T(8,128)(2,1)S(1)}, bf16[16,4224]{1,0:T(8,128)(2,1)S(1)}, u32[]{:S(2)}, u32[]{:S(2)}) %collective-permute-start.1) | collective-permute-done | bytes 135200 | tf_op jit(solution)/shard_map/ppermute | solution.py:282
  14.2 1.7 %collective-permute-start.6 = (bf16[16,4224]{1,0:T(8,128)(2,1)S(1)}, bf16[16,4224]{1,0:T(8,128)(2,1)S(1)}, u32[]{:S(2)}, u32[]{:S(2)}) collective-permute-start(bf16[16,4224]{1,0:T(8,128)(2,1)S(1)} %collective-permute-done.3.refs_0_), channel_id=1, source_target_pairs={{0,6},{1,7},{2,4},{3,5},{4,2},{5,3},{6,0},{7,1},{8,14},{9,15},{10,... | collective-permute-start | bytes 405512 | tf_op jit(solution)/shard_map/ppermute | solution.py:282
  15.9 1.3 %collective-permute-start.5 = (bf16[16,4224]{1,0:T(8,128)(2,1)S(1)}, bf16[16,4224]{1,0:T(8,128)(2,1)S(1)}, u32[]{:S(2)}, u32[]{:S(2)}) collective-permute-start(bf16[16,4224]{1,0:T(8,128)(2,1)S(1)} %collective-permute-done.3.refs_0_), channel_id=1, source_target_pairs={{0,4},{1,5},{2,6},{3,7},{4,0},{5,1},{6,2},{7,3},{8,12},{9,13},{10,... | collective-permute-start | bytes 405512 | tf_op jit(solution)/shard_map/ppermute | solution.py:282
  17.7 1.6 %collective-permute-start.8 = (bf16[16,4224]{1,0:T(8,128)(2,1)S(1)}, bf16[16,4224]{1,0:T(8,128)(2,1)S(1)}, u32[]{:S(2)}, u32[]{:S(2)}) collective-permute-start(bf16[16,4224]{1,0:T(8,128)(2,1)S(1)} %pack.1.refs_0_), channel_id=1, source_target_pairs={{0,8},{8,16},{16,24},{24,0},{1,9},{9,17},{17,25},{25,1},{2,10},{10... | collective-permute-start | bytes 405512 | tf_op jit(solution)/shard_map/ppermute | solution.py:287
  19.3 2.2 %collective-permute-start.7 = (bf16[16,4224]{1,0:T(8,128)(2,1)S(1)}, bf16[16,4224]{1,0:T(8,128)(2,1)S(1)}, u32[]{:S(2)}, u32[]{:S(2)}) collective-permute-start(bf16[16,4224]{1,0:T(8,128)(2,1)S(1)} %pack.1.refs_0_), channel_id=1, source_target_pairs={{0,24},{8,0},{16,8},{24,16},{1,25},{9,1},{17,9},{25,17},{2,26},{10... | collective-permute-start | bytes 405512 | tf_op jit(solution)/shard_map/ppermute | solution.py:287
  21.5 0.8 fetch.1.refs_7_.refs_13_
  22.4 0.9 %collective-permute-done.5.refs_2_ = bf16[16,4224]{1,0:T(8,128)(2,1)S(1)} collective-permute-done((bf16[16,4224]{1,0:T(8,128)(2,1)S(1)}, bf16[16,4224]{1,0:T(8,128)(2,1)S(1)}, u32[]{:S(2)}, u32[]{:S(2)}) %collective-permute-start.5) | collective-permute-done | bytes 135200 | tf_op jit(solution)/shard_map/ppermute | solution.py:282
  23.4 2.2 %collective-permute-done.8.refs_1_ = bf16[16,4224]{1,0:T(8,128)(2,1)S(1)} collective-permute-done((bf16[16,4224]{1,0:T(8,128)(2,1)S(1)}, bf16[16,4224]{1,0:T(8,128)(2,1)S(1)}, u32[]{:S(2)}, u32[]{:S(2)}) %collective-permute-start.8) | collective-permute-done | bytes 135200 | tf_op jit(solution)/shard_map/ppermute | solution.py:287
  26.7 3.5 %collective-permute-start.13 = (bf16[16,4224]{1,0:T(8,128)(2,1)S(1)}, bf16[16,4224]{1,0:T(8,128)(2,1)S(1)}, u32[]{:S(2)}, u32[]{:S(2)}) collective-permute-start(bf16[16,4224]{1,0:T(8,128)(2,1)S(1)} %collective-permute-done.2.refs_3_), channel_id=1, source_target_pairs={{0,24},{8,0},{16,8},{24,16},{1,25},{9,1},{17,9},{25,17},{2,26},{10... | collective-permute-start | bytes 405512 | tf_op jit(solution)/shard_map/ppermute | solution.py:287
  30.2 1.6 %collective-permute-start.12 = (bf16[32,4224]{1,0:T(8,128)(2,1)S(1)}, bf16[32,4224]{1,0:T(8,128)(2,1)S(1)}, u32[]{:S(2)}, u32[]{:S(2)}) collective-permute-start(bf16[32,4224]{1,0:T(8,128)(2,1)S(1)} %gather.5.refs_1_), channel_id=1, source_target_pairs={{0,4},{1,5},{2,6},{3,7},{4,0},{5,1},{6,2},{7,3},{8,12},{9,13},{10,... | collective-permute-start | bytes 811016 | tf_op jit(solution)/shard_map/ppermute | solution.py:282
  32.1 5.7 %experts.2 = (bf16[32,4096]{1,0:T(8,128)(2,1)S(1)}, bf16[32,4096]{1,0:T(8,128)(2,1)S(1)}, bf16[16,4096]{1,0:T(8,128)(2,1)S(1)}, bf16[80,4096]{1,0:T(8,128)(2,1)S...) custom-call(s32[1]{0:T(128)} %begin.1.refs_0_, bf16[64,4224]{1,0:T(8,128)(2,1)S(1)} %gather.3.refs_1_, ...), custom_call_target="tpu_custom_call" | custom-call | flops 4831838208 | bytes 4194304 | tf_op jit(solution)/shard_map/experts/pallas_call | solution.py:197
  37.8 0.8 %collective-permute-done.12.refs_3_ = bf16[32,4224]{1,0:T(8,128)(2,1)S(1)} collective-permute-done((bf16[32,4224]{1,0:T(8,128)(2,1)S(1)}, bf16[32,4224]{1,0:T(8,128)(2,1)S(1)}, u32[]{:S(2)}, u32[]{:S(2)}) %collective-permute-start.12) | collective-permute-done | bytes 270368 | tf_op jit(solution)/shard_map/ppermute | solution.py:282
  38.6 1.2 %collective-permute-done.11.refs_2_ = bf16[32,4224]{1,0:T(8,128)(2,1)S(1)} collective-permute-done((bf16[32,4224]{1,0:T(8,128)(2,1)S(1)}, bf16[32,4224]{1,0:T(8,128)(2,1)S(1)}, u32[]{:S(2)}, u32[]{:S(2)}) %collective-permute-start.11) | collective-permute-done | bytes 270368 | tf_op jit(solution)/shard_map/ppermute | solution.py:282
  40.9 1.1 %collective-permute-done.15 = bf16[80,4096]{1,0:T(8,128)(2,1)S(1)} collective-permute-done((bf16[80,4096]{1,0:T(8,128)(2,1)S(1)}, bf16[80,4096]{1,0:T(8,128)(2,1)S(1)}, u32[]{:S(2)}, u32[]{:S(2)}) %collective-permute-start.15) | collective-permute-done | bytes 655392 | tf_op jit(solution)/shard_map/ppermute | solution.py:282
  42.3 1.5 %collective-permute-start.24 = (bf16[16,4096]{1,0:T(8,128)(2,1)S(1)}, bf16[16,4096]{1,0:T(8,128)(2,1)S(1)}, u32[]{:S(2)}, u32[]{:S(2)}) collective-permute-start(bf16[16,4096]{1,0:T(8,128)(2,1)S(1)} %add_convert_fusion.7), channel_id=1, source_target_pairs={{0,6},{1,7},{2,4},{3,5},{4,2},{5,3},{6,0},{7,1},{8,14},{9,15},{10,... | collective-permute-start | bytes 393224 | tf_op jit(solution)/shard_map/ppermute | solution.py:282
  44.3 1.5 %collective-permute-start.23 = (bf16[32,4096]{1,0:T(8,128)(2,1)S(1)}, bf16[32,4096]{1,0:T(8,128)(2,1)S(1)}, u32[]{:S(2)}, u32[]{:S(2)}) collective-permute-start(bf16[32,4096]{1,0:T(8,128)(2,1)S(1)} %get-tuple-element.90), channel_id=1, source_target_pairs={{0,4},{1,5},{2,6},{3,7},{4,0},{5,1},{6,2},{7,3},{8,12},{9,13},{10,... | collective-permute-start | bytes 786440 | tf_op jit(solution)/shard_map/ppermute | solution.py:282
  45.9 5.7 %experts.3 = (bf16[16,4096]{1,0:T(8,128)(2,1)S(1)}, bf16[16,4096]{1,0:T(8,128)(2,1)S(1)}, bf16[32,4096]{1,0:T(8,128)(2,1)S(1)}, bf16[32,4096]{1,0:T(8,128)(2,1)S...) custom-call(s32[1]{0:T(128)} %begin.1.refs_0_, bf16[32,4224]{1,0:T(8,128)(2,1)S(1)} %gather.5.refs_1_, ...), custom_call_target="tpu_custom_call" | custom-call | flops 4831838208 | bytes 4194304 | tf_op jit(solution)/shard_map/experts/pallas_call | solution.py:197
  52.2 1.5 %collective-permute-done.22 = bf16[32,4096]{1,0:T(8,128)(2,1)S(1)} collective-permute-done((bf16[32,4096]{1,0:T(8,128)(2,1)S(1)}, bf16[32,4096]{1,0:T(8,128)(2,1)S(1)}, u32[]{:S(2)}, u32[]{:S(2)}) %collective-permute-start.22) | collective-permute-done | bytes 262176 | tf_op jit(solution)/shard_map/ppermute | solution.py:282
  53.7 0.9 %collective-permute-done.23 = bf16[32,4096]{1,0:T(8,128)(2,1)S(1)} collective-permute-done((bf16[32,4096]{1,0:T(8,128)(2,1)S(1)}, bf16[32,4096]{1,0:T(8,128)(2,1)S(1)}, u32[]{:S(2)}, u32[]{:S(2)}) %collective-permute-start.23) | collective-permute-done | bytes 262176 | tf_op jit(solution)/shard_map/ppermute | solution.py:282
  55.1 3.8 %collective-permute-start.28 = (bf16[16,4096]{1,0:T(8,128)(2,1)S(1)}, bf16[16,4096]{1,0:T(8,128)(2,1)S(1)}, u32[]{:S(2)}, u32[]{:S(2)}) collective-permute-start(bf16[16,4096]{1,0:T(8,128)(2,1)S(1)} %get-tuple-element.117), channel_id=1, source_target_pairs={{0,24},{8,0},{16,8},{24,16},{1,25},{9,1},{17,9},{25,17},{2,26},{10... | collective-permute-start | bytes 393224 | tf_op jit(solution)/shard_map/ppermute | solution.py:287
  59.5 1.4 %collective-permute-start.31 = (bf16[32,4096]{1,0:T(8,128)(2,1)S(1)}, bf16[32,4096]{1,0:T(8,128)(2,1)S(1)}, u32[]{:S(2)}, u32[]{:S(2)}) collective-permute-start(bf16[32,4096]{1,0:T(8,128)(2,1)S(1)} %get-tuple-element.120), channel_id=1, source_target_pairs={{0,4},{1,5},{2,6},{3,7},{4,0},{5,1},{6,2},{7,3},{8,12},{9,13},{10,... | collective-permute-start | bytes 786440 | tf_op jit(solution)/shard_map/ppermute | solution.py:282
  60.9 2.4 %collective-permute-done.27 = bf16[16,4096]{1,0:T(8,128)(2,1)S(1)} collective-permute-done((bf16[16,4096]{1,0:T(8,128)(2,1)S(1)}, bf16[16,4096]{1,0:T(8,128)(2,1)S(1)}, u32[]{:S(2)}, u32[]{:S(2)}) %collective-permute-start.27) | collective-permute-done | bytes 131104 | tf_op jit(solution)/shard_map/ppermute | solution.py:287
  63.3 2.4 %collective-permute-done.28 = bf16[16,4096]{1,0:T(8,128)(2,1)S(1)} collective-permute-done((bf16[16,4096]{1,0:T(8,128)(2,1)S(1)}, bf16[16,4096]{1,0:T(8,128)(2,1)S(1)}, u32[]{:S(2)}, u32[]{:S(2)}) %collective-permute-start.28) | collective-permute-done | bytes 131104 | tf_op jit(solution)/shard_map/ppermute | solution.py:287
  65.7 1.5 %collective-permute-start.29 = (bf16[16,4096]{1,0:T(8,128)(2,1)S(1)}, bf16[16,4096]{1,0:T(8,128)(2,1)S(1)}, u32[]{:S(2)}, u32[]{:S(2)}) collective-permute-start(bf16[16,4096]{1,0:T(8,128)(2,1)S(1)} %fusion), channel_id=1, source_target_pairs={{0,6},{1,7},{2,4},{3,5},{4,2},{5,3},{6,0},{7,1},{8,14},{9,15},{10,... | collective-permute-start | bytes 393224 | tf_op jit(solution)/shard_map/ppermute | solution.py:282
  67.2 0.8 collective-permute-done.30
  68.8 3.3 %collective-permute-start.33 = (bf16[16,4096]{1,0:T(8,128)(2,1)S(1)}, bf16[16,4096]{1,0:T(8,128)(2,1)S(1)}, u32[]{:S(2)}, u32[]{:S(2)}) collective-permute-start(bf16[16,4096]{1,0:T(8,128)(2,1)S(1)} %get-tuple-element.128), channel_id=1, source_target_pairs={{0,24},{8,0},{16,8},{24,16},{1,25},{9,1},{17,9},{25,17},{2,26},{10... | collective-permute-start | bytes 393224 | tf_op jit(solution)/shard_map/ppermute | solution.py:287
  72.1 3.1 %collective-permute-done.32 = bf16[16,4096]{1,0:T(8,128)(2,1)S(1)} collective-permute-done((bf16[16,4096]{1,0:T(8,128)(2,1)S(1)}, bf16[16,4096]{1,0:T(8,128)(2,1)S(1)}, u32[]{:S(2)}, u32[]{:S(2)}) %collective-permute-start.32) | collective-permute-done | bytes 131104 | tf_op jit(solution)/shard_map/ppermute | solution.py:287
  75.8 0.8 %fusion.8 = bf16[16,4096]{1,0:T(8,128)(2,1)} fusion(f32[48,4096]{1,0:T(8,128)S(1)} %convert_add_fusion, bf16[16,4096]{1,0:T(8,128)(2,1)S(1)} %collective-permute-done.33, bf16[16,4096]{1,0:T(8,128)(2,1)S(1)} %collective-permute-done.32, bf16[16,4096]{1,0:T(8,128)(2,1)S(1)} %collective-permute-done.29, bf16[16,4096]{1,0:T(8,128)(2,1)S(1)} %collective-permute-done.26, ...), kind=kLoop, calls=%fused_computation.17 | loop fusion | flops 851968 | bytes 1179648 | tf_op jit(solution)/shard_map/convert_element_type | solution.py:298
  (74 shorter events, 9.4 us)
Async XLA Ops:
  1.2 11.8 %collective-permute-start.3 = (bf16[16,4224]{1,0:T(8,128)(2,1)S(1)}, bf16[16,4224]{1,0:T(8,128)(2,1)S(1)}, u32[]{:S(2)}, u32[]{:S(2)}) collective-permute-start(bf16[16,4224]{1,0:T(8,128)(2,1)S(1)} %pack.1.refs_0_), channel_id=1, source_target_pairs={{0,16},{8,24},{16,0},{24,8},{1,17},{9,25},{17,1},{25,9},{2,18},{10... | collective-permute-start | bytes 405512 | tf_op jit(solution)/shard_map/ppermute | solution.py:287
  5.3 7.7 %collective-permute-start.2 = (bf16[16,4224]{1,0:T(8,128)(2,1)S(1)}, bf16[16,4224]{1,0:T(8,128)(2,1)S(1)}, u32[]{:S(2)}, u32[]{:S(2)}) collective-permute-start(bf16[16,4224]{1,0:T(8,128)(2,1)S(1)} %pack.1.refs_0_), channel_id=1, source_target_pairs={{0,6},{1,7},{2,4},{3,5},{4,2},{5,3},{6,0},{7,1},{8,14},{9,15},{10,... | collective-permute-start | bytes 405512 | tf_op jit(solution)/shard_map/ppermute | solution.py:282
  7.8 6.4 %collective-permute-start.1 = (bf16[16,4224]{1,0:T(8,128)(2,1)S(1)}, bf16[16,4224]{1,0:T(8,128)(2,1)S(1)}, u32[]{:S(2)}, u32[]{:S(2)}) collective-permute-start(bf16[16,4224]{1,0:T(8,128)(2,1)S(1)} %pack.1.refs_0_), channel_id=1, source_target_pairs={{0,4},{1,5},{2,6},{3,7},{4,0},{5,1},{6,2},{7,3},{8,12},{9,13},{10,... | collective-permute-start | bytes 405512 | tf_op jit(solution)/shard_map/ppermute | solution.py:282
  8.3 5.9 %collective-permute-start = (bf16[16,4224]{1,0:T(8,128)(2,1)S(1)}, bf16[16,4224]{1,0:T(8,128)(2,1)S(1)}, u32[]{:S(2)}, u32[]{:S(2)}) collective-permute-start(bf16[16,4224]{1,0:T(8,128)(2,1)S(1)} %pack.1.refs_0_), channel_id=1, source_target_pairs={{0,2},{1,3},{2,0},{3,1},{4,6},{5,7},{6,4},{7,5},{8,10},{9,11},{10,... | collective-permute-start | bytes 405512 | tf_op jit(solution)/shard_map/ppermute | solution.py:282
  14.2 8.1 %collective-permute-start.6 = (bf16[16,4224]{1,0:T(8,128)(2,1)S(1)}, bf16[16,4224]{1,0:T(8,128)(2,1)S(1)}, u32[]{:S(2)}, u32[]{:S(2)}) collective-permute-start(bf16[16,4224]{1,0:T(8,128)(2,1)S(1)} %collective-permute-done.3.refs_0_), channel_id=1, source_target_pairs={{0,6},{1,7},{2,4},{3,5},{4,2},{5,3},{6,0},{7,1},{8,14},{9,15},{10,... | collective-permute-start | bytes 405512 | tf_op jit(solution)/shard_map/ppermute | solution.py:282
  15.9 7.4 %collective-permute-start.5 = (bf16[16,4224]{1,0:T(8,128)(2,1)S(1)}, bf16[16,4224]{1,0:T(8,128)(2,1)S(1)}, u32[]{:S(2)}, u32[]{:S(2)}) collective-permute-start(bf16[16,4224]{1,0:T(8,128)(2,1)S(1)} %collective-permute-done.3.refs_0_), channel_id=1, source_target_pairs={{0,4},{1,5},{2,6},{3,7},{4,0},{5,1},{6,2},{7,3},{8,12},{9,13},{10,... | collective-permute-start | bytes 405512 | tf_op jit(solution)/shard_map/ppermute | solution.py:282
  17.2 6.1 %collective-permute-start.4 = (bf16[16,4224]{1,0:T(8,128)(2,1)S(1)}, bf16[16,4224]{1,0:T(8,128)(2,1)S(1)}, u32[]{:S(2)}, u32[]{:S(2)}) collective-permute-start(bf16[16,4224]{1,0:T(8,128)(2,1)S(1)} %collective-permute-done.3.refs_0_), channel_id=1, source_target_pairs={{0,2},{1,3},{2,0},{3,1},{4,6},{5,7},{6,4},{7,5},{8,10},{9,11},{10,... | collective-permute-start | bytes 405512 | tf_op jit(solution)/shard_map/ppermute | solution.py:282
  17.7 7.9 %collective-permute-start.8 = (bf16[16,4224]{1,0:T(8,128)(2,1)S(1)}, bf16[16,4224]{1,0:T(8,128)(2,1)S(1)}, u32[]{:S(2)}, u32[]{:S(2)}) collective-permute-start(bf16[16,4224]{1,0:T(8,128)(2,1)S(1)} %pack.1.refs_0_), channel_id=1, source_target_pairs={{0,8},{8,16},{16,24},{24,0},{1,9},{9,17},{17,25},{25,1},{2,10},{10... | collective-permute-start | bytes 405512 | tf_op jit(solution)/shard_map/ppermute | solution.py:287
  19.3 7.1 %collective-permute-start.7 = (bf16[16,4224]{1,0:T(8,128)(2,1)S(1)}, bf16[16,4224]{1,0:T(8,128)(2,1)S(1)}, u32[]{:S(2)}, u32[]{:S(2)}) collective-permute-start(bf16[16,4224]{1,0:T(8,128)(2,1)S(1)} %pack.1.refs_0_), channel_id=1, source_target_pairs={{0,24},{8,0},{16,8},{24,16},{1,25},{9,1},{17,9},{25,17},{2,26},{10... | collective-permute-start | bytes 405512 | tf_op jit(solution)/shard_map/ppermute | solution.py:287
  22.4 9.4 %collective-permute-start.9 = (bf16[64,4224]{1,0:T(8,128)(2,1)S(1)}, bf16[64,4224]{1,0:T(8,128)(2,1)S(1)}, u32[]{:S(2)}, u32[]{:S(2)}) collective-permute-start(bf16[64,4224]{1,0:T(8,128)(2,1)S(1)} %gather.3.refs_1_), channel_id=1, source_target_pairs={{0,1},{1,0},{2,3},{3,2},{4,5},{5,4},{6,7},{7,6},{8,9},{9,8},{10,11... | collective-permute-start | bytes 1622024 | tf_op jit(solution)/shard_map/ppermute | solution.py:282
  26.4 5.7 %collective-permute-start.10 = (bf16[64,4224]{1,0:T(8,128)(2,1)S(1)}, bf16[64,4224]{1,0:T(8,128)(2,1)S(1)}, u32[]{:S(2)}, u32[]{:S(2)}) collective-permute-start(bf16[64,4224]{1,0:T(8,128)(2,1)S(1)} %gather.4.refs_2_), channel_id=1, source_target_pairs={{0,1},{1,0},{2,3},{3,2},{4,5},{5,4},{6,7},{7,6},{8,9},{9,8},{10,11... | collective-permute-start | bytes 1622024 | tf_op jit(solution)/shard_map/ppermute | solution.py:282
  26.4 11.5 %collective-permute-start.14 = (bf16[16,4224]{1,0:T(8,128)(2,1)S(1)}, bf16[16,4224]{1,0:T(8,128)(2,1)S(1)}, u32[]{:S(2)}, u32[]{:S(2)}) collective-permute-start(bf16[16,4224]{1,0:T(8,128)(2,1)S(1)} %collective-permute-done.2.refs_3_), channel_id=1, source_target_pairs={{0,8},{8,16},{16,24},{24,0},{1,9},{9,17},{17,25},{25,1},{2,10},{10... | collective-permute-start | bytes 405512 | tf_op jit(solution)/shard_map/ppermute | solution.py:287
  26.7 11.2 %collective-permute-start.13 = (bf16[16,4224]{1,0:T(8,128)(2,1)S(1)}, bf16[16,4224]{1,0:T(8,128)(2,1)S(1)}, u32[]{:S(2)}, u32[]{:S(2)}) collective-permute-start(bf16[16,4224]{1,0:T(8,128)(2,1)S(1)} %collective-permute-done.2.refs_3_), channel_id=1, source_target_pairs={{0,24},{8,0},{16,8},{24,16},{1,25},{9,1},{17,9},{25,17},{2,26},{10... | collective-permute-start | bytes 405512 | tf_op jit(solution)/shard_map/ppermute | solution.py:287
  30.2 8.4 %collective-permute-start.12 = (bf16[32,4224]{1,0:T(8,128)(2,1)S(1)}, bf16[32,4224]{1,0:T(8,128)(2,1)S(1)}, u32[]{:S(2)}, u32[]{:S(2)}) collective-permute-start(bf16[32,4224]{1,0:T(8,128)(2,1)S(1)} %gather.5.refs_1_), channel_id=1, source_target_pairs={{0,4},{1,5},{2,6},{3,7},{4,0},{5,1},{6,2},{7,3},{8,12},{9,13},{10,... | collective-permute-start | bytes 811016 | tf_op jit(solution)/shard_map/ppermute | solution.py:282
  31.8 8.1 %collective-permute-start.11 = (bf16[32,4224]{1,0:T(8,128)(2,1)S(1)}, bf16[32,4224]{1,0:T(8,128)(2,1)S(1)}, u32[]{:S(2)}, u32[]{:S(2)}) collective-permute-start(bf16[32,4224]{1,0:T(8,128)(2,1)S(1)} %gather.5.refs_1_), channel_id=1, source_target_pairs={{0,2},{1,3},{2,0},{3,1},{4,6},{5,7},{6,4},{7,5},{8,10},{9,11},{10,... | collective-permute-start | bytes 811016 | tf_op jit(solution)/shard_map/ppermute | solution.py:282
  40.4 3.4 %collective-permute-start.20 = (bf16[16,4224]{1,0:T(8,128)(2,1)S(1)}, bf16[16,4224]{1,0:T(8,128)(2,1)S(1)}, u32[]{:S(2)}, u32[]{:S(2)}) collective-permute-start(bf16[16,4224]{1,0:T(8,128)(2,1)S(1)} %collective-permute-done.13.refs_4_), channel_id=1, source_target_pairs={{0,1},{1,0},{2,3},{3,2},{4,5},{5,4},{6,7},{7,6},{8,9},{9,8},{10,11... | collective-permute-start | bytes 405512 | tf_op jit(solution)/shard_map/ppermute | solution.py:282
  40.4 4.0 %collective-permute-start.21 = (bf16[16,4224]{1,0:T(8,128)(2,1)S(1)}, bf16[16,4224]{1,0:T(8,128)(2,1)S(1)}, u32[]{:S(2)}, u32[]{:S(2)}) collective-permute-start(bf16[16,4224]{1,0:T(8,128)(2,1)S(1)} %collective-permute-done.14.refs_5_), channel_id=1, source_target_pairs={{0,1},{1,0},{2,3},{3,2},{4,5},{5,4},{6,7},{7,6},{8,9},{9,8},{10,11... | collective-permute-start | bytes 405512 | tf_op jit(solution)/shard_map/ppermute | solution.py:282
  40.9 5.0 %collective-permute-start.18 = (bf16[32,4224]{1,0:T(8,128)(2,1)S(1)}, bf16[32,4224]{1,0:T(8,128)(2,1)S(1)}, u32[]{:S(2)}, u32[]{:S(2)}) collective-permute-start(bf16[32,4224]{1,0:T(8,128)(2,1)S(1)} %collective-permute-done.11.refs_2_), channel_id=1, source_target_pairs={{0,1},{1,0},{2,3},{3,2},{4,5},{5,4},{6,7},{7,6},{8,9},{9,8},{10,11... | collective-permute-start | bytes 811016 | tf_op jit(solution)/shard_map/ppermute | solution.py:282
  42.0 3.9 %collective-permute-start.19 = (bf16[32,4224]{1,0:T(8,128)(2,1)S(1)}, bf16[32,4224]{1,0:T(8,128)(2,1)S(1)}, u32[]{:S(2)}, u32[]{:S(2)}) collective-permute-start(bf16[32,4224]{1,0:T(8,128)(2,1)S(1)} %collective-permute-done.12.refs_3_), channel_id=1, source_target_pairs={{0,1},{1,0},{2,3},{3,2},{4,5},{5,4},{6,7},{7,6},{8,9},{9,8},{10,11... | collective-permute-start | bytes 811016 | tf_op jit(solution)/shard_map/ppermute | solution.py:282
  42.3 9.9 %collective-permute-start.24 = (bf16[16,4096]{1,0:T(8,128)(2,1)S(1)}, bf16[16,4096]{1,0:T(8,128)(2,1)S(1)}, u32[]{:S(2)}, u32[]{:S(2)}) collective-permute-start(bf16[16,4096]{1,0:T(8,128)(2,1)S(1)} %add_convert_fusion.7), channel_id=1, source_target_pairs={{0,6},{1,7},{2,4},{3,5},{4,2},{5,3},{6,0},{7,1},{8,14},{9,15},{10,... | collective-permute-start | bytes 393224 | tf_op jit(solution)/shard_map/ppermute | solution.py:282
  43.8 9.9 %collective-permute-start.22 = (bf16[32,4096]{1,0:T(8,128)(2,1)S(1)}, bf16[32,4096]{1,0:T(8,128)(2,1)S(1)}, u32[]{:S(2)}, u32[]{:S(2)}) collective-permute-start(bf16[32,4096]{1,0:T(8,128)(2,1)S(1)} %get-tuple-element.89), channel_id=1, source_target_pairs={{0,2},{1,3},{2,0},{3,1},{4,6},{5,7},{6,4},{7,5},{8,10},{9,11},{10,... | collective-permute-start | bytes 786440 | tf_op jit(solution)/shard_map/ppermute | solution.py:282
  44.3 10.3 %collective-permute-start.23 = (bf16[32,4096]{1,0:T(8,128)(2,1)S(1)}, bf16[32,4096]{1,0:T(8,128)(2,1)S(1)}, u32[]{:S(2)}, u32[]{:S(2)}) collective-permute-start(bf16[32,4096]{1,0:T(8,128)(2,1)S(1)} %get-tuple-element.90), channel_id=1, source_target_pairs={{0,4},{1,5},{2,6},{3,7},{4,0},{5,1},{6,2},{7,3},{8,12},{9,13},{10,... | collective-permute-start | bytes 786440 | tf_op jit(solution)/shard_map/ppermute | solution.py:282
  45.9 8.8 %collective-permute-start.16 = (bf16[48,4096]{1,0:T(8,128)(2,1)S(1)}, bf16[48,4096]{1,0:T(8,128)(2,1)S(1)}, u32[]{:S(2)}, u32[]{:S(2)}) collective-permute-start(bf16[48,4096]{1,0:T(8,128)(2,1)S(1)} %get-tuple-element.88), channel_id=1, source_target_pairs={{0,1},{1,0},{2,3},{3,2},{4,5},{5,4},{6,7},{7,6},{8,9},{9,8},{10,11... | collective-permute-start | bytes 1179656 | tf_op jit(solution)/shard_map/ppermute | solution.py:282
  51.6 3.2 %collective-permute-start.25 = (bf16[128,4096]{1,0:T(8,128)(2,1)S(1)}, bf16[128,4096]{1,0:T(8,128)(2,1)S(1)}, u32[]{:S(2)}, u32[]{:S(2)}) collective-permute-start(bf16[128,4096]{1,0:T(8,128)(2,1)S(1)} %get-tuple-element.111), channel_id=1, source_target_pairs={{0,1},{1,0},{2,3},{3,2},{4,5},{5,4},{6,7},{7,6},{8,9},{9,8},{10,11... | collective-permute-start | bytes 3145736 | tf_op jit(solution)/shard_map/ppermute | solution.py:282
  55.0 8.3 %collective-permute-start.27 = (bf16[16,4096]{1,0:T(8,128)(2,1)S(1)}, bf16[16,4096]{1,0:T(8,128)(2,1)S(1)}, u32[]{:S(2)}, u32[]{:S(2)}) collective-permute-start(bf16[16,4096]{1,0:T(8,128)(2,1)S(1)} %get-tuple-element.116), channel_id=1, source_target_pairs={{0,8},{8,16},{16,24},{24,0},{1,9},{9,17},{17,25},{25,1},{2,10},{10... | collective-permute-start | bytes 393224 | tf_op jit(solution)/shard_map/ppermute | solution.py:287
  55.1 10.6 %collective-permute-start.28 = (bf16[16,4096]{1,0:T(8,128)(2,1)S(1)}, bf16[16,4096]{1,0:T(8,128)(2,1)S(1)}, u32[]{:S(2)}, u32[]{:S(2)}) collective-permute-start(bf16[16,4096]{1,0:T(8,128)(2,1)S(1)} %get-tuple-element.117), channel_id=1, source_target_pairs={{0,24},{8,0},{16,8},{24,16},{1,25},{9,1},{17,9},{25,17},{2,26},{10... | collective-permute-start | bytes 393224 | tf_op jit(solution)/shard_map/ppermute | solution.py:287
  58.9 13.2 %collective-permute-start.26 = (bf16[16,4096]{1,0:T(8,128)(2,1)S(1)}, bf16[16,4096]{1,0:T(8,128)(2,1)S(1)}, u32[]{:S(2)}, u32[]{:S(2)}) collective-permute-start(bf16[16,4096]{1,0:T(8,128)(2,1)S(1)} %fusion.3), channel_id=1, source_target_pairs={{0,16},{8,24},{16,0},{24,8},{1,17},{9,25},{17,1},{25,9},{2,18},{10... | collective-permute-start | bytes 393224 | tf_op jit(solution)/shard_map/ppermute | solution.py:287
  58.9 9.1 %collective-permute-start.30 = (bf16[32,4096]{1,0:T(8,128)(2,1)S(1)}, bf16[32,4096]{1,0:T(8,128)(2,1)S(1)}, u32[]{:S(2)}, u32[]{:S(2)}) collective-permute-start(bf16[32,4096]{1,0:T(8,128)(2,1)S(1)} %get-tuple-element.119), channel_id=1, source_target_pairs={{0,2},{1,3},{2,0},{3,1},{4,6},{5,7},{6,4},{7,5},{8,10},{9,11},{10,... | collective-permute-start | bytes 786440 | tf_op jit(solution)/shard_map/ppermute | solution.py:282
  59.5 8.6 %collective-permute-start.31 = (bf16[32,4096]{1,0:T(8,128)(2,1)S(1)}, bf16[32,4096]{1,0:T(8,128)(2,1)S(1)}, u32[]{:S(2)}, u32[]{:S(2)}) collective-permute-start(bf16[32,4096]{1,0:T(8,128)(2,1)S(1)} %get-tuple-element.120), channel_id=1, source_target_pairs={{0,4},{1,5},{2,6},{3,7},{4,0},{5,1},{6,2},{7,3},{8,12},{9,13},{10,... | collective-permute-start | bytes 786440 | tf_op jit(solution)/shard_map/ppermute | solution.py:282
  65.7 6.4 %collective-permute-start.29 = (bf16[16,4096]{1,0:T(8,128)(2,1)S(1)}, bf16[16,4096]{1,0:T(8,128)(2,1)S(1)}, u32[]{:S(2)}, u32[]{:S(2)}) collective-permute-start(bf16[16,4096]{1,0:T(8,128)(2,1)S(1)} %fusion), channel_id=1, source_target_pairs={{0,6},{1,7},{2,4},{3,5},{4,2},{5,3},{6,0},{7,1},{8,14},{9,15},{10,... | collective-permute-start | bytes 393224 | tf_op jit(solution)/shard_map/ppermute | solution.py:282
  68.2 7.0 %collective-permute-start.32 = (bf16[16,4096]{1,0:T(8,128)(2,1)S(1)}, bf16[16,4096]{1,0:T(8,128)(2,1)S(1)}, u32[]{:S(2)}, u32[]{:S(2)}) collective-permute-start(bf16[16,4096]{1,0:T(8,128)(2,1)S(1)} %get-tuple-element.127), channel_id=1, source_target_pairs={{0,8},{8,16},{16,24},{24,0},{1,9},{9,17},{17,25},{25,1},{2,10},{10... | collective-permute-start | bytes 393224 | tf_op jit(solution)/shard_map/ppermute | solution.py:287
  68.8 7.0 %collective-permute-start.33 = (bf16[16,4096]{1,0:T(8,128)(2,1)S(1)}, bf16[16,4096]{1,0:T(8,128)(2,1)S(1)}, u32[]{:S(2)}, u32[]{:S(2)}) collective-permute-start(bf16[16,4096]{1,0:T(8,128)(2,1)S(1)} %get-tuple-element.128), channel_id=1, source_target_pairs={{0,24},{8,0},{16,8},{24,16},{1,25},{9,1},{17,9},{25,17},{2,26},{10... | collective-permute-start | bytes 393224 | tf_op jit(solution)/shard_map/ppermute | solution.py:287
  (10 other events, 59.1 us)

commit v7 on v6

--- a/solution.py
+++ b/solution.py
@@ -282,9 +282,9 @@
     return lax.ppermute(value, "exp", [(i, i ^ bits) for i in range(owners)])
 
 
-def turn_rep(value, shift):
+def swap_rep(value, bits):
     replicas = lax.axis_size("rep")
-    return lax.ppermute(value, "rep", [(i, (i - shift) % replicas) for i in range(replicas)])
+    return lax.ppermute(value, "rep", [(i, i ^ bits) for i in range(replicas)])
 
 
 def added(*terms):
@@ -319,29 +319,27 @@
     tokens, own = ordered(tokens, own)
     packed = with_routing(tokens, routed_experts, route_weights)
 
-    two = turn_rep(packed, 2)
+    three = swap_rep(packed, 3)
     x_own, y_own, far_own = [swap_exp(packed, bits) for bits in (2, 4, 6)]
     gates, ups = fetched(gate_weight, True), fetched(up_weight, True)
-    x_own, y_own, far_own, two, gates, ups, again = ordered(
-        x_own, y_own, far_own, two, gates, ups, packed
-    )
-    one, three = turn_rep(again, 1), turn_rep(again, 3)
-    x_two, y_two, far_two = [swap_exp(two, bits) for bits in (2, 4, 6)]
-    far_one, far_three = turn_rep(far_own, 1), turn_rep(far_own, 3)
+    x_own, y_own, far_own, three, gates, ups, again = ordered(
+        x_own, y_own, far_own, three, gates, ups, packed
+    )
+    one, two = swap_rep(again, 1), swap_rep(again, 2)
+    x_three, y_three, far_three = [swap_exp(three, bits) for bits in (2, 4, 6)]
+    far_one, far_two = swap_rep(far_own, 1), swap_rep(far_own, 2)
     first = gathered(packed, x_own, y_own, far_own)
     first_other = swap_exp(first, 1)
-    second = gathered(two, x_two, y_two, far_two)
+    second = gathered(three, x_three, y_three, far_three)
     downs = fetched(down_weight, False)
-    second, downs, one, three = ordered(second, downs, one, three)
-    pair = gathered(one, three)
+    second, downs, one, two = ordered(second, downs, one, two)
+    pair = gathered(one, two)
     x_pair, y_pair = swap_exp(pair, 2), swap_exp(pair, 4)
 
     near = [first, second, first_other, swap_exp(second, 1)]
     groups = row_groups([[5, 1], [6, 2], [7], [13, 9, 14, 10, 15], [4, 0, 3], [12, 8, 11]], rows)
     parts = experts_of(own, near, groups, gates, ups, downs, shard_units, top)
-    *parts, x_pair, y_pair, far_one, far_three = ordered(
-        *parts, x_pair, y_pair, far_one, far_three
-    )
+    *parts, x_pair, y_pair, far_one, far_two = ordered(*parts, x_pair, y_pair, far_one, far_two)
     to_x, to_y, to_far, other, near_kept, near_other = parts
     back = swap_exp(other, 1)
     to_x = rounded(to_x, back[: 2 * rows])
@@ -351,30 +349,31 @@
     near_x, near_y, near_far = swap_exp(to_x, 2), swap_exp(to_y, 4), swap_exp(to_far, 6)
     near_back = swap_exp(near_other, 1)
 
-    far = [pair, x_pair, y_pair, far_one, far_three]
+    far = [pair, x_pair, y_pair, far_one, far_two]
     far = far + [swap_exp(piece, 1) for piece in far]
     to_x, to_y, to_far, *far = ordered(to_x, to_y, to_far, *far)
-    groups = row_groups([[6], [7], [2, 3], [4, 5], [14, 15, 10, 11, 12, 13, 8, 9], [0, 1]], rows)
+    groups = row_groups([[6], [7], [2, 3], [4, 5], [14], [10, 11, 12, 13, 15, 8, 9], [0, 1]], rows)
     parts = experts_of(own, far, groups, gates, ups, downs, shard_units, top)
-    to_one, to_three, to_x, to_y, other, far_kept = parts
+    to_one, to_far, to_x, to_y, other_one, other, far_kept = parts
     far_kept, near_x, near_y, near_far = ordered(far_kept, near_x, near_y, near_far)
     back = swap_exp(other, 1)
-    to_one, to_three = rounded(to_one, back[:rows]), rounded(to_three, back[rows : 2 * rows])
-    to_x = rounded(to_x, back[2 * rows : 4 * rows])
-    to_y = rounded(to_y, back[4 * rows : 6 * rows])
+    to_x, to_y = rounded(to_x, back[: 2 * rows]), rounded(to_y, back[2 * rows : 4 * rows])
+    to_far = rounded(to_far, back[4 * rows : 5 * rows])
+    to_x, to_y, to_far, other_one = ordered(to_x, to_y, to_far, other_one)
+    far_x, far_y, far_far = swap_exp(to_x, 2), swap_exp(to_y, 4), swap_exp(to_far, 6)
+    to_one = rounded(to_one, swap_exp(other_one, 1))
     kept = added(near_kept, near_back)
-    to_two = rounded(kept[:rows], near_x[:rows], near_y[:rows], near_far)
-    to_two, to_one, to_three, to_x, to_y = ordered(to_two, to_one, to_three, to_x, to_y)
-    from_two = turn_rep(to_two, -2)
-    from_one, from_three = turn_rep(to_one, -1), turn_rep(to_three, -3)
-    far_x, far_y = swap_exp(to_x, 2), swap_exp(to_y, 4)
+    to_three = rounded(kept[:rows], near_x[:rows], near_y[:rows], near_far)
+    to_three, to_one = ordered(to_three, to_one)
+    from_three, from_one = swap_rep(to_three, 3), swap_rep(to_one, 1)
 
     own_sum = kept[rows : 2 * rows] + added(near_x[rows:], near_y[rows:])
-    to_far = (kept[2 * rows :] + added(from_one, from_three)).astype(jnp.bfloat16)
+    to_far = rounded(kept[2 * rows :], from_one)
     from_far = swap_exp(to_far, 6)
-    sums = added(far_kept, back[6 * rows :], far_x, far_y).astype(jnp.bfloat16)
-    arrived = [turn_rep(sums[:rows], -1), turn_rep(sums[rows:], -3)]
-    return rounded(own_sum, from_two, from_far, *arrived)
+    to_one = rounded(far_kept[:rows], back[5 * rows : 6 * rows], far_x[:rows], far_y[:rows])
+    to_two = rounded(far_kept[rows:], back[6 * rows :], far_x[rows:], far_y[rows:], far_far)
+    arrived = [swap_rep(to_one, 1), swap_rep(to_two, 2)]
+    return rounded(own_sum, from_three, from_far, *arrived)
 
 
 def solution(mesh):

time: 76.8 us -> 76.4 us (level)
  starting transfers between devices: 37.1 us -> 32.5 us
  waiting for transfers between devices: 20.1 us -> 24.4 us
    ppermute x24 -> x26, waiting for transfers between devices: 8.57 us -> 17.4 us  [swap_exp(): return lax.ppermute(value, 'exp', [(i, i ^ bits) for i in range(owners)])]
    ppermute x10 -> x9, starting transfers between devices: 19.5 us -> 13.2 us  [swap_rep(): return lax.ppermute(value, 'rep', [(i, i ^ bits) for i in range(replicas)])]
    ppermute x10 -> x9, waiting for transfers between devices: 11.5 us -> 7.02 us  [swap_rep(): return lax.ppermute(value, 'rep', [(i, i ^ bits) for i in range(replicas)])]
    ppermute x24 -> x26, starting transfers between devices: 17.6 us -> 19.3 us  [swap_exp(): return lax.ppermute(value, 'exp', [(i, i ^ bits) for i in range(owners)])]
  transfers between devices with their start and end apart: 34 -> 35, of which waited for: 18 -> 18; matrix products, arithmetic and copies ran while one was open for 1% -> 1% of each run, Pallas kernels for 21% -> 22%
where the time goes in v7:
time: 76.4 us; the launch traced here: 76.3 us
  starting transfers between devices  32.5 us (43%)
  waiting for transfers between devices  24.4 us (32%)
  Pallas kernels  17.3 us (23%)
  other arithmetic  1.47 us (2%)
    ppermute x26, starting transfers between devices, swap_exp(): return lax.ppermute(value, 'exp', [(i, i ^ bits) for i in range(owners)])  19.3 us
    ppermute x26, waiting for transfers between devices, swap_exp(): return lax.ppermute(value, 'exp', [(i, i ^ bits) for i in range(owners)])  17.4 us
    ppermute x9, starting transfers between devices, swap_rep(): return lax.ppermute(value, 'rep', [(i, i ^ bits) for i in range(replicas)])  13.2 us
    pallas_call x2, Pallas kernels, experts_of(): pl.pallas_call(kernel, out_shape=[jax.ShapeDtypeStruct((count, model_widt...  11.5 us
    ppermute x9, waiting for transfers between devices, swap_rep(): return lax.ppermute(value, 'rep', [(i, i ^ bits) for i in range(replicas)])  7.02 us
    pallas_call x3, Pallas kernels, fetched(): pl.pallas_call(functools.partial(fetch_kernel, turn), out_shape=jax.Shape...  4.88 us
  transfers between devices with their start and end apart: 35, of which 18 were waited for; matrix products, arithmetic and copies ran while one was open for 1% of the time, Pallas kernels for 22%

profile of v7, /device:TPU:0, one launch (start us, length us, event | category | flops | bytes accessed | tf_op | source)
XLA Modules:
  0.0 76.3 jit_solution(11654267666630955020)
XLA Ops:
  1.2 5.1 %collective-permute-start.3 = (bf16[16,4224]{1,0:T(8,128)(2,1)S(1)}, bf16[16,4224]{1,0:T(8,128)(2,1)S(1)}, u32[]{:S(2)}, u32[]{:S(2)}) collective-permute-start(bf16[16,4224]{1,0:T(8,128)(2,1)S(1)} %pack.1.refs_0_), channel_id=1, source_target_pairs={{0,24},{8,16},{16,8},{24,0},{1,25},{9,17},{17,9},{25,1},{2,26},{10... | collective-permute-start | bytes 405512 | tf_op jit(solution)/shard_map/ppermute | solution.py:287
  6.3 2.4 %collective-permute-start.2 = (bf16[16,4224]{1,0:T(8,128)(2,1)S(1)}, bf16[16,4224]{1,0:T(8,128)(2,1)S(1)}, u32[]{:S(2)}, u32[]{:S(2)}) collective-permute-start(bf16[16,4224]{1,0:T(8,128)(2,1)S(1)} %pack.1.refs_0_), channel_id=1, source_target_pairs={{0,6},{1,7},{2,4},{3,5},{4,2},{5,3},{6,0},{7,1},{8,14},{9,15},{10,... | collective-permute-start | bytes 405512 | tf_op jit(solution)/shard_map/ppermute | solution.py:282
  9.8 2.1 %fetch_turned.2.refs_5_.refs_11_ = bf16[4096,768]{1,0:T(8,128)(2,1)S(1)} custom-call(bf16[768,4096]{1,0:T(8,128)(2,1)S(1)} %bitcast.7), custom_call_target="tpu_custom_call" | custom-call | bytes 12582912 | tf_op jit(solution)/shard_map/fetch_turned/pallas_call | solution.py:103
  11.9 2.1 %fetch_turned.3.refs_6_.refs_12_ = bf16[4096,768]{1,0:T(8,128)(2,1)S(1)} custom-call(bf16[768,4096]{1,0:T(8,128)(2,1)S(1)} %bitcast.11), custom_call_target="tpu_custom_call" | custom-call | bytes 12582912 | tf_op jit(solution)/shard_map/fetch_turned/pallas_call | solution.py:103
  14.0 1.1 %collective-permute-done.1.refs_2_ = bf16[16,4224]{1,0:T(8,128)(2,1)S(1)} collective-permute-done((bf16[16,4224]{1,0:T(8,128)(2,1)S(1)}, bf16[16,4224]{1,0:T(8,128)(2,1)S(1)}, u32[]{:S(2)}, u32[]{:S(2)}) %collective-permute-start.1) | collective-permute-done | bytes 135200 | tf_op jit(solution)/shard_map/ppermute | solution.py:282
  15.2 1.7 %collective-permute-start.6 = (bf16[16,4224]{1,0:T(8,128)(2,1)S(1)}, bf16[16,4224]{1,0:T(8,128)(2,1)S(1)}, u32[]{:S(2)}, u32[]{:S(2)}) collective-permute-start(bf16[16,4224]{1,0:T(8,128)(2,1)S(1)} %collective-permute-done.3.refs_0_), channel_id=1, source_target_pairs={{0,6},{1,7},{2,4},{3,5},{4,2},{5,3},{6,0},{7,1},{8,14},{9,15},{10,... | collective-permute-start | bytes 405512 | tf_op jit(solution)/shard_map/ppermute | solution.py:282
  16.9 1.3 %collective-permute-start.5 = (bf16[16,4224]{1,0:T(8,128)(2,1)S(1)}, bf16[16,4224]{1,0:T(8,128)(2,1)S(1)}, u32[]{:S(2)}, u32[]{:S(2)}) collective-permute-start(bf16[16,4224]{1,0:T(8,128)(2,1)S(1)} %collective-permute-done.3.refs_0_), channel_id=1, source_target_pairs={{0,4},{1,5},{2,6},{3,7},{4,0},{5,1},{6,2},{7,3},{8,12},{9,13},{10,... | collective-permute-start | bytes 405512 | tf_op jit(solution)/shard_map/ppermute | solution.py:282
  18.7 0.9 %collective-permute-start.7 = (bf16[16,4224]{1,0:T(8,128)(2,1)S(1)}, bf16[16,4224]{1,0:T(8,128)(2,1)S(1)}, u32[]{:S(2)}, u32[]{:S(2)}) collective-permute-start(bf16[16,4224]{1,0:T(8,128)(2,1)S(1)} %pack.1.refs_0_), channel_id=1, source_target_pairs={{0,8},{8,0},{16,24},{24,16},{1,9},{9,1},{17,25},{25,17},{2,10},{10... | collective-permute-start | bytes 405512 | tf_op jit(solution)/shard_map/ppermute | solution.py:287
  20.5 2.2 %collective-permute-done.6.refs_3_ = bf16[16,4224]{1,0:T(8,128)(2,1)S(1)} collective-permute-done((bf16[16,4224]{1,0:T(8,128)(2,1)S(1)}, bf16[16,4224]{1,0:T(8,128)(2,1)S(1)}, u32[]{:S(2)}, u32[]{:S(2)}) %collective-permute-start.6) | collective-permute-done | bytes 135200 | tf_op jit(solution)/shard_map/ppermute | solution.py:282
  22.6 1.7 %collective-permute-done.5.refs_2_ = bf16[16,4224]{1,0:T(8,128)(2,1)S(1)} collective-permute-done((bf16[16,4224]{1,0:T(8,128)(2,1)S(1)}, bf16[16,4224]{1,0:T(8,128)(2,1)S(1)}, u32[]{:S(2)}, u32[]{:S(2)}) %collective-permute-start.5) | collective-permute-done | bytes 135200 | tf_op jit(solution)/shard_map/ppermute | solution.py:282
  24.4 1.6 %collective-permute-done.8.refs_1_ = bf16[16,4224]{1,0:T(8,128)(2,1)S(1)} collective-permute-done((bf16[16,4224]{1,0:T(8,128)(2,1)S(1)}, bf16[16,4224]{1,0:T(8,128)(2,1)S(1)}, u32[]{:S(2)}, u32[]{:S(2)}) %collective-permute-start.8) | collective-permute-done | bytes 135200 | tf_op jit(solution)/shard_map/ppermute | solution.py:287
  26.1 1.0 %collective-permute-start.14 = (bf16[16,4224]{1,0:T(8,128)(2,1)S(1)}, bf16[16,4224]{1,0:T(8,128)(2,1)S(1)}, u32[]{:S(2)}, u32[]{:S(2)}) collective-permute-start(bf16[16,4224]{1,0:T(8,128)(2,1)S(1)} %collective-permute-done.2.refs_3_), channel_id=1, source_target_pairs={{0,16},{8,24},{16,0},{24,8},{1,17},{9,25},{17,1},{25,9},{2,18},{10... | collective-permute-start | bytes 405512 | tf_op jit(solution)/shard_map/ppermute | solution.py:287
  27.1 1.1 %collective-permute-start.13 = (bf16[16,4224]{1,0:T(8,128)(2,1)S(1)}, bf16[16,4224]{1,0:T(8,128)(2,1)S(1)}, u32[]{:S(2)}, u32[]{:S(2)}) collective-permute-start(bf16[16,4224]{1,0:T(8,128)(2,1)S(1)} %collective-permute-done.2.refs_3_), channel_id=1, source_target_pairs={{0,8},{8,0},{16,24},{24,16},{1,9},{9,1},{17,25},{25,17},{2,10},{10... | collective-permute-start | bytes 405512 | tf_op jit(solution)/shard_map/ppermute | solution.py:287
  28.3 1.6 %collective-permute-start.12 = (bf16[32,4224]{1,0:T(8,128)(2,1)S(1)}, bf16[32,4224]{1,0:T(8,128)(2,1)S(1)}, u32[]{:S(2)}, u32[]{:S(2)}) collective-permute-start(bf16[32,4224]{1,0:T(8,128)(2,1)S(1)} %gather.5.refs_1_), channel_id=1, source_target_pairs={{0,4},{1,5},{2,6},{3,7},{4,0},{5,1},{6,2},{7,3},{8,12},{9,13},{10,... | collective-permute-start | bytes 811016 | tf_op jit(solution)/shard_map/ppermute | solution.py:282
  30.2 5.7 %experts.2 = (bf16[32,4096]{1,0:T(8,128)(2,1)S(1)}, bf16[32,4096]{1,0:T(8,128)(2,1)S(1)}, bf16[16,4096]{1,0:T(8,128)(2,1)S(1)}, bf16[80,4096]{1,0:T(8,128)(2,1)S...) custom-call(s32[1]{0:T(128)} %begin.1.refs_0_, bf16[64,4224]{1,0:T(8,128)(2,1)S(1)} %gather.3.refs_1_, ...), custom_call_target="tpu_custom_call" | custom-call | flops 4831838208 | bytes 4194304 | tf_op jit(solution)/shard_map/experts/pallas_call | solution.py:197
  36.7 1.3 %collective-permute-done.11.refs_2_ = bf16[32,4224]{1,0:T(8,128)(2,1)S(1)} collective-permute-done((bf16[32,4224]{1,0:T(8,128)(2,1)S(1)}, bf16[32,4224]{1,0:T(8,128)(2,1)S(1)}, u32[]{:S(2)}, u32[]{:S(2)}) %collective-permute-start.11) | collective-permute-done | bytes 270368 | tf_op jit(solution)/shard_map/ppermute | solution.py:282
  39.0 1.1 %collective-permute-done.15 = bf16[80,4096]{1,0:T(8,128)(2,1)S(1)} collective-permute-done((bf16[80,4096]{1,0:T(8,128)(2,1)S(1)}, bf16[80,4096]{1,0:T(8,128)(2,1)S(1)}, u32[]{:S(2)}, u32[]{:S(2)}) %collective-permute-start.15) | collective-permute-done | bytes 655392 | tf_op jit(solution)/shard_map/ppermute | solution.py:282
  40.4 1.4 %collective-permute-start.24 = (bf16[16,4096]{1,0:T(8,128)(2,1)S(1)}, bf16[16,4096]{1,0:T(8,128)(2,1)S(1)}, u32[]{:S(2)}, u32[]{:S(2)}) collective-permute-start(bf16[16,4096]{1,0:T(8,128)(2,1)S(1)} %add_convert_fusion.8), channel_id=1, source_target_pairs={{0,6},{1,7},{2,4},{3,5},{4,2},{5,3},{6,0},{7,1},{8,14},{9,15},{10,... | collective-permute-start | bytes 393224 | tf_op jit(solution)/shard_map/ppermute | solution.py:282
  42.4 1.6 %collective-permute-start.23 = (bf16[32,4096]{1,0:T(8,128)(2,1)S(1)}, bf16[32,4096]{1,0:T(8,128)(2,1)S(1)}, u32[]{:S(2)}, u32[]{:S(2)}) collective-permute-start(bf16[32,4096]{1,0:T(8,128)(2,1)S(1)} %get-tuple-element.92), channel_id=1, source_target_pairs={{0,4},{1,5},{2,6},{3,7},{4,0},{5,1},{6,2},{7,3},{8,12},{9,13},{10,... | collective-permute-start | bytes 786440 | tf_op jit(solution)/shard_map/ppermute | solution.py:282
  44.0 5.7 %experts.3 = (bf16[16,4096]{1,0:T(8,128)(2,1)S(1)}, bf16[16,4096]{1,0:T(8,128)(2,1)S(1)}, bf16[32,4096]{1,0:T(8,128)(2,1)S(1)}, bf16[32,4096]{1,0:T(8,128)(2,1)S...) custom-call(s32[1]{0:T(128)} %begin.1.refs_0_, ...), custom_call_target="tpu_custom_call" | custom-call | flops 4831838208 | bytes 4194304 | tf_op jit(solution)/shard_map/experts/pallas_call | solution.py:197
  50.3 1.4 %collective-permute-done.22 = bf16[32,4096]{1,0:T(8,128)(2,1)S(1)} collective-permute-done((bf16[32,4096]{1,0:T(8,128)(2,1)S(1)}, bf16[32,4096]{1,0:T(8,128)(2,1)S(1)}, u32[]{:S(2)}, u32[]{:S(2)}) %collective-permute-start.22) | collective-permute-done | bytes 262176 | tf_op jit(solution)/shard_map/ppermute | solution.py:282
  51.7 1.0 %collective-permute-done.23 = bf16[32,4096]{1,0:T(8,128)(2,1)S(1)} collective-permute-done((bf16[32,4096]{1,0:T(8,128)(2,1)S(1)}, bf16[32,4096]{1,0:T(8,128)(2,1)S(1)}, u32[]{:S(2)}, u32[]{:S(2)}) %collective-permute-start.23) | collective-permute-done | bytes 262176 | tf_op jit(solution)/shard_map/ppermute | solution.py:282
  53.2 1.5 %collective-permute-start.33 = (bf16[16,4096]{1,0:T(8,128)(2,1)S(1)}, bf16[16,4096]{1,0:T(8,128)(2,1)S(1)}, u32[]{:S(2)}, u32[]{:S(2)}) collective-permute-start(bf16[16,4096]{1,0:T(8,128)(2,1)S(1)} %add_convert_fusion.7), channel_id=1, source_target_pairs={{0,6},{1,7},{2,4},{3,5},{4,2},{5,3},{6,0},{7,1},{8,14},{9,15},{10,... | collective-permute-start | bytes 393224 | tf_op jit(solution)/shard_map/ppermute | solution.py:282
  55.3 1.4 %collective-permute-start.31 = (bf16[32,4096]{1,0:T(8,128)(2,1)S(1)}, bf16[32,4096]{1,0:T(8,128)(2,1)S(1)}, u32[]{:S(2)}, u32[]{:S(2)}) collective-permute-start(bf16[32,4096]{1,0:T(8,128)(2,1)S(1)} %get-tuple-element.123), channel_id=1, source_target_pairs={{0,4},{1,5},{2,6},{3,7},{4,0},{5,1},{6,2},{7,3},{8,12},{9,13},{10,... | collective-permute-start | bytes 786440 | tf_op jit(solution)/shard_map/ppermute | solution.py:282
  56.8 2.2 %collective-permute-start.27 = (bf16[16,4096]{1,0:T(8,128)(2,1)S(1)}, bf16[16,4096]{1,0:T(8,128)(2,1)S(1)}, u32[]{:S(2)}, u32[]{:S(2)}) collective-permute-start(bf16[16,4096]{1,0:T(8,128)(2,1)S(1)} %fusion.3), channel_id=1, source_target_pairs={{0,24},{8,16},{16,8},{24,0},{1,25},{9,17},{17,9},{25,1},{2,26},{10... | collective-permute-start | bytes 393224 | tf_op jit(solution)/shard_map/ppermute | solution.py:287
  59.0 1.4 %collective-permute-done.33 = bf16[16,4096]{1,0:T(8,128)(2,1)S(1)} collective-permute-done((bf16[16,4096]{1,0:T(8,128)(2,1)S(1)}, bf16[16,4096]{1,0:T(8,128)(2,1)S(1)}, u32[]{:S(2)}, u32[]{:S(2)}) %collective-permute-start.33) | collective-permute-done | bytes 131104 | tf_op jit(solution)/shard_map/ppermute | solution.py:282
  60.5 4.3 %collective-permute-done.30 = bf16[32,4096]{1,0:T(8,128)(2,1)S(1)} collective-permute-done((bf16[32,4096]{1,0:T(8,128)(2,1)S(1)}, bf16[32,4096]{1,0:T(8,128)(2,1)S(1)}, u32[]{:S(2)}, u32[]{:S(2)}) %collective-permute-start.30) | collective-permute-done | bytes 262176 | tf_op jit(solution)/shard_map/ppermute | solution.py:282
  64.8 0.9 %collective-permute-done.31 = bf16[32,4096]{1,0:T(8,128)(2,1)S(1)} collective-permute-done((bf16[32,4096]{1,0:T(8,128)(2,1)S(1)}, bf16[32,4096]{1,0:T(8,128)(2,1)S(1)}, u32[]{:S(2)}, u32[]{:S(2)}) %collective-permute-start.31) | collective-permute-done | bytes 262176 | tf_op jit(solution)/shard_map/ppermute | solution.py:282
  66.6 2.0 %collective-permute-start.34 = (bf16[16,4096]{1,0:T(8,128)(2,1)S(1)}, bf16[16,4096]{1,0:T(8,128)(2,1)S(1)}, u32[]{:S(2)}, u32[]{:S(2)}) collective-permute-start(bf16[16,4096]{1,0:T(8,128)(2,1)S(1)} %get-tuple-element.126), channel_id=1, source_target_pairs={{0,16},{8,24},{16,0},{24,8},{1,17},{9,25},{17,1},{25,9},{2,18},{10... | collective-permute-start | bytes 393224 | tf_op jit(solution)/shard_map/ppermute | solution.py:287
  68.7 1.5 %collective-permute-start.29 = (bf16[16,4096]{1,0:T(8,128)(2,1)S(1)}, bf16[16,4096]{1,0:T(8,128)(2,1)S(1)}, u32[]{:S(2)}, u32[]{:S(2)}) collective-permute-start(bf16[16,4096]{1,0:T(8,128)(2,1)S(1)} %fusion), channel_id=1, source_target_pairs={{0,6},{1,7},{2,4},{3,5},{4,2},{5,3},{6,0},{7,1},{8,14},{9,15},{10,... | collective-permute-start | bytes 393224 | tf_op jit(solution)/shard_map/ppermute | solution.py:282
  70.2 3.0 %collective-permute-done.32 = bf16[16,4096]{1,0:T(8,128)(2,1)S(1)} collective-permute-done((bf16[16,4096]{1,0:T(8,128)(2,1)S(1)}, bf16[16,4096]{1,0:T(8,128)(2,1)S(1)}, u32[]{:S(2)}, u32[]{:S(2)}) %collective-permute-start.32) | collective-permute-done | bytes 131104 | tf_op jit(solution)/shard_map/ppermute | solution.py:287
  73.2 2.3 %collective-permute-done.34 = bf16[16,4096]{1,0:T(8,128)(2,1)S(1)} collective-permute-done((bf16[16,4096]{1,0:T(8,128)(2,1)S(1)}, bf16[16,4096]{1,0:T(8,128)(2,1)S(1)}, u32[]{:S(2)}, u32[]{:S(2)}) %collective-permute-start.34) | collective-permute-done | bytes 131104 | tf_op jit(solution)/shard_map/ppermute | solution.py:287
  (76 shorter events, 10.2 us)
Async XLA Ops:
  1.2 12.8 %collective-permute-start.3 = (bf16[16,4224]{1,0:T(8,128)(2,1)S(1)}, bf16[16,4224]{1,0:T(8,128)(2,1)S(1)}, u32[]{:S(2)}, u32[]{:S(2)}) collective-permute-start(bf16[16,4224]{1,0:T(8,128)(2,1)S(1)} %pack.1.refs_0_), channel_id=1, source_target_pairs={{0,24},{8,16},{16,8},{24,0},{1,25},{9,17},{17,9},{25,1},{2,26},{10... | collective-permute-start | bytes 405512 | tf_op jit(solution)/shard_map/ppermute | solution.py:287
  6.3 7.7 %collective-permute-start.2 = (bf16[16,4224]{1,0:T(8,128)(2,1)S(1)}, bf16[16,4224]{1,0:T(8,128)(2,1)S(1)}, u32[]{:S(2)}, u32[]{:S(2)}) collective-permute-start(bf16[16,4224]{1,0:T(8,128)(2,1)S(1)} %pack.1.refs_0_), channel_id=1, source_target_pairs={{0,6},{1,7},{2,4},{3,5},{4,2},{5,3},{6,0},{7,1},{8,14},{9,15},{10,... | collective-permute-start | bytes 405512 | tf_op jit(solution)/shard_map/ppermute | solution.py:282
  8.8 6.4 %collective-permute-start.1 = (bf16[16,4224]{1,0:T(8,128)(2,1)S(1)}, bf16[16,4224]{1,0:T(8,128)(2,1)S(1)}, u32[]{:S(2)}, u32[]{:S(2)}) collective-permute-start(bf16[16,4224]{1,0:T(8,128)(2,1)S(1)} %pack.1.refs_0_), channel_id=1, source_target_pairs={{0,4},{1,5},{2,6},{3,7},{4,0},{5,1},{6,2},{7,3},{8,12},{9,13},{10,... | collective-permute-start | bytes 405512 | tf_op jit(solution)/shard_map/ppermute | solution.py:282
  9.3 5.9 %collective-permute-start = (bf16[16,4224]{1,0:T(8,128)(2,1)S(1)}, bf16[16,4224]{1,0:T(8,128)(2,1)S(1)}, u32[]{:S(2)}, u32[]{:S(2)}) collective-permute-start(bf16[16,4224]{1,0:T(8,128)(2,1)S(1)} %pack.1.refs_0_), channel_id=1, source_target_pairs={{0,2},{1,3},{2,0},{3,1},{4,6},{5,7},{6,4},{7,5},{8,10},{9,11},{10,... | collective-permute-start | bytes 405512 | tf_op jit(solution)/shard_map/ppermute | solution.py:282
  15.2 7.4 %collective-permute-start.6 = (bf16[16,4224]{1,0:T(8,128)(2,1)S(1)}, bf16[16,4224]{1,0:T(8,128)(2,1)S(1)}, u32[]{:S(2)}, u32[]{:S(2)}) collective-permute-start(bf16[16,4224]{1,0:T(8,128)(2,1)S(1)} %collective-permute-done.3.refs_0_), channel_id=1, source_target_pairs={{0,6},{1,7},{2,4},{3,5},{4,2},{5,3},{6,0},{7,1},{8,14},{9,15},{10,... | collective-permute-start | bytes 405512 | tf_op jit(solution)/shard_map/ppermute | solution.py:282
  16.9 7.4 %collective-permute-start.5 = (bf16[16,4224]{1,0:T(8,128)(2,1)S(1)}, bf16[16,4224]{1,0:T(8,128)(2,1)S(1)}, u32[]{:S(2)}, u32[]{:S(2)}) collective-permute-start(bf16[16,4224]{1,0:T(8,128)(2,1)S(1)} %collective-permute-done.3.refs_0_), channel_id=1, source_target_pairs={{0,4},{1,5},{2,6},{3,7},{4,0},{5,1},{6,2},{7,3},{8,12},{9,13},{10,... | collective-permute-start | bytes 405512 | tf_op jit(solution)/shard_map/ppermute | solution.py:282
  18.2 6.1 %collective-permute-start.4 = (bf16[16,4224]{1,0:T(8,128)(2,1)S(1)}, bf16[16,4224]{1,0:T(8,128)(2,1)S(1)}, u32[]{:S(2)}, u32[]{:S(2)}) collective-permute-start(bf16[16,4224]{1,0:T(8,128)(2,1)S(1)} %collective-permute-done.3.refs_0_), channel_id=1, source_target_pairs={{0,2},{1,3},{2,0},{3,1},{4,6},{5,7},{6,4},{7,5},{8,10},{9,11},{10,... | collective-permute-start | bytes 405512 | tf_op jit(solution)/shard_map/ppermute | solution.py:282
  18.7 7.3 %collective-permute-start.8 = (bf16[16,4224]{1,0:T(8,128)(2,1)S(1)}, bf16[16,4224]{1,0:T(8,128)(2,1)S(1)}, u32[]{:S(2)}, u32[]{:S(2)}) collective-permute-start(bf16[16,4224]{1,0:T(8,128)(2,1)S(1)} %pack.1.refs_0_), channel_id=1, source_target_pairs={{0,16},{8,24},{16,0},{24,8},{1,17},{9,25},{17,1},{25,9},{2,18},{10... | collective-permute-start | bytes 405512 | tf_op jit(solution)/shard_map/ppermute | solution.py:287
  18.7 7.4 %collective-permute-start.7 = (bf16[16,4224]{1,0:T(8,128)(2,1)S(1)}, bf16[16,4224]{1,0:T(8,128)(2,1)S(1)}, u32[]{:S(2)}, u32[]{:S(2)}) collective-permute-start(bf16[16,4224]{1,0:T(8,128)(2,1)S(1)} %pack.1.refs_0_), channel_id=1, source_target_pairs={{0,8},{8,0},{16,24},{24,16},{1,9},{9,1},{17,25},{25,17},{2,10},{10... | collective-permute-start | bytes 405512 | tf_op jit(solution)/shard_map/ppermute | solution.py:287
  22.6 7.3 %collective-permute-start.9 = (bf16[64,4224]{1,0:T(8,128)(2,1)S(1)}, bf16[64,4224]{1,0:T(8,128)(2,1)S(1)}, u32[]{:S(2)}, u32[]{:S(2)}) collective-permute-start(bf16[64,4224]{1,0:T(8,128)(2,1)S(1)} %gather.3.refs_1_), channel_id=1, source_target_pairs={{0,1},{1,0},{2,3},{3,2},{4,5},{5,4},{6,7},{7,6},{8,9},{9,8},{10,11... | collective-permute-start | bytes 1622024 | tf_op jit(solution)/shard_map/ppermute | solution.py:282
  26.1 4.1 %collective-permute-start.10 = (bf16[64,4224]{1,0:T(8,128)(2,1)S(1)}, bf16[64,4224]{1,0:T(8,128)(2,1)S(1)}, u32[]{:S(2)}, u32[]{:S(2)}) collective-permute-start(bf16[64,4224]{1,0:T(8,128)(2,1)S(1)} %gather.4.refs_2_), channel_id=1, source_target_pairs={{0,1},{1,0},{2,3},{3,2},{4,5},{5,4},{6,7},{7,6},{8,9},{9,8},{10,11... | collective-permute-start | bytes 1622024 | tf_op jit(solution)/shard_map/ppermute | solution.py:282
  26.1 9.8 %collective-permute-start.14 = (bf16[16,4224]{1,0:T(8,128)(2,1)S(1)}, bf16[16,4224]{1,0:T(8,128)(2,1)S(1)}, u32[]{:S(2)}, u32[]{:S(2)}) collective-permute-start(bf16[16,4224]{1,0:T(8,128)(2,1)S(1)} %collective-permute-done.2.refs_3_), channel_id=1, source_target_pairs={{0,16},{8,24},{16,0},{24,8},{1,17},{9,25},{17,1},{25,9},{2,18},{10... | collective-permute-start | bytes 405512 | tf_op jit(solution)/shard_map/ppermute | solution.py:287
  27.1 8.9 %collective-permute-start.13 = (bf16[16,4224]{1,0:T(8,128)(2,1)S(1)}, bf16[16,4224]{1,0:T(8,128)(2,1)S(1)}, u32[]{:S(2)}, u32[]{:S(2)}) collective-permute-start(bf16[16,4224]{1,0:T(8,128)(2,1)S(1)} %collective-permute-done.2.refs_3_), channel_id=1, source_target_pairs={{0,8},{8,0},{16,24},{24,16},{1,9},{9,1},{17,25},{25,17},{2,10},{10... | collective-permute-start | bytes 405512 | tf_op jit(solution)/shard_map/ppermute | solution.py:287
  28.3 8.4 %collective-permute-start.12 = (bf16[32,4224]{1,0:T(8,128)(2,1)S(1)}, bf16[32,4224]{1,0:T(8,128)(2,1)S(1)}, u32[]{:S(2)}, u32[]{:S(2)}) collective-permute-start(bf16[32,4224]{1,0:T(8,128)(2,1)S(1)} %gather.5.refs_1_), channel_id=1, source_target_pairs={{0,4},{1,5},{2,6},{3,7},{4,0},{5,1},{6,2},{7,3},{8,12},{9,13},{10,... | collective-permute-start | bytes 811016 | tf_op jit(solution)/shard_map/ppermute | solution.py:282
  29.9 8.1 %collective-permute-start.11 = (bf16[32,4224]{1,0:T(8,128)(2,1)S(1)}, bf16[32,4224]{1,0:T(8,128)(2,1)S(1)}, u32[]{:S(2)}, u32[]{:S(2)}) collective-permute-start(bf16[32,4224]{1,0:T(8,128)(2,1)S(1)} %gather.5.refs_1_), channel_id=1, source_target_pairs={{0,2},{1,3},{2,0},{3,1},{4,6},{5,7},{6,4},{7,5},{8,10},{9,11},{10,... | collective-permute-start | bytes 811016 | tf_op jit(solution)/shard_map/ppermute | solution.py:282
  38.5 3.4 %collective-permute-start.20 = (bf16[16,4224]{1,0:T(8,128)(2,1)S(1)}, bf16[16,4224]{1,0:T(8,128)(2,1)S(1)}, u32[]{:S(2)}, u32[]{:S(2)}) collective-permute-start(bf16[16,4224]{1,0:T(8,128)(2,1)S(1)} %collective-permute-done.13.refs_4_), channel_id=1, source_target_pairs={{0,1},{1,0},{2,3},{3,2},{4,5},{5,4},{6,7},{7,6},{8,9},{9,8},{10,11... | collective-permute-start | bytes 405512 | tf_op jit(solution)/shard_map/ppermute | solution.py:282
  38.5 3.9 %collective-permute-start.21 = (bf16[16,4224]{1,0:T(8,128)(2,1)S(1)}, bf16[16,4224]{1,0:T(8,128)(2,1)S(1)}, u32[]{:S(2)}, u32[]{:S(2)}) collective-permute-start(bf16[16,4224]{1,0:T(8,128)(2,1)S(1)} %collective-permute-done.14.refs_5_), channel_id=1, source_target_pairs={{0,1},{1,0},{2,3},{3,2},{4,5},{5,4},{6,7},{7,6},{8,9},{9,8},{10,11... | collective-permute-start | bytes 405512 | tf_op jit(solution)/shard_map/ppermute | solution.py:282
  39.0 5.0 %collective-permute-start.18 = (bf16[32,4224]{1,0:T(8,128)(2,1)S(1)}, bf16[32,4224]{1,0:T(8,128)(2,1)S(1)}, u32[]{:S(2)}, u32[]{:S(2)}) collective-permute-start(bf16[32,4224]{1,0:T(8,128)(2,1)S(1)} %collective-permute-done.11.refs_2_), channel_id=1, source_target_pairs={{0,1},{1,0},{2,3},{3,2},{4,5},{5,4},{6,7},{7,6},{8,9},{9,8},{10,11... | collective-permute-start | bytes 811016 | tf_op jit(solution)/shard_map/ppermute | solution.py:282
  40.1 3.9 %collective-permute-start.19 = (bf16[32,4224]{1,0:T(8,128)(2,1)S(1)}, bf16[32,4224]{1,0:T(8,128)(2,1)S(1)}, u32[]{:S(2)}, u32[]{:S(2)}) collective-permute-start(bf16[32,4224]{1,0:T(8,128)(2,1)S(1)} %collective-permute-done.12.refs_3_), channel_id=1, source_target_pairs={{0,1},{1,0},{2,3},{3,2},{4,5},{5,4},{6,7},{7,6},{8,9},{9,8},{10,11... | collective-permute-start | bytes 811016 | tf_op jit(solution)/shard_map/ppermute | solution.py:282
  40.4 9.9 %collective-permute-start.24 = (bf16[16,4096]{1,0:T(8,128)(2,1)S(1)}, bf16[16,4096]{1,0:T(8,128)(2,1)S(1)}, u32[]{:S(2)}, u32[]{:S(2)}) collective-permute-start(bf16[16,4096]{1,0:T(8,128)(2,1)S(1)} %add_convert_fusion.8), channel_id=1, source_target_pairs={{0,6},{1,7},{2,4},{3,5},{4,2},{5,3},{6,0},{7,1},{8,14},{9,15},{10,... | collective-permute-start | bytes 393224 | tf_op jit(solution)/shard_map/ppermute | solution.py:282
  41.9 9.9 %collective-permute-start.22 = (bf16[32,4096]{1,0:T(8,128)(2,1)S(1)}, bf16[32,4096]{1,0:T(8,128)(2,1)S(1)}, u32[]{:S(2)}, u32[]{:S(2)}) collective-permute-start(bf16[32,4096]{1,0:T(8,128)(2,1)S(1)} %get-tuple-element.91), channel_id=1, source_target_pairs={{0,2},{1,3},{2,0},{3,1},{4,6},{5,7},{6,4},{7,5},{8,10},{9,11},{10,... | collective-permute-start | bytes 786440 | tf_op jit(solution)/shard_map/ppermute | solution.py:282
  42.4 10.3 %collective-permute-start.23 = (bf16[32,4096]{1,0:T(8,128)(2,1)S(1)}, bf16[32,4096]{1,0:T(8,128)(2,1)S(1)}, u32[]{:S(2)}, u32[]{:S(2)}) collective-permute-start(bf16[32,4096]{1,0:T(8,128)(2,1)S(1)} %get-tuple-element.92), channel_id=1, source_target_pairs={{0,4},{1,5},{2,6},{3,7},{4,0},{5,1},{6,2},{7,3},{8,12},{9,13},{10,... | collective-permute-start | bytes 786440 | tf_op jit(solution)/shard_map/ppermute | solution.py:282
  44.0 8.8 %collective-permute-start.16 = (bf16[48,4096]{1,0:T(8,128)(2,1)S(1)}, bf16[48,4096]{1,0:T(8,128)(2,1)S(1)}, u32[]{:S(2)}, u32[]{:S(2)}) collective-permute-start(bf16[48,4096]{1,0:T(8,128)(2,1)S(1)} %get-tuple-element.90), channel_id=1, source_target_pairs={{0,1},{1,0},{2,3},{3,2},{4,5},{5,4},{6,7},{7,6},{8,9},{9,8},{10,11... | collective-permute-start | bytes 1179656 | tf_op jit(solution)/shard_map/ppermute | solution.py:282
  53.0 3.7 %collective-permute-start.26 = (bf16[16,4096]{1,0:T(8,128)(2,1)S(1)}, bf16[16,4096]{1,0:T(8,128)(2,1)S(1)}, u32[]{:S(2)}, u32[]{:S(2)}) collective-permute-start(bf16[16,4096]{1,0:T(8,128)(2,1)S(1)} %get-tuple-element.118), channel_id=1, source_target_pairs={{0,1},{1,0},{2,3},{3,2},{4,5},{5,4},{6,7},{7,6},{8,9},{9,8},{10,11... | collective-permute-start | bytes 393224 | tf_op jit(solution)/shard_map/ppermute | solution.py:282
  53.2 7.3 %collective-permute-start.33 = (bf16[16,4096]{1,0:T(8,128)(2,1)S(1)}, bf16[16,4096]{1,0:T(8,128)(2,1)S(1)}, u32[]{:S(2)}, u32[]{:S(2)}) collective-permute-start(bf16[16,4096]{1,0:T(8,128)(2,1)S(1)} %add_convert_fusion.7), channel_id=1, source_target_pairs={{0,6},{1,7},{2,4},{3,5},{4,2},{5,3},{6,0},{7,1},{8,14},{9,15},{10,... | collective-permute-start | bytes 393224 | tf_op jit(solution)/shard_map/ppermute | solution.py:282
  54.6 10.1 %collective-permute-start.30 = (bf16[32,4096]{1,0:T(8,128)(2,1)S(1)}, bf16[32,4096]{1,0:T(8,128)(2,1)S(1)}, u32[]{:S(2)}, u32[]{:S(2)}) collective-permute-start(bf16[32,4096]{1,0:T(8,128)(2,1)S(1)} %get-tuple-element.122), channel_id=1, source_target_pairs={{0,2},{1,3},{2,0},{3,1},{4,6},{5,7},{6,4},{7,5},{8,10},{9,11},{10,... | collective-permute-start | bytes 786440 | tf_op jit(solution)/shard_map/ppermute | solution.py:282
  55.3 10.3 %collective-permute-start.31 = (bf16[32,4096]{1,0:T(8,128)(2,1)S(1)}, bf16[32,4096]{1,0:T(8,128)(2,1)S(1)}, u32[]{:S(2)}, u32[]{:S(2)}) collective-permute-start(bf16[32,4096]{1,0:T(8,128)(2,1)S(1)} %get-tuple-element.123), channel_id=1, source_target_pairs={{0,4},{1,5},{2,6},{3,7},{4,0},{5,1},{6,2},{7,3},{8,12},{9,13},{10,... | collective-permute-start | bytes 786440 | tf_op jit(solution)/shard_map/ppermute | solution.py:282
  56.8 13.4 %collective-permute-start.27 = (bf16[16,4096]{1,0:T(8,128)(2,1)S(1)}, bf16[16,4096]{1,0:T(8,128)(2,1)S(1)}, u32[]{:S(2)}, u32[]{:S(2)}) collective-permute-start(bf16[16,4096]{1,0:T(8,128)(2,1)S(1)} %fusion.3), channel_id=1, source_target_pairs={{0,24},{8,16},{16,8},{24,0},{1,25},{9,17},{17,9},{25,1},{2,26},{10... | collective-permute-start | bytes 393224 | tf_op jit(solution)/shard_map/ppermute | solution.py:287
  59.0 9.6 %collective-permute-start.28 = (bf16[16,4096]{1,0:T(8,128)(2,1)S(1)}, bf16[16,4096]{1,0:T(8,128)(2,1)S(1)}, u32[]{:S(2)}, u32[]{:S(2)}) collective-permute-start(bf16[16,4096]{1,0:T(8,128)(2,1)S(1)} %add_convert_fusion.6), channel_id=1, source_target_pairs={{0,8},{8,0},{16,24},{24,16},{1,9},{9,1},{17,25},{25,17},{2,10},{10... | collective-permute-start | bytes 393224 | tf_op jit(solution)/shard_map/ppermute | solution.py:287
  65.8 7.4 %collective-permute-start.32 = (bf16[16,4096]{1,0:T(8,128)(2,1)S(1)}, bf16[16,4096]{1,0:T(8,128)(2,1)S(1)}, u32[]{:S(2)}, u32[]{:S(2)}) collective-permute-start(bf16[16,4096]{1,0:T(8,128)(2,1)S(1)} %get-tuple-element.125), channel_id=1, source_target_pairs={{0,8},{8,0},{16,24},{24,16},{1,9},{9,1},{17,25},{25,17},{2,10},{10... | collective-permute-start | bytes 393224 | tf_op jit(solution)/shard_map/ppermute | solution.py:287
  66.6 8.9 %collective-permute-start.34 = (bf16[16,4096]{1,0:T(8,128)(2,1)S(1)}, bf16[16,4096]{1,0:T(8,128)(2,1)S(1)}, u32[]{:S(2)}, u32[]{:S(2)}) collective-permute-start(bf16[16,4096]{1,0:T(8,128)(2,1)S(1)} %get-tuple-element.126), channel_id=1, source_target_pairs={{0,16},{8,24},{16,0},{24,8},{1,17},{9,25},{17,1},{25,9},{2,18},{10... | collective-permute-start | bytes 393224 | tf_op jit(solution)/shard_map/ppermute | solution.py:287
  68.7 6.9 %collective-permute-start.29 = (bf16[16,4096]{1,0:T(8,128)(2,1)S(1)}, bf16[16,4096]{1,0:T(8,128)(2,1)S(1)}, u32[]{:S(2)}, u32[]{:S(2)}) collective-permute-start(bf16[16,4096]{1,0:T(8,128)(2,1)S(1)} %fusion), channel_id=1, source_target_pairs={{0,6},{1,7},{2,4},{3,5},{4,2},{5,3},{6,0},{7,1},{8,14},{9,15},{10,... | collective-permute-start | bytes 393224 | tf_op jit(solution)/shard_map/ppermute | solution.py:282
  (11 other events, 59.5 us)

commit v8 on v7

--- a/solution.py
+++ b/solution.py
@@ -272,7 +272,9 @@
         out_shape=jax.ShapeDtypeStruct((1,), jnp.int32),
         in_specs=[scalar] + [pl.BlockSpec(memory_space=pl.ANY)] * 3,
         out_specs=scalar,
-        compiler_params=pltpu.CompilerParams(vmem_limit_bytes=50 * 1024 * 1024),
+        compiler_params=pltpu.CompilerParams(
+            vmem_limit_bytes=50 * 1024 * 1024, has_side_effects=True
+        ),
         name="begin",
     )(own, *weights)
 
@@ -315,24 +317,26 @@
     up_weight = up_weight.reshape(units, model_width)
     down_weight = down_weight.reshape(units, model_width)
     own = jnp.full((1,), lax.axis_index("exp") * local_experts, jnp.int32)
-    own = begun(own, gate_weight, up_weight, down_weight)
-    tokens, own = ordered(tokens, own)
+    begin = begun(own, gate_weight, up_weight, down_weight)
+    tokens, own, begin = ordered(tokens, own, begin)
     packed = with_routing(tokens, routed_experts, route_weights)
 
     three = swap_rep(packed, 3)
     x_own, y_own, far_own = [swap_exp(packed, bits) for bits in (2, 4, 6)]
     gates, ups = fetched(gate_weight, True), fetched(up_weight, True)
-    x_own, y_own, far_own, three, gates, ups, again = ordered(
-        x_own, y_own, far_own, three, gates, ups, packed
-    )
-    one, two = swap_rep(again, 1), swap_rep(again, 2)
+    one = swap_rep(packed, 1)
+    x_own, y_own, far_own, one, three, gates, ups, again = ordered(
+        x_own, y_own, far_own, one, three, gates, ups, packed
+    )
+    two = swap_rep(again, 2)
     x_three, y_three, far_three = [swap_exp(three, bits) for bits in (2, 4, 6)]
     far_one, far_two = swap_rep(far_own, 1), swap_rep(far_own, 2)
     first = gathered(packed, x_own, y_own, far_own)
     first_other = swap_exp(first, 1)
     second = gathered(three, x_three, y_three, far_three)
+    two, down_weight = ordered(two, down_weight)
     downs = fetched(down_weight, False)
-    second, downs, one, two = ordered(second, downs, one, two)
+    second, downs = ordered(second, downs)
     pair = gathered(one, two)
     x_pair, y_pair = swap_exp(pair, 2), swap_exp(pair, 4)
 

time: 76.4 us -> 76.5 us (level)
  waiting for transfers between devices: 24.4 us -> 26.5 us
  Pallas kernels: 17.3 us -> 16 us
  starting transfers between devices: 32.5 us -> 31.7 us
    ppermute x9, waiting for transfers between devices: 7.02 us -> 11.1 us  [swap_rep(): return lax.ppermute(value, 'rep', [(i, i ^ bits) for i in range(replicas)])]
    ppermute x26, waiting for transfers between devices: 17.4 us -> 15.4 us  [swap_exp(): return lax.ppermute(value, 'exp', [(i, i ^ bits) for i in range(owners)])]
    pallas_call x2, Pallas kernels: 11.5 us -> 10.2 us  [experts_of(): pl.pallas_call(kernel, out_shape=[jax.ShapeDtypeStruct((count, model_widt...]
    ppermute x9, starting transfers between devices: 13.2 us -> 12.1 us  [swap_rep(): return lax.ppermute(value, 'rep', [(i, i ^ bits) for i in range(replicas)])]
  transfers between devices with their start and end apart: 35 -> 35, of which waited for: 18 -> 14; matrix products, arithmetic and copies ran while one was open for 1% -> 1% of each run, Pallas kernels for 22% -> 20%
where the time goes in v8:
time: 76.5 us; the launch traced here: 76.3 us
  starting transfers between devices  31.7 us (41%)
  waiting for transfers between devices  26.5 us (35%)
  Pallas kernels  16 us (21%)
  other arithmetic  1.47 us (2%)
    ppermute x26, starting transfers between devices, swap_exp(): return lax.ppermute(value, 'exp', [(i, i ^ bits) for i in range(owners)])  19.6 us
    ppermute x26, waiting for transfers between devices, swap_exp(): return lax.ppermute(value, 'exp', [(i, i ^ bits) for i in range(owners)])  15.4 us
    ppermute x9, starting transfers between devices, swap_rep(): return lax.ppermute(value, 'rep', [(i, i ^ bits) for i in range(replicas)])  12.1 us
    ppermute x9, waiting for transfers between devices, swap_rep(): return lax.ppermute(value, 'rep', [(i, i ^ bits) for i in range(replicas)])  11.1 us
    pallas_call x2, Pallas kernels, experts_of(): pl.pallas_call(kernel, out_shape=[jax.ShapeDtypeStruct((count, model_widt...  10.2 us
    pallas_call x3, Pallas kernels, fetched(): pl.pallas_call(functools.partial(fetch_kernel, turn), out_shape=jax.Shape...  4.88 us
  transfers between devices with their start and end apart: 35, of which 14 were waited for; matrix products, arithmetic and copies ran while one was open for 1% of the time, Pallas kernels for 20%

profile of v8, /device:TPU:0, one launch (start us, length us, event | category | flops | bytes accessed | tf_op | source)
XLA Modules:
  0.0 76.3 jit_solution(6421323054779843352)
XLA Ops:
  1.2 5.1 %collective-permute-start.4 = (bf16[16,4224]{1,0:T(8,128)(2,1)S(1)}, bf16[16,4224]{1,0:T(8,128)(2,1)S(1)}, u32[]{:S(2)}, u32[]{:S(2)}) collective-permute-start(bf16[16,4224]{1,0:T(8,128)(2,1)S(1)} %pack.1.refs_0_), channel_id=1, source_target_pairs={{0,24},{8,16},{16,8},{24,0},{1,25},{9,17},{17,9},{25,1},{2,26},{10... | collective-permute-start | bytes 405512 | tf_op jit(solution)/shard_map/ppermute | solution.py:289
  6.3 2.4 %collective-permute-start.2 = (bf16[16,4224]{1,0:T(8,128)(2,1)S(1)}, bf16[16,4224]{1,0:T(8,128)(2,1)S(1)}, u32[]{:S(2)}, u32[]{:S(2)}) collective-permute-start(bf16[16,4224]{1,0:T(8,128)(2,1)S(1)} %pack.1.refs_0_), channel_id=1, source_target_pairs={{0,6},{1,7},{2,4},{3,5},{4,2},{5,3},{6,0},{7,1},{8,14},{9,15},{10,... | collective-permute-start | bytes 405512 | tf_op jit(solution)/shard_map/ppermute | solution.py:284
  9.8 2.1 %fetch_turned.2.refs_5_.refs_11_ = bf16[4096,768]{1,0:T(8,128)(2,1)S(1)} custom-call(bf16[768,4096]{1,0:T(8,128)(2,1)S(1)} %bitcast.7), custom_call_target="tpu_custom_call" | custom-call | bytes 12582912 | tf_op jit(solution)/shard_map/fetch_turned/pallas_call | solution.py:103
  12.0 2.1 %fetch_turned.3.refs_6_.refs_12_ = bf16[4096,768]{1,0:T(8,128)(2,1)S(1)} custom-call(bf16[768,4096]{1,0:T(8,128)(2,1)S(1)} %bitcast.11), custom_call_target="tpu_custom_call" | custom-call | bytes 12582912 | tf_op jit(solution)/shard_map/fetch_turned/pallas_call | solution.py:103
  14.1 1.1 %collective-permute-done.1.refs_2_ = bf16[16,4224]{1,0:T(8,128)(2,1)S(1)} collective-permute-done((bf16[16,4224]{1,0:T(8,128)(2,1)S(1)}, bf16[16,4224]{1,0:T(8,128)(2,1)S(1)}, u32[]{:S(2)}, u32[]{:S(2)}) %collective-permute-start.1) | collective-permute-done | bytes 135200 | tf_op jit(solution)/shard_map/ppermute | solution.py:284
  15.9 1.7 %collective-permute-start.7 = (bf16[16,4224]{1,0:T(8,128)(2,1)S(1)}, bf16[16,4224]{1,0:T(8,128)(2,1)S(1)}, u32[]{:S(2)}, u32[]{:S(2)}) collective-permute-start(bf16[16,4224]{1,0:T(8,128)(2,1)S(1)} %collective-permute-done.4.refs_0_), channel_id=1, source_target_pairs={{0,6},{1,7},{2,4},{3,5},{4,2},{5,3},{6,0},{7,1},{8,14},{9,15},{10,... | collective-permute-start | bytes 405512 | tf_op jit(solution)/shard_map/ppermute | solution.py:284
  17.6 1.3 %collective-permute-start.6 = (bf16[16,4224]{1,0:T(8,128)(2,1)S(1)}, bf16[16,4224]{1,0:T(8,128)(2,1)S(1)}, u32[]{:S(2)}, u32[]{:S(2)}) collective-permute-start(bf16[16,4224]{1,0:T(8,128)(2,1)S(1)} %collective-permute-done.4.refs_0_), channel_id=1, source_target_pairs={{0,4},{1,5},{2,6},{3,7},{4,0},{5,1},{6,2},{7,3},{8,12},{9,13},{10,... | collective-permute-start | bytes 405512 | tf_op jit(solution)/shard_map/ppermute | solution.py:284
  19.5 4.8 %collective-permute-done.8.refs_1_ = bf16[16,4224]{1,0:T(8,128)(2,1)S(1)} collective-permute-done((bf16[16,4224]{1,0:T(8,128)(2,1)S(1)}, bf16[16,4224]{1,0:T(8,128)(2,1)S(1)}, u32[]{:S(2)}, u32[]{:S(2)}) %collective-permute-start.8) | collective-permute-done | bytes 135200 | tf_op jit(solution)/shard_map/ppermute | solution.py:289
  24.3 0.8 fetch.1.refs_7_.refs_13_
  25.3 2.0 %collective-permute-start.14 = (bf16[16,4224]{1,0:T(8,128)(2,1)S(1)}, bf16[16,4224]{1,0:T(8,128)(2,1)S(1)}, u32[]{:S(2)}, u32[]{:S(2)}) collective-permute-start(bf16[16,4224]{1,0:T(8,128)(2,1)S(1)} %collective-permute-done.2.refs_3_), channel_id=1, source_target_pairs={{0,16},{8,24},{16,0},{24,8},{1,17},{9,25},{17,1},{25,9},{2,18},{10... | collective-permute-start | bytes 405512 | tf_op jit(solution)/shard_map/ppermute | solution.py:289
  27.2 1.4 %collective-permute-start.13 = (bf16[16,4224]{1,0:T(8,128)(2,1)S(1)}, bf16[16,4224]{1,0:T(8,128)(2,1)S(1)}, u32[]{:S(2)}, u32[]{:S(2)}) collective-permute-start(bf16[16,4224]{1,0:T(8,128)(2,1)S(1)} %collective-permute-done.2.refs_3_), channel_id=1, source_target_pairs={{0,8},{8,0},{16,24},{24,16},{1,9},{9,1},{17,25},{25,17},{2,10},{10... | collective-permute-start | bytes 405512 | tf_op jit(solution)/shard_map/ppermute | solution.py:289
  28.6 1.5 %collective-permute-start.12 = (bf16[32,4224]{1,0:T(8,128)(2,1)S(1)}, bf16[32,4224]{1,0:T(8,128)(2,1)S(1)}, u32[]{:S(2)}, u32[]{:S(2)}) collective-permute-start(bf16[32,4224]{1,0:T(8,128)(2,1)S(1)} %gather.5.refs_1_), channel_id=1, source_target_pairs={{0,4},{1,5},{2,6},{3,7},{4,0},{5,1},{6,2},{7,3},{8,12},{9,13},{10,... | collective-permute-start | bytes 811016 | tf_op jit(solution)/shard_map/ppermute | solution.py:284
  30.7 5.1 %experts.2 = (bf16[32,4096]{1,0:T(8,128)(2,1)S(1)}, bf16[32,4096]{1,0:T(8,128)(2,1)S(1)}, bf16[16,4096]{1,0:T(8,128)(2,1)S(1)}, bf16[80,4096]{1,0:T(8,128)(2,1)S...) custom-call(s32[1]{0:T(128)} %bitcast.own_ref.refs_0_, bf16[64,4224]{1,0:T(8,128)(2,1)S(1)} %gather.3.refs_1_, ...), custom_call_target="tpu_custom_call" | custom-call | flops 4831838208 | bytes 4194304 | tf_op jit(solution)/shard_map/experts/pallas_call | solution.py:197
  35.9 1.1 %collective-permute-done.12.refs_3_ = bf16[32,4224]{1,0:T(8,128)(2,1)S(1)} collective-permute-done((bf16[32,4224]{1,0:T(8,128)(2,1)S(1)}, bf16[32,4224]{1,0:T(8,128)(2,1)S(1)}, u32[]{:S(2)}, u32[]{:S(2)}) %collective-permute-start.12) | collective-permute-done | bytes 270368 | tf_op jit(solution)/shard_map/ppermute | solution.py:284
  37.0 1.2 %collective-permute-done.11.refs_2_ = bf16[32,4224]{1,0:T(8,128)(2,1)S(1)} collective-permute-done((bf16[32,4224]{1,0:T(8,128)(2,1)S(1)}, bf16[32,4224]{1,0:T(8,128)(2,1)S(1)}, u32[]{:S(2)}, u32[]{:S(2)}) %collective-permute-start.11) | collective-permute-done | bytes 270368 | tf_op jit(solution)/shard_map/ppermute | solution.py:284
  39.2 1.1 %collective-permute-done.15 = bf16[80,4096]{1,0:T(8,128)(2,1)S(1)} collective-permute-done((bf16[80,4096]{1,0:T(8,128)(2,1)S(1)}, bf16[80,4096]{1,0:T(8,128)(2,1)S(1)}, u32[]{:S(2)}, u32[]{:S(2)}) %collective-permute-start.15) | collective-permute-done | bytes 655392 | tf_op jit(solution)/shard_map/ppermute | solution.py:284
  40.6 1.4 %collective-permute-start.24 = (bf16[16,4096]{1,0:T(8,128)(2,1)S(1)}, bf16[16,4096]{1,0:T(8,128)(2,1)S(1)}, u32[]{:S(2)}, u32[]{:S(2)}) collective-permute-start(bf16[16,4096]{1,0:T(8,128)(2,1)S(1)} %add_convert_fusion.8), channel_id=1, source_target_pairs={{0,6},{1,7},{2,4},{3,5},{4,2},{5,3},{6,0},{7,1},{8,14},{9,15},{10,... | collective-permute-start | bytes 393224 | tf_op jit(solution)/shard_map/ppermute | solution.py:284
  42.7 1.5 %collective-permute-start.23 = (bf16[32,4096]{1,0:T(8,128)(2,1)S(1)}, bf16[32,4096]{1,0:T(8,128)(2,1)S(1)}, u32[]{:S(2)}, u32[]{:S(2)}) collective-permute-start(bf16[32,4096]{1,0:T(8,128)(2,1)S(1)} %get-tuple-element.94), channel_id=1, source_target_pairs={{0,4},{1,5},{2,6},{3,7},{4,0},{5,1},{6,2},{7,3},{8,12},{9,13},{10,... | collective-permute-start | bytes 786440 | tf_op jit(solution)/shard_map/ppermute | solution.py:284
  44.2 5.1 %experts.3 = (bf16[16,4096]{1,0:T(8,128)(2,1)S(1)}, bf16[16,4096]{1,0:T(8,128)(2,1)S(1)}, bf16[32,4096]{1,0:T(8,128)(2,1)S(1)}, bf16[32,4096]{1,0:T(8,128)(2,1)S...) custom-call(s32[1]{0:T(128)} %bitcast.own_ref.refs_0_, ...), custom_call_target="tpu_custom_call" | custom-call | flops 4831838208 | bytes 4194304 | tf_op jit(solution)/shard_map/experts/pallas_call | solution.py:197
  49.9 2.2 %collective-permute-done.22 = bf16[32,4096]{1,0:T(8,128)(2,1)S(1)} collective-permute-done((bf16[32,4096]{1,0:T(8,128)(2,1)S(1)}, bf16[32,4096]{1,0:T(8,128)(2,1)S(1)}, u32[]{:S(2)}, u32[]{:S(2)}) %collective-permute-start.22) | collective-permute-done | bytes 262176 | tf_op jit(solution)/shard_map/ppermute | solution.py:284
  52.0 0.9 %collective-permute-done.23 = bf16[32,4096]{1,0:T(8,128)(2,1)S(1)} collective-permute-done((bf16[32,4096]{1,0:T(8,128)(2,1)S(1)}, bf16[32,4096]{1,0:T(8,128)(2,1)S(1)}, u32[]{:S(2)}, u32[]{:S(2)}) %collective-permute-start.23) | collective-permute-done | bytes 262176 | tf_op jit(solution)/shard_map/ppermute | solution.py:284
  53.4 1.5 %collective-permute-start.33 = (bf16[16,4096]{1,0:T(8,128)(2,1)S(1)}, bf16[16,4096]{1,0:T(8,128)(2,1)S(1)}, u32[]{:S(2)}, u32[]{:S(2)}) collective-permute-start(bf16[16,4096]{1,0:T(8,128)(2,1)S(1)} %add_convert_fusion.7), channel_id=1, source_target_pairs={{0,6},{1,7},{2,4},{3,5},{4,2},{5,3},{6,0},{7,1},{8,14},{9,15},{10,... | collective-permute-start | bytes 393224 | tf_op jit(solution)/shard_map/ppermute | solution.py:284
  55.5 1.4 %collective-permute-start.31 = (bf16[32,4096]{1,0:T(8,128)(2,1)S(1)}, bf16[32,4096]{1,0:T(8,128)(2,1)S(1)}, u32[]{:S(2)}, u32[]{:S(2)}) collective-permute-start(bf16[32,4096]{1,0:T(8,128)(2,1)S(1)} %get-tuple-element.125), channel_id=1, source_target_pairs={{0,4},{1,5},{2,6},{3,7},{4,0},{5,1},{6,2},{7,3},{8,12},{9,13},{10,... | collective-permute-start | bytes 786440 | tf_op jit(solution)/shard_map/ppermute | solution.py:284
  57.0 1.2 %collective-permute-start.27 = (bf16[16,4096]{1,0:T(8,128)(2,1)S(1)}, bf16[16,4096]{1,0:T(8,128)(2,1)S(1)}, u32[]{:S(2)}, u32[]{:S(2)}) collective-permute-start(bf16[16,4096]{1,0:T(8,128)(2,1)S(1)} %fusion.3), channel_id=1, source_target_pairs={{0,24},{8,16},{16,8},{24,0},{1,25},{9,17},{17,9},{25,1},{2,26},{10... | collective-permute-start | bytes 393224 | tf_op jit(solution)/shard_map/ppermute | solution.py:289
  58.2 2.5 %collective-permute-done.33 = bf16[16,4096]{1,0:T(8,128)(2,1)S(1)} collective-permute-done((bf16[16,4096]{1,0:T(8,128)(2,1)S(1)}, bf16[16,4096]{1,0:T(8,128)(2,1)S(1)}, u32[]{:S(2)}, u32[]{:S(2)}) %collective-permute-start.33) | collective-permute-done | bytes 131104 | tf_op jit(solution)/shard_map/ppermute | solution.py:284
  60.7 4.3 %collective-permute-done.30 = bf16[32,4096]{1,0:T(8,128)(2,1)S(1)} collective-permute-done((bf16[32,4096]{1,0:T(8,128)(2,1)S(1)}, bf16[32,4096]{1,0:T(8,128)(2,1)S(1)}, u32[]{:S(2)}, u32[]{:S(2)}) %collective-permute-start.30) | collective-permute-done | bytes 262176 | tf_op jit(solution)/shard_map/ppermute | solution.py:284
  65.0 0.9 %collective-permute-done.31 = bf16[32,4096]{1,0:T(8,128)(2,1)S(1)} collective-permute-done((bf16[32,4096]{1,0:T(8,128)(2,1)S(1)}, bf16[32,4096]{1,0:T(8,128)(2,1)S(1)}, u32[]{:S(2)}, u32[]{:S(2)}) %collective-permute-start.31) | collective-permute-done | bytes 262176 | tf_op jit(solution)/shard_map/ppermute | solution.py:284
  66.7 1.1 %collective-permute-start.34 = (bf16[16,4096]{1,0:T(8,128)(2,1)S(1)}, bf16[16,4096]{1,0:T(8,128)(2,1)S(1)}, u32[]{:S(2)}, u32[]{:S(2)}) collective-permute-start(bf16[16,4096]{1,0:T(8,128)(2,1)S(1)} %get-tuple-element.128), channel_id=1, source_target_pairs={{0,16},{8,24},{16,0},{24,8},{1,17},{9,25},{17,1},{25,9},{2,18},{10... | collective-permute-start | bytes 393224 | tf_op jit(solution)/shard_map/ppermute | solution.py:289
  67.8 1.5 %collective-permute-start.29 = (bf16[16,4096]{1,0:T(8,128)(2,1)S(1)}, bf16[16,4096]{1,0:T(8,128)(2,1)S(1)}, u32[]{:S(2)}, u32[]{:S(2)}) collective-permute-start(bf16[16,4096]{1,0:T(8,128)(2,1)S(1)} %fusion), channel_id=1, source_target_pairs={{0,6},{1,7},{2,4},{3,5},{4,2},{5,3},{6,0},{7,1},{8,14},{9,15},{10,... | collective-permute-start | bytes 393224 | tf_op jit(solution)/shard_map/ppermute | solution.py:284
  69.3 3.5 %collective-permute-done.32 = bf16[16,4096]{1,0:T(8,128)(2,1)S(1)} collective-permute-done((bf16[16,4096]{1,0:T(8,128)(2,1)S(1)}, bf16[16,4096]{1,0:T(8,128)(2,1)S(1)}, u32[]{:S(2)}, u32[]{:S(2)}) %collective-permute-start.32) | collective-permute-done | bytes 131104 | tf_op jit(solution)/shard_map/ppermute | solution.py:289
  72.9 2.7 %collective-permute-done.34 = bf16[16,4096]{1,0:T(8,128)(2,1)S(1)} collective-permute-done((bf16[16,4096]{1,0:T(8,128)(2,1)S(1)}, bf16[16,4096]{1,0:T(8,128)(2,1)S(1)}, u32[]{:S(2)}, u32[]{:S(2)}) %collective-permute-start.34) | collective-permute-done | bytes 131104 | tf_op jit(solution)/shard_map/ppermute | solution.py:289
  75.6 0.8 %fusion.8 = bf16[16,4096]{1,0:T(8,128)(2,1)} fusion(f32[48,4096]{1,0:T(8,128)S(1)} %convert_add_fusion, bf16[16,4096]{1,0:T(8,128)(2,1)S(1)} %collective-permute-done.34, bf16[16,4096]{1,0:T(8,128)(2,1)S(1)} %collective-permute-done.32, bf16[16,4096]{1,0:T(8,128)(2,1)S(1)} %collective-permute-done.29, bf16[16,4096]{1,0:T(8,128)(2,1)S(1)} %collective-permute-done.27, ...), kind=kLoop, calls=%fused_computation.16 | loop fusion | flops 851968 | bytes 1179648 | tf_op jit(solution)/shard_map/convert_element_type | solution.py:300
  (76 shorter events, 8.8 us)
Async XLA Ops:
  1.2 12.8 %collective-permute-start.4 = (bf16[16,4224]{1,0:T(8,128)(2,1)S(1)}, bf16[16,4224]{1,0:T(8,128)(2,1)S(1)}, u32[]{:S(2)}, u32[]{:S(2)}) collective-permute-start(bf16[16,4224]{1,0:T(8,128)(2,1)S(1)} %pack.1.refs_0_), channel_id=1, source_target_pairs={{0,24},{8,16},{16,8},{24,0},{1,25},{9,17},{17,9},{25,1},{2,26},{10... | collective-permute-start | bytes 405512 | tf_op jit(solution)/shard_map/ppermute | solution.py:289
  6.3 7.7 %collective-permute-start.3 = (bf16[16,4224]{1,0:T(8,128)(2,1)S(1)}, bf16[16,4224]{1,0:T(8,128)(2,1)S(1)}, u32[]{:S(2)}, u32[]{:S(2)}) collective-permute-start(bf16[16,4224]{1,0:T(8,128)(2,1)S(1)} %pack.1.refs_0_), channel_id=1, source_target_pairs={{0,8},{8,0},{16,24},{24,16},{1,9},{9,1},{17,25},{25,17},{2,10},{10... | collective-permute-start | bytes 405512 | tf_op jit(solution)/shard_map/ppermute | solution.py:289
  6.3 7.7 %collective-permute-start.2 = (bf16[16,4224]{1,0:T(8,128)(2,1)S(1)}, bf16[16,4224]{1,0:T(8,128)(2,1)S(1)}, u32[]{:S(2)}, u32[]{:S(2)}) collective-permute-start(bf16[16,4224]{1,0:T(8,128)(2,1)S(1)} %pack.1.refs_0_), channel_id=1, source_target_pairs={{0,6},{1,7},{2,4},{3,5},{4,2},{5,3},{6,0},{7,1},{8,14},{9,15},{10,... | collective-permute-start | bytes 405512 | tf_op jit(solution)/shard_map/ppermute | solution.py:284
  8.8 6.4 %collective-permute-start.1 = (bf16[16,4224]{1,0:T(8,128)(2,1)S(1)}, bf16[16,4224]{1,0:T(8,128)(2,1)S(1)}, u32[]{:S(2)}, u32[]{:S(2)}) collective-permute-start(bf16[16,4224]{1,0:T(8,128)(2,1)S(1)} %pack.1.refs_0_), channel_id=1, source_target_pairs={{0,4},{1,5},{2,6},{3,7},{4,0},{5,1},{6,2},{7,3},{8,12},{9,13},{10,... | collective-permute-start | bytes 405512 | tf_op jit(solution)/shard_map/ppermute | solution.py:284
  9.3 5.9 %collective-permute-start = (bf16[16,4224]{1,0:T(8,128)(2,1)S(1)}, bf16[16,4224]{1,0:T(8,128)(2,1)S(1)}, u32[]{:S(2)}, u32[]{:S(2)}) collective-permute-start(bf16[16,4224]{1,0:T(8,128)(2,1)S(1)} %pack.1.refs_0_), channel_id=1, source_target_pairs={{0,2},{1,3},{2,0},{3,1},{4,6},{5,7},{6,4},{7,5},{8,10},{9,11},{10,... | collective-permute-start | bytes 405512 | tf_op jit(solution)/shard_map/ppermute | solution.py:284
  15.2 9.1 %collective-permute-start.8 = (bf16[16,4224]{1,0:T(8,128)(2,1)S(1)}, bf16[16,4224]{1,0:T(8,128)(2,1)S(1)}, u32[]{:S(2)}, u32[]{:S(2)}) collective-permute-start(bf16[16,4224]{1,0:T(8,128)(2,1)S(1)} %pack.1.refs_0_), channel_id=1, source_target_pairs={{0,16},{8,24},{16,0},{24,8},{1,17},{9,25},{17,1},{25,9},{2,18},{10... | collective-permute-start | bytes 405512 | tf_op jit(solution)/shard_map/ppermute | solution.py:289
  15.9 9.2 %collective-permute-start.7 = (bf16[16,4224]{1,0:T(8,128)(2,1)S(1)}, bf16[16,4224]{1,0:T(8,128)(2,1)S(1)}, u32[]{:S(2)}, u32[]{:S(2)}) collective-permute-start(bf16[16,4224]{1,0:T(8,128)(2,1)S(1)} %collective-permute-done.4.refs_0_), channel_id=1, source_target_pairs={{0,6},{1,7},{2,4},{3,5},{4,2},{5,3},{6,0},{7,1},{8,14},{9,15},{10,... | collective-permute-start | bytes 405512 | tf_op jit(solution)/shard_map/ppermute | solution.py:284
  17.6 7.5 %collective-permute-start.6 = (bf16[16,4224]{1,0:T(8,128)(2,1)S(1)}, bf16[16,4224]{1,0:T(8,128)(2,1)S(1)}, u32[]{:S(2)}, u32[]{:S(2)}) collective-permute-start(bf16[16,4224]{1,0:T(8,128)(2,1)S(1)} %collective-permute-done.4.refs_0_), channel_id=1, source_target_pairs={{0,4},{1,5},{2,6},{3,7},{4,0},{5,1},{6,2},{7,3},{8,12},{9,13},{10,... | collective-permute-start | bytes 405512 | tf_op jit(solution)/shard_map/ppermute | solution.py:284
  18.9 6.2 %collective-permute-start.5 = (bf16[16,4224]{1,0:T(8,128)(2,1)S(1)}, bf16[16,4224]{1,0:T(8,128)(2,1)S(1)}, u32[]{:S(2)}, u32[]{:S(2)}) collective-permute-start(bf16[16,4224]{1,0:T(8,128)(2,1)S(1)} %collective-permute-done.4.refs_0_), channel_id=1, source_target_pairs={{0,2},{1,3},{2,0},{3,1},{4,6},{5,7},{6,4},{7,5},{8,10},{9,11},{10,... | collective-permute-start | bytes 405512 | tf_op jit(solution)/shard_map/ppermute | solution.py:284
  19.4 10.8 %collective-permute-start.9 = (bf16[64,4224]{1,0:T(8,128)(2,1)S(1)}, bf16[64,4224]{1,0:T(8,128)(2,1)S(1)}, u32[]{:S(2)}, u32[]{:S(2)}) collective-permute-start(bf16[64,4224]{1,0:T(8,128)(2,1)S(1)} %gather.3.refs_1_), channel_id=1, source_target_pairs={{0,1},{1,0},{2,3},{3,2},{4,5},{5,4},{6,7},{7,6},{8,9},{9,8},{10,11... | collective-permute-start | bytes 1622024 | tf_op jit(solution)/shard_map/ppermute | solution.py:284
  25.2 5.6 %collective-permute-start.10 = (bf16[64,4224]{1,0:T(8,128)(2,1)S(1)}, bf16[64,4224]{1,0:T(8,128)(2,1)S(1)}, u32[]{:S(2)}, u32[]{:S(2)}) collective-permute-start(bf16[64,4224]{1,0:T(8,128)(2,1)S(1)} %gather.4.refs_2_), channel_id=1, source_target_pairs={{0,1},{1,0},{2,3},{3,2},{4,5},{5,4},{6,7},{7,6},{8,9},{9,8},{10,11... | collective-permute-start | bytes 1622024 | tf_op jit(solution)/shard_map/ppermute | solution.py:284
  25.3 10.6 %collective-permute-start.14 = (bf16[16,4224]{1,0:T(8,128)(2,1)S(1)}, bf16[16,4224]{1,0:T(8,128)(2,1)S(1)}, u32[]{:S(2)}, u32[]{:S(2)}) collective-permute-start(bf16[16,4224]{1,0:T(8,128)(2,1)S(1)} %collective-permute-done.2.refs_3_), channel_id=1, source_target_pairs={{0,16},{8,24},{16,0},{24,8},{1,17},{9,25},{17,1},{25,9},{2,18},{10... | collective-permute-start | bytes 405512 | tf_op jit(solution)/shard_map/ppermute | solution.py:289
  27.2 8.7 %collective-permute-start.13 = (bf16[16,4224]{1,0:T(8,128)(2,1)S(1)}, bf16[16,4224]{1,0:T(8,128)(2,1)S(1)}, u32[]{:S(2)}, u32[]{:S(2)}) collective-permute-start(bf16[16,4224]{1,0:T(8,128)(2,1)S(1)} %collective-permute-done.2.refs_3_), channel_id=1, source_target_pairs={{0,8},{8,0},{16,24},{24,16},{1,9},{9,1},{17,25},{25,17},{2,10},{10... | collective-permute-start | bytes 405512 | tf_op jit(solution)/shard_map/ppermute | solution.py:289
  28.6 8.3 %collective-permute-start.12 = (bf16[32,4224]{1,0:T(8,128)(2,1)S(1)}, bf16[32,4224]{1,0:T(8,128)(2,1)S(1)}, u32[]{:S(2)}, u32[]{:S(2)}) collective-permute-start(bf16[32,4224]{1,0:T(8,128)(2,1)S(1)} %gather.5.refs_1_), channel_id=1, source_target_pairs={{0,4},{1,5},{2,6},{3,7},{4,0},{5,1},{6,2},{7,3},{8,12},{9,13},{10,... | collective-permute-start | bytes 811016 | tf_op jit(solution)/shard_map/ppermute | solution.py:284
  30.2 8.0 %collective-permute-start.11 = (bf16[32,4224]{1,0:T(8,128)(2,1)S(1)}, bf16[32,4224]{1,0:T(8,128)(2,1)S(1)}, u32[]{:S(2)}, u32[]{:S(2)}) collective-permute-start(bf16[32,4224]{1,0:T(8,128)(2,1)S(1)} %gather.5.refs_1_), channel_id=1, source_target_pairs={{0,2},{1,3},{2,0},{3,1},{4,6},{5,7},{6,4},{7,5},{8,10},{9,11},{10,... | collective-permute-start | bytes 811016 | tf_op jit(solution)/shard_map/ppermute | solution.py:284
  38.7 4.0 %collective-permute-start.21 = (bf16[16,4224]{1,0:T(8,128)(2,1)S(1)}, bf16[16,4224]{1,0:T(8,128)(2,1)S(1)}, u32[]{:S(2)}, u32[]{:S(2)}) collective-permute-start(bf16[16,4224]{1,0:T(8,128)(2,1)S(1)} %collective-permute-done.14.refs_5_), channel_id=1, source_target_pairs={{0,1},{1,0},{2,3},{3,2},{4,5},{5,4},{6,7},{7,6},{8,9},{9,8},{10,11... | collective-permute-start | bytes 405512 | tf_op jit(solution)/shard_map/ppermute | solution.py:284
  39.2 5.0 %collective-permute-start.18 = (bf16[32,4224]{1,0:T(8,128)(2,1)S(1)}, bf16[32,4224]{1,0:T(8,128)(2,1)S(1)}, u32[]{:S(2)}, u32[]{:S(2)}) collective-permute-start(bf16[32,4224]{1,0:T(8,128)(2,1)S(1)} %collective-permute-done.11.refs_2_), channel_id=1, source_target_pairs={{0,1},{1,0},{2,3},{3,2},{4,5},{5,4},{6,7},{7,6},{8,9},{9,8},{10,11... | collective-permute-start | bytes 811016 | tf_op jit(solution)/shard_map/ppermute | solution.py:284
  40.3 3.9 %collective-permute-start.19 = (bf16[32,4224]{1,0:T(8,128)(2,1)S(1)}, bf16[32,4224]{1,0:T(8,128)(2,1)S(1)}, u32[]{:S(2)}, u32[]{:S(2)}) collective-permute-start(bf16[32,4224]{1,0:T(8,128)(2,1)S(1)} %collective-permute-done.12.refs_3_), channel_id=1, source_target_pairs={{0,1},{1,0},{2,3},{3,2},{4,5},{5,4},{6,7},{7,6},{8,9},{9,8},{10,11... | collective-permute-start | bytes 811016 | tf_op jit(solution)/shard_map/ppermute | solution.py:284
  40.6 9.2 %collective-permute-start.24 = (bf16[16,4096]{1,0:T(8,128)(2,1)S(1)}, bf16[16,4096]{1,0:T(8,128)(2,1)S(1)}, u32[]{:S(2)}, u32[]{:S(2)}) collective-permute-start(bf16[16,4096]{1,0:T(8,128)(2,1)S(1)} %add_convert_fusion.8), channel_id=1, source_target_pairs={{0,6},{1,7},{2,4},{3,5},{4,2},{5,3},{6,0},{7,1},{8,14},{9,15},{10,... | collective-permute-start | bytes 393224 | tf_op jit(solution)/shard_map/ppermute | solution.py:284
  42.1 9.9 %collective-permute-start.22 = (bf16[32,4096]{1,0:T(8,128)(2,1)S(1)}, bf16[32,4096]{1,0:T(8,128)(2,1)S(1)}, u32[]{:S(2)}, u32[]{:S(2)}) collective-permute-start(bf16[32,4096]{1,0:T(8,128)(2,1)S(1)} %get-tuple-element.93), channel_id=1, source_target_pairs={{0,2},{1,3},{2,0},{3,1},{4,6},{5,7},{6,4},{7,5},{8,10},{9,11},{10,... | collective-permute-start | bytes 786440 | tf_op jit(solution)/shard_map/ppermute | solution.py:284
  42.7 10.2 %collective-permute-start.23 = (bf16[32,4096]{1,0:T(8,128)(2,1)S(1)}, bf16[32,4096]{1,0:T(8,128)(2,1)S(1)}, u32[]{:S(2)}, u32[]{:S(2)}) collective-permute-start(bf16[32,4096]{1,0:T(8,128)(2,1)S(1)} %get-tuple-element.94), channel_id=1, source_target_pairs={{0,4},{1,5},{2,6},{3,7},{4,0},{5,1},{6,2},{7,3},{8,12},{9,13},{10,... | collective-permute-start | bytes 786440 | tf_op jit(solution)/shard_map/ppermute | solution.py:284
  44.2 8.8 %collective-permute-start.16 = (bf16[48,4096]{1,0:T(8,128)(2,1)S(1)}, bf16[48,4096]{1,0:T(8,128)(2,1)S(1)}, u32[]{:S(2)}, u32[]{:S(2)}) collective-permute-start(bf16[48,4096]{1,0:T(8,128)(2,1)S(1)} %get-tuple-element.92), channel_id=1, source_target_pairs={{0,1},{1,0},{2,3},{3,2},{4,5},{5,4},{6,7},{7,6},{8,9},{9,8},{10,11... | collective-permute-start | bytes 1179656 | tf_op jit(solution)/shard_map/ppermute | solution.py:284
  49.3 3.7 %collective-permute-start.25 = (bf16[112,4096]{1,0:T(8,128)(2,1)S(1)}, bf16[112,4096]{1,0:T(8,128)(2,1)S(1)}, u32[]{:S(2)}, u32[]{:S(2)}) collective-permute-start(bf16[112,4096]{1,0:T(8,128)(2,1)S(1)} %get-tuple-element.116), channel_id=1, source_target_pairs={{0,1},{1,0},{2,3},{3,2},{4,5},{5,4},{6,7},{7,6},{8,9},{9,8},{10,11... | collective-permute-start | bytes 2752520 | tf_op jit(solution)/shard_map/ppermute | solution.py:284
  53.2 3.7 %collective-permute-start.26 = (bf16[16,4096]{1,0:T(8,128)(2,1)S(1)}, bf16[16,4096]{1,0:T(8,128)(2,1)S(1)}, u32[]{:S(2)}, u32[]{:S(2)}) collective-permute-start(bf16[16,4096]{1,0:T(8,128)(2,1)S(1)} %get-tuple-element.120), channel_id=1, source_target_pairs={{0,1},{1,0},{2,3},{3,2},{4,5},{5,4},{6,7},{7,6},{8,9},{9,8},{10,11... | collective-permute-start | bytes 393224 | tf_op jit(solution)/shard_map/ppermute | solution.py:284
  53.4 7.3 %collective-permute-start.33 = (bf16[16,4096]{1,0:T(8,128)(2,1)S(1)}, bf16[16,4096]{1,0:T(8,128)(2,1)S(1)}, u32[]{:S(2)}, u32[]{:S(2)}) collective-permute-start(bf16[16,4096]{1,0:T(8,128)(2,1)S(1)} %add_convert_fusion.7), channel_id=1, source_target_pairs={{0,6},{1,7},{2,4},{3,5},{4,2},{5,3},{6,0},{7,1},{8,14},{9,15},{10,... | collective-permute-start | bytes 393224 | tf_op jit(solution)/shard_map/ppermute | solution.py:284
  54.9 10.1 %collective-permute-start.30 = (bf16[32,4096]{1,0:T(8,128)(2,1)S(1)}, bf16[32,4096]{1,0:T(8,128)(2,1)S(1)}, u32[]{:S(2)}, u32[]{:S(2)}) collective-permute-start(bf16[32,4096]{1,0:T(8,128)(2,1)S(1)} %get-tuple-element.124), channel_id=1, source_target_pairs={{0,2},{1,3},{2,0},{3,1},{4,6},{5,7},{6,4},{7,5},{8,10},{9,11},{10,... | collective-permute-start | bytes 786440 | tf_op jit(solution)/shard_map/ppermute | solution.py:284
  55.5 10.4 %collective-permute-start.31 = (bf16[32,4096]{1,0:T(8,128)(2,1)S(1)}, bf16[32,4096]{1,0:T(8,128)(2,1)S(1)}, u32[]{:S(2)}, u32[]{:S(2)}) collective-permute-start(bf16[32,4096]{1,0:T(8,128)(2,1)S(1)} %get-tuple-element.125), channel_id=1, source_target_pairs={{0,4},{1,5},{2,6},{3,7},{4,0},{5,1},{6,2},{7,3},{8,12},{9,13},{10,... | collective-permute-start | bytes 786440 | tf_op jit(solution)/shard_map/ppermute | solution.py:284
  57.0 12.4 %collective-permute-start.27 = (bf16[16,4096]{1,0:T(8,128)(2,1)S(1)}, bf16[16,4096]{1,0:T(8,128)(2,1)S(1)}, u32[]{:S(2)}, u32[]{:S(2)}) collective-permute-start(bf16[16,4096]{1,0:T(8,128)(2,1)S(1)} %fusion.3), channel_id=1, source_target_pairs={{0,24},{8,16},{16,8},{24,0},{1,25},{9,17},{17,9},{25,1},{2,26},{10... | collective-permute-start | bytes 393224 | tf_op jit(solution)/shard_map/ppermute | solution.py:289
  58.2 9.6 %collective-permute-start.28 = (bf16[16,4096]{1,0:T(8,128)(2,1)S(1)}, bf16[16,4096]{1,0:T(8,128)(2,1)S(1)}, u32[]{:S(2)}, u32[]{:S(2)}) collective-permute-start(bf16[16,4096]{1,0:T(8,128)(2,1)S(1)} %add_convert_fusion.6), channel_id=1, source_target_pairs={{0,8},{8,0},{16,24},{24,16},{1,9},{9,1},{17,25},{25,17},{2,10},{10... | collective-permute-start | bytes 393224 | tf_op jit(solution)/shard_map/ppermute | solution.py:289
  66.0 6.9 %collective-permute-start.32 = (bf16[16,4096]{1,0:T(8,128)(2,1)S(1)}, bf16[16,4096]{1,0:T(8,128)(2,1)S(1)}, u32[]{:S(2)}, u32[]{:S(2)}) collective-permute-start(bf16[16,4096]{1,0:T(8,128)(2,1)S(1)} %get-tuple-element.127), channel_id=1, source_target_pairs={{0,8},{8,0},{16,24},{24,16},{1,9},{9,1},{17,25},{25,17},{2,10},{10... | collective-permute-start | bytes 393224 | tf_op jit(solution)/shard_map/ppermute | solution.py:289
  66.7 8.8 %collective-permute-start.34 = (bf16[16,4096]{1,0:T(8,128)(2,1)S(1)}, bf16[16,4096]{1,0:T(8,128)(2,1)S(1)}, u32[]{:S(2)}, u32[]{:S(2)}) collective-permute-start(bf16[16,4096]{1,0:T(8,128)(2,1)S(1)} %get-tuple-element.128), channel_id=1, source_target_pairs={{0,16},{8,24},{16,0},{24,8},{1,17},{9,25},{17,1},{25,9},{2,18},{10... | collective-permute-start | bytes 393224 | tf_op jit(solution)/shard_map/ppermute | solution.py:289
  67.8 7.7 %collective-permute-start.29 = (bf16[16,4096]{1,0:T(8,128)(2,1)S(1)}, bf16[16,4096]{1,0:T(8,128)(2,1)S(1)}, u32[]{:S(2)}, u32[]{:S(2)}) collective-permute-start(bf16[16,4096]{1,0:T(8,128)(2,1)S(1)} %fusion), channel_id=1, source_target_pairs={{0,6},{1,7},{2,4},{3,5},{4,2},{5,3},{6,0},{7,1},{8,14},{9,15},{10,... | collective-permute-start | bytes 393224 | tf_op jit(solution)/shard_map/ppermute | solution.py:284
  (11 other events, 69.2 us)

commit v9 on v8

--- a/solution.py
+++ b/solution.py
@@ -350,32 +350,34 @@
     to_y = rounded(to_y, back[2 * rows : 4 * rows])
     to_far = rounded(to_far, back[4 * rows :])
     to_x, to_y, to_far, near_other = ordered(to_x, to_y, to_far, near_other)
-    near_x, near_y, near_far = swap_exp(to_x, 2), swap_exp(to_y, 4), swap_exp(to_far, 6)
+    near_x, near_y, near_far = swap_exp(to_x, 2), swap_exp(to_y, 4), swap_rep(to_far, 3)
     near_back = swap_exp(near_other, 1)
 
     far = [pair, x_pair, y_pair, far_one, far_two]
     far = far + [swap_exp(piece, 1) for piece in far]
     to_x, to_y, to_far, *far = ordered(to_x, to_y, to_far, *far)
-    groups = row_groups([[6], [7], [2, 3], [4, 5], [14], [10, 11, 12, 13, 15, 8, 9], [0, 1]], rows)
+    groups = row_groups([[6], [7], [2, 3], [4, 5], [10, 11, 12, 13, 8, 9], [14, 15], [0, 1]], rows)
     parts = experts_of(own, far, groups, gates, ups, downs, shard_units, top)
-    to_one, to_far, to_x, to_y, other_one, other, far_kept = parts
-    far_kept, near_x, near_y, near_far = ordered(far_kept, near_x, near_y, near_far)
+    to_one, to_two, to_x, to_y, other, other_far, far_kept = parts
+    far_kept, near_far, near_y, near_x = ordered(far_kept, near_far, near_y, near_x)
     back = swap_exp(other, 1)
+    kept = added(near_kept, near_back)
+    to_three = rounded(kept[:rows], near_x[:rows], near_y[:rows])
+    back, to_three = ordered(back, to_three)
+    from_three = swap_rep(to_three, 3)
     to_x, to_y = rounded(to_x, back[: 2 * rows]), rounded(to_y, back[2 * rows : 4 * rows])
-    to_far = rounded(to_far, back[4 * rows : 5 * rows])
-    to_x, to_y, to_far, other_one = ordered(to_x, to_y, to_far, other_one)
-    far_x, far_y, far_far = swap_exp(to_x, 2), swap_exp(to_y, 4), swap_exp(to_far, 6)
-    to_one = rounded(to_one, swap_exp(other_one, 1))
-    kept = added(near_kept, near_back)
-    to_three = rounded(kept[:rows], near_x[:rows], near_y[:rows], near_far)
-    to_three, to_one = ordered(to_three, to_one)
-    from_three, from_one = swap_rep(to_three, 3), swap_rep(to_one, 1)
+    to_x, to_y, other_far = ordered(to_x, to_y, other_far)
+    far_x, far_y = swap_exp(to_x, 2), swap_exp(to_y, 4)
+    back_far = swap_exp(other_far, 1)
+    to_one, to_two = rounded(to_one, back_far[:rows]), rounded(to_two, back_far[rows:])
+    from_two, from_one = swap_rep(to_two, 2), swap_rep(to_one, 1)
 
     own_sum = kept[rows : 2 * rows] + added(near_x[rows:], near_y[rows:])
-    to_far = rounded(kept[2 * rows :], from_one)
+    from_one, from_two, from_three = ordered(from_one, from_two, from_three)
+    to_far = rounded(kept[2 * rows :], from_one, from_two, near_far)
     from_far = swap_exp(to_far, 6)
-    to_one = rounded(far_kept[:rows], back[5 * rows : 6 * rows], far_x[:rows], far_y[:rows])
-    to_two = rounded(far_kept[rows:], back[6 * rows :], far_x[rows:], far_y[rows:], far_far)
+    to_one = rounded(far_kept[:rows], back[4 * rows : 5 * rows], far_x[:rows], far_y[:rows])
+    to_two = rounded(far_kept[rows:], back[5 * rows :], far_x[rows:], far_y[rows:])
     arrived = [swap_rep(to_one, 1), swap_rep(to_two, 2)]
     return rounded(own_sum, from_three, from_far, *arrived)
 

time: 76.5 us -> 72.6 us (0.949)
  waiting for transfers between devices: 26.5 us -> 20.8 us
  starting transfers between devices: 31.7 us -> 33.5 us
    ppermute x9 -> x11, starting transfers between devices: 12.1 us -> 16.5 us  [swap_rep(): return lax.ppermute(value, 'rep', [(i, i ^ bits) for i in range(replicas)])]
    ppermute x26 -> x24, waiting for transfers between devices: 15.4 us -> 11.1 us  [swap_exp(): return lax.ppermute(value, 'exp', [(i, i ^ bits) for i in range(owners)])]
    ppermute x26 -> x24, starting transfers between devices: 19.6 us -> 17 us  [swap_exp(): return lax.ppermute(value, 'exp', [(i, i ^ bits) for i in range(owners)])]
    ppermute x9 -> x11, waiting for transfers between devices: 11.1 us -> 9.77 us  [swap_rep(): return lax.ppermute(value, 'rep', [(i, i ^ bits) for i in range(replicas)])]
  transfers between devices with their start and end apart: 35 -> 35, of which waited for: 14 -> 16; matrix products, arithmetic and copies ran while one was open for 1% -> 1% of each run, Pallas kernels for 20% -> 21%
where the time goes in v9:
time: 72.6 us; the launch traced here: 72.5 us
  starting transfers between devices  33.5 us (46%)
  waiting for transfers between devices  20.8 us (29%)
  Pallas kernels  16 us (22%)
  other arithmetic  1.48 us (2%)
    ppermute x24, starting transfers between devices, swap_exp(): return lax.ppermute(value, 'exp', [(i, i ^ bits) for i in range(owners)])  17 us
    ppermute x11, starting transfers between devices, swap_rep(): return lax.ppermute(value, 'rep', [(i, i ^ bits) for i in range(replicas)])  16.5 us
    ppermute x24, waiting for transfers between devices, swap_exp(): return lax.ppermute(value, 'exp', [(i, i ^ bits) for i in range(owners)])  11.1 us
    pallas_call x2, Pallas kernels, experts_of(): pl.pallas_call(kernel, out_shape=[jax.ShapeDtypeStruct((count, model_widt...  10.2 us
    ppermute x11, waiting for transfers between devices, swap_rep(): return lax.ppermute(value, 'rep', [(i, i ^ bits) for i in range(replicas)])  9.77 us
    pallas_call x3, Pallas kernels, fetched(): pl.pallas_call(functools.partial(fetch_kernel, turn), out_shape=jax.Shape...  4.88 us
  transfers between devices with their start and end apart: 35, of which 16 were waited for; matrix products, arithmetic and copies ran while one was open for 1% of the time, Pallas kernels for 21%

profile of v9, /device:TPU:0, one launch (start us, length us, event | category | flops | bytes accessed | tf_op | source)
XLA Modules:
  0.0 72.5 jit_solution(8772056822547566023)
XLA Ops:
  1.2 5.1 %collective-permute-start.4 = (bf16[16,4224]{1,0:T(8,128)(2,1)S(1)}, bf16[16,4224]{1,0:T(8,128)(2,1)S(1)}, u32[]{:S(2)}, u32[]{:S(2)}) collective-permute-start(bf16[16,4224]{1,0:T(8,128)(2,1)S(1)} %pack.1.refs_0_), channel_id=1, source_target_pairs={{0,24},{8,16},{16,8},{24,0},{1,25},{9,17},{17,9},{25,1},{2,26},{10... | collective-permute-start | bytes 405512 | tf_op jit(solution)/shard_map/ppermute | solution.py:289
  6.3 2.4 %collective-permute-start.2 = (bf16[16,4224]{1,0:T(8,128)(2,1)S(1)}, bf16[16,4224]{1,0:T(8,128)(2,1)S(1)}, u32[]{:S(2)}, u32[]{:S(2)}) collective-permute-start(bf16[16,4224]{1,0:T(8,128)(2,1)S(1)} %pack.1.refs_0_), channel_id=1, source_target_pairs={{0,6},{1,7},{2,4},{3,5},{4,2},{5,3},{6,0},{7,1},{8,14},{9,15},{10,... | collective-permute-start | bytes 405512 | tf_op jit(solution)/shard_map/ppermute | solution.py:284
  9.8 2.1 %fetch_turned.2.refs_5_.refs_11_ = bf16[4096,768]{1,0:T(8,128)(2,1)S(1)} custom-call(bf16[768,4096]{1,0:T(8,128)(2,1)S(1)} %bitcast.7), custom_call_target="tpu_custom_call" | custom-call | bytes 12582912 | tf_op jit(solution)/shard_map/fetch_turned/pallas_call | solution.py:103
  12.0 2.1 %fetch_turned.3.refs_6_.refs_12_ = bf16[4096,768]{1,0:T(8,128)(2,1)S(1)} custom-call(bf16[768,4096]{1,0:T(8,128)(2,1)S(1)} %bitcast.11), custom_call_target="tpu_custom_call" | custom-call | bytes 12582912 | tf_op jit(solution)/shard_map/fetch_turned/pallas_call | solution.py:103
  14.1 1.1 %collective-permute-done.1.refs_2_ = bf16[16,4224]{1,0:T(8,128)(2,1)S(1)} collective-permute-done((bf16[16,4224]{1,0:T(8,128)(2,1)S(1)}, bf16[16,4224]{1,0:T(8,128)(2,1)S(1)}, u32[]{:S(2)}, u32[]{:S(2)}) %collective-permute-start.1) | collective-permute-done | bytes 135200 | tf_op jit(solution)/shard_map/ppermute | solution.py:284
  15.2 0.6 collective-permute-start.8
  15.9 1.7 %collective-permute-start.7 = (bf16[16,4224]{1,0:T(8,128)(2,1)S(1)}, bf16[16,4224]{1,0:T(8,128)(2,1)S(1)}, u32[]{:S(2)}, u32[]{:S(2)}) collective-permute-start(bf16[16,4224]{1,0:T(8,128)(2,1)S(1)} %collective-permute-done.4.refs_0_), channel_id=1, source_target_pairs={{0,6},{1,7},{2,4},{3,5},{4,2},{5,3},{6,0},{7,1},{8,14},{9,15},{10,... | collective-permute-start | bytes 405512 | tf_op jit(solution)/shard_map/ppermute | solution.py:284
  17.6 1.3 %collective-permute-start.6 = (bf16[16,4224]{1,0:T(8,128)(2,1)S(1)}, bf16[16,4224]{1,0:T(8,128)(2,1)S(1)}, u32[]{:S(2)}, u32[]{:S(2)}) collective-permute-start(bf16[16,4224]{1,0:T(8,128)(2,1)S(1)} %collective-permute-done.4.refs_0_), channel_id=1, source_target_pairs={{0,4},{1,5},{2,6},{3,7},{4,0},{5,1},{6,2},{7,3},{8,12},{9,13},{10,... | collective-permute-start | bytes 405512 | tf_op jit(solution)/shard_map/ppermute | solution.py:284
  19.5 4.8 %collective-permute-done.8.refs_1_ = bf16[16,4224]{1,0:T(8,128)(2,1)S(1)} collective-permute-done((bf16[16,4224]{1,0:T(8,128)(2,1)S(1)}, bf16[16,4224]{1,0:T(8,128)(2,1)S(1)}, u32[]{:S(2)}, u32[]{:S(2)}) %collective-permute-start.8) | collective-permute-done | bytes 135200 | tf_op jit(solution)/shard_map/ppermute | solution.py:289
  24.3 0.8 %fetch.1.refs_7_.refs_13_ = bf16[768,4096]{1,0:T(8,128)(2,1)S(1)} custom-call(bf16[768,4096]{1,0:T(8,128)(2,1)S(1)} %bitcast.15), custom_call_target="tpu_custom_call" | custom-call | bytes 12582912 | tf_op jit(solution)/shard_map/fetch/pallas_call | solution.py:103
  25.3 2.0 %collective-permute-start.14 = (bf16[16,4224]{1,0:T(8,128)(2,1)S(1)}, bf16[16,4224]{1,0:T(8,128)(2,1)S(1)}, u32[]{:S(2)}, u32[]{:S(2)}) collective-permute-start(bf16[16,4224]{1,0:T(8,128)(2,1)S(1)} %collective-permute-done.2.refs_3_), channel_id=1, source_target_pairs={{0,16},{8,24},{16,0},{24,8},{1,17},{9,25},{17,1},{25,9},{2,18},{10... | collective-permute-start | bytes 405512 | tf_op jit(solution)/shard_map/ppermute | solution.py:289
  27.2 1.4 %collective-permute-start.13 = (bf16[16,4224]{1,0:T(8,128)(2,1)S(1)}, bf16[16,4224]{1,0:T(8,128)(2,1)S(1)}, u32[]{:S(2)}, u32[]{:S(2)}) collective-permute-start(bf16[16,4224]{1,0:T(8,128)(2,1)S(1)} %collective-permute-done.2.refs_3_), channel_id=1, source_target_pairs={{0,8},{8,0},{16,24},{24,16},{1,9},{9,1},{17,25},{25,17},{2,10},{10... | collective-permute-start | bytes 405512 | tf_op jit(solution)/shard_map/ppermute | solution.py:289
  28.6 1.5 %collective-permute-start.12 = (bf16[32,4224]{1,0:T(8,128)(2,1)S(1)}, bf16[32,4224]{1,0:T(8,128)(2,1)S(1)}, u32[]{:S(2)}, u32[]{:S(2)}) collective-permute-start(bf16[32,4224]{1,0:T(8,128)(2,1)S(1)} %gather.5.refs_1_), channel_id=1, source_target_pairs={{0,4},{1,5},{2,6},{3,7},{4,0},{5,1},{6,2},{7,3},{8,12},{9,13},{10,... | collective-permute-start | bytes 811016 | tf_op jit(solution)/shard_map/ppermute | solution.py:284
  30.2 0.6 collective-permute-start.11
  30.7 5.1 %experts.2 = (bf16[32,4096]{1,0:T(8,128)(2,1)S(1)}, bf16[32,4096]{1,0:T(8,128)(2,1)S(1)}, bf16[16,4096]{1,0:T(8,128)(2,1)S(1)}, bf16[80,4096]{1,0:T(8,128)(2,1)S...) custom-call(s32[1]{0:T(128)} %bitcast.own_ref.refs_0_, bf16[64,4224]{1,0:T(8,128)(2,1)S(1)} %gather.3.refs_1_, ...), custom_call_target="tpu_custom_call" | custom-call | flops 4831838208 | bytes 4194304 | tf_op jit(solution)/shard_map/experts/pallas_call | solution.py:197
  35.9 1.1 %collective-permute-done.12.refs_3_ = bf16[32,4224]{1,0:T(8,128)(2,1)S(1)} collective-permute-done((bf16[32,4224]{1,0:T(8,128)(2,1)S(1)}, bf16[32,4224]{1,0:T(8,128)(2,1)S(1)}, u32[]{:S(2)}, u32[]{:S(2)}) %collective-permute-start.12) | collective-permute-done | bytes 270368 | tf_op jit(solution)/shard_map/ppermute | solution.py:284
  37.0 1.2 %collective-permute-done.11.refs_2_ = bf16[32,4224]{1,0:T(8,128)(2,1)S(1)} collective-permute-done((bf16[32,4224]{1,0:T(8,128)(2,1)S(1)}, bf16[32,4224]{1,0:T(8,128)(2,1)S(1)}, u32[]{:S(2)}, u32[]{:S(2)}) %collective-permute-start.11) | collective-permute-done | bytes 270368 | tf_op jit(solution)/shard_map/ppermute | solution.py:284
  39.2 1.1 %collective-permute-done.15 = bf16[80,4096]{1,0:T(8,128)(2,1)S(1)} collective-permute-done((bf16[80,4096]{1,0:T(8,128)(2,1)S(1)}, bf16[80,4096]{1,0:T(8,128)(2,1)S(1)}, u32[]{:S(2)}, u32[]{:S(2)}) %collective-permute-start.15) | collective-permute-done | bytes 655392 | tf_op jit(solution)/shard_map/ppermute | solution.py:284
  40.6 1.2 %collective-permute-start.22 = (bf16[16,4096]{1,0:T(8,128)(2,1)S(1)}, bf16[16,4096]{1,0:T(8,128)(2,1)S(1)}, u32[]{:S(2)}, u32[]{:S(2)}) collective-permute-start(bf16[16,4096]{1,0:T(8,128)(2,1)S(1)} %add_convert_fusion.8), channel_id=1, source_target_pairs={{0,24},{8,16},{16,8},{24,0},{1,25},{9,17},{17,9},{25,1},{2,26},{10... | collective-permute-start | bytes 393224 | tf_op jit(solution)/shard_map/ppermute | solution.py:289
  42.2 1.7 %collective-permute-start.23 = (bf16[32,4096]{1,0:T(8,128)(2,1)S(1)}, bf16[32,4096]{1,0:T(8,128)(2,1)S(1)}, u32[]{:S(2)}, u32[]{:S(2)}) collective-permute-start(bf16[32,4096]{1,0:T(8,128)(2,1)S(1)} %get-tuple-element.96), channel_id=1, source_target_pairs={{0,4},{1,5},{2,6},{3,7},{4,0},{5,1},{6,2},{7,3},{8,12},{9,13},{10,... | collective-permute-start | bytes 786440 | tf_op jit(solution)/shard_map/ppermute | solution.py:284
  43.8 5.1 %experts.3 = (bf16[16,4096]{1,0:T(8,128)(2,1)S(1)}, bf16[16,4096]{1,0:T(8,128)(2,1)S(1)}, bf16[32,4096]{1,0:T(8,128)(2,1)S(1)}, bf16[32,4096]{1,0:T(8,128)(2,1)S...) custom-call(s32[1]{0:T(128)} %bitcast.own_ref.refs_0_, ...), custom_call_target="tpu_custom_call" | custom-call | flops 4831838208 | bytes 4194304 | tf_op jit(solution)/shard_map/experts/pallas_call | solution.py:197
  50.3 1.1 %collective-permute-done.25 = bf16[96,4096]{1,0:T(8,128)(2,1)S(1)} collective-permute-done((bf16[96,4096]{1,0:T(8,128)(2,1)S(1)}, bf16[96,4096]{1,0:T(8,128)(2,1)S(1)}, u32[]{:S(2)}, u32[]{:S(2)}) %collective-permute-start.25) | collective-permute-done | bytes 786464 | tf_op jit(solution)/shard_map/ppermute | solution.py:284
  52.0 2.7 %collective-permute-start.29 = (bf16[16,4096]{1,0:T(8,128)(2,1)S(1)}, bf16[16,4096]{1,0:T(8,128)(2,1)S(1)}, u32[]{:S(2)}, u32[]{:S(2)}) collective-permute-start(bf16[16,4096]{1,0:T(8,128)(2,1)S(1)} %fusion.4), channel_id=1, source_target_pairs={{0,24},{8,16},{16,8},{24,0},{1,25},{9,17},{17,9},{25,1},{2,26},{10... | collective-permute-start | bytes 393224 | tf_op jit(solution)/shard_map/ppermute | solution.py:289
  54.7 0.6 collective-permute-start.31
  55.3 1.5 %collective-permute-start.32 = (bf16[32,4096]{1,0:T(8,128)(2,1)S(1)}, bf16[32,4096]{1,0:T(8,128)(2,1)S(1)}, u32[]{:S(2)}, u32[]{:S(2)}) collective-permute-start(bf16[32,4096]{1,0:T(8,128)(2,1)S(1)} %get-tuple-element.130), channel_id=1, source_target_pairs={{0,4},{1,5},{2,6},{3,7},{4,0},{5,1},{6,2},{7,3},{8,12},{9,13},{10,... | collective-permute-start | bytes 786440 | tf_op jit(solution)/shard_map/ppermute | solution.py:284
  56.9 1.7 %collective-permute-start.27 = (bf16[16,4096]{1,0:T(8,128)(2,1)S(1)}, bf16[16,4096]{1,0:T(8,128)(2,1)S(1)}, u32[]{:S(2)}, u32[]{:S(2)}) collective-permute-start(bf16[16,4096]{1,0:T(8,128)(2,1)S(1)} %get-tuple-element.138), channel_id=1, source_target_pairs={{0,8},{8,0},{16,24},{24,16},{1,9},{9,1},{17,25},{25,17},{2,10},{10... | collective-permute-start | bytes 393224 | tf_op jit(solution)/shard_map/ppermute | solution.py:289
  58.6 4.2 %collective-permute-done.31 = bf16[32,4096]{1,0:T(8,128)(2,1)S(1)} collective-permute-done((bf16[32,4096]{1,0:T(8,128)(2,1)S(1)}, bf16[32,4096]{1,0:T(8,128)(2,1)S(1)}, u32[]{:S(2)}, u32[]{:S(2)}) %collective-permute-start.31) | collective-permute-done | bytes 262176 | tf_op jit(solution)/shard_map/ppermute | solution.py:284
  63.3 1.7 %collective-permute-start.34 = (bf16[16,4096]{1,0:T(8,128)(2,1)S(1)}, bf16[16,4096]{1,0:T(8,128)(2,1)S(1)}, u32[]{:S(2)}, u32[]{:S(2)}) collective-permute-start(bf16[16,4096]{1,0:T(8,128)(2,1)S(1)} %get-tuple-element.132), channel_id=1, source_target_pairs={{0,16},{8,24},{16,0},{24,8},{1,17},{9,25},{17,1},{25,9},{2,18},{10... | collective-permute-start | bytes 393224 | tf_op jit(solution)/shard_map/ppermute | solution.py:289
  65.3 1.6 %collective-permute-start.30 = (bf16[16,4096]{1,0:T(8,128)(2,1)S(1)}, bf16[16,4096]{1,0:T(8,128)(2,1)S(1)}, u32[]{:S(2)}, u32[]{:S(2)}) collective-permute-start(bf16[16,4096]{1,0:T(8,128)(2,1)S(1)} %fusion.2), channel_id=1, source_target_pairs={{0,6},{1,7},{2,4},{3,5},{4,2},{5,3},{6,0},{7,1},{8,14},{9,15},{10,... | collective-permute-start | bytes 393224 | tf_op jit(solution)/shard_map/ppermute | solution.py:284
  66.9 3.1 %collective-permute-done.33 = bf16[16,4096]{1,0:T(8,128)(2,1)S(1)} collective-permute-done((bf16[16,4096]{1,0:T(8,128)(2,1)S(1)}, bf16[16,4096]{1,0:T(8,128)(2,1)S(1)}, u32[]{:S(2)}, u32[]{:S(2)}) %collective-permute-start.33) | collective-permute-done | bytes 131104 | tf_op jit(solution)/shard_map/ppermute | solution.py:289
  70.0 1.5 %collective-permute-done.34 = bf16[16,4096]{1,0:T(8,128)(2,1)S(1)} collective-permute-done((bf16[16,4096]{1,0:T(8,128)(2,1)S(1)}, bf16[16,4096]{1,0:T(8,128)(2,1)S(1)}, u32[]{:S(2)}, u32[]{:S(2)}) %collective-permute-start.34) | collective-permute-done | bytes 131104 | tf_op jit(solution)/shard_map/ppermute | solution.py:289
  71.7 0.8 %fusion.9 = bf16[16,4096]{1,0:T(8,128)(2,1)} fusion(f32[48,4096]{1,0:T(8,128)S(1)} %convert_add_fusion, bf16[16,4096]{1,0:T(8,128)(2,1)S(1)} %collective-permute-done.34, bf16[16,4096]{1,0:T(8,128)(2,1)S(1)} %collective-permute-done.33, bf16[16,4096]{1,0:T(8,128)(2,1)S(1)} %collective-permute-done.30, bf16[16,4096]{1,0:T(8,128)(2,1)S(1)} %collective-permute-done.29, ...), kind=kLoop, calls=%fused_computation.17 | loop fusion | flops 851968 | bytes 1179648 | tf_op jit(solution)/shard_map/convert_element_type | solution.py:300
  (75 shorter events, 7.9 us)
Async XLA Ops:
  1.2 12.8 %collective-permute-start.4 = (bf16[16,4224]{1,0:T(8,128)(2,1)S(1)}, bf16[16,4224]{1,0:T(8,128)(2,1)S(1)}, u32[]{:S(2)}, u32[]{:S(2)}) collective-permute-start(bf16[16,4224]{1,0:T(8,128)(2,1)S(1)} %pack.1.refs_0_), channel_id=1, source_target_pairs={{0,24},{8,16},{16,8},{24,0},{1,25},{9,17},{17,9},{25,1},{2,26},{10... | collective-permute-start | bytes 405512 | tf_op jit(solution)/shard_map/ppermute | solution.py:289
  6.3 7.7 %collective-permute-start.3 = (bf16[16,4224]{1,0:T(8,128)(2,1)S(1)}, bf16[16,4224]{1,0:T(8,128)(2,1)S(1)}, u32[]{:S(2)}, u32[]{:S(2)}) collective-permute-start(bf16[16,4224]{1,0:T(8,128)(2,1)S(1)} %pack.1.refs_0_), channel_id=1, source_target_pairs={{0,8},{8,0},{16,24},{24,16},{1,9},{9,1},{17,25},{25,17},{2,10},{10... | collective-permute-start | bytes 405512 | tf_op jit(solution)/shard_map/ppermute | solution.py:289
  6.3 7.7 %collective-permute-start.2 = (bf16[16,4224]{1,0:T(8,128)(2,1)S(1)}, bf16[16,4224]{1,0:T(8,128)(2,1)S(1)}, u32[]{:S(2)}, u32[]{:S(2)}) collective-permute-start(bf16[16,4224]{1,0:T(8,128)(2,1)S(1)} %pack.1.refs_0_), channel_id=1, source_target_pairs={{0,6},{1,7},{2,4},{3,5},{4,2},{5,3},{6,0},{7,1},{8,14},{9,15},{10,... | collective-permute-start | bytes 405512 | tf_op jit(solution)/shard_map/ppermute | solution.py:284
  8.8 6.4 %collective-permute-start.1 = (bf16[16,4224]{1,0:T(8,128)(2,1)S(1)}, bf16[16,4224]{1,0:T(8,128)(2,1)S(1)}, u32[]{:S(2)}, u32[]{:S(2)}) collective-permute-start(bf16[16,4224]{1,0:T(8,128)(2,1)S(1)} %pack.1.refs_0_), channel_id=1, source_target_pairs={{0,4},{1,5},{2,6},{3,7},{4,0},{5,1},{6,2},{7,3},{8,12},{9,13},{10,... | collective-permute-start | bytes 405512 | tf_op jit(solution)/shard_map/ppermute | solution.py:284
  9.3 5.9 %collective-permute-start = (bf16[16,4224]{1,0:T(8,128)(2,1)S(1)}, bf16[16,4224]{1,0:T(8,128)(2,1)S(1)}, u32[]{:S(2)}, u32[]{:S(2)}) collective-permute-start(bf16[16,4224]{1,0:T(8,128)(2,1)S(1)} %pack.1.refs_0_), channel_id=1, source_target_pairs={{0,2},{1,3},{2,0},{3,1},{4,6},{5,7},{6,4},{7,5},{8,10},{9,11},{10,... | collective-permute-start | bytes 405512 | tf_op jit(solution)/shard_map/ppermute | solution.py:284
  15.2 9.1 %collective-permute-start.8 = (bf16[16,4224]{1,0:T(8,128)(2,1)S(1)}, bf16[16,4224]{1,0:T(8,128)(2,1)S(1)}, u32[]{:S(2)}, u32[]{:S(2)}) collective-permute-start(bf16[16,4224]{1,0:T(8,128)(2,1)S(1)} %pack.1.refs_0_), channel_id=1, source_target_pairs={{0,16},{8,24},{16,0},{24,8},{1,17},{9,25},{17,1},{25,9},{2,18},{10... | collective-permute-start | bytes 405512 | tf_op jit(solution)/shard_map/ppermute | solution.py:289
  15.9 9.2 %collective-permute-start.7 = (bf16[16,4224]{1,0:T(8,128)(2,1)S(1)}, bf16[16,4224]{1,0:T(8,128)(2,1)S(1)}, u32[]{:S(2)}, u32[]{:S(2)}) collective-permute-start(bf16[16,4224]{1,0:T(8,128)(2,1)S(1)} %collective-permute-done.4.refs_0_), channel_id=1, source_target_pairs={{0,6},{1,7},{2,4},{3,5},{4,2},{5,3},{6,0},{7,1},{8,14},{9,15},{10,... | collective-permute-start | bytes 405512 | tf_op jit(solution)/shard_map/ppermute | solution.py:284
  17.6 7.5 %collective-permute-start.6 = (bf16[16,4224]{1,0:T(8,128)(2,1)S(1)}, bf16[16,4224]{1,0:T(8,128)(2,1)S(1)}, u32[]{:S(2)}, u32[]{:S(2)}) collective-permute-start(bf16[16,4224]{1,0:T(8,128)(2,1)S(1)} %collective-permute-done.4.refs_0_), channel_id=1, source_target_pairs={{0,4},{1,5},{2,6},{3,7},{4,0},{5,1},{6,2},{7,3},{8,12},{9,13},{10,... | collective-permute-start | bytes 405512 | tf_op jit(solution)/shard_map/ppermute | solution.py:284
  18.9 6.2 %collective-permute-start.5 = (bf16[16,4224]{1,0:T(8,128)(2,1)S(1)}, bf16[16,4224]{1,0:T(8,128)(2,1)S(1)}, u32[]{:S(2)}, u32[]{:S(2)}) collective-permute-start(bf16[16,4224]{1,0:T(8,128)(2,1)S(1)} %collective-permute-done.4.refs_0_), channel_id=1, source_target_pairs={{0,2},{1,3},{2,0},{3,1},{4,6},{5,7},{6,4},{7,5},{8,10},{9,11},{10,... | collective-permute-start | bytes 405512 | tf_op jit(solution)/shard_map/ppermute | solution.py:284
  19.4 10.8 %collective-permute-start.9 = (bf16[64,4224]{1,0:T(8,128)(2,1)S(1)}, bf16[64,4224]{1,0:T(8,128)(2,1)S(1)}, u32[]{:S(2)}, u32[]{:S(2)}) collective-permute-start(bf16[64,4224]{1,0:T(8,128)(2,1)S(1)} %gather.3.refs_1_), channel_id=1, source_target_pairs={{0,1},{1,0},{2,3},{3,2},{4,5},{5,4},{6,7},{7,6},{8,9},{9,8},{10,11... | collective-permute-start | bytes 1622024 | tf_op jit(solution)/shard_map/ppermute | solution.py:284
  25.2 5.6 %collective-permute-start.10 = (bf16[64,4224]{1,0:T(8,128)(2,1)S(1)}, bf16[64,4224]{1,0:T(8,128)(2,1)S(1)}, u32[]{:S(2)}, u32[]{:S(2)}) collective-permute-start(bf16[64,4224]{1,0:T(8,128)(2,1)S(1)} %gather.4.refs_2_), channel_id=1, source_target_pairs={{0,1},{1,0},{2,3},{3,2},{4,5},{5,4},{6,7},{7,6},{8,9},{9,8},{10,11... | collective-permute-start | bytes 1622024 | tf_op jit(solution)/shard_map/ppermute | solution.py:284
  25.3 10.6 %collective-permute-start.14 = (bf16[16,4224]{1,0:T(8,128)(2,1)S(1)}, bf16[16,4224]{1,0:T(8,128)(2,1)S(1)}, u32[]{:S(2)}, u32[]{:S(2)}) collective-permute-start(bf16[16,4224]{1,0:T(8,128)(2,1)S(1)} %collective-permute-done.2.refs_3_), channel_id=1, source_target_pairs={{0,16},{8,24},{16,0},{24,8},{1,17},{9,25},{17,1},{25,9},{2,18},{10... | collective-permute-start | bytes 405512 | tf_op jit(solution)/shard_map/ppermute | solution.py:289
  27.2 8.7 %collective-permute-start.13 = (bf16[16,4224]{1,0:T(8,128)(2,1)S(1)}, bf16[16,4224]{1,0:T(8,128)(2,1)S(1)}, u32[]{:S(2)}, u32[]{:S(2)}) collective-permute-start(bf16[16,4224]{1,0:T(8,128)(2,1)S(1)} %collective-permute-done.2.refs_3_), channel_id=1, source_target_pairs={{0,8},{8,0},{16,24},{24,16},{1,9},{9,1},{17,25},{25,17},{2,10},{10... | collective-permute-start | bytes 405512 | tf_op jit(solution)/shard_map/ppermute | solution.py:289
  28.6 8.3 %collective-permute-start.12 = (bf16[32,4224]{1,0:T(8,128)(2,1)S(1)}, bf16[32,4224]{1,0:T(8,128)(2,1)S(1)}, u32[]{:S(2)}, u32[]{:S(2)}) collective-permute-start(bf16[32,4224]{1,0:T(8,128)(2,1)S(1)} %gather.5.refs_1_), channel_id=1, source_target_pairs={{0,4},{1,5},{2,6},{3,7},{4,0},{5,1},{6,2},{7,3},{8,12},{9,13},{10,... | collective-permute-start | bytes 811016 | tf_op jit(solution)/shard_map/ppermute | solution.py:284
  30.2 8.0 %collective-permute-start.11 = (bf16[32,4224]{1,0:T(8,128)(2,1)S(1)}, bf16[32,4224]{1,0:T(8,128)(2,1)S(1)}, u32[]{:S(2)}, u32[]{:S(2)}) collective-permute-start(bf16[32,4224]{1,0:T(8,128)(2,1)S(1)} %gather.5.refs_1_), channel_id=1, source_target_pairs={{0,2},{1,3},{2,0},{3,1},{4,6},{5,7},{6,4},{7,5},{8,10},{9,11},{10,... | collective-permute-start | bytes 811016 | tf_op jit(solution)/shard_map/ppermute | solution.py:284
  38.7 3.1 %collective-permute-start.20 = (bf16[16,4224]{1,0:T(8,128)(2,1)S(1)}, bf16[16,4224]{1,0:T(8,128)(2,1)S(1)}, u32[]{:S(2)}, u32[]{:S(2)}) collective-permute-start(bf16[16,4224]{1,0:T(8,128)(2,1)S(1)} %collective-permute-done.13.refs_4_), channel_id=1, source_target_pairs={{0,1},{1,0},{2,3},{3,2},{4,5},{5,4},{6,7},{7,6},{8,9},{9,8},{10,11... | collective-permute-start | bytes 405512 | tf_op jit(solution)/shard_map/ppermute | solution.py:284
  38.7 3.5 %collective-permute-start.21 = (bf16[16,4224]{1,0:T(8,128)(2,1)S(1)}, bf16[16,4224]{1,0:T(8,128)(2,1)S(1)}, u32[]{:S(2)}, u32[]{:S(2)}) collective-permute-start(bf16[16,4224]{1,0:T(8,128)(2,1)S(1)} %collective-permute-done.14.refs_5_), channel_id=1, source_target_pairs={{0,1},{1,0},{2,3},{3,2},{4,5},{5,4},{6,7},{7,6},{8,9},{9,8},{10,11... | collective-permute-start | bytes 405512 | tf_op jit(solution)/shard_map/ppermute | solution.py:284
  39.2 4.6 %collective-permute-start.18 = (bf16[32,4224]{1,0:T(8,128)(2,1)S(1)}, bf16[32,4224]{1,0:T(8,128)(2,1)S(1)}, u32[]{:S(2)}, u32[]{:S(2)}) collective-permute-start(bf16[32,4224]{1,0:T(8,128)(2,1)S(1)} %collective-permute-done.11.refs_2_), channel_id=1, source_target_pairs={{0,1},{1,0},{2,3},{3,2},{4,5},{5,4},{6,7},{7,6},{8,9},{9,8},{10,11... | collective-permute-start | bytes 811016 | tf_op jit(solution)/shard_map/ppermute | solution.py:284
  40.3 3.6 %collective-permute-start.19 = (bf16[32,4224]{1,0:T(8,128)(2,1)S(1)}, bf16[32,4224]{1,0:T(8,128)(2,1)S(1)}, u32[]{:S(2)}, u32[]{:S(2)}) collective-permute-start(bf16[32,4224]{1,0:T(8,128)(2,1)S(1)} %collective-permute-done.12.refs_3_), channel_id=1, source_target_pairs={{0,1},{1,0},{2,3},{3,2},{4,5},{5,4},{6,7},{7,6},{8,9},{9,8},{10,11... | collective-permute-start | bytes 811016 | tf_op jit(solution)/shard_map/ppermute | solution.py:284
  40.6 8.9 %collective-permute-start.22 = (bf16[16,4096]{1,0:T(8,128)(2,1)S(1)}, bf16[16,4096]{1,0:T(8,128)(2,1)S(1)}, u32[]{:S(2)}, u32[]{:S(2)}) collective-permute-start(bf16[16,4096]{1,0:T(8,128)(2,1)S(1)} %add_convert_fusion.8), channel_id=1, source_target_pairs={{0,24},{8,16},{16,8},{24,0},{1,25},{9,17},{17,9},{25,1},{2,26},{10... | collective-permute-start | bytes 393224 | tf_op jit(solution)/shard_map/ppermute | solution.py:289
  41.8 8.3 %collective-permute-start.24 = (bf16[32,4096]{1,0:T(8,128)(2,1)S(1)}, bf16[32,4096]{1,0:T(8,128)(2,1)S(1)}, u32[]{:S(2)}, u32[]{:S(2)}) collective-permute-start(bf16[32,4096]{1,0:T(8,128)(2,1)S(1)} %get-tuple-element.95), channel_id=1, source_target_pairs={{0,2},{1,3},{2,0},{3,1},{4,6},{5,7},{6,4},{7,5},{8,10},{9,11},{10,... | collective-permute-start | bytes 786440 | tf_op jit(solution)/shard_map/ppermute | solution.py:284
  42.2 8.0 %collective-permute-start.23 = (bf16[32,4096]{1,0:T(8,128)(2,1)S(1)}, bf16[32,4096]{1,0:T(8,128)(2,1)S(1)}, u32[]{:S(2)}, u32[]{:S(2)}) collective-permute-start(bf16[32,4096]{1,0:T(8,128)(2,1)S(1)} %get-tuple-element.96), channel_id=1, source_target_pairs={{0,4},{1,5},{2,6},{3,7},{4,0},{5,1},{6,2},{7,3},{8,12},{9,13},{10,... | collective-permute-start | bytes 786440 | tf_op jit(solution)/shard_map/ppermute | solution.py:284
  43.8 6.3 %collective-permute-start.16 = (bf16[48,4096]{1,0:T(8,128)(2,1)S(1)}, bf16[48,4096]{1,0:T(8,128)(2,1)S(1)}, u32[]{:S(2)}, u32[]{:S(2)}) collective-permute-start(bf16[48,4096]{1,0:T(8,128)(2,1)S(1)} %get-tuple-element.94), channel_id=1, source_target_pairs={{0,1},{1,0},{2,3},{3,2},{4,5},{5,4},{6,7},{7,6},{8,9},{9,8},{10,11... | collective-permute-start | bytes 1179656 | tf_op jit(solution)/shard_map/ppermute | solution.py:284
  51.6 5.2 %collective-permute-start.26 = (bf16[32,4096]{1,0:T(8,128)(2,1)S(1)}, bf16[32,4096]{1,0:T(8,128)(2,1)S(1)}, u32[]{:S(2)}, u32[]{:S(2)}) collective-permute-start(bf16[32,4096]{1,0:T(8,128)(2,1)S(1)} %get-tuple-element.121), channel_id=1, source_target_pairs={{0,1},{1,0},{2,3},{3,2},{4,5},{5,4},{6,7},{7,6},{8,9},{9,8},{10,11... | collective-permute-start | bytes 786440 | tf_op jit(solution)/shard_map/ppermute | solution.py:284
  52.0 13.0 %collective-permute-start.29 = (bf16[16,4096]{1,0:T(8,128)(2,1)S(1)}, bf16[16,4096]{1,0:T(8,128)(2,1)S(1)}, u32[]{:S(2)}, u32[]{:S(2)}) collective-permute-start(bf16[16,4096]{1,0:T(8,128)(2,1)S(1)} %fusion.4), channel_id=1, source_target_pairs={{0,24},{8,16},{16,8},{24,0},{1,25},{9,17},{17,9},{25,1},{2,26},{10... | collective-permute-start | bytes 393224 | tf_op jit(solution)/shard_map/ppermute | solution.py:289
  54.7 8.1 %collective-permute-start.31 = (bf16[32,4096]{1,0:T(8,128)(2,1)S(1)}, bf16[32,4096]{1,0:T(8,128)(2,1)S(1)}, u32[]{:S(2)}, u32[]{:S(2)}) collective-permute-start(bf16[32,4096]{1,0:T(8,128)(2,1)S(1)} %get-tuple-element.129), channel_id=1, source_target_pairs={{0,2},{1,3},{2,0},{3,1},{4,6},{5,7},{6,4},{7,5},{8,10},{9,11},{10,... | collective-permute-start | bytes 786440 | tf_op jit(solution)/shard_map/ppermute | solution.py:284
  55.3 7.8 %collective-permute-start.32 = (bf16[32,4096]{1,0:T(8,128)(2,1)S(1)}, bf16[32,4096]{1,0:T(8,128)(2,1)S(1)}, u32[]{:S(2)}, u32[]{:S(2)}) collective-permute-start(bf16[32,4096]{1,0:T(8,128)(2,1)S(1)} %get-tuple-element.130), channel_id=1, source_target_pairs={{0,4},{1,5},{2,6},{3,7},{4,0},{5,1},{6,2},{7,3},{8,12},{9,13},{10,... | collective-permute-start | bytes 786440 | tf_op jit(solution)/shard_map/ppermute | solution.py:284
  56.8 8.4 %collective-permute-start.28 = (bf16[16,4096]{1,0:T(8,128)(2,1)S(1)}, bf16[16,4096]{1,0:T(8,128)(2,1)S(1)}, u32[]{:S(2)}, u32[]{:S(2)}) collective-permute-start(bf16[16,4096]{1,0:T(8,128)(2,1)S(1)} %get-tuple-element.137), channel_id=1, source_target_pairs={{0,16},{8,24},{16,0},{24,8},{1,17},{9,25},{17,1},{25,9},{2,18},{10... | collective-permute-start | bytes 393224 | tf_op jit(solution)/shard_map/ppermute | solution.py:289
  56.9 8.4 %collective-permute-start.27 = (bf16[16,4096]{1,0:T(8,128)(2,1)S(1)}, bf16[16,4096]{1,0:T(8,128)(2,1)S(1)}, u32[]{:S(2)}, u32[]{:S(2)}) collective-permute-start(bf16[16,4096]{1,0:T(8,128)(2,1)S(1)} %get-tuple-element.138), channel_id=1, source_target_pairs={{0,8},{8,0},{16,24},{24,16},{1,9},{9,1},{17,25},{25,17},{2,10},{10... | collective-permute-start | bytes 393224 | tf_op jit(solution)/shard_map/ppermute | solution.py:289
  63.2 6.8 %collective-permute-start.33 = (bf16[16,4096]{1,0:T(8,128)(2,1)S(1)}, bf16[16,4096]{1,0:T(8,128)(2,1)S(1)}, u32[]{:S(2)}, u32[]{:S(2)}) collective-permute-start(bf16[16,4096]{1,0:T(8,128)(2,1)S(1)} %get-tuple-element.131), channel_id=1, source_target_pairs={{0,8},{8,0},{16,24},{24,16},{1,9},{9,1},{17,25},{25,17},{2,10},{10... | collective-permute-start | bytes 393224 | tf_op jit(solution)/shard_map/ppermute | solution.py:289
  63.3 8.2 %collective-permute-start.34 = (bf16[16,4096]{1,0:T(8,128)(2,1)S(1)}, bf16[16,4096]{1,0:T(8,128)(2,1)S(1)}, u32[]{:S(2)}, u32[]{:S(2)}) collective-permute-start(bf16[16,4096]{1,0:T(8,128)(2,1)S(1)} %get-tuple-element.132), channel_id=1, source_target_pairs={{0,16},{8,24},{16,0},{24,8},{1,17},{9,25},{17,1},{25,9},{2,18},{10... | collective-permute-start | bytes 393224 | tf_op jit(solution)/shard_map/ppermute | solution.py:289
  65.3 6.4 %collective-permute-start.30 = (bf16[16,4096]{1,0:T(8,128)(2,1)S(1)}, bf16[16,4096]{1,0:T(8,128)(2,1)S(1)}, u32[]{:S(2)}, u32[]{:S(2)}) collective-permute-start(bf16[16,4096]{1,0:T(8,128)(2,1)S(1)} %fusion.2), channel_id=1, source_target_pairs={{0,6},{1,7},{2,4},{3,5},{4,2},{5,3},{6,0},{7,1},{8,14},{9,15},{10,... | collective-permute-start | bytes 393224 | tf_op jit(solution)/shard_map/ppermute | solution.py:284
  (11 other events, 68.2 us)

commit v10 on v9

--- a/solution.py
+++ b/solution.py
@@ -325,8 +325,8 @@
     x_own, y_own, far_own = [swap_exp(packed, bits) for bits in (2, 4, 6)]
     gates, ups = fetched(gate_weight, True), fetched(up_weight, True)
     one = swap_rep(packed, 1)
-    x_own, y_own, far_own, one, three, gates, ups, again = ordered(
-        x_own, y_own, far_own, one, three, gates, ups, packed
+    three, one, far_own, y_own, x_own, gates, ups, again = ordered(
+        three, one, far_own, y_own, x_own, gates, ups, packed
     )
     two = swap_rep(again, 2)
     x_three, y_three, far_three = [swap_exp(three, bits) for bits in (2, 4, 6)]
@@ -336,14 +336,14 @@
     second = gathered(three, x_three, y_three, far_three)
     two, down_weight = ordered(two, down_weight)
     downs = fetched(down_weight, False)
-    second, downs = ordered(second, downs)
+    second, downs, far_one, far_two = ordered(second, downs, far_one, far_two)
     pair = gathered(one, two)
     x_pair, y_pair = swap_exp(pair, 2), swap_exp(pair, 4)
 
     near = [first, second, first_other, swap_exp(second, 1)]
     groups = row_groups([[5, 1], [6, 2], [7], [13, 9, 14, 10, 15], [4, 0, 3], [12, 8, 11]], rows)
     parts = experts_of(own, near, groups, gates, ups, downs, shard_units, top)
-    *parts, x_pair, y_pair, far_one, far_two = ordered(*parts, x_pair, y_pair, far_one, far_two)
+    *parts, x_pair, y_pair = ordered(*parts, x_pair, y_pair)
     to_x, to_y, to_far, other, near_kept, near_other = parts
     back = swap_exp(other, 1)
     to_x = rounded(to_x, back[: 2 * rows])
@@ -359,7 +359,7 @@
     groups = row_groups([[6], [7], [2, 3], [4, 5], [10, 11, 12, 13, 8, 9], [14, 15], [0, 1]], rows)
     parts = experts_of(own, far, groups, gates, ups, downs, shard_units, top)
     to_one, to_two, to_x, to_y, other, other_far, far_kept = parts
-    far_kept, near_far, near_y, near_x = ordered(far_kept, near_far, near_y, near_x)
+    far_kept, near_x, near_y, near_far = ordered(far_kept, near_x, near_y, near_far)
     back = swap_exp(other, 1)
     kept = added(near_kept, near_back)
     to_three = rounded(kept[:rows], near_x[:rows], near_y[:rows])

time: 72.6 us -> 80.7 us (1.11)
  waiting for transfers between devices: 20.8 us -> 30.8 us
  starting transfers between devices: 33.5 us -> 31.6 us
    ppermute x11, waiting for transfers between devices: 9.77 us -> 17.8 us  [swap_rep(): return lax.ppermute(value, 'rep', [(i, i ^ bits) for i in range(replicas)])]
    ppermute x24, waiting for transfers between devices: 11.1 us -> 13 us  [swap_exp(): return lax.ppermute(value, 'exp', [(i, i ^ bits) for i in range(owners)])]
    ppermute x24, starting transfers between devices: 17 us -> 16 us  [swap_exp(): return lax.ppermute(value, 'exp', [(i, i ^ bits) for i in range(owners)])]
    ppermute x11, starting transfers between devices: 16.5 us -> 15.6 us  [swap_rep(): return lax.ppermute(value, 'rep', [(i, i ^ bits) for i in range(replicas)])]
  transfers between devices with their start and end apart: 35 -> 35, of which waited for: 16 -> 17; matrix products, arithmetic and copies ran while one was open for 1% -> 1% of each run, Pallas kernels for 21% -> 19%
where the time goes in v10:
time: 80.7 us; the launch traced here: 80.6 us
  starting transfers between devices  31.6 us (39%)
  waiting for transfers between devices  30.8 us (38%)
  Pallas kernels  16 us (20%)
  other arithmetic  1.45 us (2%)
    ppermute x11, waiting for transfers between devices, swap_rep(): return lax.ppermute(value, 'rep', [(i, i ^ bits) for i in range(replicas)])  17.8 us
    ppermute x24, starting transfers between devices, swap_exp(): return lax.ppermute(value, 'exp', [(i, i ^ bits) for i in range(owners)])  16 us
    ppermute x11, starting transfers between devices, swap_rep(): return lax.ppermute(value, 'rep', [(i, i ^ bits) for i in range(replicas)])  15.6 us
    ppermute x24, waiting for transfers between devices, swap_exp(): return lax.ppermute(value, 'exp', [(i, i ^ bits) for i in range(owners)])  13 us
    pallas_call x2, Pallas kernels, experts_of(): pl.pallas_call(kernel, out_shape=[jax.ShapeDtypeStruct((count, model_widt...  10.2 us
    pallas_call x3, Pallas kernels, fetched(): pl.pallas_call(functools.partial(fetch_kernel, turn), out_shape=jax.Shape...  4.88 us
  transfers between devices with their start and end apart: 35, of which 17 were waited for; matrix products, arithmetic and copies ran while one was open for 1% of the time, Pallas kernels for 19%

profile of v10, /device:TPU:0, one launch (start us, length us, event | category | flops | bytes accessed | tf_op | source)
XLA Modules:
  0.0 80.6 jit_solution(286642720608953099)
XLA Ops:
  1.2 5.1 %collective-permute-start = (bf16[16,4224]{1,0:T(8,128)(2,1)S(1)}, bf16[16,4224]{1,0:T(8,128)(2,1)S(1)}, u32[]{:S(2)}, u32[]{:S(2)}) collective-permute-start(bf16[16,4224]{1,0:T(8,128)(2,1)S(1)} %pack.1.refs_0_), channel_id=1, source_target_pairs={{0,24},{8,16},{16,8},{24,0},{1,25},{9,17},{17,9},{25,1},{2,26},{10... | collective-permute-start | bytes 405512 | tf_op jit(solution)/shard_map/ppermute | solution.py:289
  6.3 2.4 %collective-permute-start.2 = (bf16[16,4224]{1,0:T(8,128)(2,1)S(1)}, bf16[16,4224]{1,0:T(8,128)(2,1)S(1)}, u32[]{:S(2)}, u32[]{:S(2)}) collective-permute-start(bf16[16,4224]{1,0:T(8,128)(2,1)S(1)} %pack.1.refs_0_), channel_id=1, source_target_pairs={{0,6},{1,7},{2,4},{3,5},{4,2},{5,3},{6,0},{7,1},{8,14},{9,15},{10,... | collective-permute-start | bytes 405512 | tf_op jit(solution)/shard_map/ppermute | solution.py:284
  9.8 2.1 %fetch_turned.2.refs_5_.refs_11_ = bf16[4096,768]{1,0:T(8,128)(2,1)S(1)} custom-call(bf16[768,4096]{1,0:T(8,128)(2,1)S(1)} %bitcast.7), custom_call_target="tpu_custom_call" | custom-call | bytes 12582912 | tf_op jit(solution)/shard_map/fetch_turned/pallas_call | solution.py:103
  12.0 2.1 %fetch_turned.3.refs_6_.refs_12_ = bf16[4096,768]{1,0:T(8,128)(2,1)S(1)} custom-call(bf16[768,4096]{1,0:T(8,128)(2,1)S(1)} %bitcast.11), custom_call_target="tpu_custom_call" | custom-call | bytes 12582912 | tf_op jit(solution)/shard_map/fetch_turned/pallas_call | solution.py:103
  14.1 1.1 %collective-permute-done.3.refs_2_ = bf16[16,4224]{1,0:T(8,128)(2,1)S(1)} collective-permute-done((bf16[16,4224]{1,0:T(8,128)(2,1)S(1)}, bf16[16,4224]{1,0:T(8,128)(2,1)S(1)}, u32[]{:S(2)}, u32[]{:S(2)}) %collective-permute-start.3) | collective-permute-done | bytes 135200 | tf_op jit(solution)/shard_map/ppermute | solution.py:284
  15.9 1.5 %collective-permute-start.5 = (bf16[16,4224]{1,0:T(8,128)(2,1)S(1)}, bf16[16,4224]{1,0:T(8,128)(2,1)S(1)}, u32[]{:S(2)}, u32[]{:S(2)}) collective-permute-start(bf16[16,4224]{1,0:T(8,128)(2,1)S(1)} %collective-permute-done.refs_0_), channel_id=1, source_target_pairs={{0,2},{1,3},{2,0},{3,1},{4,6},{5,7},{6,4},{7,5},{8,10},{9,11},{10,... | collective-permute-start | bytes 405512 | tf_op jit(solution)/shard_map/ppermute | solution.py:284
  17.4 0.7 collective-permute-start.6
  18.1 1.2 %collective-permute-start.7 = (bf16[16,4224]{1,0:T(8,128)(2,1)S(1)}, bf16[16,4224]{1,0:T(8,128)(2,1)S(1)}, u32[]{:S(2)}, u32[]{:S(2)}) collective-permute-start(bf16[16,4224]{1,0:T(8,128)(2,1)S(1)} %collective-permute-done.refs_0_), channel_id=1, source_target_pairs={{0,6},{1,7},{2,4},{3,5},{4,2},{5,3},{6,0},{7,1},{8,14},{9,15},{10,... | collective-permute-start | bytes 405512 | tf_op jit(solution)/shard_map/ppermute | solution.py:284
  19.4 1.1 %collective-permute-start.9 = (bf16[16,4224]{1,0:T(8,128)(2,1)S(1)}, bf16[16,4224]{1,0:T(8,128)(2,1)S(1)}, u32[]{:S(2)}, u32[]{:S(2)}) collective-permute-start(bf16[16,4224]{1,0:T(8,128)(2,1)S(1)} %collective-permute-done.2.refs_3_), channel_id=1, source_target_pairs={{0,8},{8,0},{16,24},{24,16},{1,9},{9,1},{17,25},{25,17},{2,10},{10... | collective-permute-start | bytes 405512 | tf_op jit(solution)/shard_map/ppermute | solution.py:289
  20.5 4.0 %collective-permute-done.8.refs_1_ = bf16[16,4224]{1,0:T(8,128)(2,1)S(1)} collective-permute-done((bf16[16,4224]{1,0:T(8,128)(2,1)S(1)}, bf16[16,4224]{1,0:T(8,128)(2,1)S(1)}, u32[]{:S(2)}, u32[]{:S(2)}) %collective-permute-start.8) | collective-permute-done | bytes 135200 | tf_op jit(solution)/shard_map/ppermute | solution.py:289
  24.5 0.8 fetch.1.refs_7_.refs_13_
  25.8 6.1 %collective-permute-done.10.refs_5_ = bf16[16,4224]{1,0:T(8,128)(2,1)S(1)} collective-permute-done((bf16[16,4224]{1,0:T(8,128)(2,1)S(1)}, bf16[16,4224]{1,0:T(8,128)(2,1)S(1)}, u32[]{:S(2)}, u32[]{:S(2)}) %collective-permute-start.10) | collective-permute-done | bytes 135200 | tf_op jit(solution)/shard_map/ppermute | solution.py:289
  31.9 1.6 %collective-permute-start.13 = (bf16[32,4224]{1,0:T(8,128)(2,1)S(1)}, bf16[32,4224]{1,0:T(8,128)(2,1)S(1)}, u32[]{:S(2)}, u32[]{:S(2)}) collective-permute-start(bf16[32,4224]{1,0:T(8,128)(2,1)S(1)} %gather.5.refs_1_), channel_id=1, source_target_pairs={{0,2},{1,3},{2,0},{3,1},{4,6},{5,7},{6,4},{7,5},{8,10},{9,11},{10,... | collective-permute-start | bytes 811016 | tf_op jit(solution)/shard_map/ppermute | solution.py:284
  33.8 5.1 %experts.2 = (bf16[32,4096]{1,0:T(8,128)(2,1)S(1)}, bf16[32,4096]{1,0:T(8,128)(2,1)S(1)}, bf16[16,4096]{1,0:T(8,128)(2,1)S(1)}, bf16[80,4096]{1,0:T(8,128)(2,1)S...) custom-call(s32[1]{0:T(128)} %bitcast.own_ref.refs_0_, bf16[64,4224]{1,0:T(8,128)(2,1)S(1)} %gather.3.refs_1_, ...), custom_call_target="tpu_custom_call" | custom-call | flops 4831838208 | bytes 4194304 | tf_op jit(solution)/shard_map/experts/pallas_call | solution.py:197
  38.9 1.9 %collective-permute-done.13.refs_2_ = bf16[32,4224]{1,0:T(8,128)(2,1)S(1)} collective-permute-done((bf16[32,4224]{1,0:T(8,128)(2,1)S(1)}, bf16[32,4224]{1,0:T(8,128)(2,1)S(1)}, u32[]{:S(2)}, u32[]{:S(2)}) %collective-permute-start.13) | collective-permute-done | bytes 270368 | tf_op jit(solution)/shard_map/ppermute | solution.py:284
  40.9 1.3 %collective-permute-done.14.refs_3_ = bf16[32,4224]{1,0:T(8,128)(2,1)S(1)} collective-permute-done((bf16[32,4224]{1,0:T(8,128)(2,1)S(1)}, bf16[32,4224]{1,0:T(8,128)(2,1)S(1)}, u32[]{:S(2)}, u32[]{:S(2)}) %collective-permute-start.14) | collective-permute-done | bytes 270368 | tf_op jit(solution)/shard_map/ppermute | solution.py:284
  43.2 1.1 %collective-permute-done.15 = bf16[80,4096]{1,0:T(8,128)(2,1)S(1)} collective-permute-done((bf16[80,4096]{1,0:T(8,128)(2,1)S(1)}, bf16[80,4096]{1,0:T(8,128)(2,1)S(1)}, u32[]{:S(2)}, u32[]{:S(2)}) %collective-permute-start.15) | collective-permute-done | bytes 655392 | tf_op jit(solution)/shard_map/ppermute | solution.py:284
  45.5 1.5 %collective-permute-start.23 = (bf16[32,4096]{1,0:T(8,128)(2,1)S(1)}, bf16[32,4096]{1,0:T(8,128)(2,1)S(1)}, u32[]{:S(2)}, u32[]{:S(2)}) collective-permute-start(bf16[32,4096]{1,0:T(8,128)(2,1)S(1)} %get-tuple-element.96), channel_id=1, source_target_pairs={{0,4},{1,5},{2,6},{3,7},{4,0},{5,1},{6,2},{7,3},{8,12},{9,13},{10,... | collective-permute-start | bytes 786440 | tf_op jit(solution)/shard_map/ppermute | solution.py:284
  47.0 2.1 %collective-permute-start.24 = (bf16[16,4096]{1,0:T(8,128)(2,1)S(1)}, bf16[16,4096]{1,0:T(8,128)(2,1)S(1)}, u32[]{:S(2)}, u32[]{:S(2)}) collective-permute-start(bf16[16,4096]{1,0:T(8,128)(2,1)S(1)} %add_convert_fusion.8), channel_id=1, source_target_pairs={{0,24},{8,16},{16,8},{24,0},{1,25},{9,17},{17,9},{25,1},{2,26},{10... | collective-permute-start | bytes 393224 | tf_op jit(solution)/shard_map/ppermute | solution.py:289
  49.1 5.1 %experts.3 = (bf16[16,4096]{1,0:T(8,128)(2,1)S(1)}, bf16[16,4096]{1,0:T(8,128)(2,1)S(1)}, bf16[32,4096]{1,0:T(8,128)(2,1)S(1)}, bf16[32,4096]{1,0:T(8,128)(2,1)S...) custom-call(s32[1]{0:T(128)} %bitcast.own_ref.refs_0_, ...), custom_call_target="tpu_custom_call" | custom-call | flops 4831838208 | bytes 4194304 | tf_op jit(solution)/shard_map/experts/pallas_call | solution.py:197
  54.5 2.1 %collective-permute-done.25 = bf16[96,4096]{1,0:T(8,128)(2,1)S(1)} collective-permute-done((bf16[96,4096]{1,0:T(8,128)(2,1)S(1)}, bf16[96,4096]{1,0:T(8,128)(2,1)S(1)}, u32[]{:S(2)}, u32[]{:S(2)}) %collective-permute-start.25) | collective-permute-done | bytes 786464 | tf_op jit(solution)/shard_map/ppermute | solution.py:284
  57.5 1.4 %collective-permute-start.31 = (bf16[32,4096]{1,0:T(8,128)(2,1)S(1)}, bf16[32,4096]{1,0:T(8,128)(2,1)S(1)}, u32[]{:S(2)}, u32[]{:S(2)}) collective-permute-start(bf16[32,4096]{1,0:T(8,128)(2,1)S(1)} %get-tuple-element.129), channel_id=1, source_target_pairs={{0,2},{1,3},{2,0},{3,1},{4,6},{5,7},{6,4},{7,5},{8,10},{9,11},{10,... | collective-permute-start | bytes 786440 | tf_op jit(solution)/shard_map/ppermute | solution.py:284
  58.9 1.8 %collective-permute-start.29 = (bf16[16,4096]{1,0:T(8,128)(2,1)S(1)}, bf16[16,4096]{1,0:T(8,128)(2,1)S(1)}, u32[]{:S(2)}, u32[]{:S(2)}) collective-permute-start(bf16[16,4096]{1,0:T(8,128)(2,1)S(1)} %fusion.4), channel_id=1, source_target_pairs={{0,24},{8,16},{16,8},{24,0},{1,25},{9,17},{17,9},{25,1},{2,26},{10... | collective-permute-start | bytes 393224 | tf_op jit(solution)/shard_map/ppermute | solution.py:289
  60.9 2.6 %collective-permute-start.28 = (bf16[16,4096]{1,0:T(8,128)(2,1)S(1)}, bf16[16,4096]{1,0:T(8,128)(2,1)S(1)}, u32[]{:S(2)}, u32[]{:S(2)}) collective-permute-start(bf16[16,4096]{1,0:T(8,128)(2,1)S(1)} %get-tuple-element.137), channel_id=1, source_target_pairs={{0,16},{8,24},{16,0},{24,8},{1,17},{9,25},{17,1},{25,9},{2,18},{10... | collective-permute-start | bytes 393224 | tf_op jit(solution)/shard_map/ppermute | solution.py:289
  63.4 2.0 %collective-permute-done.32 = bf16[32,4096]{1,0:T(8,128)(2,1)S(1)} collective-permute-done((bf16[32,4096]{1,0:T(8,128)(2,1)S(1)}, bf16[32,4096]{1,0:T(8,128)(2,1)S(1)}, u32[]{:S(2)}, u32[]{:S(2)}) %collective-permute-start.32) | collective-permute-done | bytes 262176 | tf_op jit(solution)/shard_map/ppermute | solution.py:284
  66.1 2.2 %collective-permute-start.33 = (bf16[16,4096]{1,0:T(8,128)(2,1)S(1)}, bf16[16,4096]{1,0:T(8,128)(2,1)S(1)}, u32[]{:S(2)}, u32[]{:S(2)}) collective-permute-start(bf16[16,4096]{1,0:T(8,128)(2,1)S(1)} %get-tuple-element.131), channel_id=1, source_target_pairs={{0,8},{8,0},{16,24},{24,16},{1,9},{9,1},{17,25},{25,17},{2,10},{10... | collective-permute-start | bytes 393224 | tf_op jit(solution)/shard_map/ppermute | solution.py:289
  68.2 3.3 %collective-permute-done.27 = bf16[16,4096]{1,0:T(8,128)(2,1)S(1)} collective-permute-done((bf16[16,4096]{1,0:T(8,128)(2,1)S(1)}, bf16[16,4096]{1,0:T(8,128)(2,1)S(1)}, u32[]{:S(2)}, u32[]{:S(2)}) %collective-permute-start.27) | collective-permute-done | bytes 131104 | tf_op jit(solution)/shard_map/ppermute | solution.py:289
  71.6 2.2 %collective-permute-done.28 = bf16[16,4096]{1,0:T(8,128)(2,1)S(1)} collective-permute-done((bf16[16,4096]{1,0:T(8,128)(2,1)S(1)}, bf16[16,4096]{1,0:T(8,128)(2,1)S(1)}, u32[]{:S(2)}, u32[]{:S(2)}) %collective-permute-start.28) | collective-permute-done | bytes 131104 | tf_op jit(solution)/shard_map/ppermute | solution.py:289
  73.9 1.5 %collective-permute-start.30 = (bf16[16,4096]{1,0:T(8,128)(2,1)S(1)}, bf16[16,4096]{1,0:T(8,128)(2,1)S(1)}, u32[]{:S(2)}, u32[]{:S(2)}) collective-permute-start(bf16[16,4096]{1,0:T(8,128)(2,1)S(1)} %fusion.2), channel_id=1, source_target_pairs={{0,6},{1,7},{2,4},{3,5},{4,2},{5,3},{6,0},{7,1},{8,14},{9,15},{10,... | collective-permute-start | bytes 393224 | tf_op jit(solution)/shard_map/ppermute | solution.py:284
  75.4 1.8 %collective-permute-done.34 = bf16[16,4096]{1,0:T(8,128)(2,1)S(1)} collective-permute-done((bf16[16,4096]{1,0:T(8,128)(2,1)S(1)}, bf16[16,4096]{1,0:T(8,128)(2,1)S(1)}, u32[]{:S(2)}, u32[]{:S(2)}) %collective-permute-start.34) | collective-permute-done | bytes 131104 | tf_op jit(solution)/shard_map/ppermute | solution.py:289
  77.2 2.6 %collective-permute-done.30 = bf16[16,4096]{1,0:T(8,128)(2,1)S(1)} collective-permute-done((bf16[16,4096]{1,0:T(8,128)(2,1)S(1)}, bf16[16,4096]{1,0:T(8,128)(2,1)S(1)}, u32[]{:S(2)}, u32[]{:S(2)}) %collective-permute-start.30) | collective-permute-done | bytes 131104 | tf_op jit(solution)/shard_map/ppermute | solution.py:284
  79.8 0.8 fusion.9
  (75 shorter events, 8.0 us)
Async XLA Ops:
  1.2 12.8 %collective-permute-start = (bf16[16,4224]{1,0:T(8,128)(2,1)S(1)}, bf16[16,4224]{1,0:T(8,128)(2,1)S(1)}, u32[]{:S(2)}, u32[]{:S(2)}) collective-permute-start(bf16[16,4224]{1,0:T(8,128)(2,1)S(1)} %pack.1.refs_0_), channel_id=1, source_target_pairs={{0,24},{8,16},{16,8},{24,0},{1,25},{9,17},{17,9},{25,1},{2,26},{10... | collective-permute-start | bytes 405512 | tf_op jit(solution)/shard_map/ppermute | solution.py:289
  6.3 7.7 %collective-permute-start.1 = (bf16[16,4224]{1,0:T(8,128)(2,1)S(1)}, bf16[16,4224]{1,0:T(8,128)(2,1)S(1)}, u32[]{:S(2)}, u32[]{:S(2)}) collective-permute-start(bf16[16,4224]{1,0:T(8,128)(2,1)S(1)} %pack.1.refs_0_), channel_id=1, source_target_pairs={{0,8},{8,0},{16,24},{24,16},{1,9},{9,1},{17,25},{25,17},{2,10},{10... | collective-permute-start | bytes 405512 | tf_op jit(solution)/shard_map/ppermute | solution.py:289
  6.3 7.7 %collective-permute-start.2 = (bf16[16,4224]{1,0:T(8,128)(2,1)S(1)}, bf16[16,4224]{1,0:T(8,128)(2,1)S(1)}, u32[]{:S(2)}, u32[]{:S(2)}) collective-permute-start(bf16[16,4224]{1,0:T(8,128)(2,1)S(1)} %pack.1.refs_0_), channel_id=1, source_target_pairs={{0,6},{1,7},{2,4},{3,5},{4,2},{5,3},{6,0},{7,1},{8,14},{9,15},{10,... | collective-permute-start | bytes 405512 | tf_op jit(solution)/shard_map/ppermute | solution.py:284
  8.8 6.4 %collective-permute-start.3 = (bf16[16,4224]{1,0:T(8,128)(2,1)S(1)}, bf16[16,4224]{1,0:T(8,128)(2,1)S(1)}, u32[]{:S(2)}, u32[]{:S(2)}) collective-permute-start(bf16[16,4224]{1,0:T(8,128)(2,1)S(1)} %pack.1.refs_0_), channel_id=1, source_target_pairs={{0,4},{1,5},{2,6},{3,7},{4,0},{5,1},{6,2},{7,3},{8,12},{9,13},{10,... | collective-permute-start | bytes 405512 | tf_op jit(solution)/shard_map/ppermute | solution.py:284
  9.3 5.9 %collective-permute-start.4 = (bf16[16,4224]{1,0:T(8,128)(2,1)S(1)}, bf16[16,4224]{1,0:T(8,128)(2,1)S(1)}, u32[]{:S(2)}, u32[]{:S(2)}) collective-permute-start(bf16[16,4224]{1,0:T(8,128)(2,1)S(1)} %pack.1.refs_0_), channel_id=1, source_target_pairs={{0,2},{1,3},{2,0},{3,1},{4,6},{5,7},{6,4},{7,5},{8,10},{9,11},{10,... | collective-permute-start | bytes 405512 | tf_op jit(solution)/shard_map/ppermute | solution.py:284
  15.2 9.2 %collective-permute-start.8 = (bf16[16,4224]{1,0:T(8,128)(2,1)S(1)}, bf16[16,4224]{1,0:T(8,128)(2,1)S(1)}, u32[]{:S(2)}, u32[]{:S(2)}) collective-permute-start(bf16[16,4224]{1,0:T(8,128)(2,1)S(1)} %pack.1.refs_0_), channel_id=1, source_target_pairs={{0,16},{8,24},{16,0},{24,8},{1,17},{9,25},{17,1},{25,9},{2,18},{10... | collective-permute-start | bytes 405512 | tf_op jit(solution)/shard_map/ppermute | solution.py:289
  15.9 9.4 %collective-permute-start.5 = (bf16[16,4224]{1,0:T(8,128)(2,1)S(1)}, bf16[16,4224]{1,0:T(8,128)(2,1)S(1)}, u32[]{:S(2)}, u32[]{:S(2)}) collective-permute-start(bf16[16,4224]{1,0:T(8,128)(2,1)S(1)} %collective-permute-done.refs_0_), channel_id=1, source_target_pairs={{0,2},{1,3},{2,0},{3,1},{4,6},{5,7},{6,4},{7,5},{8,10},{9,11},{10,... | collective-permute-start | bytes 405512 | tf_op jit(solution)/shard_map/ppermute | solution.py:284
  17.4 7.9 %collective-permute-start.6 = (bf16[16,4224]{1,0:T(8,128)(2,1)S(1)}, bf16[16,4224]{1,0:T(8,128)(2,1)S(1)}, u32[]{:S(2)}, u32[]{:S(2)}) collective-permute-start(bf16[16,4224]{1,0:T(8,128)(2,1)S(1)} %collective-permute-done.refs_0_), channel_id=1, source_target_pairs={{0,4},{1,5},{2,6},{3,7},{4,0},{5,1},{6,2},{7,3},{8,12},{9,13},{10,... | collective-permute-start | bytes 405512 | tf_op jit(solution)/shard_map/ppermute | solution.py:284
  18.1 7.2 %collective-permute-start.7 = (bf16[16,4224]{1,0:T(8,128)(2,1)S(1)}, bf16[16,4224]{1,0:T(8,128)(2,1)S(1)}, u32[]{:S(2)}, u32[]{:S(2)}) collective-permute-start(bf16[16,4224]{1,0:T(8,128)(2,1)S(1)} %collective-permute-done.refs_0_), channel_id=1, source_target_pairs={{0,6},{1,7},{2,4},{3,5},{4,2},{5,3},{6,0},{7,1},{8,14},{9,15},{10,... | collective-permute-start | bytes 405512 | tf_op jit(solution)/shard_map/ppermute | solution.py:284
  19.4 6.4 %collective-permute-start.9 = (bf16[16,4224]{1,0:T(8,128)(2,1)S(1)}, bf16[16,4224]{1,0:T(8,128)(2,1)S(1)}, u32[]{:S(2)}, u32[]{:S(2)}) collective-permute-start(bf16[16,4224]{1,0:T(8,128)(2,1)S(1)} %collective-permute-done.2.refs_3_), channel_id=1, source_target_pairs={{0,8},{8,0},{16,24},{24,16},{1,9},{9,1},{17,25},{25,17},{2,10},{10... | collective-permute-start | bytes 405512 | tf_op jit(solution)/shard_map/ppermute | solution.py:289
  24.4 7.5 %collective-permute-start.10 = (bf16[16,4224]{1,0:T(8,128)(2,1)S(1)}, bf16[16,4224]{1,0:T(8,128)(2,1)S(1)}, u32[]{:S(2)}, u32[]{:S(2)}) collective-permute-start(bf16[16,4224]{1,0:T(8,128)(2,1)S(1)} %collective-permute-done.2.refs_3_), channel_id=1, source_target_pairs={{0,16},{8,24},{16,0},{24,8},{1,17},{9,25},{17,1},{25,9},{2,18},{10... | collective-permute-start | bytes 405512 | tf_op jit(solution)/shard_map/ppermute | solution.py:289
  25.3 8.5 %collective-permute-start.11 = (bf16[64,4224]{1,0:T(8,128)(2,1)S(1)}, bf16[64,4224]{1,0:T(8,128)(2,1)S(1)}, u32[]{:S(2)}, u32[]{:S(2)}) collective-permute-start(bf16[64,4224]{1,0:T(8,128)(2,1)S(1)} %gather.3.refs_1_), channel_id=1, source_target_pairs={{0,1},{1,0},{2,3},{3,2},{4,5},{5,4},{6,7},{7,6},{8,9},{9,8},{10,11... | collective-permute-start | bytes 1622024 | tf_op jit(solution)/shard_map/ppermute | solution.py:284
  31.9 8.9 %collective-permute-start.13 = (bf16[32,4224]{1,0:T(8,128)(2,1)S(1)}, bf16[32,4224]{1,0:T(8,128)(2,1)S(1)}, u32[]{:S(2)}, u32[]{:S(2)}) collective-permute-start(bf16[32,4224]{1,0:T(8,128)(2,1)S(1)} %gather.5.refs_1_), channel_id=1, source_target_pairs={{0,2},{1,3},{2,0},{3,1},{4,6},{5,7},{6,4},{7,5},{8,10},{9,11},{10,... | collective-permute-start | bytes 811016 | tf_op jit(solution)/shard_map/ppermute | solution.py:284
  33.5 8.6 %collective-permute-start.14 = (bf16[32,4224]{1,0:T(8,128)(2,1)S(1)}, bf16[32,4224]{1,0:T(8,128)(2,1)S(1)}, u32[]{:S(2)}, u32[]{:S(2)}) collective-permute-start(bf16[32,4224]{1,0:T(8,128)(2,1)S(1)} %gather.5.refs_1_), channel_id=1, source_target_pairs={{0,4},{1,5},{2,6},{3,7},{4,0},{5,1},{6,2},{7,3},{8,12},{9,13},{10,... | collective-permute-start | bytes 811016 | tf_op jit(solution)/shard_map/ppermute | solution.py:284
  42.1 3.4 %collective-permute-start.17 = (bf16[32,4224]{1,0:T(8,128)(2,1)S(1)}, bf16[32,4224]{1,0:T(8,128)(2,1)S(1)}, u32[]{:S(2)}, u32[]{:S(2)}) collective-permute-start(bf16[32,4224]{1,0:T(8,128)(2,1)S(1)} %gather.5.refs_1_), channel_id=1, source_target_pairs={{0,1},{1,0},{2,3},{3,2},{4,5},{5,4},{6,7},{7,6},{8,9},{9,8},{10,11... | collective-permute-start | bytes 811016 | tf_op jit(solution)/shard_map/ppermute | solution.py:284
  42.7 2.4 %collective-permute-start.21 = (bf16[16,4224]{1,0:T(8,128)(2,1)S(1)}, bf16[16,4224]{1,0:T(8,128)(2,1)S(1)}, u32[]{:S(2)}, u32[]{:S(2)}) collective-permute-start(bf16[16,4224]{1,0:T(8,128)(2,1)S(1)} %collective-permute-done.10.refs_5_), channel_id=1, source_target_pairs={{0,1},{1,0},{2,3},{3,2},{4,5},{5,4},{6,7},{7,6},{8,9},{9,8},{10,11... | collective-permute-start | bytes 405512 | tf_op jit(solution)/shard_map/ppermute | solution.py:284
  43.2 3.9 %collective-permute-start.18 = (bf16[32,4224]{1,0:T(8,128)(2,1)S(1)}, bf16[32,4224]{1,0:T(8,128)(2,1)S(1)}, u32[]{:S(2)}, u32[]{:S(2)}) collective-permute-start(bf16[32,4224]{1,0:T(8,128)(2,1)S(1)} %collective-permute-done.13.refs_2_), channel_id=1, source_target_pairs={{0,1},{1,0},{2,3},{3,2},{4,5},{5,4},{6,7},{7,6},{8,9},{9,8},{10,11... | collective-permute-start | bytes 811016 | tf_op jit(solution)/shard_map/ppermute | solution.py:284
  44.2 4.9 %collective-permute-start.19 = (bf16[32,4224]{1,0:T(8,128)(2,1)S(1)}, bf16[32,4224]{1,0:T(8,128)(2,1)S(1)}, u32[]{:S(2)}, u32[]{:S(2)}) collective-permute-start(bf16[32,4224]{1,0:T(8,128)(2,1)S(1)} %collective-permute-done.14.refs_3_), channel_id=1, source_target_pairs={{0,1},{1,0},{2,3},{3,2},{4,5},{5,4},{6,7},{7,6},{8,9},{9,8},{10,11... | collective-permute-start | bytes 811016 | tf_op jit(solution)/shard_map/ppermute | solution.py:284
  44.8 9.5 %collective-permute-start.16 = (bf16[48,4096]{1,0:T(8,128)(2,1)S(1)}, bf16[48,4096]{1,0:T(8,128)(2,1)S(1)}, u32[]{:S(2)}, u32[]{:S(2)}) collective-permute-start(bf16[48,4096]{1,0:T(8,128)(2,1)S(1)} %get-tuple-element.94), channel_id=1, source_target_pairs={{0,1},{1,0},{2,3},{3,2},{4,5},{5,4},{6,7},{7,6},{8,9},{9,8},{10,11... | collective-permute-start | bytes 1179656 | tf_op jit(solution)/shard_map/ppermute | solution.py:284
  45.0 9.3 %collective-permute-start.22 = (bf16[32,4096]{1,0:T(8,128)(2,1)S(1)}, bf16[32,4096]{1,0:T(8,128)(2,1)S(1)}, u32[]{:S(2)}, u32[]{:S(2)}) collective-permute-start(bf16[32,4096]{1,0:T(8,128)(2,1)S(1)} %get-tuple-element.95), channel_id=1, source_target_pairs={{0,2},{1,3},{2,0},{3,1},{4,6},{5,7},{6,4},{7,5},{8,10},{9,11},{10,... | collective-permute-start | bytes 786440 | tf_op jit(solution)/shard_map/ppermute | solution.py:284
  45.5 8.8 %collective-permute-start.23 = (bf16[32,4096]{1,0:T(8,128)(2,1)S(1)}, bf16[32,4096]{1,0:T(8,128)(2,1)S(1)}, u32[]{:S(2)}, u32[]{:S(2)}) collective-permute-start(bf16[32,4096]{1,0:T(8,128)(2,1)S(1)} %get-tuple-element.96), channel_id=1, source_target_pairs={{0,4},{1,5},{2,6},{3,7},{4,0},{5,1},{6,2},{7,3},{8,12},{9,13},{10,... | collective-permute-start | bytes 786440 | tf_op jit(solution)/shard_map/ppermute | solution.py:284
  47.0 7.3 %collective-permute-start.24 = (bf16[16,4096]{1,0:T(8,128)(2,1)S(1)}, bf16[16,4096]{1,0:T(8,128)(2,1)S(1)}, u32[]{:S(2)}, u32[]{:S(2)}) collective-permute-start(bf16[16,4096]{1,0:T(8,128)(2,1)S(1)} %add_convert_fusion.8), channel_id=1, source_target_pairs={{0,24},{8,16},{16,8},{24,0},{1,25},{9,17},{17,9},{25,1},{2,26},{10... | collective-permute-start | bytes 393224 | tf_op jit(solution)/shard_map/ppermute | solution.py:289
  54.2 2.4 %collective-permute-start.25 = (bf16[96,4096]{1,0:T(8,128)(2,1)S(1)}, bf16[96,4096]{1,0:T(8,128)(2,1)S(1)}, u32[]{:S(2)}, u32[]{:S(2)}) collective-permute-start(bf16[96,4096]{1,0:T(8,128)(2,1)S(1)} %get-tuple-element.117), channel_id=1, source_target_pairs={{0,1},{1,0},{2,3},{3,2},{4,5},{5,4},{6,7},{7,6},{8,9},{9,8},{10,11... | collective-permute-start | bytes 2359304 | tf_op jit(solution)/shard_map/ppermute | solution.py:284
  56.7 4.0 %collective-permute-start.26 = (bf16[32,4096]{1,0:T(8,128)(2,1)S(1)}, bf16[32,4096]{1,0:T(8,128)(2,1)S(1)}, u32[]{:S(2)}, u32[]{:S(2)}) collective-permute-start(bf16[32,4096]{1,0:T(8,128)(2,1)S(1)} %get-tuple-element.121), channel_id=1, source_target_pairs={{0,1},{1,0},{2,3},{3,2},{4,5},{5,4},{6,7},{7,6},{8,9},{9,8},{10,11... | collective-permute-start | bytes 786440 | tf_op jit(solution)/shard_map/ppermute | solution.py:284
  56.9 8.6 %collective-permute-start.32 = (bf16[32,4096]{1,0:T(8,128)(2,1)S(1)}, bf16[32,4096]{1,0:T(8,128)(2,1)S(1)}, u32[]{:S(2)}, u32[]{:S(2)}) collective-permute-start(bf16[32,4096]{1,0:T(8,128)(2,1)S(1)} %get-tuple-element.130), channel_id=1, source_target_pairs={{0,4},{1,5},{2,6},{3,7},{4,0},{5,1},{6,2},{7,3},{8,12},{9,13},{10,... | collective-permute-start | bytes 786440 | tf_op jit(solution)/shard_map/ppermute | solution.py:284
  57.5 8.3 %collective-permute-start.31 = (bf16[32,4096]{1,0:T(8,128)(2,1)S(1)}, bf16[32,4096]{1,0:T(8,128)(2,1)S(1)}, u32[]{:S(2)}, u32[]{:S(2)}) collective-permute-start(bf16[32,4096]{1,0:T(8,128)(2,1)S(1)} %get-tuple-element.129), channel_id=1, source_target_pairs={{0,2},{1,3},{2,0},{3,1},{4,6},{5,7},{6,4},{7,5},{8,10},{9,11},{10,... | collective-permute-start | bytes 786440 | tf_op jit(solution)/shard_map/ppermute | solution.py:284
  58.9 9.3 %collective-permute-start.29 = (bf16[16,4096]{1,0:T(8,128)(2,1)S(1)}, bf16[16,4096]{1,0:T(8,128)(2,1)S(1)}, u32[]{:S(2)}, u32[]{:S(2)}) collective-permute-start(bf16[16,4096]{1,0:T(8,128)(2,1)S(1)} %fusion.4), channel_id=1, source_target_pairs={{0,24},{8,16},{16,8},{24,0},{1,25},{9,17},{17,9},{25,1},{2,26},{10... | collective-permute-start | bytes 393224 | tf_op jit(solution)/shard_map/ppermute | solution.py:289
  60.8 10.8 %collective-permute-start.27 = (bf16[16,4096]{1,0:T(8,128)(2,1)S(1)}, bf16[16,4096]{1,0:T(8,128)(2,1)S(1)}, u32[]{:S(2)}, u32[]{:S(2)}) collective-permute-start(bf16[16,4096]{1,0:T(8,128)(2,1)S(1)} %get-tuple-element.138), channel_id=1, source_target_pairs={{0,8},{8,0},{16,24},{24,16},{1,9},{9,1},{17,25},{25,17},{2,10},{10... | collective-permute-start | bytes 393224 | tf_op jit(solution)/shard_map/ppermute | solution.py:289
  60.9 12.9 %collective-permute-start.28 = (bf16[16,4096]{1,0:T(8,128)(2,1)S(1)}, bf16[16,4096]{1,0:T(8,128)(2,1)S(1)}, u32[]{:S(2)}, u32[]{:S(2)}) collective-permute-start(bf16[16,4096]{1,0:T(8,128)(2,1)S(1)} %get-tuple-element.137), channel_id=1, source_target_pairs={{0,16},{8,24},{16,0},{24,8},{1,17},{9,25},{17,1},{25,9},{2,18},{10... | collective-permute-start | bytes 393224 | tf_op jit(solution)/shard_map/ppermute | solution.py:289
  66.0 11.2 %collective-permute-start.34 = (bf16[16,4096]{1,0:T(8,128)(2,1)S(1)}, bf16[16,4096]{1,0:T(8,128)(2,1)S(1)}, u32[]{:S(2)}, u32[]{:S(2)}) collective-permute-start(bf16[16,4096]{1,0:T(8,128)(2,1)S(1)} %get-tuple-element.132), channel_id=1, source_target_pairs={{0,16},{8,24},{16,0},{24,8},{1,17},{9,25},{17,1},{25,9},{2,18},{10... | collective-permute-start | bytes 393224 | tf_op jit(solution)/shard_map/ppermute | solution.py:289
  66.1 11.2 %collective-permute-start.33 = (bf16[16,4096]{1,0:T(8,128)(2,1)S(1)}, bf16[16,4096]{1,0:T(8,128)(2,1)S(1)}, u32[]{:S(2)}, u32[]{:S(2)}) collective-permute-start(bf16[16,4096]{1,0:T(8,128)(2,1)S(1)} %get-tuple-element.131), channel_id=1, source_target_pairs={{0,8},{8,0},{16,24},{24,16},{1,9},{9,1},{17,25},{25,17},{2,10},{10... | collective-permute-start | bytes 393224 | tf_op jit(solution)/shard_map/ppermute | solution.py:289
  73.9 5.9 %collective-permute-start.30 = (bf16[16,4096]{1,0:T(8,128)(2,1)S(1)}, bf16[16,4096]{1,0:T(8,128)(2,1)S(1)}, u32[]{:S(2)}, u32[]{:S(2)}) collective-permute-start(bf16[16,4096]{1,0:T(8,128)(2,1)S(1)} %fusion.2), channel_id=1, source_target_pairs={{0,6},{1,7},{2,4},{3,5},{4,2},{5,3},{6,0},{7,1},{8,14},{9,15},{10,... | collective-permute-start | bytes 393224 | tf_op jit(solution)/shard_map/ppermute | solution.py:284
  (11 other events, 67.7 us)

commit v11 on v9

--- a/solution.py
+++ b/solution.py
@@ -321,65 +321,67 @@
     tokens, own, begin = ordered(tokens, own, begin)
     packed = with_routing(tokens, routed_experts, route_weights)
 
-    three = swap_rep(packed, 3)
+    two = swap_rep(packed, 2)
     x_own, y_own, far_own = [swap_exp(packed, bits) for bits in (2, 4, 6)]
     gates, ups = fetched(gate_weight, True), fetched(up_weight, True)
     one = swap_rep(packed, 1)
-    x_own, y_own, far_own, one, three, gates, ups, again = ordered(
-        x_own, y_own, far_own, one, three, gates, ups, packed
-    )
-    two = swap_rep(again, 2)
-    x_three, y_three, far_three = [swap_exp(three, bits) for bits in (2, 4, 6)]
-    far_one, far_two = swap_rep(far_own, 1), swap_rep(far_own, 2)
+    x_own, y_own, far_own, one, two, gates, ups = ordered(
+        x_own, y_own, far_own, one, two, gates, ups
+    )
+    three = swap_rep(two, 1)
+    x_two, y_two, far_two = [swap_exp(two, bits) for bits in (2, 4, 6)]
+    far_one, far_three = swap_rep(far_own, 1), swap_rep(far_two, 1)
     first = gathered(packed, x_own, y_own, far_own)
     first_other = swap_exp(first, 1)
-    second = gathered(three, x_three, y_three, far_three)
-    two, down_weight = ordered(two, down_weight)
+    second = gathered(two, x_two, y_two, far_two)
+    three, down_weight = ordered(three, down_weight)
     downs = fetched(down_weight, False)
     second, downs = ordered(second, downs)
-    pair = gathered(one, two)
+    pair = gathered(one, three)
     x_pair, y_pair = swap_exp(pair, 2), swap_exp(pair, 4)
 
     near = [first, second, first_other, swap_exp(second, 1)]
     groups = row_groups([[5, 1], [6, 2], [7], [13, 9, 14, 10, 15], [4, 0, 3], [12, 8, 11]], rows)
     parts = experts_of(own, near, groups, gates, ups, downs, shard_units, top)
-    *parts, x_pair, y_pair, far_one, far_two = ordered(*parts, x_pair, y_pair, far_one, far_two)
+    *parts, x_pair, y_pair, far_one, far_three = ordered(
+        *parts, x_pair, y_pair, far_one, far_three
+    )
     to_x, to_y, to_far, other, near_kept, near_other = parts
     back = swap_exp(other, 1)
     to_x = rounded(to_x, back[: 2 * rows])
     to_y = rounded(to_y, back[2 * rows : 4 * rows])
     to_far = rounded(to_far, back[4 * rows :])
     to_x, to_y, to_far, near_other = ordered(to_x, to_y, to_far, near_other)
-    near_x, near_y, near_far = swap_exp(to_x, 2), swap_exp(to_y, 4), swap_rep(to_far, 3)
+    near_x, near_y, near_far = swap_exp(to_x, 2), swap_exp(to_y, 4), swap_rep(to_far, 2)
     near_back = swap_exp(near_other, 1)
 
-    far = [pair, x_pair, y_pair, far_one, far_two]
+    far = [pair, x_pair, y_pair, far_one, far_three]
     far = far + [swap_exp(piece, 1) for piece in far]
     to_x, to_y, to_far, *far = ordered(to_x, to_y, to_far, *far)
     groups = row_groups([[6], [7], [2, 3], [4, 5], [10, 11, 12, 13, 8, 9], [14, 15], [0, 1]], rows)
     parts = experts_of(own, far, groups, gates, ups, downs, shard_units, top)
-    to_one, to_two, to_x, to_y, other, other_far, far_kept = parts
+    to_one, to_three, to_x, to_y, other, other_far, far_kept = parts
     far_kept, near_far, near_y, near_x = ordered(far_kept, near_far, near_y, near_x)
     back = swap_exp(other, 1)
     kept = added(near_kept, near_back)
-    to_three = rounded(kept[:rows], near_x[:rows], near_y[:rows])
-    back, to_three = ordered(back, to_three)
-    from_three = swap_rep(to_three, 3)
+    to_two = rounded(kept[:rows], near_x[:rows], near_y[:rows])
+    back, to_two = ordered(back, to_two)
+    from_two = swap_rep(to_two, 2)
     to_x, to_y = rounded(to_x, back[: 2 * rows]), rounded(to_y, back[2 * rows : 4 * rows])
     to_x, to_y, other_far = ordered(to_x, to_y, other_far)
     far_x, far_y = swap_exp(to_x, 2), swap_exp(to_y, 4)
     back_far = swap_exp(other_far, 1)
-    to_one, to_two = rounded(to_one, back_far[:rows]), rounded(to_two, back_far[rows:])
-    from_two, from_one = swap_rep(to_two, 2), swap_rep(to_one, 1)
+    to_one, to_three = rounded(to_one, back_far[:rows]), rounded(to_three, back_far[rows:])
+    from_three, from_one = swap_rep(to_three, 3), swap_rep(to_one, 1)
 
     own_sum = kept[rows : 2 * rows] + added(near_x[rows:], near_y[rows:])
-    from_one, from_two, from_three = ordered(from_one, from_two, from_three)
-    to_far = rounded(kept[2 * rows :], from_one, from_two, near_far)
+    from_one, from_three, from_two = ordered(from_one, from_three, from_two)
+    to_far = rounded(kept[2 * rows :], from_one, from_three, near_far)
     from_far = swap_exp(to_far, 6)
     to_one = rounded(far_kept[:rows], back[4 * rows : 5 * rows], far_x[:rows], far_y[:rows])
-    to_two = rounded(far_kept[rows:], back[5 * rows :], far_x[rows:], far_y[rows:])
-    arrived = [swap_rep(to_one, 1), swap_rep(to_two, 2)]
-    return rounded(own_sum, from_three, from_far, *arrived)
+    to_three = rounded(far_kept[rows:], back[5 * rows :], far_x[rows:], far_y[rows:])
+    arrived = [swap_rep(to_one, 1), swap_rep(to_three, 3)]
+    return rounded(own_sum, from_two, from_far, *arrived)
 
 
 def solution(mesh):

time: 72.6 us -> 71.4 us (0.983)
  starting transfers between devices: 33.5 us -> 31.1 us
  waiting for transfers between devices: 20.8 us -> 22.1 us
    ppermute x24, waiting for transfers between devices: 11.1 us -> 14 us  [swap_exp(): return lax.ppermute(value, 'exp', [(i, i ^ bits) for i in range(owners)])]
    ppermute x11, starting transfers between devices: 16.5 us -> 14.1 us  [swap_rep(): return lax.ppermute(value, 'rep', [(i, i ^ bits) for i in range(replicas)])]
    ppermute x11, waiting for transfers between devices: 9.77 us -> 8.11 us  [swap_rep(): return lax.ppermute(value, 'rep', [(i, i ^ bits) for i in range(replicas)])]
  transfers between devices with their start and end apart: 35 -> 35, of which waited for: 16 -> 17; matrix products, arithmetic and copies ran while one was open for 1% -> 1% of each run, Pallas kernels for 21% -> 21%
where the time goes in v11:
time: 71.4 us; the launch traced here: 71.3 us
  starting transfers between devices  31.1 us (44%)
  waiting for transfers between devices  22.1 us (31%)
  Pallas kernels  16 us (22%)
  other arithmetic  1.48 us (2%)
    ppermute x24, starting transfers between devices, swap_exp(): return lax.ppermute(value, 'exp', [(i, i ^ bits) for i in range(owners)])  17 us
    ppermute x11, starting transfers between devices, swap_rep(): return lax.ppermute(value, 'rep', [(i, i ^ bits) for i in range(replicas)])  14.1 us
    ppermute x24, waiting for transfers between devices, swap_exp(): return lax.ppermute(value, 'exp', [(i, i ^ bits) for i in range(owners)])  14 us
    pallas_call x2, Pallas kernels, experts_of(): pl.pallas_call(kernel, out_shape=[jax.ShapeDtypeStruct((count, model_widt...  10.2 us
    ppermute x11, waiting for transfers between devices, swap_rep(): return lax.ppermute(value, 'rep', [(i, i ^ bits) for i in range(replicas)])  8.11 us
    pallas_call x3, Pallas kernels, fetched(): pl.pallas_call(functools.partial(fetch_kernel, turn), out_shape=jax.Shape...  4.88 us
  transfers between devices with their start and end apart: 35, of which 17 were waited for; matrix products, arithmetic and copies ran while one was open for 1% of the time, Pallas kernels for 21%

profile of v11, /device:TPU:0, one launch (start us, length us, event | category | flops | bytes accessed | tf_op | source)
XLA Modules:
  0.0 71.3 jit_solution(9774634092745863902)
XLA Ops:
  1.2 4.1 %collective-permute-start.4 = (bf16[16,4224]{1,0:T(8,128)(2,1)S(1)}, bf16[16,4224]{1,0:T(8,128)(2,1)S(1)}, u32[]{:S(2)}, u32[]{:S(2)}) collective-permute-start(bf16[16,4224]{1,0:T(8,128)(2,1)S(1)} %pack.1.refs_0_), channel_id=1, source_target_pairs={{0,16},{8,24},{16,0},{24,8},{1,17},{9,25},{17,1},{25,9},{2,18},{10... | collective-permute-start | bytes 405512 | tf_op jit(solution)/shard_map/ppermute | solution.py:289
  5.3 1.6 %collective-permute-start.3 = (bf16[16,4224]{1,0:T(8,128)(2,1)S(1)}, bf16[16,4224]{1,0:T(8,128)(2,1)S(1)}, u32[]{:S(2)}, u32[]{:S(2)}) collective-permute-start(bf16[16,4224]{1,0:T(8,128)(2,1)S(1)} %pack.1.refs_0_), channel_id=1, source_target_pairs={{0,8},{8,0},{16,24},{24,16},{1,9},{9,1},{17,25},{25,17},{2,10},{10... | collective-permute-start | bytes 405512 | tf_op jit(solution)/shard_map/ppermute | solution.py:289
  6.9 2.4 %collective-permute-start.2 = (bf16[16,4224]{1,0:T(8,128)(2,1)S(1)}, bf16[16,4224]{1,0:T(8,128)(2,1)S(1)}, u32[]{:S(2)}, u32[]{:S(2)}) collective-permute-start(bf16[16,4224]{1,0:T(8,128)(2,1)S(1)} %pack.1.refs_0_), channel_id=1, source_target_pairs={{0,6},{1,7},{2,4},{3,5},{4,2},{5,3},{6,0},{7,1},{8,14},{9,15},{10,... | collective-permute-start | bytes 405512 | tf_op jit(solution)/shard_map/ppermute | solution.py:284
  10.4 2.1 %fetch_turned.2.refs_5_.refs_11_ = bf16[4096,768]{1,0:T(8,128)(2,1)S(1)} custom-call(bf16[768,4096]{1,0:T(8,128)(2,1)S(1)} %bitcast.7), custom_call_target="tpu_custom_call" | custom-call | bytes 12582912 | tf_op jit(solution)/shard_map/fetch_turned/pallas_call | solution.py:103
  12.5 2.1 %fetch_turned.3.refs_6_.refs_12_ = bf16[4096,768]{1,0:T(8,128)(2,1)S(1)} custom-call(bf16[768,4096]{1,0:T(8,128)(2,1)S(1)} %bitcast.11), custom_call_target="tpu_custom_call" | custom-call | bytes 12582912 | tf_op jit(solution)/shard_map/fetch_turned/pallas_call | solution.py:103
  14.6 0.8 %collective-permute-done.1.refs_2_ = bf16[16,4224]{1,0:T(8,128)(2,1)S(1)} collective-permute-done((bf16[16,4224]{1,0:T(8,128)(2,1)S(1)}, bf16[16,4224]{1,0:T(8,128)(2,1)S(1)}, u32[]{:S(2)}, u32[]{:S(2)}) %collective-permute-start.1) | collective-permute-done | bytes 135200 | tf_op jit(solution)/shard_map/ppermute | solution.py:284
  16.0 1.7 %collective-permute-start.7 = (bf16[16,4224]{1,0:T(8,128)(2,1)S(1)}, bf16[16,4224]{1,0:T(8,128)(2,1)S(1)}, u32[]{:S(2)}, u32[]{:S(2)}) collective-permute-start(bf16[16,4224]{1,0:T(8,128)(2,1)S(1)} %collective-permute-done.4.refs_0_), channel_id=1, source_target_pairs={{0,6},{1,7},{2,4},{3,5},{4,2},{5,3},{6,0},{7,1},{8,14},{9,15},{10,... | collective-permute-start | bytes 405512 | tf_op jit(solution)/shard_map/ppermute | solution.py:284
  17.7 1.3 %collective-permute-start.6 = (bf16[16,4224]{1,0:T(8,128)(2,1)S(1)}, bf16[16,4224]{1,0:T(8,128)(2,1)S(1)}, u32[]{:S(2)}, u32[]{:S(2)}) collective-permute-start(bf16[16,4224]{1,0:T(8,128)(2,1)S(1)} %collective-permute-done.4.refs_0_), channel_id=1, source_target_pairs={{0,4},{1,5},{2,6},{3,7},{4,0},{5,1},{6,2},{7,3},{8,12},{9,13},{10,... | collective-permute-start | bytes 405512 | tf_op jit(solution)/shard_map/ppermute | solution.py:284
  19.6 1.0 %collective-permute-done.8.refs_1_ = bf16[16,4224]{1,0:T(8,128)(2,1)S(1)} collective-permute-done((bf16[16,4224]{1,0:T(8,128)(2,1)S(1)}, bf16[16,4224]{1,0:T(8,128)(2,1)S(1)}, u32[]{:S(2)}, u32[]{:S(2)}) %collective-permute-start.8) | collective-permute-done | bytes 135200 | tf_op jit(solution)/shard_map/ppermute | solution.py:289
  20.5 0.8 %fetch.1.refs_7_.refs_13_ = bf16[768,4096]{1,0:T(8,128)(2,1)S(1)} custom-call(bf16[768,4096]{1,0:T(8,128)(2,1)S(1)} %bitcast.15), custom_call_target="tpu_custom_call" | custom-call | bytes 12582912 | tf_op jit(solution)/shard_map/fetch/pallas_call | solution.py:103
  21.3 1.6 %collective-permute-done.7.refs_3_ = bf16[16,4224]{1,0:T(8,128)(2,1)S(1)} collective-permute-done((bf16[16,4224]{1,0:T(8,128)(2,1)S(1)}, bf16[16,4224]{1,0:T(8,128)(2,1)S(1)}, u32[]{:S(2)}, u32[]{:S(2)}) %collective-permute-start.7) | collective-permute-done | bytes 135200 | tf_op jit(solution)/shard_map/ppermute | solution.py:284
  22.9 1.4 %collective-permute-done.6.refs_2_ = bf16[16,4224]{1,0:T(8,128)(2,1)S(1)} collective-permute-done((bf16[16,4224]{1,0:T(8,128)(2,1)S(1)}, bf16[16,4224]{1,0:T(8,128)(2,1)S(1)}, u32[]{:S(2)}, u32[]{:S(2)}) %collective-permute-start.6) | collective-permute-done | bytes 135200 | tf_op jit(solution)/shard_map/ppermute | solution.py:284
  24.6 1.6 %collective-permute-start.13 = (bf16[16,4224]{1,0:T(8,128)(2,1)S(1)}, bf16[16,4224]{1,0:T(8,128)(2,1)S(1)}, u32[]{:S(2)}, u32[]{:S(2)}) collective-permute-start(bf16[16,4224]{1,0:T(8,128)(2,1)S(1)} %collective-permute-done.2.refs_3_), channel_id=1, source_target_pairs={{0,8},{8,0},{16,24},{24,16},{1,9},{9,1},{17,25},{25,17},{2,10},{10... | collective-permute-start | bytes 405512 | tf_op jit(solution)/shard_map/ppermute | solution.py:289
  26.3 1.5 %collective-permute-start.12 = (bf16[32,4224]{1,0:T(8,128)(2,1)S(1)}, bf16[32,4224]{1,0:T(8,128)(2,1)S(1)}, u32[]{:S(2)}, u32[]{:S(2)}) collective-permute-start(bf16[32,4224]{1,0:T(8,128)(2,1)S(1)} %gather.5.refs_1_), channel_id=1, source_target_pairs={{0,4},{1,5},{2,6},{3,7},{4,0},{5,1},{6,2},{7,3},{8,12},{9,13},{10,... | collective-permute-start | bytes 811016 | tf_op jit(solution)/shard_map/ppermute | solution.py:284
  28.8 5.1 %experts.2 = (bf16[32,4096]{1,0:T(8,128)(2,1)S(1)}, bf16[32,4096]{1,0:T(8,128)(2,1)S(1)}, bf16[16,4096]{1,0:T(8,128)(2,1)S(1)}, bf16[80,4096]{1,0:T(8,128)(2,1)S...) custom-call(s32[1]{0:T(128)} %bitcast.own_ref.refs_0_, bf16[64,4224]{1,0:T(8,128)(2,1)S(1)} %gather.3.refs_1_, ...), custom_call_target="tpu_custom_call" | custom-call | flops 4831838208 | bytes 4194304 | tf_op jit(solution)/shard_map/experts/pallas_call | solution.py:197
  34.0 0.9 %collective-permute-done.12.refs_3_ = bf16[32,4224]{1,0:T(8,128)(2,1)S(1)} collective-permute-done((bf16[32,4224]{1,0:T(8,128)(2,1)S(1)}, bf16[32,4224]{1,0:T(8,128)(2,1)S(1)}, u32[]{:S(2)}, u32[]{:S(2)}) %collective-permute-start.12) | collective-permute-done | bytes 270368 | tf_op jit(solution)/shard_map/ppermute | solution.py:284
  34.9 1.2 %collective-permute-done.11.refs_2_ = bf16[32,4224]{1,0:T(8,128)(2,1)S(1)} collective-permute-done((bf16[32,4224]{1,0:T(8,128)(2,1)S(1)}, bf16[32,4224]{1,0:T(8,128)(2,1)S(1)}, u32[]{:S(2)}, u32[]{:S(2)}) %collective-permute-start.11) | collective-permute-done | bytes 270368 | tf_op jit(solution)/shard_map/ppermute | solution.py:284
  37.1 1.1 %collective-permute-done.15 = bf16[80,4096]{1,0:T(8,128)(2,1)S(1)} collective-permute-done((bf16[80,4096]{1,0:T(8,128)(2,1)S(1)}, bf16[80,4096]{1,0:T(8,128)(2,1)S(1)}, u32[]{:S(2)}, u32[]{:S(2)}) %collective-permute-start.15) | collective-permute-done | bytes 655392 | tf_op jit(solution)/shard_map/ppermute | solution.py:284
  39.0 0.6 collective-permute-start.24
  39.5 1.4 %collective-permute-start.23 = (bf16[32,4096]{1,0:T(8,128)(2,1)S(1)}, bf16[32,4096]{1,0:T(8,128)(2,1)S(1)}, u32[]{:S(2)}, u32[]{:S(2)}) collective-permute-start(bf16[32,4096]{1,0:T(8,128)(2,1)S(1)} %get-tuple-element.94), channel_id=1, source_target_pairs={{0,4},{1,5},{2,6},{3,7},{4,0},{5,1},{6,2},{7,3},{8,12},{9,13},{10,... | collective-permute-start | bytes 786440 | tf_op jit(solution)/shard_map/ppermute | solution.py:284
  41.0 5.1 %experts.3 = (bf16[16,4096]{1,0:T(8,128)(2,1)S(1)}, bf16[16,4096]{1,0:T(8,128)(2,1)S(1)}, bf16[32,4096]{1,0:T(8,128)(2,1)S(1)}, bf16[32,4096]{1,0:T(8,128)(2,1)S...) custom-call(s32[1]{0:T(128)} %bitcast.own_ref.refs_0_, ...), custom_call_target="tpu_custom_call" | custom-call | flops 4831838208 | bytes 4194304 | tf_op jit(solution)/shard_map/experts/pallas_call | solution.py:197
  46.7 1.3 %collective-permute-done.22 = bf16[16,4096]{1,0:T(8,128)(2,1)S(1)} collective-permute-done((bf16[16,4096]{1,0:T(8,128)(2,1)S(1)}, bf16[16,4096]{1,0:T(8,128)(2,1)S(1)}, u32[]{:S(2)}, u32[]{:S(2)}) %collective-permute-start.22) | collective-permute-done | bytes 131104 | tf_op jit(solution)/shard_map/ppermute | solution.py:289
  49.1 2.5 %collective-permute-start.29 = (bf16[16,4096]{1,0:T(8,128)(2,1)S(1)}, bf16[16,4096]{1,0:T(8,128)(2,1)S(1)}, u32[]{:S(2)}, u32[]{:S(2)}) collective-permute-start(bf16[16,4096]{1,0:T(8,128)(2,1)S(1)} %fusion.4), channel_id=1, source_target_pairs={{0,16},{8,24},{16,0},{24,8},{1,17},{9,25},{17,1},{25,9},{2,18},{10... | collective-permute-start | bytes 393224 | tf_op jit(solution)/shard_map/ppermute | solution.py:289
  51.7 0.6 collective-permute-start.31
  52.3 1.5 %collective-permute-start.32 = (bf16[32,4096]{1,0:T(8,128)(2,1)S(1)}, bf16[32,4096]{1,0:T(8,128)(2,1)S(1)}, u32[]{:S(2)}, u32[]{:S(2)}) collective-permute-start(bf16[32,4096]{1,0:T(8,128)(2,1)S(1)} %get-tuple-element.128), channel_id=1, source_target_pairs={{0,4},{1,5},{2,6},{3,7},{4,0},{5,1},{6,2},{7,3},{8,12},{9,13},{10,... | collective-permute-start | bytes 786440 | tf_op jit(solution)/shard_map/ppermute | solution.py:284
  54.8 4.9 %collective-permute-done.31 = bf16[32,4096]{1,0:T(8,128)(2,1)S(1)} collective-permute-done((bf16[32,4096]{1,0:T(8,128)(2,1)S(1)}, bf16[32,4096]{1,0:T(8,128)(2,1)S(1)}, u32[]{:S(2)}, u32[]{:S(2)}) %collective-permute-start.31) | collective-permute-done | bytes 262176 | tf_op jit(solution)/shard_map/ppermute | solution.py:284
  60.7 1.4 %collective-permute-start.34 = (bf16[16,4096]{1,0:T(8,128)(2,1)S(1)}, bf16[16,4096]{1,0:T(8,128)(2,1)S(1)}, u32[]{:S(2)}, u32[]{:S(2)}) collective-permute-start(bf16[16,4096]{1,0:T(8,128)(2,1)S(1)} %get-tuple-element.130), channel_id=1, source_target_pairs={{0,24},{8,16},{16,8},{24,0},{1,25},{9,17},{17,9},{25,1},{2,26},{10... | collective-permute-start | bytes 393224 | tf_op jit(solution)/shard_map/ppermute | solution.py:289
  62.1 2.0 %collective-permute-done.27 = bf16[16,4096]{1,0:T(8,128)(2,1)S(1)} collective-permute-done((bf16[16,4096]{1,0:T(8,128)(2,1)S(1)}, bf16[16,4096]{1,0:T(8,128)(2,1)S(1)}, u32[]{:S(2)}, u32[]{:S(2)}) %collective-permute-start.27) | collective-permute-done | bytes 131104 | tf_op jit(solution)/shard_map/ppermute | solution.py:289
  64.2 1.6 %collective-permute-start.30 = (bf16[16,4096]{1,0:T(8,128)(2,1)S(1)}, bf16[16,4096]{1,0:T(8,128)(2,1)S(1)}, u32[]{:S(2)}, u32[]{:S(2)}) collective-permute-start(bf16[16,4096]{1,0:T(8,128)(2,1)S(1)} %fusion.2), channel_id=1, source_target_pairs={{0,6},{1,7},{2,4},{3,5},{4,2},{5,3},{6,0},{7,1},{8,14},{9,15},{10,... | collective-permute-start | bytes 393224 | tf_op jit(solution)/shard_map/ppermute | solution.py:284
  65.7 3.9 %collective-permute-done.33 = bf16[16,4096]{1,0:T(8,128)(2,1)S(1)} collective-permute-done((bf16[16,4096]{1,0:T(8,128)(2,1)S(1)}, bf16[16,4096]{1,0:T(8,128)(2,1)S(1)}, u32[]{:S(2)}, u32[]{:S(2)}) %collective-permute-start.33) | collective-permute-done | bytes 131104 | tf_op jit(solution)/shard_map/ppermute | solution.py:289
  69.6 0.8 %collective-permute-done.30 = bf16[16,4096]{1,0:T(8,128)(2,1)S(1)} collective-permute-done((bf16[16,4096]{1,0:T(8,128)(2,1)S(1)}, bf16[16,4096]{1,0:T(8,128)(2,1)S(1)}, u32[]{:S(2)}, u32[]{:S(2)}) %collective-permute-start.30) | collective-permute-done | bytes 131104 | tf_op jit(solution)/shard_map/ppermute | solution.py:284
  70.5 0.8 %fusion.9 = bf16[16,4096]{1,0:T(8,128)(2,1)} fusion(f32[48,4096]{1,0:T(8,128)S(1)} %convert_add_fusion, bf16[16,4096]{1,0:T(8,128)(2,1)S(1)} %collective-permute-done.34, bf16[16,4096]{1,0:T(8,128)(2,1)S(1)} %collective-permute-done.33, bf16[16,4096]{1,0:T(8,128)(2,1)S(1)} %collective-permute-done.30, bf16[16,4096]{1,0:T(8,128)(2,1)S(1)} %collective-permute-done.29, ...), kind=kLoop, calls=%fused_computation.17 | loop fusion | flops 851968 | bytes 1179648 | tf_op jit(solution)/shard_map/convert_element_type | solution.py:300
  (75 shorter events, 10.4 us)
Async XLA Ops:
  1.2 13.4 %collective-permute-start.4 = (bf16[16,4224]{1,0:T(8,128)(2,1)S(1)}, bf16[16,4224]{1,0:T(8,128)(2,1)S(1)}, u32[]{:S(2)}, u32[]{:S(2)}) collective-permute-start(bf16[16,4224]{1,0:T(8,128)(2,1)S(1)} %pack.1.refs_0_), channel_id=1, source_target_pairs={{0,16},{8,24},{16,0},{24,8},{1,17},{9,25},{17,1},{25,9},{2,18},{10... | collective-permute-start | bytes 405512 | tf_op jit(solution)/shard_map/ppermute | solution.py:289
  5.3 9.3 %collective-permute-start.3 = (bf16[16,4224]{1,0:T(8,128)(2,1)S(1)}, bf16[16,4224]{1,0:T(8,128)(2,1)S(1)}, u32[]{:S(2)}, u32[]{:S(2)}) collective-permute-start(bf16[16,4224]{1,0:T(8,128)(2,1)S(1)} %pack.1.refs_0_), channel_id=1, source_target_pairs={{0,8},{8,0},{16,24},{24,16},{1,9},{9,1},{17,25},{25,17},{2,10},{10... | collective-permute-start | bytes 405512 | tf_op jit(solution)/shard_map/ppermute | solution.py:289
  6.9 7.7 %collective-permute-start.2 = (bf16[16,4224]{1,0:T(8,128)(2,1)S(1)}, bf16[16,4224]{1,0:T(8,128)(2,1)S(1)}, u32[]{:S(2)}, u32[]{:S(2)}) collective-permute-start(bf16[16,4224]{1,0:T(8,128)(2,1)S(1)} %pack.1.refs_0_), channel_id=1, source_target_pairs={{0,6},{1,7},{2,4},{3,5},{4,2},{5,3},{6,0},{7,1},{8,14},{9,15},{10,... | collective-permute-start | bytes 405512 | tf_op jit(solution)/shard_map/ppermute | solution.py:284
  9.4 6.1 %collective-permute-start.1 = (bf16[16,4224]{1,0:T(8,128)(2,1)S(1)}, bf16[16,4224]{1,0:T(8,128)(2,1)S(1)}, u32[]{:S(2)}, u32[]{:S(2)}) collective-permute-start(bf16[16,4224]{1,0:T(8,128)(2,1)S(1)} %pack.1.refs_0_), channel_id=1, source_target_pairs={{0,4},{1,5},{2,6},{3,7},{4,0},{5,1},{6,2},{7,3},{8,12},{9,13},{10,... | collective-permute-start | bytes 405512 | tf_op jit(solution)/shard_map/ppermute | solution.py:284
  9.9 5.7 %collective-permute-start = (bf16[16,4224]{1,0:T(8,128)(2,1)S(1)}, bf16[16,4224]{1,0:T(8,128)(2,1)S(1)}, u32[]{:S(2)}, u32[]{:S(2)}) collective-permute-start(bf16[16,4224]{1,0:T(8,128)(2,1)S(1)} %pack.1.refs_0_), channel_id=1, source_target_pairs={{0,2},{1,3},{2,0},{3,1},{4,6},{5,7},{6,4},{7,5},{8,10},{9,11},{10,... | collective-permute-start | bytes 405512 | tf_op jit(solution)/shard_map/ppermute | solution.py:284
  15.5 5.0 %collective-permute-start.8 = (bf16[16,4224]{1,0:T(8,128)(2,1)S(1)}, bf16[16,4224]{1,0:T(8,128)(2,1)S(1)}, u32[]{:S(2)}, u32[]{:S(2)}) collective-permute-start(bf16[16,4224]{1,0:T(8,128)(2,1)S(1)} %collective-permute-done.4.refs_0_), channel_id=1, source_target_pairs={{0,8},{8,0},{16,24},{24,16},{1,9},{9,1},{17,25},{25,17},{2,10},{10... | collective-permute-start | bytes 405512 | tf_op jit(solution)/shard_map/ppermute | solution.py:289
  16.0 6.9 %collective-permute-start.7 = (bf16[16,4224]{1,0:T(8,128)(2,1)S(1)}, bf16[16,4224]{1,0:T(8,128)(2,1)S(1)}, u32[]{:S(2)}, u32[]{:S(2)}) collective-permute-start(bf16[16,4224]{1,0:T(8,128)(2,1)S(1)} %collective-permute-done.4.refs_0_), channel_id=1, source_target_pairs={{0,6},{1,7},{2,4},{3,5},{4,2},{5,3},{6,0},{7,1},{8,14},{9,15},{10,... | collective-permute-start | bytes 405512 | tf_op jit(solution)/shard_map/ppermute | solution.py:284
  17.7 6.6 %collective-permute-start.6 = (bf16[16,4224]{1,0:T(8,128)(2,1)S(1)}, bf16[16,4224]{1,0:T(8,128)(2,1)S(1)}, u32[]{:S(2)}, u32[]{:S(2)}) collective-permute-start(bf16[16,4224]{1,0:T(8,128)(2,1)S(1)} %collective-permute-done.4.refs_0_), channel_id=1, source_target_pairs={{0,4},{1,5},{2,6},{3,7},{4,0},{5,1},{6,2},{7,3},{8,12},{9,13},{10,... | collective-permute-start | bytes 405512 | tf_op jit(solution)/shard_map/ppermute | solution.py:284
  19.0 5.5 %collective-permute-start.5 = (bf16[16,4224]{1,0:T(8,128)(2,1)S(1)}, bf16[16,4224]{1,0:T(8,128)(2,1)S(1)}, u32[]{:S(2)}, u32[]{:S(2)}) collective-permute-start(bf16[16,4224]{1,0:T(8,128)(2,1)S(1)} %collective-permute-done.4.refs_0_), channel_id=1, source_target_pairs={{0,2},{1,3},{2,0},{3,1},{4,6},{5,7},{6,4},{7,5},{8,10},{9,11},{10,... | collective-permute-start | bytes 405512 | tf_op jit(solution)/shard_map/ppermute | solution.py:284
  19.5 8.9 %collective-permute-start.9 = (bf16[64,4224]{1,0:T(8,128)(2,1)S(1)}, bf16[64,4224]{1,0:T(8,128)(2,1)S(1)}, u32[]{:S(2)}, u32[]{:S(2)}) collective-permute-start(bf16[64,4224]{1,0:T(8,128)(2,1)S(1)} %gather.3.refs_1_), channel_id=1, source_target_pairs={{0,1},{1,0},{2,3},{3,2},{4,5},{5,4},{6,7},{7,6},{8,9},{9,8},{10,11... | collective-permute-start | bytes 1622024 | tf_op jit(solution)/shard_map/ppermute | solution.py:284
  24.5 4.3 %collective-permute-start.10 = (bf16[64,4224]{1,0:T(8,128)(2,1)S(1)}, bf16[64,4224]{1,0:T(8,128)(2,1)S(1)}, u32[]{:S(2)}, u32[]{:S(2)}) collective-permute-start(bf16[64,4224]{1,0:T(8,128)(2,1)S(1)} %gather.4.refs_2_), channel_id=1, source_target_pairs={{0,1},{1,0},{2,3},{3,2},{4,5},{5,4},{6,7},{7,6},{8,9},{9,8},{10,11... | collective-permute-start | bytes 1622024 | tf_op jit(solution)/shard_map/ppermute | solution.py:284
  24.6 9.3 %collective-permute-start.13 = (bf16[16,4224]{1,0:T(8,128)(2,1)S(1)}, bf16[16,4224]{1,0:T(8,128)(2,1)S(1)}, u32[]{:S(2)}, u32[]{:S(2)}) collective-permute-start(bf16[16,4224]{1,0:T(8,128)(2,1)S(1)} %collective-permute-done.2.refs_3_), channel_id=1, source_target_pairs={{0,8},{8,0},{16,24},{24,16},{1,9},{9,1},{17,25},{25,17},{2,10},{10... | collective-permute-start | bytes 405512 | tf_op jit(solution)/shard_map/ppermute | solution.py:289
  26.3 8.6 %collective-permute-start.12 = (bf16[32,4224]{1,0:T(8,128)(2,1)S(1)}, bf16[32,4224]{1,0:T(8,128)(2,1)S(1)}, u32[]{:S(2)}, u32[]{:S(2)}) collective-permute-start(bf16[32,4224]{1,0:T(8,128)(2,1)S(1)} %gather.5.refs_1_), channel_id=1, source_target_pairs={{0,4},{1,5},{2,6},{3,7},{4,0},{5,1},{6,2},{7,3},{8,12},{9,13},{10,... | collective-permute-start | bytes 811016 | tf_op jit(solution)/shard_map/ppermute | solution.py:284
  27.8 8.3 %collective-permute-start.11 = (bf16[32,4224]{1,0:T(8,128)(2,1)S(1)}, bf16[32,4224]{1,0:T(8,128)(2,1)S(1)}, u32[]{:S(2)}, u32[]{:S(2)}) collective-permute-start(bf16[32,4224]{1,0:T(8,128)(2,1)S(1)} %gather.5.refs_1_), channel_id=1, source_target_pairs={{0,2},{1,3},{2,0},{3,1},{4,6},{5,7},{6,4},{7,5},{8,10},{9,11},{10,... | collective-permute-start | bytes 811016 | tf_op jit(solution)/shard_map/ppermute | solution.py:284
  28.4 5.6 %collective-permute-start.14 = (bf16[16,4224]{1,0:T(8,128)(2,1)S(1)}, bf16[16,4224]{1,0:T(8,128)(2,1)S(1)}, u32[]{:S(2)}, u32[]{:S(2)}) collective-permute-start(bf16[16,4224]{1,0:T(8,128)(2,1)S(1)} %collective-permute-done.7.refs_3_), channel_id=1, source_target_pairs={{0,8},{8,0},{16,24},{24,16},{1,9},{9,1},{17,25},{25,17},{2,10},{10... | collective-permute-start | bytes 405512 | tf_op jit(solution)/shard_map/ppermute | solution.py:289
  36.1 2.5 %collective-permute-start.17 = (bf16[32,4224]{1,0:T(8,128)(2,1)S(1)}, bf16[32,4224]{1,0:T(8,128)(2,1)S(1)}, u32[]{:S(2)}, u32[]{:S(2)}) collective-permute-start(bf16[32,4224]{1,0:T(8,128)(2,1)S(1)} %gather.5.refs_1_), channel_id=1, source_target_pairs={{0,1},{1,0},{2,3},{3,2},{4,5},{5,4},{6,7},{7,6},{8,9},{9,8},{10,11... | collective-permute-start | bytes 811016 | tf_op jit(solution)/shard_map/ppermute | solution.py:284
  36.6 3.0 %collective-permute-start.21 = (bf16[16,4224]{1,0:T(8,128)(2,1)S(1)}, bf16[16,4224]{1,0:T(8,128)(2,1)S(1)}, u32[]{:S(2)}, u32[]{:S(2)}) collective-permute-start(bf16[16,4224]{1,0:T(8,128)(2,1)S(1)} %collective-permute-done.14.refs_5_), channel_id=1, source_target_pairs={{0,1},{1,0},{2,3},{3,2},{4,5},{5,4},{6,7},{7,6},{8,9},{9,8},{10,11... | collective-permute-start | bytes 405512 | tf_op jit(solution)/shard_map/ppermute | solution.py:284
  37.1 3.9 %collective-permute-start.18 = (bf16[32,4224]{1,0:T(8,128)(2,1)S(1)}, bf16[32,4224]{1,0:T(8,128)(2,1)S(1)}, u32[]{:S(2)}, u32[]{:S(2)}) collective-permute-start(bf16[32,4224]{1,0:T(8,128)(2,1)S(1)} %collective-permute-done.11.refs_2_), channel_id=1, source_target_pairs={{0,1},{1,0},{2,3},{3,2},{4,5},{5,4},{6,7},{7,6},{8,9},{9,8},{10,11... | collective-permute-start | bytes 811016 | tf_op jit(solution)/shard_map/ppermute | solution.py:284
  38.2 2.8 %collective-permute-start.19 = (bf16[32,4224]{1,0:T(8,128)(2,1)S(1)}, bf16[32,4224]{1,0:T(8,128)(2,1)S(1)}, u32[]{:S(2)}, u32[]{:S(2)}) collective-permute-start(bf16[32,4224]{1,0:T(8,128)(2,1)S(1)} %collective-permute-done.12.refs_3_), channel_id=1, source_target_pairs={{0,1},{1,0},{2,3},{3,2},{4,5},{5,4},{6,7},{7,6},{8,9},{9,8},{10,11... | collective-permute-start | bytes 811016 | tf_op jit(solution)/shard_map/ppermute | solution.py:284
  38.6 9.4 %collective-permute-start.22 = (bf16[16,4096]{1,0:T(8,128)(2,1)S(1)}, bf16[16,4096]{1,0:T(8,128)(2,1)S(1)}, u32[]{:S(2)}, u32[]{:S(2)}) collective-permute-start(bf16[16,4096]{1,0:T(8,128)(2,1)S(1)} %add_convert_fusion.8), channel_id=1, source_target_pairs={{0,16},{8,24},{16,0},{24,8},{1,17},{9,25},{17,1},{25,9},{2,18},{10... | collective-permute-start | bytes 393224 | tf_op jit(solution)/shard_map/ppermute | solution.py:289
  39.0 9.0 %collective-permute-start.24 = (bf16[32,4096]{1,0:T(8,128)(2,1)S(1)}, bf16[32,4096]{1,0:T(8,128)(2,1)S(1)}, u32[]{:S(2)}, u32[]{:S(2)}) collective-permute-start(bf16[32,4096]{1,0:T(8,128)(2,1)S(1)} %get-tuple-element.93), channel_id=1, source_target_pairs={{0,2},{1,3},{2,0},{3,1},{4,6},{5,7},{6,4},{7,5},{8,10},{9,11},{10,... | collective-permute-start | bytes 786440 | tf_op jit(solution)/shard_map/ppermute | solution.py:284
  39.5 8.4 %collective-permute-start.23 = (bf16[32,4096]{1,0:T(8,128)(2,1)S(1)}, bf16[32,4096]{1,0:T(8,128)(2,1)S(1)}, u32[]{:S(2)}, u32[]{:S(2)}) collective-permute-start(bf16[32,4096]{1,0:T(8,128)(2,1)S(1)} %get-tuple-element.94), channel_id=1, source_target_pairs={{0,4},{1,5},{2,6},{3,7},{4,0},{5,1},{6,2},{7,3},{8,12},{9,13},{10,... | collective-permute-start | bytes 786440 | tf_op jit(solution)/shard_map/ppermute | solution.py:284
  41.0 7.0 %collective-permute-start.16 = (bf16[48,4096]{1,0:T(8,128)(2,1)S(1)}, bf16[48,4096]{1,0:T(8,128)(2,1)S(1)}, u32[]{:S(2)}, u32[]{:S(2)}) collective-permute-start(bf16[48,4096]{1,0:T(8,128)(2,1)S(1)} %get-tuple-element.92), channel_id=1, source_target_pairs={{0,1},{1,0},{2,3},{3,2},{4,5},{5,4},{6,7},{7,6},{8,9},{9,8},{10,11... | collective-permute-start | bytes 1179656 | tf_op jit(solution)/shard_map/ppermute | solution.py:284
  48.7 5.0 %collective-permute-start.26 = (bf16[32,4096]{1,0:T(8,128)(2,1)S(1)}, bf16[32,4096]{1,0:T(8,128)(2,1)S(1)}, u32[]{:S(2)}, u32[]{:S(2)}) collective-permute-start(bf16[32,4096]{1,0:T(8,128)(2,1)S(1)} %get-tuple-element.119), channel_id=1, source_target_pairs={{0,1},{1,0},{2,3},{3,2},{4,5},{5,4},{6,7},{7,6},{8,9},{9,8},{10,11... | collective-permute-start | bytes 786440 | tf_op jit(solution)/shard_map/ppermute | solution.py:284
  49.1 13.0 %collective-permute-start.29 = (bf16[16,4096]{1,0:T(8,128)(2,1)S(1)}, bf16[16,4096]{1,0:T(8,128)(2,1)S(1)}, u32[]{:S(2)}, u32[]{:S(2)}) collective-permute-start(bf16[16,4096]{1,0:T(8,128)(2,1)S(1)} %fusion.4), channel_id=1, source_target_pairs={{0,16},{8,24},{16,0},{24,8},{1,17},{9,25},{17,1},{25,9},{2,18},{10... | collective-permute-start | bytes 393224 | tf_op jit(solution)/shard_map/ppermute | solution.py:289
  51.7 8.1 %collective-permute-start.31 = (bf16[32,4096]{1,0:T(8,128)(2,1)S(1)}, bf16[32,4096]{1,0:T(8,128)(2,1)S(1)}, u32[]{:S(2)}, u32[]{:S(2)}) collective-permute-start(bf16[32,4096]{1,0:T(8,128)(2,1)S(1)} %get-tuple-element.127), channel_id=1, source_target_pairs={{0,2},{1,3},{2,0},{3,1},{4,6},{5,7},{6,4},{7,5},{8,10},{9,11},{10,... | collective-permute-start | bytes 786440 | tf_op jit(solution)/shard_map/ppermute | solution.py:284
  52.3 7.8 %collective-permute-start.32 = (bf16[32,4096]{1,0:T(8,128)(2,1)S(1)}, bf16[32,4096]{1,0:T(8,128)(2,1)S(1)}, u32[]{:S(2)}, u32[]{:S(2)}) collective-permute-start(bf16[32,4096]{1,0:T(8,128)(2,1)S(1)} %get-tuple-element.128), channel_id=1, source_target_pairs={{0,4},{1,5},{2,6},{3,7},{4,0},{5,1},{6,2},{7,3},{8,12},{9,13},{10,... | collective-permute-start | bytes 786440 | tf_op jit(solution)/shard_map/ppermute | solution.py:284
  53.8 8.3 %collective-permute-start.28 = (bf16[16,4096]{1,0:T(8,128)(2,1)S(1)}, bf16[16,4096]{1,0:T(8,128)(2,1)S(1)}, u32[]{:S(2)}, u32[]{:S(2)}) collective-permute-start(bf16[16,4096]{1,0:T(8,128)(2,1)S(1)} %get-tuple-element.135), channel_id=1, source_target_pairs={{0,24},{8,16},{16,8},{24,0},{1,25},{9,17},{17,9},{25,1},{2,26},{10... | collective-permute-start | bytes 393224 | tf_op jit(solution)/shard_map/ppermute | solution.py:289
  54.4 9.7 %collective-permute-start.27 = (bf16[16,4096]{1,0:T(8,128)(2,1)S(1)}, bf16[16,4096]{1,0:T(8,128)(2,1)S(1)}, u32[]{:S(2)}, u32[]{:S(2)}) collective-permute-start(bf16[16,4096]{1,0:T(8,128)(2,1)S(1)} %get-tuple-element.136), channel_id=1, source_target_pairs={{0,8},{8,0},{16,24},{24,16},{1,9},{9,1},{17,25},{25,17},{2,10},{10... | collective-permute-start | bytes 393224 | tf_op jit(solution)/shard_map/ppermute | solution.py:289
  60.2 9.4 %collective-permute-start.33 = (bf16[16,4096]{1,0:T(8,128)(2,1)S(1)}, bf16[16,4096]{1,0:T(8,128)(2,1)S(1)}, u32[]{:S(2)}, u32[]{:S(2)}) collective-permute-start(bf16[16,4096]{1,0:T(8,128)(2,1)S(1)} %get-tuple-element.129), channel_id=1, source_target_pairs={{0,8},{8,0},{16,24},{24,16},{1,9},{9,1},{17,25},{25,17},{2,10},{10... | collective-permute-start | bytes 393224 | tf_op jit(solution)/shard_map/ppermute | solution.py:289
  60.7 8.9 %collective-permute-start.34 = (bf16[16,4096]{1,0:T(8,128)(2,1)S(1)}, bf16[16,4096]{1,0:T(8,128)(2,1)S(1)}, u32[]{:S(2)}, u32[]{:S(2)}) collective-permute-start(bf16[16,4096]{1,0:T(8,128)(2,1)S(1)} %get-tuple-element.130), channel_id=1, source_target_pairs={{0,24},{8,16},{16,8},{24,0},{1,25},{9,17},{17,9},{25,1},{2,26},{10... | collective-permute-start | bytes 393224 | tf_op jit(solution)/shard_map/ppermute | solution.py:289
  64.2 6.3 %collective-permute-start.30 = (bf16[16,4096]{1,0:T(8,128)(2,1)S(1)}, bf16[16,4096]{1,0:T(8,128)(2,1)S(1)}, u32[]{:S(2)}, u32[]{:S(2)}) collective-permute-start(bf16[16,4096]{1,0:T(8,128)(2,1)S(1)} %fusion.2), channel_id=1, source_target_pairs={{0,6},{1,7},{2,4},{3,5},{4,2},{5,3},{6,0},{7,1},{8,14},{9,15},{10,... | collective-permute-start | bytes 393224 | tf_op jit(solution)/shard_map/ppermute | solution.py:284
  (11 other events, 61.1 us)

commit v12 on v11

--- a/solution.py
+++ b/solution.py
@@ -330,7 +330,6 @@
     )
     three = swap_rep(two, 1)
     x_two, y_two, far_two = [swap_exp(two, bits) for bits in (2, 4, 6)]
-    far_one, far_three = swap_rep(far_own, 1), swap_rep(far_two, 1)
     first = gathered(packed, x_own, y_own, far_own)
     first_other = swap_exp(first, 1)
     second = gathered(two, x_two, y_two, far_two)
@@ -338,7 +337,9 @@
     downs = fetched(down_weight, False)
     second, downs = ordered(second, downs)
     pair = gathered(one, three)
+    pair, far_own, far_two = ordered(pair, far_own, far_two)
     x_pair, y_pair = swap_exp(pair, 2), swap_exp(pair, 4)
+    far_one, far_three = swap_rep(far_own, 1), swap_rep(far_two, 1)
 
     near = [first, second, first_other, swap_exp(second, 1)]
     groups = row_groups([[5, 1], [6, 2], [7], [13, 9, 14, 10, 15], [4, 0, 3], [12, 8, 11]], rows)

time: 71.4 us -> 70.6 us (0.989)
  waiting for transfers between devices: 22.1 us -> 20.1 us
  starting transfers between devices: 31.1 us -> 32.3 us
    ppermute x24, waiting for transfers between devices: 14 us -> 12 us  [swap_exp(): return lax.ppermute(value, 'exp', [(i, i ^ bits) for i in range(owners)])]
    ppermute x11, starting transfers between devices: 14.1 us -> 15.2 us  [swap_rep(): return lax.ppermute(value, 'rep', [(i, i ^ bits) for i in range(replicas)])]
  transfers between devices with their start and end apart: 35 -> 35, of which waited for: 17 -> 16; matrix products, arithmetic and copies ran while one was open for 1% -> 1% of each run, Pallas kernels for 21% -> 22%
where the time goes in v12:
time: 70.6 us; the launch traced here: 70.5 us
  starting transfers between devices  32.3 us (46%)
  waiting for transfers between devices  20.1 us (28%)
  Pallas kernels  16 us (23%)
  other arithmetic  1.48 us (2%)
    ppermute x24, starting transfers between devices, swap_exp(): return lax.ppermute(value, 'exp', [(i, i ^ bits) for i in range(owners)])  17 us
    ppermute x11, starting transfers between devices, swap_rep(): return lax.ppermute(value, 'rep', [(i, i ^ bits) for i in range(replicas)])  15.2 us
    ppermute x24, waiting for transfers between devices, swap_exp(): return lax.ppermute(value, 'exp', [(i, i ^ bits) for i in range(owners)])  12 us
    pallas_call x2, Pallas kernels, experts_of(): pl.pallas_call(kernel, out_shape=[jax.ShapeDtypeStruct((count, model_widt...  10.2 us
    ppermute x11, waiting for transfers between devices, swap_rep(): return lax.ppermute(value, 'rep', [(i, i ^ bits) for i in range(replicas)])  8.01 us
    pallas_call x3, Pallas kernels, fetched(): pl.pallas_call(functools.partial(fetch_kernel, turn), out_shape=jax.Shape...  4.88 us
  transfers between devices with their start and end apart: 35, of which 16 were waited for; matrix products, arithmetic and copies ran while one was open for 1% of the time, Pallas kernels for 22%

profile of v12, /device:TPU:0, one launch (start us, length us, event | category | flops | bytes accessed | tf_op | source)
XLA Modules:
  0.0 70.5 jit_solution(10482136429987915996)
XLA Ops:
  1.2 4.1 %collective-permute-start.4 = (bf16[16,4224]{1,0:T(8,128)(2,1)S(1)}, bf16[16,4224]{1,0:T(8,128)(2,1)S(1)}, u32[]{:S(2)}, u32[]{:S(2)}) collective-permute-start(bf16[16,4224]{1,0:T(8,128)(2,1)S(1)} %pack.1.refs_0_), channel_id=1, source_target_pairs={{0,16},{8,24},{16,0},{24,8},{1,17},{9,25},{17,1},{25,9},{2,18},{10... | collective-permute-start | bytes 405512 | tf_op jit(solution)/shard_map/ppermute | solution.py:289
  5.3 1.6 %collective-permute-start.3 = (bf16[16,4224]{1,0:T(8,128)(2,1)S(1)}, bf16[16,4224]{1,0:T(8,128)(2,1)S(1)}, u32[]{:S(2)}, u32[]{:S(2)}) collective-permute-start(bf16[16,4224]{1,0:T(8,128)(2,1)S(1)} %pack.1.refs_0_), channel_id=1, source_target_pairs={{0,8},{8,0},{16,24},{24,16},{1,9},{9,1},{17,25},{25,17},{2,10},{10... | collective-permute-start | bytes 405512 | tf_op jit(solution)/shard_map/ppermute | solution.py:289
  6.9 2.4 %collective-permute-start.2 = (bf16[16,4224]{1,0:T(8,128)(2,1)S(1)}, bf16[16,4224]{1,0:T(8,128)(2,1)S(1)}, u32[]{:S(2)}, u32[]{:S(2)}) collective-permute-start(bf16[16,4224]{1,0:T(8,128)(2,1)S(1)} %pack.1.refs_0_), channel_id=1, source_target_pairs={{0,6},{1,7},{2,4},{3,5},{4,2},{5,3},{6,0},{7,1},{8,14},{9,15},{10,... | collective-permute-start | bytes 405512 | tf_op jit(solution)/shard_map/ppermute | solution.py:284
  10.4 2.1 %fetch_turned.2.refs_5_.refs_11_ = bf16[4096,768]{1,0:T(8,128)(2,1)S(1)} custom-call(bf16[768,4096]{1,0:T(8,128)(2,1)S(1)} %bitcast.7), custom_call_target="tpu_custom_call" | custom-call | bytes 12582912 | tf_op jit(solution)/shard_map/fetch_turned/pallas_call | solution.py:103
  12.5 2.1 %fetch_turned.3.refs_6_.refs_12_ = bf16[4096,768]{1,0:T(8,128)(2,1)S(1)} custom-call(bf16[768,4096]{1,0:T(8,128)(2,1)S(1)} %bitcast.11), custom_call_target="tpu_custom_call" | custom-call | bytes 12582912 | tf_op jit(solution)/shard_map/fetch_turned/pallas_call | solution.py:103
  14.6 0.8 %collective-permute-done.1.refs_2_ = bf16[16,4224]{1,0:T(8,128)(2,1)S(1)} collective-permute-done((bf16[16,4224]{1,0:T(8,128)(2,1)S(1)}, bf16[16,4224]{1,0:T(8,128)(2,1)S(1)}, u32[]{:S(2)}, u32[]{:S(2)}) %collective-permute-start.1) | collective-permute-done | bytes 135200 | tf_op jit(solution)/shard_map/ppermute | solution.py:284
  16.0 1.7 %collective-permute-start.7 = (bf16[16,4224]{1,0:T(8,128)(2,1)S(1)}, bf16[16,4224]{1,0:T(8,128)(2,1)S(1)}, u32[]{:S(2)}, u32[]{:S(2)}) collective-permute-start(bf16[16,4224]{1,0:T(8,128)(2,1)S(1)} %collective-permute-done.4.refs_0_), channel_id=1, source_target_pairs={{0,6},{1,7},{2,4},{3,5},{4,2},{5,3},{6,0},{7,1},{8,14},{9,15},{10,... | collective-permute-start | bytes 405512 | tf_op jit(solution)/shard_map/ppermute | solution.py:284
  17.7 1.3 %collective-permute-start.6 = (bf16[16,4224]{1,0:T(8,128)(2,1)S(1)}, bf16[16,4224]{1,0:T(8,128)(2,1)S(1)}, u32[]{:S(2)}, u32[]{:S(2)}) collective-permute-start(bf16[16,4224]{1,0:T(8,128)(2,1)S(1)} %collective-permute-done.4.refs_0_), channel_id=1, source_target_pairs={{0,4},{1,5},{2,6},{3,7},{4,0},{5,1},{6,2},{7,3},{8,12},{9,13},{10,... | collective-permute-start | bytes 405512 | tf_op jit(solution)/shard_map/ppermute | solution.py:284
  19.6 1.0 %collective-permute-done.8.refs_1_ = bf16[16,4224]{1,0:T(8,128)(2,1)S(1)} collective-permute-done((bf16[16,4224]{1,0:T(8,128)(2,1)S(1)}, bf16[16,4224]{1,0:T(8,128)(2,1)S(1)}, u32[]{:S(2)}, u32[]{:S(2)}) %collective-permute-start.8) | collective-permute-done | bytes 135200 | tf_op jit(solution)/shard_map/ppermute | solution.py:289
  20.5 0.8 %fetch.1.refs_7_.refs_13_ = bf16[768,4096]{1,0:T(8,128)(2,1)S(1)} custom-call(bf16[768,4096]{1,0:T(8,128)(2,1)S(1)} %bitcast.15), custom_call_target="tpu_custom_call" | custom-call | bytes 12582912 | tf_op jit(solution)/shard_map/fetch/pallas_call | solution.py:103
  21.3 1.6 %collective-permute-done.7.refs_3_ = bf16[16,4224]{1,0:T(8,128)(2,1)S(1)} collective-permute-done((bf16[16,4224]{1,0:T(8,128)(2,1)S(1)}, bf16[16,4224]{1,0:T(8,128)(2,1)S(1)}, u32[]{:S(2)}, u32[]{:S(2)}) %collective-permute-start.7) | collective-permute-done | bytes 135200 | tf_op jit(solution)/shard_map/ppermute | solution.py:284
  22.9 1.4 %collective-permute-done.6.refs_2_ = bf16[16,4224]{1,0:T(8,128)(2,1)S(1)} collective-permute-done((bf16[16,4224]{1,0:T(8,128)(2,1)S(1)}, bf16[16,4224]{1,0:T(8,128)(2,1)S(1)}, u32[]{:S(2)}, u32[]{:S(2)}) %collective-permute-start.6) | collective-permute-done | bytes 135200 | tf_op jit(solution)/shard_map/ppermute | solution.py:284
  24.6 1.5 %collective-permute-start.12 = (bf16[32,4224]{1,0:T(8,128)(2,1)S(1)}, bf16[32,4224]{1,0:T(8,128)(2,1)S(1)}, u32[]{:S(2)}, u32[]{:S(2)}) collective-permute-start(bf16[32,4224]{1,0:T(8,128)(2,1)S(1)} %gather.5.refs_1_), channel_id=1, source_target_pairs={{0,4},{1,5},{2,6},{3,7},{4,0},{5,1},{6,2},{7,3},{8,12},{9,13},{10,... | collective-permute-start | bytes 811016 | tf_op jit(solution)/shard_map/ppermute | solution.py:284
  26.7 1.6 %collective-permute-start.13 = (bf16[16,4224]{1,0:T(8,128)(2,1)S(1)}, bf16[16,4224]{1,0:T(8,128)(2,1)S(1)}, u32[]{:S(2)}, u32[]{:S(2)}) collective-permute-start(bf16[16,4224]{1,0:T(8,128)(2,1)S(1)} %collective-permute-done.2.refs_3_), channel_id=1, source_target_pairs={{0,8},{8,0},{16,24},{24,16},{1,9},{9,1},{17,25},{25,17},{2,10},{10... | collective-permute-start | bytes 405512 | tf_op jit(solution)/shard_map/ppermute | solution.py:289
  28.8 5.1 %experts.2 = (bf16[32,4096]{1,0:T(8,128)(2,1)S(1)}, bf16[32,4096]{1,0:T(8,128)(2,1)S(1)}, bf16[16,4096]{1,0:T(8,128)(2,1)S(1)}, bf16[80,4096]{1,0:T(8,128)(2,1)S...) custom-call(s32[1]{0:T(128)} %bitcast.own_ref.refs_0_, bf16[64,4224]{1,0:T(8,128)(2,1)S(1)} %gather.3.refs_1_, ...), custom_call_target="tpu_custom_call" | custom-call | flops 4831838208 | bytes 4194304 | tf_op jit(solution)/shard_map/experts/pallas_call | solution.py:197
  33.9 1.2 %collective-permute-done.14.refs_5_ = bf16[16,4224]{1,0:T(8,128)(2,1)S(1)} collective-permute-done((bf16[16,4224]{1,0:T(8,128)(2,1)S(1)}, bf16[16,4224]{1,0:T(8,128)(2,1)S(1)}, u32[]{:S(2)}, u32[]{:S(2)}) %collective-permute-start.14) | collective-permute-done | bytes 135200 | tf_op jit(solution)/shard_map/ppermute | solution.py:289
  36.2 1.0 %collective-permute-done.15 = bf16[80,4096]{1,0:T(8,128)(2,1)S(1)} collective-permute-done((bf16[80,4096]{1,0:T(8,128)(2,1)S(1)}, bf16[80,4096]{1,0:T(8,128)(2,1)S(1)}, u32[]{:S(2)}, u32[]{:S(2)}) %collective-permute-start.15) | collective-permute-done | bytes 655392 | tf_op jit(solution)/shard_map/ppermute | solution.py:284
  37.6 0.8 %collective-permute-start.22 = (bf16[16,4096]{1,0:T(8,128)(2,1)S(1)}, bf16[16,4096]{1,0:T(8,128)(2,1)S(1)}, u32[]{:S(2)}, u32[]{:S(2)}) collective-permute-start(bf16[16,4096]{1,0:T(8,128)(2,1)S(1)} %add_convert_fusion.8), channel_id=1, source_target_pairs={{0,16},{8,24},{16,0},{24,8},{1,17},{9,25},{17,1},{25,9},{2,18},{10... | collective-permute-start | bytes 393224 | tf_op jit(solution)/shard_map/ppermute | solution.py:289
  38.4 1.2 %collective-permute-start.24 = (bf16[32,4096]{1,0:T(8,128)(2,1)S(1)}, bf16[32,4096]{1,0:T(8,128)(2,1)S(1)}, u32[]{:S(2)}, u32[]{:S(2)}) collective-permute-start(bf16[32,4096]{1,0:T(8,128)(2,1)S(1)} %get-tuple-element.99), channel_id=1, source_target_pairs={{0,2},{1,3},{2,0},{3,1},{4,6},{5,7},{6,4},{7,5},{8,10},{9,11},{10,... | collective-permute-start | bytes 786440 | tf_op jit(solution)/shard_map/ppermute | solution.py:284
  40.2 5.1 %experts.3 = (bf16[16,4096]{1,0:T(8,128)(2,1)S(1)}, bf16[16,4096]{1,0:T(8,128)(2,1)S(1)}, bf16[32,4096]{1,0:T(8,128)(2,1)S(1)}, bf16[32,4096]{1,0:T(8,128)(2,1)S...) custom-call(s32[1]{0:T(128)} %bitcast.own_ref.refs_0_, ...), custom_call_target="tpu_custom_call" | custom-call | flops 4831838208 | bytes 4194304 | tf_op jit(solution)/shard_map/experts/pallas_call | solution.py:197
  45.9 1.2 %collective-permute-done.22 = bf16[16,4096]{1,0:T(8,128)(2,1)S(1)} collective-permute-done((bf16[16,4096]{1,0:T(8,128)(2,1)S(1)}, bf16[16,4096]{1,0:T(8,128)(2,1)S(1)}, u32[]{:S(2)}, u32[]{:S(2)}) %collective-permute-start.22) | collective-permute-done | bytes 131104 | tf_op jit(solution)/shard_map/ppermute | solution.py:289
  48.4 2.3 %collective-permute-start.29 = (bf16[16,4096]{1,0:T(8,128)(2,1)S(1)}, bf16[16,4096]{1,0:T(8,128)(2,1)S(1)}, u32[]{:S(2)}, u32[]{:S(2)}) collective-permute-start(bf16[16,4096]{1,0:T(8,128)(2,1)S(1)} %fusion.4), channel_id=1, source_target_pairs={{0,16},{8,24},{16,0},{24,8},{1,17},{9,25},{17,1},{25,9},{2,18},{10... | collective-permute-start | bytes 393224 | tf_op jit(solution)/shard_map/ppermute | solution.py:289
  50.7 1.4 %collective-permute-start.31 = (bf16[32,4096]{1,0:T(8,128)(2,1)S(1)}, bf16[32,4096]{1,0:T(8,128)(2,1)S(1)}, u32[]{:S(2)}, u32[]{:S(2)}) collective-permute-start(bf16[32,4096]{1,0:T(8,128)(2,1)S(1)} %get-tuple-element.133), channel_id=1, source_target_pairs={{0,2},{1,3},{2,0},{3,1},{4,6},{5,7},{6,4},{7,5},{8,10},{9,11},{10,... | collective-permute-start | bytes 786440 | tf_op jit(solution)/shard_map/ppermute | solution.py:284
  52.8 1.5 %collective-permute-start.28 = (bf16[16,4096]{1,0:T(8,128)(2,1)S(1)}, bf16[16,4096]{1,0:T(8,128)(2,1)S(1)}, u32[]{:S(2)}, u32[]{:S(2)}) collective-permute-start(bf16[16,4096]{1,0:T(8,128)(2,1)S(1)} %get-tuple-element.141), channel_id=1, source_target_pairs={{0,24},{8,16},{16,8},{24,0},{1,25},{9,17},{17,9},{25,1},{2,26},{10... | collective-permute-start | bytes 393224 | tf_op jit(solution)/shard_map/ppermute | solution.py:289
  54.5 4.2 %collective-permute-done.31 = bf16[32,4096]{1,0:T(8,128)(2,1)S(1)} collective-permute-done((bf16[32,4096]{1,0:T(8,128)(2,1)S(1)}, bf16[32,4096]{1,0:T(8,128)(2,1)S(1)}, u32[]{:S(2)}, u32[]{:S(2)}) %collective-permute-start.31) | collective-permute-done | bytes 262176 | tf_op jit(solution)/shard_map/ppermute | solution.py:284
  58.8 1.2 %collective-permute-done.32 = bf16[32,4096]{1,0:T(8,128)(2,1)S(1)} collective-permute-done((bf16[32,4096]{1,0:T(8,128)(2,1)S(1)}, bf16[32,4096]{1,0:T(8,128)(2,1)S(1)}, u32[]{:S(2)}, u32[]{:S(2)}) %collective-permute-start.32) | collective-permute-done | bytes 262176 | tf_op jit(solution)/shard_map/ppermute | solution.py:284
  60.1 1.6 %collective-permute-start.33 = (bf16[16,4096]{1,0:T(8,128)(2,1)S(1)}, bf16[16,4096]{1,0:T(8,128)(2,1)S(1)}, u32[]{:S(2)}, u32[]{:S(2)}) collective-permute-start(bf16[16,4096]{1,0:T(8,128)(2,1)S(1)} %get-tuple-element.135), channel_id=1, source_target_pairs={{0,8},{8,0},{16,24},{24,16},{1,9},{9,1},{17,25},{25,17},{2,10},{10... | collective-permute-start | bytes 393224 | tf_op jit(solution)/shard_map/ppermute | solution.py:289
  62.3 1.0 %collective-permute-done.27 = bf16[16,4096]{1,0:T(8,128)(2,1)S(1)} collective-permute-done((bf16[16,4096]{1,0:T(8,128)(2,1)S(1)}, bf16[16,4096]{1,0:T(8,128)(2,1)S(1)}, u32[]{:S(2)}, u32[]{:S(2)}) %collective-permute-start.27) | collective-permute-done | bytes 131104 | tf_op jit(solution)/shard_map/ppermute | solution.py:289
  63.4 1.8 %collective-permute-start.30 = (bf16[16,4096]{1,0:T(8,128)(2,1)S(1)}, bf16[16,4096]{1,0:T(8,128)(2,1)S(1)}, u32[]{:S(2)}, u32[]{:S(2)}) collective-permute-start(bf16[16,4096]{1,0:T(8,128)(2,1)S(1)} %fusion.2), channel_id=1, source_target_pairs={{0,6},{1,7},{2,4},{3,5},{4,2},{5,3},{6,0},{7,1},{8,14},{9,15},{10,... | collective-permute-start | bytes 393224 | tf_op jit(solution)/shard_map/ppermute | solution.py:284
  65.2 3.7 %collective-permute-done.33 = bf16[16,4096]{1,0:T(8,128)(2,1)S(1)} collective-permute-done((bf16[16,4096]{1,0:T(8,128)(2,1)S(1)}, bf16[16,4096]{1,0:T(8,128)(2,1)S(1)}, u32[]{:S(2)}, u32[]{:S(2)}) %collective-permute-start.33) | collective-permute-done | bytes 131104 | tf_op jit(solution)/shard_map/ppermute | solution.py:289
  68.8 0.8 %collective-permute-done.30 = bf16[16,4096]{1,0:T(8,128)(2,1)S(1)} collective-permute-done((bf16[16,4096]{1,0:T(8,128)(2,1)S(1)}, bf16[16,4096]{1,0:T(8,128)(2,1)S(1)}, u32[]{:S(2)}, u32[]{:S(2)}) %collective-permute-start.30) | collective-permute-done | bytes 131104 | tf_op jit(solution)/shard_map/ppermute | solution.py:284
  69.7 0.8 %fusion.9 = bf16[16,4096]{1,0:T(8,128)(2,1)} fusion(f32[48,4096]{1,0:T(8,128)S(1)} %convert_add_fusion, bf16[16,4096]{1,0:T(8,128)(2,1)S(1)} %collective-permute-done.34, bf16[16,4096]{1,0:T(8,128)(2,1)S(1)} %collective-permute-done.33, bf16[16,4096]{1,0:T(8,128)(2,1)S(1)} %collective-permute-done.30, bf16[16,4096]{1,0:T(8,128)(2,1)S(1)} %collective-permute-done.29, ...), kind=kLoop, calls=%fused_computation.17 | loop fusion | flops 851968 | bytes 1179648 | tf_op jit(solution)/shard_map/convert_element_type | solution.py:300
  (75 shorter events, 10.3 us)
Async XLA Ops:
  1.2 13.4 %collective-permute-start.4 = (bf16[16,4224]{1,0:T(8,128)(2,1)S(1)}, bf16[16,4224]{1,0:T(8,128)(2,1)S(1)}, u32[]{:S(2)}, u32[]{:S(2)}) collective-permute-start(bf16[16,4224]{1,0:T(8,128)(2,1)S(1)} %pack.1.refs_0_), channel_id=1, source_target_pairs={{0,16},{8,24},{16,0},{24,8},{1,17},{9,25},{17,1},{25,9},{2,18},{10... | collective-permute-start | bytes 405512 | tf_op jit(solution)/shard_map/ppermute | solution.py:289
  5.3 9.3 %collective-permute-start.3 = (bf16[16,4224]{1,0:T(8,128)(2,1)S(1)}, bf16[16,4224]{1,0:T(8,128)(2,1)S(1)}, u32[]{:S(2)}, u32[]{:S(2)}) collective-permute-start(bf16[16,4224]{1,0:T(8,128)(2,1)S(1)} %pack.1.refs_0_), channel_id=1, source_target_pairs={{0,8},{8,0},{16,24},{24,16},{1,9},{9,1},{17,25},{25,17},{2,10},{10... | collective-permute-start | bytes 405512 | tf_op jit(solution)/shard_map/ppermute | solution.py:289
  6.9 7.7 %collective-permute-start.2 = (bf16[16,4224]{1,0:T(8,128)(2,1)S(1)}, bf16[16,4224]{1,0:T(8,128)(2,1)S(1)}, u32[]{:S(2)}, u32[]{:S(2)}) collective-permute-start(bf16[16,4224]{1,0:T(8,128)(2,1)S(1)} %pack.1.refs_0_), channel_id=1, source_target_pairs={{0,6},{1,7},{2,4},{3,5},{4,2},{5,3},{6,0},{7,1},{8,14},{9,15},{10,... | collective-permute-start | bytes 405512 | tf_op jit(solution)/shard_map/ppermute | solution.py:284
  9.4 6.1 %collective-permute-start.1 = (bf16[16,4224]{1,0:T(8,128)(2,1)S(1)}, bf16[16,4224]{1,0:T(8,128)(2,1)S(1)}, u32[]{:S(2)}, u32[]{:S(2)}) collective-permute-start(bf16[16,4224]{1,0:T(8,128)(2,1)S(1)} %pack.1.refs_0_), channel_id=1, source_target_pairs={{0,4},{1,5},{2,6},{3,7},{4,0},{5,1},{6,2},{7,3},{8,12},{9,13},{10,... | collective-permute-start | bytes 405512 | tf_op jit(solution)/shard_map/ppermute | solution.py:284
  9.9 5.7 %collective-permute-start = (bf16[16,4224]{1,0:T(8,128)(2,1)S(1)}, bf16[16,4224]{1,0:T(8,128)(2,1)S(1)}, u32[]{:S(2)}, u32[]{:S(2)}) collective-permute-start(bf16[16,4224]{1,0:T(8,128)(2,1)S(1)} %pack.1.refs_0_), channel_id=1, source_target_pairs={{0,2},{1,3},{2,0},{3,1},{4,6},{5,7},{6,4},{7,5},{8,10},{9,11},{10,... | collective-permute-start | bytes 405512 | tf_op jit(solution)/shard_map/ppermute | solution.py:284
  15.5 5.0 %collective-permute-start.8 = (bf16[16,4224]{1,0:T(8,128)(2,1)S(1)}, bf16[16,4224]{1,0:T(8,128)(2,1)S(1)}, u32[]{:S(2)}, u32[]{:S(2)}) collective-permute-start(bf16[16,4224]{1,0:T(8,128)(2,1)S(1)} %collective-permute-done.4.refs_0_), channel_id=1, source_target_pairs={{0,8},{8,0},{16,24},{24,16},{1,9},{9,1},{17,25},{25,17},{2,10},{10... | collective-permute-start | bytes 405512 | tf_op jit(solution)/shard_map/ppermute | solution.py:289
  16.0 6.9 %collective-permute-start.7 = (bf16[16,4224]{1,0:T(8,128)(2,1)S(1)}, bf16[16,4224]{1,0:T(8,128)(2,1)S(1)}, u32[]{:S(2)}, u32[]{:S(2)}) collective-permute-start(bf16[16,4224]{1,0:T(8,128)(2,1)S(1)} %collective-permute-done.4.refs_0_), channel_id=1, source_target_pairs={{0,6},{1,7},{2,4},{3,5},{4,2},{5,3},{6,0},{7,1},{8,14},{9,15},{10,... | collective-permute-start | bytes 405512 | tf_op jit(solution)/shard_map/ppermute | solution.py:284
  17.7 6.6 %collective-permute-start.6 = (bf16[16,4224]{1,0:T(8,128)(2,1)S(1)}, bf16[16,4224]{1,0:T(8,128)(2,1)S(1)}, u32[]{:S(2)}, u32[]{:S(2)}) collective-permute-start(bf16[16,4224]{1,0:T(8,128)(2,1)S(1)} %collective-permute-done.4.refs_0_), channel_id=1, source_target_pairs={{0,4},{1,5},{2,6},{3,7},{4,0},{5,1},{6,2},{7,3},{8,12},{9,13},{10,... | collective-permute-start | bytes 405512 | tf_op jit(solution)/shard_map/ppermute | solution.py:284
  19.0 5.5 %collective-permute-start.5 = (bf16[16,4224]{1,0:T(8,128)(2,1)S(1)}, bf16[16,4224]{1,0:T(8,128)(2,1)S(1)}, u32[]{:S(2)}, u32[]{:S(2)}) collective-permute-start(bf16[16,4224]{1,0:T(8,128)(2,1)S(1)} %collective-permute-done.4.refs_0_), channel_id=1, source_target_pairs={{0,2},{1,3},{2,0},{3,1},{4,6},{5,7},{6,4},{7,5},{8,10},{9,11},{10,... | collective-permute-start | bytes 405512 | tf_op jit(solution)/shard_map/ppermute | solution.py:284
  19.5 8.8 %collective-permute-start.9 = (bf16[64,4224]{1,0:T(8,128)(2,1)S(1)}, bf16[64,4224]{1,0:T(8,128)(2,1)S(1)}, u32[]{:S(2)}, u32[]{:S(2)}) collective-permute-start(bf16[64,4224]{1,0:T(8,128)(2,1)S(1)} %gather.3.refs_1_), channel_id=1, source_target_pairs={{0,1},{1,0},{2,3},{3,2},{4,5},{5,4},{6,7},{7,6},{8,9},{9,8},{10,11... | collective-permute-start | bytes 1622024 | tf_op jit(solution)/shard_map/ppermute | solution.py:284
  24.5 4.3 %collective-permute-start.10 = (bf16[64,4224]{1,0:T(8,128)(2,1)S(1)}, bf16[64,4224]{1,0:T(8,128)(2,1)S(1)}, u32[]{:S(2)}, u32[]{:S(2)}) collective-permute-start(bf16[64,4224]{1,0:T(8,128)(2,1)S(1)} %gather.4.refs_2_), channel_id=1, source_target_pairs={{0,1},{1,0},{2,3},{3,2},{4,5},{5,4},{6,7},{7,6},{8,9},{9,8},{10,11... | collective-permute-start | bytes 1622024 | tf_op jit(solution)/shard_map/ppermute | solution.py:284
  24.6 10.4 %collective-permute-start.12 = (bf16[32,4224]{1,0:T(8,128)(2,1)S(1)}, bf16[32,4224]{1,0:T(8,128)(2,1)S(1)}, u32[]{:S(2)}, u32[]{:S(2)}) collective-permute-start(bf16[32,4224]{1,0:T(8,128)(2,1)S(1)} %gather.5.refs_1_), channel_id=1, source_target_pairs={{0,4},{1,5},{2,6},{3,7},{4,0},{5,1},{6,2},{7,3},{8,12},{9,13},{10,... | collective-permute-start | bytes 811016 | tf_op jit(solution)/shard_map/ppermute | solution.py:284
  26.2 8.9 %collective-permute-start.11 = (bf16[32,4224]{1,0:T(8,128)(2,1)S(1)}, bf16[32,4224]{1,0:T(8,128)(2,1)S(1)}, u32[]{:S(2)}, u32[]{:S(2)}) collective-permute-start(bf16[32,4224]{1,0:T(8,128)(2,1)S(1)} %gather.5.refs_1_), channel_id=1, source_target_pairs={{0,2},{1,3},{2,0},{3,1},{4,6},{5,7},{6,4},{7,5},{8,10},{9,11},{10,... | collective-permute-start | bytes 811016 | tf_op jit(solution)/shard_map/ppermute | solution.py:284
  26.7 7.1 %collective-permute-start.13 = (bf16[16,4224]{1,0:T(8,128)(2,1)S(1)}, bf16[16,4224]{1,0:T(8,128)(2,1)S(1)}, u32[]{:S(2)}, u32[]{:S(2)}) collective-permute-start(bf16[16,4224]{1,0:T(8,128)(2,1)S(1)} %collective-permute-done.2.refs_3_), channel_id=1, source_target_pairs={{0,8},{8,0},{16,24},{24,16},{1,9},{9,1},{17,25},{25,17},{2,10},{10... | collective-permute-start | bytes 405512 | tf_op jit(solution)/shard_map/ppermute | solution.py:289
  28.3 6.7 %collective-permute-start.14 = (bf16[16,4224]{1,0:T(8,128)(2,1)S(1)}, bf16[16,4224]{1,0:T(8,128)(2,1)S(1)}, u32[]{:S(2)}, u32[]{:S(2)}) collective-permute-start(bf16[16,4224]{1,0:T(8,128)(2,1)S(1)} %collective-permute-done.7.refs_3_), channel_id=1, source_target_pairs={{0,8},{8,0},{16,24},{24,16},{1,9},{9,1},{17,25},{25,17},{2,10},{10... | collective-permute-start | bytes 405512 | tf_op jit(solution)/shard_map/ppermute | solution.py:289
  35.6 2.8 %collective-permute-start.20 = (bf16[16,4224]{1,0:T(8,128)(2,1)S(1)}, bf16[16,4224]{1,0:T(8,128)(2,1)S(1)}, u32[]{:S(2)}, u32[]{:S(2)}) collective-permute-start(bf16[16,4224]{1,0:T(8,128)(2,1)S(1)} %collective-permute-done.13.refs_4_), channel_id=1, source_target_pairs={{0,1},{1,0},{2,3},{3,2},{4,5},{5,4},{6,7},{7,6},{8,9},{9,8},{10,11... | collective-permute-start | bytes 405512 | tf_op jit(solution)/shard_map/ppermute | solution.py:284
  35.7 4.0 %collective-permute-start.21 = (bf16[16,4224]{1,0:T(8,128)(2,1)S(1)}, bf16[16,4224]{1,0:T(8,128)(2,1)S(1)}, u32[]{:S(2)}, u32[]{:S(2)}) collective-permute-start(bf16[16,4224]{1,0:T(8,128)(2,1)S(1)} %collective-permute-done.14.refs_5_), channel_id=1, source_target_pairs={{0,1},{1,0},{2,3},{3,2},{4,5},{5,4},{6,7},{7,6},{8,9},{9,8},{10,11... | collective-permute-start | bytes 405512 | tf_op jit(solution)/shard_map/ppermute | solution.py:284
  36.1 4.1 %collective-permute-start.18 = (bf16[32,4224]{1,0:T(8,128)(2,1)S(1)}, bf16[32,4224]{1,0:T(8,128)(2,1)S(1)}, u32[]{:S(2)}, u32[]{:S(2)}) collective-permute-start(bf16[32,4224]{1,0:T(8,128)(2,1)S(1)} %collective-permute-done.11.refs_2_), channel_id=1, source_target_pairs={{0,1},{1,0},{2,3},{3,2},{4,5},{5,4},{6,7},{7,6},{8,9},{9,8},{10,11... | collective-permute-start | bytes 811016 | tf_op jit(solution)/shard_map/ppermute | solution.py:284
  37.2 3.0 %collective-permute-start.19 = (bf16[32,4224]{1,0:T(8,128)(2,1)S(1)}, bf16[32,4224]{1,0:T(8,128)(2,1)S(1)}, u32[]{:S(2)}, u32[]{:S(2)}) collective-permute-start(bf16[32,4224]{1,0:T(8,128)(2,1)S(1)} %collective-permute-done.12.refs_3_), channel_id=1, source_target_pairs={{0,1},{1,0},{2,3},{3,2},{4,5},{5,4},{6,7},{7,6},{8,9},{9,8},{10,11... | collective-permute-start | bytes 811016 | tf_op jit(solution)/shard_map/ppermute | solution.py:284
  37.6 9.5 %collective-permute-start.22 = (bf16[16,4096]{1,0:T(8,128)(2,1)S(1)}, bf16[16,4096]{1,0:T(8,128)(2,1)S(1)}, u32[]{:S(2)}, u32[]{:S(2)}) collective-permute-start(bf16[16,4096]{1,0:T(8,128)(2,1)S(1)} %add_convert_fusion.8), channel_id=1, source_target_pairs={{0,16},{8,24},{16,0},{24,8},{1,17},{9,25},{17,1},{25,9},{2,18},{10... | collective-permute-start | bytes 393224 | tf_op jit(solution)/shard_map/ppermute | solution.py:289
  38.4 8.7 %collective-permute-start.24 = (bf16[32,4096]{1,0:T(8,128)(2,1)S(1)}, bf16[32,4096]{1,0:T(8,128)(2,1)S(1)}, u32[]{:S(2)}, u32[]{:S(2)}) collective-permute-start(bf16[32,4096]{1,0:T(8,128)(2,1)S(1)} %get-tuple-element.99), channel_id=1, source_target_pairs={{0,2},{1,3},{2,0},{3,1},{4,6},{5,7},{6,4},{7,5},{8,10},{9,11},{10,... | collective-permute-start | bytes 786440 | tf_op jit(solution)/shard_map/ppermute | solution.py:284
  39.6 8.0 %collective-permute-start.23 = (bf16[32,4096]{1,0:T(8,128)(2,1)S(1)}, bf16[32,4096]{1,0:T(8,128)(2,1)S(1)}, u32[]{:S(2)}, u32[]{:S(2)}) collective-permute-start(bf16[32,4096]{1,0:T(8,128)(2,1)S(1)} %get-tuple-element.100), channel_id=1, source_target_pairs={{0,4},{1,5},{2,6},{3,7},{4,0},{5,1},{6,2},{7,3},{8,12},{9,13},{10,... | collective-permute-start | bytes 786440 | tf_op jit(solution)/shard_map/ppermute | solution.py:284
  40.2 7.4 %collective-permute-start.16 = (bf16[48,4096]{1,0:T(8,128)(2,1)S(1)}, bf16[48,4096]{1,0:T(8,128)(2,1)S(1)}, u32[]{:S(2)}, u32[]{:S(2)}) collective-permute-start(bf16[48,4096]{1,0:T(8,128)(2,1)S(1)} %get-tuple-element.98), channel_id=1, source_target_pairs={{0,1},{1,0},{2,3},{3,2},{4,5},{5,4},{6,7},{7,6},{8,9},{9,8},{10,11... | collective-permute-start | bytes 1179656 | tf_op jit(solution)/shard_map/ppermute | solution.py:284
  47.9 4.8 %collective-permute-start.26 = (bf16[32,4096]{1,0:T(8,128)(2,1)S(1)}, bf16[32,4096]{1,0:T(8,128)(2,1)S(1)}, u32[]{:S(2)}, u32[]{:S(2)}) collective-permute-start(bf16[32,4096]{1,0:T(8,128)(2,1)S(1)} %get-tuple-element.125), channel_id=1, source_target_pairs={{0,1},{1,0},{2,3},{3,2},{4,5},{5,4},{6,7},{7,6},{8,9},{9,8},{10,11... | collective-permute-start | bytes 786440 | tf_op jit(solution)/shard_map/ppermute | solution.py:284
  48.4 13.9 %collective-permute-start.29 = (bf16[16,4096]{1,0:T(8,128)(2,1)S(1)}, bf16[16,4096]{1,0:T(8,128)(2,1)S(1)}, u32[]{:S(2)}, u32[]{:S(2)}) collective-permute-start(bf16[16,4096]{1,0:T(8,128)(2,1)S(1)} %fusion.4), channel_id=1, source_target_pairs={{0,16},{8,24},{16,0},{24,8},{1,17},{9,25},{17,1},{25,9},{2,18},{10... | collective-permute-start | bytes 393224 | tf_op jit(solution)/shard_map/ppermute | solution.py:289
  50.7 8.1 %collective-permute-start.31 = (bf16[32,4096]{1,0:T(8,128)(2,1)S(1)}, bf16[32,4096]{1,0:T(8,128)(2,1)S(1)}, u32[]{:S(2)}, u32[]{:S(2)}) collective-permute-start(bf16[32,4096]{1,0:T(8,128)(2,1)S(1)} %get-tuple-element.133), channel_id=1, source_target_pairs={{0,2},{1,3},{2,0},{3,1},{4,6},{5,7},{6,4},{7,5},{8,10},{9,11},{10,... | collective-permute-start | bytes 786440 | tf_op jit(solution)/shard_map/ppermute | solution.py:284
  52.1 7.8 %collective-permute-start.32 = (bf16[32,4096]{1,0:T(8,128)(2,1)S(1)}, bf16[32,4096]{1,0:T(8,128)(2,1)S(1)}, u32[]{:S(2)}, u32[]{:S(2)}) collective-permute-start(bf16[32,4096]{1,0:T(8,128)(2,1)S(1)} %get-tuple-element.134), channel_id=1, source_target_pairs={{0,4},{1,5},{2,6},{3,7},{4,0},{5,1},{6,2},{7,3},{8,12},{9,13},{10,... | collective-permute-start | bytes 786440 | tf_op jit(solution)/shard_map/ppermute | solution.py:284
  52.8 9.5 %collective-permute-start.28 = (bf16[16,4096]{1,0:T(8,128)(2,1)S(1)}, bf16[16,4096]{1,0:T(8,128)(2,1)S(1)}, u32[]{:S(2)}, u32[]{:S(2)}) collective-permute-start(bf16[16,4096]{1,0:T(8,128)(2,1)S(1)} %get-tuple-element.141), channel_id=1, source_target_pairs={{0,24},{8,16},{16,8},{24,0},{1,25},{9,17},{17,9},{25,1},{2,26},{10... | collective-permute-start | bytes 393224 | tf_op jit(solution)/shard_map/ppermute | solution.py:289
  54.3 9.1 %collective-permute-start.27 = (bf16[16,4096]{1,0:T(8,128)(2,1)S(1)}, bf16[16,4096]{1,0:T(8,128)(2,1)S(1)}, u32[]{:S(2)}, u32[]{:S(2)}) collective-permute-start(bf16[16,4096]{1,0:T(8,128)(2,1)S(1)} %get-tuple-element.142), channel_id=1, source_target_pairs={{0,8},{8,0},{16,24},{24,16},{1,9},{9,1},{17,25},{25,17},{2,10},{10... | collective-permute-start | bytes 393224 | tf_op jit(solution)/shard_map/ppermute | solution.py:289
  60.1 8.8 %collective-permute-start.33 = (bf16[16,4096]{1,0:T(8,128)(2,1)S(1)}, bf16[16,4096]{1,0:T(8,128)(2,1)S(1)}, u32[]{:S(2)}, u32[]{:S(2)}) collective-permute-start(bf16[16,4096]{1,0:T(8,128)(2,1)S(1)} %get-tuple-element.135), channel_id=1, source_target_pairs={{0,8},{8,0},{16,24},{24,16},{1,9},{9,1},{17,25},{25,17},{2,10},{10... | collective-permute-start | bytes 393224 | tf_op jit(solution)/shard_map/ppermute | solution.py:289
  61.7 7.1 %collective-permute-start.34 = (bf16[16,4096]{1,0:T(8,128)(2,1)S(1)}, bf16[16,4096]{1,0:T(8,128)(2,1)S(1)}, u32[]{:S(2)}, u32[]{:S(2)}) collective-permute-start(bf16[16,4096]{1,0:T(8,128)(2,1)S(1)} %get-tuple-element.136), channel_id=1, source_target_pairs={{0,24},{8,16},{16,8},{24,0},{1,25},{9,17},{17,9},{25,1},{2,26},{10... | collective-permute-start | bytes 393224 | tf_op jit(solution)/shard_map/ppermute | solution.py:289
  63.4 6.3 %collective-permute-start.30 = (bf16[16,4096]{1,0:T(8,128)(2,1)S(1)}, bf16[16,4096]{1,0:T(8,128)(2,1)S(1)}, u32[]{:S(2)}, u32[]{:S(2)}) collective-permute-start(bf16[16,4096]{1,0:T(8,128)(2,1)S(1)} %fusion.2), channel_id=1, source_target_pairs={{0,6},{1,7},{2,4},{3,5},{4,2},{5,3},{6,0},{7,1},{8,14},{9,15},{10,... | collective-permute-start | bytes 393224 | tf_op jit(solution)/shard_map/ppermute | solution.py:284
  (11 other events, 61.2 us)

commit v13 on v12

--- a/solution.py
+++ b/solution.py
@@ -333,11 +333,10 @@
     first = gathered(packed, x_own, y_own, far_own)
     first_other = swap_exp(first, 1)
     second = gathered(two, x_two, y_two, far_two)
-    three, down_weight = ordered(three, down_weight)
     downs = fetched(down_weight, False)
-    second, downs = ordered(second, downs)
+    second, downs, three = ordered(second, downs, three)
     pair = gathered(one, three)
-    pair, far_own, far_two = ordered(pair, far_own, far_two)
+    pair, far_own = ordered(pair, far_own)
     x_pair, y_pair = swap_exp(pair, 2), swap_exp(pair, 4)
     far_one, far_three = swap_rep(far_own, 1), swap_rep(far_two, 1)
 

time: 70.6 us -> 70.3 us (level)
  starting transfers between devices: 32.3 us -> 31.1 us
  waiting for transfers between devices: 20.1 us -> 20.9 us
    ppermute x24, waiting for transfers between devices: 12 us -> 13.4 us  [swap_exp(): return lax.ppermute(value, 'exp', [(i, i ^ bits) for i in range(owners)])]
    ppermute x11, starting transfers between devices: 15.2 us -> 14 us  [swap_rep(): return lax.ppermute(value, 'rep', [(i, i ^ bits) for i in range(replicas)])]
  transfers between devices with their start and end apart: 35 -> 35, of which waited for: 16 -> 15; matrix products, arithmetic and copies ran while one was open for 1% -> 1% of each run, Pallas kernels for 22% -> 22%
where the time goes in v13:
time: 70.3 us; the launch traced here: 70.2 us
  starting transfers between devices  31.1 us (44%)
  waiting for transfers between devices  20.9 us (30%)
  Pallas kernels  16 us (23%)
  other arithmetic  1.48 us (2%)
    ppermute x24, starting transfers between devices, swap_exp(): return lax.ppermute(value, 'exp', [(i, i ^ bits) for i in range(owners)])  17.1 us
    ppermute x11, starting transfers between devices, swap_rep(): return lax.ppermute(value, 'rep', [(i, i ^ bits) for i in range(replicas)])  14 us
    ppermute x24, waiting for transfers between devices, swap_exp(): return lax.ppermute(value, 'exp', [(i, i ^ bits) for i in range(owners)])  13.4 us
    pallas_call x2, Pallas kernels, experts_of(): pl.pallas_call(kernel, out_shape=[jax.ShapeDtypeStruct((count, model_widt...  10.2 us
    ppermute x11, waiting for transfers between devices, swap_rep(): return lax.ppermute(value, 'rep', [(i, i ^ bits) for i in range(replicas)])  7.48 us
    pallas_call x3, Pallas kernels, fetched(): pl.pallas_call(functools.partial(fetch_kernel, turn), out_shape=jax.Shape...  4.88 us
  transfers between devices with their start and end apart: 35, of which 15 were waited for; matrix products, arithmetic and copies ran while one was open for 1% of the time, Pallas kernels for 22%

profile of v13, /device:TPU:0, one launch (start us, length us, event | category | flops | bytes accessed | tf_op | source)
XLA Modules:
  0.0 70.2 jit_solution(11347937249891216612)
XLA Ops:
  1.2 4.1 %collective-permute-start.4 = (bf16[16,4224]{1,0:T(8,128)(2,1)S(1)}, bf16[16,4224]{1,0:T(8,128)(2,1)S(1)}, u32[]{:S(2)}, u32[]{:S(2)}) collective-permute-start(bf16[16,4224]{1,0:T(8,128)(2,1)S(1)} %pack.1.refs_0_), channel_id=1, source_target_pairs={{0,16},{8,24},{16,0},{24,8},{1,17},{9,25},{17,1},{25,9},{2,18},{10... | collective-permute-start | bytes 405512 | tf_op jit(solution)/shard_map/ppermute | solution.py:289
  5.3 1.6 %collective-permute-start.3 = (bf16[16,4224]{1,0:T(8,128)(2,1)S(1)}, bf16[16,4224]{1,0:T(8,128)(2,1)S(1)}, u32[]{:S(2)}, u32[]{:S(2)}) collective-permute-start(bf16[16,4224]{1,0:T(8,128)(2,1)S(1)} %pack.1.refs_0_), channel_id=1, source_target_pairs={{0,8},{8,0},{16,24},{24,16},{1,9},{9,1},{17,25},{25,17},{2,10},{10... | collective-permute-start | bytes 405512 | tf_op jit(solution)/shard_map/ppermute | solution.py:289
  6.9 2.4 %collective-permute-start.2 = (bf16[16,4224]{1,0:T(8,128)(2,1)S(1)}, bf16[16,4224]{1,0:T(8,128)(2,1)S(1)}, u32[]{:S(2)}, u32[]{:S(2)}) collective-permute-start(bf16[16,4224]{1,0:T(8,128)(2,1)S(1)} %pack.1.refs_0_), channel_id=1, source_target_pairs={{0,6},{1,7},{2,4},{3,5},{4,2},{5,3},{6,0},{7,1},{8,14},{9,15},{10,... | collective-permute-start | bytes 405512 | tf_op jit(solution)/shard_map/ppermute | solution.py:284
  10.4 2.1 %fetch_turned.2.refs_5_.refs_11_ = bf16[4096,768]{1,0:T(8,128)(2,1)S(1)} custom-call(bf16[768,4096]{1,0:T(8,128)(2,1)S(1)} %bitcast.7), custom_call_target="tpu_custom_call" | custom-call | bytes 12582912 | tf_op jit(solution)/shard_map/fetch_turned/pallas_call | solution.py:103
  12.5 2.1 %fetch_turned.3.refs_6_.refs_12_ = bf16[4096,768]{1,0:T(8,128)(2,1)S(1)} custom-call(bf16[768,4096]{1,0:T(8,128)(2,1)S(1)} %bitcast.11), custom_call_target="tpu_custom_call" | custom-call | bytes 12582912 | tf_op jit(solution)/shard_map/fetch_turned/pallas_call | solution.py:103
  14.6 0.8 %collective-permute-done.1.refs_2_ = bf16[16,4224]{1,0:T(8,128)(2,1)S(1)} collective-permute-done((bf16[16,4224]{1,0:T(8,128)(2,1)S(1)}, bf16[16,4224]{1,0:T(8,128)(2,1)S(1)}, u32[]{:S(2)}, u32[]{:S(2)}) %collective-permute-start.1) | collective-permute-done | bytes 135200 | tf_op jit(solution)/shard_map/ppermute | solution.py:284
  15.5 1.7 %collective-permute-start.7 = (bf16[16,4224]{1,0:T(8,128)(2,1)S(1)}, bf16[16,4224]{1,0:T(8,128)(2,1)S(1)}, u32[]{:S(2)}, u32[]{:S(2)}) collective-permute-start(bf16[16,4224]{1,0:T(8,128)(2,1)S(1)} %collective-permute-done.4.refs_0_), channel_id=1, source_target_pairs={{0,6},{1,7},{2,4},{3,5},{4,2},{5,3},{6,0},{7,1},{8,14},{9,15},{10,... | collective-permute-start | bytes 405512 | tf_op jit(solution)/shard_map/ppermute | solution.py:284
  17.2 1.3 %collective-permute-start.6 = (bf16[16,4224]{1,0:T(8,128)(2,1)S(1)}, bf16[16,4224]{1,0:T(8,128)(2,1)S(1)}, u32[]{:S(2)}, u32[]{:S(2)}) collective-permute-start(bf16[16,4224]{1,0:T(8,128)(2,1)S(1)} %collective-permute-done.4.refs_0_), channel_id=1, source_target_pairs={{0,4},{1,5},{2,6},{3,7},{4,0},{5,1},{6,2},{7,3},{8,12},{9,13},{10,... | collective-permute-start | bytes 405512 | tf_op jit(solution)/shard_map/ppermute | solution.py:284
  19.5 0.8 %fetch.1.refs_7_.refs_13_ = bf16[768,4096]{1,0:T(8,128)(2,1)S(1)} custom-call(bf16[768,4096]{1,0:T(8,128)(2,1)S(1)} %bitcast.15), custom_call_target="tpu_custom_call" | custom-call | bytes 12582912 | tf_op jit(solution)/shard_map/fetch/pallas_call | solution.py:103
  20.4 2.4 %collective-permute-done.7.refs_3_ = bf16[16,4224]{1,0:T(8,128)(2,1)S(1)} collective-permute-done((bf16[16,4224]{1,0:T(8,128)(2,1)S(1)}, bf16[16,4224]{1,0:T(8,128)(2,1)S(1)}, u32[]{:S(2)}, u32[]{:S(2)}) %collective-permute-start.7) | collective-permute-done | bytes 135200 | tf_op jit(solution)/shard_map/ppermute | solution.py:284
  22.7 1.4 %collective-permute-done.6.refs_2_ = bf16[16,4224]{1,0:T(8,128)(2,1)S(1)} collective-permute-done((bf16[16,4224]{1,0:T(8,128)(2,1)S(1)}, bf16[16,4224]{1,0:T(8,128)(2,1)S(1)}, u32[]{:S(2)}, u32[]{:S(2)}) %collective-permute-start.6) | collective-permute-done | bytes 135200 | tf_op jit(solution)/shard_map/ppermute | solution.py:284
  24.5 1.5 %collective-permute-start.12 = (bf16[32,4224]{1,0:T(8,128)(2,1)S(1)}, bf16[32,4224]{1,0:T(8,128)(2,1)S(1)}, u32[]{:S(2)}, u32[]{:S(2)}) collective-permute-start(bf16[32,4224]{1,0:T(8,128)(2,1)S(1)} %gather.5.refs_1_), channel_id=1, source_target_pairs={{0,4},{1,5},{2,6},{3,7},{4,0},{5,1},{6,2},{7,3},{8,12},{9,13},{10,... | collective-permute-start | bytes 811016 | tf_op jit(solution)/shard_map/ppermute | solution.py:284
  26.0 0.6 collective-permute-start.11
  27.0 1.6 %collective-permute-start.14 = (bf16[16,4224]{1,0:T(8,128)(2,1)S(1)}, bf16[16,4224]{1,0:T(8,128)(2,1)S(1)}, u32[]{:S(2)}, u32[]{:S(2)}) collective-permute-start(bf16[16,4224]{1,0:T(8,128)(2,1)S(1)} %collective-permute-done.7.refs_3_), channel_id=1, source_target_pairs={{0,8},{8,0},{16,24},{24,16},{1,9},{9,1},{17,25},{25,17},{2,10},{10... | collective-permute-start | bytes 405512 | tf_op jit(solution)/shard_map/ppermute | solution.py:289
  28.6 5.1 %experts.2 = (bf16[32,4096]{1,0:T(8,128)(2,1)S(1)}, bf16[32,4096]{1,0:T(8,128)(2,1)S(1)}, bf16[16,4096]{1,0:T(8,128)(2,1)S(1)}, bf16[80,4096]{1,0:T(8,128)(2,1)S...) custom-call(s32[1]{0:T(128)} %bitcast.own_ref.refs_0_, bf16[64,4224]{1,0:T(8,128)(2,1)S(1)} %gather.3.refs_1_, ...), custom_call_target="tpu_custom_call" | custom-call | flops 4831838208 | bytes 4194304 | tf_op jit(solution)/shard_map/experts/pallas_call | solution.py:197
  33.7 1.2 %collective-permute-done.14.refs_5_ = bf16[16,4224]{1,0:T(8,128)(2,1)S(1)} collective-permute-done((bf16[16,4224]{1,0:T(8,128)(2,1)S(1)}, bf16[16,4224]{1,0:T(8,128)(2,1)S(1)}, u32[]{:S(2)}, u32[]{:S(2)}) %collective-permute-start.14) | collective-permute-done | bytes 135200 | tf_op jit(solution)/shard_map/ppermute | solution.py:289
  36.1 1.0 %collective-permute-done.15 = bf16[80,4096]{1,0:T(8,128)(2,1)S(1)} collective-permute-done((bf16[80,4096]{1,0:T(8,128)(2,1)S(1)}, bf16[80,4096]{1,0:T(8,128)(2,1)S(1)}, u32[]{:S(2)}, u32[]{:S(2)}) %collective-permute-start.15) | collective-permute-done | bytes 655392 | tf_op jit(solution)/shard_map/ppermute | solution.py:284
  37.9 1.4 %collective-permute-start.24 = (bf16[32,4096]{1,0:T(8,128)(2,1)S(1)}, bf16[32,4096]{1,0:T(8,128)(2,1)S(1)}, u32[]{:S(2)}, u32[]{:S(2)}) collective-permute-start(bf16[32,4096]{1,0:T(8,128)(2,1)S(1)} %get-tuple-element.95), channel_id=1, source_target_pairs={{0,2},{1,3},{2,0},{3,1},{4,6},{5,7},{6,4},{7,5},{8,10},{9,11},{10,... | collective-permute-start | bytes 786440 | tf_op jit(solution)/shard_map/ppermute | solution.py:284
  39.9 5.1 %experts.3 = (bf16[16,4096]{1,0:T(8,128)(2,1)S(1)}, bf16[16,4096]{1,0:T(8,128)(2,1)S(1)}, bf16[32,4096]{1,0:T(8,128)(2,1)S(1)}, bf16[32,4096]{1,0:T(8,128)(2,1)S...) custom-call(s32[1]{0:T(128)} %bitcast.own_ref.refs_0_, ...), custom_call_target="tpu_custom_call" | custom-call | flops 4831838208 | bytes 4194304 | tf_op jit(solution)/shard_map/experts/pallas_call | solution.py:197
  45.6 1.3 %collective-permute-done.22 = bf16[16,4096]{1,0:T(8,128)(2,1)S(1)} collective-permute-done((bf16[16,4096]{1,0:T(8,128)(2,1)S(1)}, bf16[16,4096]{1,0:T(8,128)(2,1)S(1)}, u32[]{:S(2)}, u32[]{:S(2)}) %collective-permute-start.22) | collective-permute-done | bytes 131104 | tf_op jit(solution)/shard_map/ppermute | solution.py:289
  48.1 2.5 %collective-permute-start.29 = (bf16[16,4096]{1,0:T(8,128)(2,1)S(1)}, bf16[16,4096]{1,0:T(8,128)(2,1)S(1)}, u32[]{:S(2)}, u32[]{:S(2)}) collective-permute-start(bf16[16,4096]{1,0:T(8,128)(2,1)S(1)} %fusion.4), channel_id=1, source_target_pairs={{0,16},{8,24},{16,0},{24,8},{1,17},{9,25},{17,1},{25,9},{2,18},{10... | collective-permute-start | bytes 393224 | tf_op jit(solution)/shard_map/ppermute | solution.py:289
  50.6 1.4 %collective-permute-start.31 = (bf16[32,4096]{1,0:T(8,128)(2,1)S(1)}, bf16[32,4096]{1,0:T(8,128)(2,1)S(1)}, u32[]{:S(2)}, u32[]{:S(2)}) collective-permute-start(bf16[32,4096]{1,0:T(8,128)(2,1)S(1)} %get-tuple-element.129), channel_id=1, source_target_pairs={{0,2},{1,3},{2,0},{3,1},{4,6},{5,7},{6,4},{7,5},{8,10},{9,11},{10,... | collective-permute-start | bytes 786440 | tf_op jit(solution)/shard_map/ppermute | solution.py:284
  52.0 0.6 collective-permute-start.32
  52.7 0.8 %collective-permute-start.28 = (bf16[16,4096]{1,0:T(8,128)(2,1)S(1)}, bf16[16,4096]{1,0:T(8,128)(2,1)S(1)}, u32[]{:S(2)}, u32[]{:S(2)}) collective-permute-start(bf16[16,4096]{1,0:T(8,128)(2,1)S(1)} %get-tuple-element.137), channel_id=1, source_target_pairs={{0,24},{8,16},{16,8},{24,0},{1,25},{9,17},{17,9},{25,1},{2,26},{10... | collective-permute-start | bytes 393224 | tf_op jit(solution)/shard_map/ppermute | solution.py:289
  53.7 4.9 %collective-permute-done.31 = bf16[32,4096]{1,0:T(8,128)(2,1)S(1)} collective-permute-done((bf16[32,4096]{1,0:T(8,128)(2,1)S(1)}, bf16[32,4096]{1,0:T(8,128)(2,1)S(1)}, u32[]{:S(2)}, u32[]{:S(2)}) %collective-permute-start.31) | collective-permute-done | bytes 262176 | tf_op jit(solution)/shard_map/ppermute | solution.py:284
  58.7 1.2 %collective-permute-done.32 = bf16[32,4096]{1,0:T(8,128)(2,1)S(1)} collective-permute-done((bf16[32,4096]{1,0:T(8,128)(2,1)S(1)}, bf16[32,4096]{1,0:T(8,128)(2,1)S(1)}, u32[]{:S(2)}, u32[]{:S(2)}) %collective-permute-start.32) | collective-permute-done | bytes 262176 | tf_op jit(solution)/shard_map/ppermute | solution.py:284
  60.5 1.4 %collective-permute-start.34 = (bf16[16,4096]{1,0:T(8,128)(2,1)S(1)}, bf16[16,4096]{1,0:T(8,128)(2,1)S(1)}, u32[]{:S(2)}, u32[]{:S(2)}) collective-permute-start(bf16[16,4096]{1,0:T(8,128)(2,1)S(1)} %get-tuple-element.132), channel_id=1, source_target_pairs={{0,24},{8,16},{16,8},{24,0},{1,25},{9,17},{17,9},{25,1},{2,26},{10... | collective-permute-start | bytes 393224 | tf_op jit(solution)/shard_map/ppermute | solution.py:289
  61.9 1.1 %collective-permute-done.27 = bf16[16,4096]{1,0:T(8,128)(2,1)S(1)} collective-permute-done((bf16[16,4096]{1,0:T(8,128)(2,1)S(1)}, bf16[16,4096]{1,0:T(8,128)(2,1)S(1)}, u32[]{:S(2)}, u32[]{:S(2)}) %collective-permute-start.27) | collective-permute-done | bytes 131104 | tf_op jit(solution)/shard_map/ppermute | solution.py:289
  63.1 1.5 %collective-permute-start.30 = (bf16[16,4096]{1,0:T(8,128)(2,1)S(1)}, bf16[16,4096]{1,0:T(8,128)(2,1)S(1)}, u32[]{:S(2)}, u32[]{:S(2)}) collective-permute-start(bf16[16,4096]{1,0:T(8,128)(2,1)S(1)} %fusion.2), channel_id=1, source_target_pairs={{0,6},{1,7},{2,4},{3,5},{4,2},{5,3},{6,0},{7,1},{8,14},{9,15},{10,... | collective-permute-start | bytes 393224 | tf_op jit(solution)/shard_map/ppermute | solution.py:284
  64.6 3.9 %collective-permute-done.33 = bf16[16,4096]{1,0:T(8,128)(2,1)S(1)} collective-permute-done((bf16[16,4096]{1,0:T(8,128)(2,1)S(1)}, bf16[16,4096]{1,0:T(8,128)(2,1)S(1)}, u32[]{:S(2)}, u32[]{:S(2)}) %collective-permute-start.33) | collective-permute-done | bytes 131104 | tf_op jit(solution)/shard_map/ppermute | solution.py:289
  68.5 0.8 %collective-permute-done.30 = bf16[16,4096]{1,0:T(8,128)(2,1)S(1)} collective-permute-done((bf16[16,4096]{1,0:T(8,128)(2,1)S(1)}, bf16[16,4096]{1,0:T(8,128)(2,1)S(1)}, u32[]{:S(2)}, u32[]{:S(2)}) %collective-permute-start.30) | collective-permute-done | bytes 131104 | tf_op jit(solution)/shard_map/ppermute | solution.py:284
  69.4 0.8 %fusion.9 = bf16[16,4096]{1,0:T(8,128)(2,1)} fusion(f32[48,4096]{1,0:T(8,128)S(1)} %convert_add_fusion, bf16[16,4096]{1,0:T(8,128)(2,1)S(1)} %collective-permute-done.34, bf16[16,4096]{1,0:T(8,128)(2,1)S(1)} %collective-permute-done.33, bf16[16,4096]{1,0:T(8,128)(2,1)S(1)} %collective-permute-done.30, bf16[16,4096]{1,0:T(8,128)(2,1)S(1)} %collective-permute-done.29, ...), kind=kLoop, calls=%fused_computation.17 | loop fusion | flops 851968 | bytes 1179648 | tf_op jit(solution)/shard_map/convert_element_type | solution.py:300
  (75 shorter events, 9.5 us)
Async XLA Ops:
  1.2 13.4 %collective-permute-start.4 = (bf16[16,4224]{1,0:T(8,128)(2,1)S(1)}, bf16[16,4224]{1,0:T(8,128)(2,1)S(1)}, u32[]{:S(2)}, u32[]{:S(2)}) collective-permute-start(bf16[16,4224]{1,0:T(8,128)(2,1)S(1)} %pack.1.refs_0_), channel_id=1, source_target_pairs={{0,16},{8,24},{16,0},{24,8},{1,17},{9,25},{17,1},{25,9},{2,18},{10... | collective-permute-start | bytes 405512 | tf_op jit(solution)/shard_map/ppermute | solution.py:289
  5.3 9.3 %collective-permute-start.3 = (bf16[16,4224]{1,0:T(8,128)(2,1)S(1)}, bf16[16,4224]{1,0:T(8,128)(2,1)S(1)}, u32[]{:S(2)}, u32[]{:S(2)}) collective-permute-start(bf16[16,4224]{1,0:T(8,128)(2,1)S(1)} %pack.1.refs_0_), channel_id=1, source_target_pairs={{0,8},{8,0},{16,24},{24,16},{1,9},{9,1},{17,25},{25,17},{2,10},{10... | collective-permute-start | bytes 405512 | tf_op jit(solution)/shard_map/ppermute | solution.py:289
  6.9 7.7 %collective-permute-start.2 = (bf16[16,4224]{1,0:T(8,128)(2,1)S(1)}, bf16[16,4224]{1,0:T(8,128)(2,1)S(1)}, u32[]{:S(2)}, u32[]{:S(2)}) collective-permute-start(bf16[16,4224]{1,0:T(8,128)(2,1)S(1)} %pack.1.refs_0_), channel_id=1, source_target_pairs={{0,6},{1,7},{2,4},{3,5},{4,2},{5,3},{6,0},{7,1},{8,14},{9,15},{10,... | collective-permute-start | bytes 405512 | tf_op jit(solution)/shard_map/ppermute | solution.py:284
  9.4 6.1 %collective-permute-start.1 = (bf16[16,4224]{1,0:T(8,128)(2,1)S(1)}, bf16[16,4224]{1,0:T(8,128)(2,1)S(1)}, u32[]{:S(2)}, u32[]{:S(2)}) collective-permute-start(bf16[16,4224]{1,0:T(8,128)(2,1)S(1)} %pack.1.refs_0_), channel_id=1, source_target_pairs={{0,4},{1,5},{2,6},{3,7},{4,0},{5,1},{6,2},{7,3},{8,12},{9,13},{10,... | collective-permute-start | bytes 405512 | tf_op jit(solution)/shard_map/ppermute | solution.py:284
  9.9 5.7 %collective-permute-start = (bf16[16,4224]{1,0:T(8,128)(2,1)S(1)}, bf16[16,4224]{1,0:T(8,128)(2,1)S(1)}, u32[]{:S(2)}, u32[]{:S(2)}) collective-permute-start(bf16[16,4224]{1,0:T(8,128)(2,1)S(1)} %pack.1.refs_0_), channel_id=1, source_target_pairs={{0,2},{1,3},{2,0},{3,1},{4,6},{5,7},{6,4},{7,5},{8,10},{9,11},{10,... | collective-permute-start | bytes 405512 | tf_op jit(solution)/shard_map/ppermute | solution.py:284
  15.5 7.2 %collective-permute-start.7 = (bf16[16,4224]{1,0:T(8,128)(2,1)S(1)}, bf16[16,4224]{1,0:T(8,128)(2,1)S(1)}, u32[]{:S(2)}, u32[]{:S(2)}) collective-permute-start(bf16[16,4224]{1,0:T(8,128)(2,1)S(1)} %collective-permute-done.4.refs_0_), channel_id=1, source_target_pairs={{0,6},{1,7},{2,4},{3,5},{4,2},{5,3},{6,0},{7,1},{8,14},{9,15},{10,... | collective-permute-start | bytes 405512 | tf_op jit(solution)/shard_map/ppermute | solution.py:284
  17.2 6.9 %collective-permute-start.6 = (bf16[16,4224]{1,0:T(8,128)(2,1)S(1)}, bf16[16,4224]{1,0:T(8,128)(2,1)S(1)}, u32[]{:S(2)}, u32[]{:S(2)}) collective-permute-start(bf16[16,4224]{1,0:T(8,128)(2,1)S(1)} %collective-permute-done.4.refs_0_), channel_id=1, source_target_pairs={{0,4},{1,5},{2,6},{3,7},{4,0},{5,1},{6,2},{7,3},{8,12},{9,13},{10,... | collective-permute-start | bytes 405512 | tf_op jit(solution)/shard_map/ppermute | solution.py:284
  18.5 5.8 %collective-permute-start.5 = (bf16[16,4224]{1,0:T(8,128)(2,1)S(1)}, bf16[16,4224]{1,0:T(8,128)(2,1)S(1)}, u32[]{:S(2)}, u32[]{:S(2)}) collective-permute-start(bf16[16,4224]{1,0:T(8,128)(2,1)S(1)} %collective-permute-done.4.refs_0_), channel_id=1, source_target_pairs={{0,2},{1,3},{2,0},{3,1},{4,6},{5,7},{6,4},{7,5},{8,10},{9,11},{10,... | collective-permute-start | bytes 405512 | tf_op jit(solution)/shard_map/ppermute | solution.py:284
  19.0 5.3 %collective-permute-start.8 = (bf16[16,4224]{1,0:T(8,128)(2,1)S(1)}, bf16[16,4224]{1,0:T(8,128)(2,1)S(1)}, u32[]{:S(2)}, u32[]{:S(2)}) collective-permute-start(bf16[16,4224]{1,0:T(8,128)(2,1)S(1)} %collective-permute-done.4.refs_0_), channel_id=1, source_target_pairs={{0,8},{8,0},{16,24},{24,16},{1,9},{9,1},{17,25},{25,17},{2,10},{10... | collective-permute-start | bytes 405512 | tf_op jit(solution)/shard_map/ppermute | solution.py:289
  20.3 6.8 %collective-permute-start.9 = (bf16[64,4224]{1,0:T(8,128)(2,1)S(1)}, bf16[64,4224]{1,0:T(8,128)(2,1)S(1)}, u32[]{:S(2)}, u32[]{:S(2)}) collective-permute-start(bf16[64,4224]{1,0:T(8,128)(2,1)S(1)} %gather.3.refs_1_), channel_id=1, source_target_pairs={{0,1},{1,0},{2,3},{3,2},{4,5},{5,4},{6,7},{7,6},{8,9},{9,8},{10,11... | collective-permute-start | bytes 1622024 | tf_op jit(solution)/shard_map/ppermute | solution.py:284
  24.4 4.3 %collective-permute-start.10 = (bf16[64,4224]{1,0:T(8,128)(2,1)S(1)}, bf16[64,4224]{1,0:T(8,128)(2,1)S(1)}, u32[]{:S(2)}, u32[]{:S(2)}) collective-permute-start(bf16[64,4224]{1,0:T(8,128)(2,1)S(1)} %gather.4.refs_2_), channel_id=1, source_target_pairs={{0,1},{1,0},{2,3},{3,2},{4,5},{5,4},{6,7},{7,6},{8,9},{9,8},{10,11... | collective-permute-start | bytes 1622024 | tf_op jit(solution)/shard_map/ppermute | solution.py:284
  24.5 10.4 %collective-permute-start.12 = (bf16[32,4224]{1,0:T(8,128)(2,1)S(1)}, bf16[32,4224]{1,0:T(8,128)(2,1)S(1)}, u32[]{:S(2)}, u32[]{:S(2)}) collective-permute-start(bf16[32,4224]{1,0:T(8,128)(2,1)S(1)} %gather.5.refs_1_), channel_id=1, source_target_pairs={{0,4},{1,5},{2,6},{3,7},{4,0},{5,1},{6,2},{7,3},{8,12},{9,13},{10,... | collective-permute-start | bytes 811016 | tf_op jit(solution)/shard_map/ppermute | solution.py:284
  26.0 8.9 %collective-permute-start.11 = (bf16[32,4224]{1,0:T(8,128)(2,1)S(1)}, bf16[32,4224]{1,0:T(8,128)(2,1)S(1)}, u32[]{:S(2)}, u32[]{:S(2)}) collective-permute-start(bf16[32,4224]{1,0:T(8,128)(2,1)S(1)} %gather.5.refs_1_), channel_id=1, source_target_pairs={{0,2},{1,3},{2,0},{3,1},{4,6},{5,7},{6,4},{7,5},{8,10},{9,11},{10,... | collective-permute-start | bytes 811016 | tf_op jit(solution)/shard_map/ppermute | solution.py:284
  26.6 8.3 %collective-permute-start.13 = (bf16[16,4224]{1,0:T(8,128)(2,1)S(1)}, bf16[16,4224]{1,0:T(8,128)(2,1)S(1)}, u32[]{:S(2)}, u32[]{:S(2)}) collective-permute-start(bf16[16,4224]{1,0:T(8,128)(2,1)S(1)} %collective-permute-done.2.refs_3_), channel_id=1, source_target_pairs={{0,8},{8,0},{16,24},{24,16},{1,9},{9,1},{17,25},{25,17},{2,10},{10... | collective-permute-start | bytes 405512 | tf_op jit(solution)/shard_map/ppermute | solution.py:289
  27.0 7.9 %collective-permute-start.14 = (bf16[16,4224]{1,0:T(8,128)(2,1)S(1)}, bf16[16,4224]{1,0:T(8,128)(2,1)S(1)}, u32[]{:S(2)}, u32[]{:S(2)}) collective-permute-start(bf16[16,4224]{1,0:T(8,128)(2,1)S(1)} %collective-permute-done.7.refs_3_), channel_id=1, source_target_pairs={{0,8},{8,0},{16,24},{24,16},{1,9},{9,1},{17,25},{25,17},{2,10},{10... | collective-permute-start | bytes 405512 | tf_op jit(solution)/shard_map/ppermute | solution.py:289
  35.0 2.5 %collective-permute-start.17 = (bf16[32,4224]{1,0:T(8,128)(2,1)S(1)}, bf16[32,4224]{1,0:T(8,128)(2,1)S(1)}, u32[]{:S(2)}, u32[]{:S(2)}) collective-permute-start(bf16[32,4224]{1,0:T(8,128)(2,1)S(1)} %gather.5.refs_1_), channel_id=1, source_target_pairs={{0,1},{1,0},{2,3},{3,2},{4,5},{5,4},{6,7},{7,6},{8,9},{9,8},{10,11... | collective-permute-start | bytes 811016 | tf_op jit(solution)/shard_map/ppermute | solution.py:284
  35.6 3.7 %collective-permute-start.21 = (bf16[16,4224]{1,0:T(8,128)(2,1)S(1)}, bf16[16,4224]{1,0:T(8,128)(2,1)S(1)}, u32[]{:S(2)}, u32[]{:S(2)}) collective-permute-start(bf16[16,4224]{1,0:T(8,128)(2,1)S(1)} %collective-permute-done.14.refs_5_), channel_id=1, source_target_pairs={{0,1},{1,0},{2,3},{3,2},{4,5},{5,4},{6,7},{7,6},{8,9},{9,8},{10,11... | collective-permute-start | bytes 405512 | tf_op jit(solution)/shard_map/ppermute | solution.py:284
  36.0 3.9 %collective-permute-start.18 = (bf16[32,4224]{1,0:T(8,128)(2,1)S(1)}, bf16[32,4224]{1,0:T(8,128)(2,1)S(1)}, u32[]{:S(2)}, u32[]{:S(2)}) collective-permute-start(bf16[32,4224]{1,0:T(8,128)(2,1)S(1)} %collective-permute-done.11.refs_2_), channel_id=1, source_target_pairs={{0,1},{1,0},{2,3},{3,2},{4,5},{5,4},{6,7},{7,6},{8,9},{9,8},{10,11... | collective-permute-start | bytes 811016 | tf_op jit(solution)/shard_map/ppermute | solution.py:284
  37.1 2.8 %collective-permute-start.19 = (bf16[32,4224]{1,0:T(8,128)(2,1)S(1)}, bf16[32,4224]{1,0:T(8,128)(2,1)S(1)}, u32[]{:S(2)}, u32[]{:S(2)}) collective-permute-start(bf16[32,4224]{1,0:T(8,128)(2,1)S(1)} %collective-permute-done.12.refs_3_), channel_id=1, source_target_pairs={{0,1},{1,0},{2,3},{3,2},{4,5},{5,4},{6,7},{7,6},{8,9},{9,8},{10,11... | collective-permute-start | bytes 811016 | tf_op jit(solution)/shard_map/ppermute | solution.py:284
  37.5 9.4 %collective-permute-start.22 = (bf16[16,4096]{1,0:T(8,128)(2,1)S(1)}, bf16[16,4096]{1,0:T(8,128)(2,1)S(1)}, u32[]{:S(2)}, u32[]{:S(2)}) collective-permute-start(bf16[16,4096]{1,0:T(8,128)(2,1)S(1)} %add_convert_fusion.8), channel_id=1, source_target_pairs={{0,16},{8,24},{16,0},{24,8},{1,17},{9,25},{17,1},{25,9},{2,18},{10... | collective-permute-start | bytes 393224 | tf_op jit(solution)/shard_map/ppermute | solution.py:289
  37.9 9.0 %collective-permute-start.24 = (bf16[32,4096]{1,0:T(8,128)(2,1)S(1)}, bf16[32,4096]{1,0:T(8,128)(2,1)S(1)}, u32[]{:S(2)}, u32[]{:S(2)}) collective-permute-start(bf16[32,4096]{1,0:T(8,128)(2,1)S(1)} %get-tuple-element.95), channel_id=1, source_target_pairs={{0,2},{1,3},{2,0},{3,1},{4,6},{5,7},{6,4},{7,5},{8,10},{9,11},{10,... | collective-permute-start | bytes 786440 | tf_op jit(solution)/shard_map/ppermute | solution.py:284
  39.3 8.0 %collective-permute-start.23 = (bf16[32,4096]{1,0:T(8,128)(2,1)S(1)}, bf16[32,4096]{1,0:T(8,128)(2,1)S(1)}, u32[]{:S(2)}, u32[]{:S(2)}) collective-permute-start(bf16[32,4096]{1,0:T(8,128)(2,1)S(1)} %get-tuple-element.96), channel_id=1, source_target_pairs={{0,4},{1,5},{2,6},{3,7},{4,0},{5,1},{6,2},{7,3},{8,12},{9,13},{10,... | collective-permute-start | bytes 786440 | tf_op jit(solution)/shard_map/ppermute | solution.py:284
  39.9 7.4 %collective-permute-start.16 = (bf16[48,4096]{1,0:T(8,128)(2,1)S(1)}, bf16[48,4096]{1,0:T(8,128)(2,1)S(1)}, u32[]{:S(2)}, u32[]{:S(2)}) collective-permute-start(bf16[48,4096]{1,0:T(8,128)(2,1)S(1)} %get-tuple-element.94), channel_id=1, source_target_pairs={{0,1},{1,0},{2,3},{3,2},{4,5},{5,4},{6,7},{7,6},{8,9},{9,8},{10,11... | collective-permute-start | bytes 1179656 | tf_op jit(solution)/shard_map/ppermute | solution.py:284
  47.6 5.0 %collective-permute-start.26 = (bf16[32,4096]{1,0:T(8,128)(2,1)S(1)}, bf16[32,4096]{1,0:T(8,128)(2,1)S(1)}, u32[]{:S(2)}, u32[]{:S(2)}) collective-permute-start(bf16[32,4096]{1,0:T(8,128)(2,1)S(1)} %get-tuple-element.121), channel_id=1, source_target_pairs={{0,1},{1,0},{2,3},{3,2},{4,5},{5,4},{6,7},{7,6},{8,9},{9,8},{10,11... | collective-permute-start | bytes 786440 | tf_op jit(solution)/shard_map/ppermute | solution.py:284
  48.1 13.8 %collective-permute-start.29 = (bf16[16,4096]{1,0:T(8,128)(2,1)S(1)}, bf16[16,4096]{1,0:T(8,128)(2,1)S(1)}, u32[]{:S(2)}, u32[]{:S(2)}) collective-permute-start(bf16[16,4096]{1,0:T(8,128)(2,1)S(1)} %fusion.4), channel_id=1, source_target_pairs={{0,16},{8,24},{16,0},{24,8},{1,17},{9,25},{17,1},{25,9},{2,18},{10... | collective-permute-start | bytes 393224 | tf_op jit(solution)/shard_map/ppermute | solution.py:289
  50.6 8.1 %collective-permute-start.31 = (bf16[32,4096]{1,0:T(8,128)(2,1)S(1)}, bf16[32,4096]{1,0:T(8,128)(2,1)S(1)}, u32[]{:S(2)}, u32[]{:S(2)}) collective-permute-start(bf16[32,4096]{1,0:T(8,128)(2,1)S(1)} %get-tuple-element.129), channel_id=1, source_target_pairs={{0,2},{1,3},{2,0},{3,1},{4,6},{5,7},{6,4},{7,5},{8,10},{9,11},{10,... | collective-permute-start | bytes 786440 | tf_op jit(solution)/shard_map/ppermute | solution.py:284
  52.0 7.8 %collective-permute-start.32 = (bf16[32,4096]{1,0:T(8,128)(2,1)S(1)}, bf16[32,4096]{1,0:T(8,128)(2,1)S(1)}, u32[]{:S(2)}, u32[]{:S(2)}) collective-permute-start(bf16[32,4096]{1,0:T(8,128)(2,1)S(1)} %get-tuple-element.130), channel_id=1, source_target_pairs={{0,4},{1,5},{2,6},{3,7},{4,0},{5,1},{6,2},{7,3},{8,12},{9,13},{10,... | collective-permute-start | bytes 786440 | tf_op jit(solution)/shard_map/ppermute | solution.py:284
  52.7 9.2 %collective-permute-start.28 = (bf16[16,4096]{1,0:T(8,128)(2,1)S(1)}, bf16[16,4096]{1,0:T(8,128)(2,1)S(1)}, u32[]{:S(2)}, u32[]{:S(2)}) collective-permute-start(bf16[16,4096]{1,0:T(8,128)(2,1)S(1)} %get-tuple-element.137), channel_id=1, source_target_pairs={{0,24},{8,16},{16,8},{24,0},{1,25},{9,17},{17,9},{25,1},{2,26},{10... | collective-permute-start | bytes 393224 | tf_op jit(solution)/shard_map/ppermute | solution.py:289
  53.5 9.5 %collective-permute-start.27 = (bf16[16,4096]{1,0:T(8,128)(2,1)S(1)}, bf16[16,4096]{1,0:T(8,128)(2,1)S(1)}, u32[]{:S(2)}, u32[]{:S(2)}) collective-permute-start(bf16[16,4096]{1,0:T(8,128)(2,1)S(1)} %get-tuple-element.138), channel_id=1, source_target_pairs={{0,8},{8,0},{16,24},{24,16},{1,9},{9,1},{17,25},{25,17},{2,10},{10... | collective-permute-start | bytes 393224 | tf_op jit(solution)/shard_map/ppermute | solution.py:289
  60.0 8.6 %collective-permute-start.33 = (bf16[16,4096]{1,0:T(8,128)(2,1)S(1)}, bf16[16,4096]{1,0:T(8,128)(2,1)S(1)}, u32[]{:S(2)}, u32[]{:S(2)}) collective-permute-start(bf16[16,4096]{1,0:T(8,128)(2,1)S(1)} %get-tuple-element.131), channel_id=1, source_target_pairs={{0,8},{8,0},{16,24},{24,16},{1,9},{9,1},{17,25},{25,17},{2,10},{10... | collective-permute-start | bytes 393224 | tf_op jit(solution)/shard_map/ppermute | solution.py:289
  60.5 8.1 %collective-permute-start.34 = (bf16[16,4096]{1,0:T(8,128)(2,1)S(1)}, bf16[16,4096]{1,0:T(8,128)(2,1)S(1)}, u32[]{:S(2)}, u32[]{:S(2)}) collective-permute-start(bf16[16,4096]{1,0:T(8,128)(2,1)S(1)} %get-tuple-element.132), channel_id=1, source_target_pairs={{0,24},{8,16},{16,8},{24,0},{1,25},{9,17},{17,9},{25,1},{2,26},{10... | collective-permute-start | bytes 393224 | tf_op jit(solution)/shard_map/ppermute | solution.py:289
  63.1 6.3 %collective-permute-start.30 = (bf16[16,4096]{1,0:T(8,128)(2,1)S(1)}, bf16[16,4096]{1,0:T(8,128)(2,1)S(1)}, u32[]{:S(2)}, u32[]{:S(2)}) collective-permute-start(bf16[16,4096]{1,0:T(8,128)(2,1)S(1)} %fusion.2), channel_id=1, source_target_pairs={{0,6},{1,7},{2,4},{3,5},{4,2},{5,3},{6,0},{7,1},{8,14},{9,15},{10,... | collective-permute-start | bytes 393224 | tf_op jit(solution)/shard_map/ppermute | solution.py:284
  (11 other events, 59.0 us)

commit v14 on v13

--- a/solution.py
+++ b/solution.py
@@ -325,8 +325,8 @@
     x_own, y_own, far_own = [swap_exp(packed, bits) for bits in (2, 4, 6)]
     gates, ups = fetched(gate_weight, True), fetched(up_weight, True)
     one = swap_rep(packed, 1)
-    x_own, y_own, far_own, one, two, gates, ups = ordered(
-        x_own, y_own, far_own, one, two, gates, ups
+    two, one, far_own, y_own, x_own, gates, ups = ordered(
+        two, one, far_own, y_own, x_own, gates, ups
     )
     three = swap_rep(two, 1)
     x_two, y_two, far_two = [swap_exp(two, bits) for bits in (2, 4, 6)]
@@ -334,18 +334,16 @@
     first_other = swap_exp(first, 1)
     second = gathered(two, x_two, y_two, far_two)
     downs = fetched(down_weight, False)
-    second, downs, three = ordered(second, downs, three)
+    far_one = swap_rep(far_own, 1)
+    second, downs, three, far_one = ordered(second, downs, three, far_one)
     pair = gathered(one, three)
-    pair, far_own = ordered(pair, far_own)
     x_pair, y_pair = swap_exp(pair, 2), swap_exp(pair, 4)
-    far_one, far_three = swap_rep(far_own, 1), swap_rep(far_two, 1)
+    far_three = swap_rep(far_two, 1)
 
     near = [first, second, first_other, swap_exp(second, 1)]
     groups = row_groups([[5, 1], [6, 2], [7], [13, 9, 14, 10, 15], [4, 0, 3], [12, 8, 11]], rows)
     parts = experts_of(own, near, groups, gates, ups, downs, shard_units, top)
-    *parts, x_pair, y_pair, far_one, far_three = ordered(
-        *parts, x_pair, y_pair, far_one, far_three
-    )
+    *parts, x_pair, y_pair, far_three = ordered(*parts, x_pair, y_pair, far_three)
     to_x, to_y, to_far, other, near_kept, near_other = parts
     back = swap_exp(other, 1)
     to_x = rounded(to_x, back[: 2 * rows])
@@ -375,7 +373,7 @@
     from_three, from_one = swap_rep(to_three, 3), swap_rep(to_one, 1)
 
     own_sum = kept[rows : 2 * rows] + added(near_x[rows:], near_y[rows:])
-    from_one, from_three, from_two = ordered(from_one, from_three, from_two)
+    from_two, from_three, from_one = ordered(from_two, from_three, from_one)
     to_far = rounded(kept[2 * rows :], from_one, from_three, near_far)
     from_far = swap_exp(to_far, 6)
     to_one = rounded(far_kept[:rows], back[4 * rows : 5 * rows], far_x[:rows], far_y[:rows])

time: 70.3 us -> 76 us (1.081)
  waiting for transfers between devices: 20.9 us -> 26.6 us
    ppermute x24, waiting for transfers between devices: 13.4 us -> 16.6 us  [swap_exp(): return lax.ppermute(value, 'exp', [(i, i ^ bits) for i in range(owners)])]
    ppermute x11, waiting for transfers between devices: 7.48 us -> 9.99 us  [swap_rep(): return lax.ppermute(value, 'rep', [(i, i ^ bits) for i in range(replicas)])]
    ppermute x24, starting transfers between devices: 17.1 us -> 16.3 us  [swap_exp(): return lax.ppermute(value, 'exp', [(i, i ^ bits) for i in range(owners)])]
    ppermute x11, starting transfers between devices: 14 us -> 14.8 us  [swap_rep(): return lax.ppermute(value, 'rep', [(i, i ^ bits) for i in range(replicas)])]
  transfers between devices with their start and end apart: 35 -> 35, of which waited for: 15 -> 16; matrix products, arithmetic and copies ran while one was open for 1% -> 1% of each run, Pallas kernels for 22% -> 20%
where the time goes in v14:
time: 76 us; the launch traced here: 75.8 us
  starting transfers between devices  31.1 us (41%)
  waiting for transfers between devices  26.6 us (35%)
  Pallas kernels  16 us (21%)
  other arithmetic  1.45 us (2%)
    ppermute x24, waiting for transfers between devices, swap_exp(): return lax.ppermute(value, 'exp', [(i, i ^ bits) for i in range(owners)])  16.6 us
    ppermute x24, starting transfers between devices, swap_exp(): return lax.ppermute(value, 'exp', [(i, i ^ bits) for i in range(owners)])  16.3 us
    ppermute x11, starting transfers between devices, swap_rep(): return lax.ppermute(value, 'rep', [(i, i ^ bits) for i in range(replicas)])  14.8 us
    pallas_call x2, Pallas kernels, experts_of(): pl.pallas_call(kernel, out_shape=[jax.ShapeDtypeStruct((count, model_widt...  10.2 us
    ppermute x11, waiting for transfers between devices, swap_rep(): return lax.ppermute(value, 'rep', [(i, i ^ bits) for i in range(replicas)])  9.99 us
    pallas_call x3, Pallas kernels, fetched(): pl.pallas_call(functools.partial(fetch_kernel, turn), out_shape=jax.Shape...  4.88 us
  transfers between devices with their start and end apart: 35, of which 16 were waited for; matrix products, arithmetic and copies ran while one was open for 1% of the time, Pallas kernels for 20%

profile of v14, /device:TPU:0, one launch (start us, length us, event | category | flops | bytes accessed | tf_op | source)
XLA Modules:
  0.0 75.8 jit_solution(14294306885858294685)
XLA Ops:
  1.2 4.1 %collective-permute-start = (bf16[16,4224]{1,0:T(8,128)(2,1)S(1)}, bf16[16,4224]{1,0:T(8,128)(2,1)S(1)}, u32[]{:S(2)}, u32[]{:S(2)}) collective-permute-start(bf16[16,4224]{1,0:T(8,128)(2,1)S(1)} %pack.1.refs_0_), channel_id=1, source_target_pairs={{0,16},{8,24},{16,0},{24,8},{1,17},{9,25},{17,1},{25,9},{2,18},{10... | collective-permute-start | bytes 405512 | tf_op jit(solution)/shard_map/ppermute | solution.py:289
  5.3 1.6 %collective-permute-start.1 = (bf16[16,4224]{1,0:T(8,128)(2,1)S(1)}, bf16[16,4224]{1,0:T(8,128)(2,1)S(1)}, u32[]{:S(2)}, u32[]{:S(2)}) collective-permute-start(bf16[16,4224]{1,0:T(8,128)(2,1)S(1)} %pack.1.refs_0_), channel_id=1, source_target_pairs={{0,8},{8,0},{16,24},{24,16},{1,9},{9,1},{17,25},{25,17},{2,10},{10... | collective-permute-start | bytes 405512 | tf_op jit(solution)/shard_map/ppermute | solution.py:289
  6.9 2.4 %collective-permute-start.2 = (bf16[16,4224]{1,0:T(8,128)(2,1)S(1)}, bf16[16,4224]{1,0:T(8,128)(2,1)S(1)}, u32[]{:S(2)}, u32[]{:S(2)}) collective-permute-start(bf16[16,4224]{1,0:T(8,128)(2,1)S(1)} %pack.1.refs_0_), channel_id=1, source_target_pairs={{0,6},{1,7},{2,4},{3,5},{4,2},{5,3},{6,0},{7,1},{8,14},{9,15},{10,... | collective-permute-start | bytes 405512 | tf_op jit(solution)/shard_map/ppermute | solution.py:284
  10.4 2.1 %fetch_turned.2.refs_5_.refs_11_ = bf16[4096,768]{1,0:T(8,128)(2,1)S(1)} custom-call(bf16[768,4096]{1,0:T(8,128)(2,1)S(1)} %bitcast.7), custom_call_target="tpu_custom_call" | custom-call | bytes 12582912 | tf_op jit(solution)/shard_map/fetch_turned/pallas_call | solution.py:103
  12.5 2.1 %fetch_turned.3.refs_6_.refs_12_ = bf16[4096,768]{1,0:T(8,128)(2,1)S(1)} custom-call(bf16[768,4096]{1,0:T(8,128)(2,1)S(1)} %bitcast.11), custom_call_target="tpu_custom_call" | custom-call | bytes 12582912 | tf_op jit(solution)/shard_map/fetch_turned/pallas_call | solution.py:103
  14.6 0.8 %collective-permute-done.3.refs_2_ = bf16[16,4224]{1,0:T(8,128)(2,1)S(1)} collective-permute-done((bf16[16,4224]{1,0:T(8,128)(2,1)S(1)}, bf16[16,4224]{1,0:T(8,128)(2,1)S(1)}, u32[]{:S(2)}, u32[]{:S(2)}) %collective-permute-start.3) | collective-permute-done | bytes 135200 | tf_op jit(solution)/shard_map/ppermute | solution.py:284
  15.5 1.5 %collective-permute-start.5 = (bf16[16,4224]{1,0:T(8,128)(2,1)S(1)}, bf16[16,4224]{1,0:T(8,128)(2,1)S(1)}, u32[]{:S(2)}, u32[]{:S(2)}) collective-permute-start(bf16[16,4224]{1,0:T(8,128)(2,1)S(1)} %collective-permute-done.refs_0_), channel_id=1, source_target_pairs={{0,2},{1,3},{2,0},{3,1},{4,6},{5,7},{6,4},{7,5},{8,10},{9,11},{10,... | collective-permute-start | bytes 405512 | tf_op jit(solution)/shard_map/ppermute | solution.py:284
  17.1 0.7 collective-permute-start.6
  17.8 1.2 %collective-permute-start.7 = (bf16[16,4224]{1,0:T(8,128)(2,1)S(1)}, bf16[16,4224]{1,0:T(8,128)(2,1)S(1)}, u32[]{:S(2)}, u32[]{:S(2)}) collective-permute-start(bf16[16,4224]{1,0:T(8,128)(2,1)S(1)} %collective-permute-done.refs_0_), channel_id=1, source_target_pairs={{0,6},{1,7},{2,4},{3,5},{4,2},{5,3},{6,0},{7,1},{8,14},{9,15},{10,... | collective-permute-start | bytes 405512 | tf_op jit(solution)/shard_map/ppermute | solution.py:284
  19.5 1.6 %collective-permute-start.9 = (bf16[16,4224]{1,0:T(8,128)(2,1)S(1)}, bf16[16,4224]{1,0:T(8,128)(2,1)S(1)}, u32[]{:S(2)}, u32[]{:S(2)}) collective-permute-start(bf16[16,4224]{1,0:T(8,128)(2,1)S(1)} %collective-permute-done.2.refs_3_), channel_id=1, source_target_pairs={{0,8},{8,0},{16,24},{24,16},{1,9},{9,1},{17,25},{25,17},{2,10},{10... | collective-permute-start | bytes 405512 | tf_op jit(solution)/shard_map/ppermute | solution.py:289
  21.0 0.8 fetch.1.refs_7_.refs_13_
  21.9 2.7 %collective-permute-done.6.refs_2_ = bf16[16,4224]{1,0:T(8,128)(2,1)S(1)} collective-permute-done((bf16[16,4224]{1,0:T(8,128)(2,1)S(1)}, bf16[16,4224]{1,0:T(8,128)(2,1)S(1)}, u32[]{:S(2)}, u32[]{:S(2)}) %collective-permute-start.6) | collective-permute-done | bytes 135200 | tf_op jit(solution)/shard_map/ppermute | solution.py:284
  24.7 1.2 %collective-permute-done.9.refs_4_ = bf16[16,4224]{1,0:T(8,128)(2,1)S(1)} collective-permute-done((bf16[16,4224]{1,0:T(8,128)(2,1)S(1)}, bf16[16,4224]{1,0:T(8,128)(2,1)S(1)}, u32[]{:S(2)}, u32[]{:S(2)}) %collective-permute-start.9) | collective-permute-done | bytes 135200 | tf_op jit(solution)/shard_map/ppermute | solution.py:289
  25.9 1.7 %collective-permute-start.12 = (bf16[32,4224]{1,0:T(8,128)(2,1)S(1)}, bf16[32,4224]{1,0:T(8,128)(2,1)S(1)}, u32[]{:S(2)}, u32[]{:S(2)}) collective-permute-start(bf16[32,4224]{1,0:T(8,128)(2,1)S(1)} %gather.5.refs_1_), channel_id=1, source_target_pairs={{0,2},{1,3},{2,0},{3,1},{4,6},{5,7},{6,4},{7,5},{8,10},{9,11},{10,... | collective-permute-start | bytes 811016 | tf_op jit(solution)/shard_map/ppermute | solution.py:284
  28.4 5.1 %experts.2 = (bf16[32,4096]{1,0:T(8,128)(2,1)S(1)}, bf16[32,4096]{1,0:T(8,128)(2,1)S(1)}, bf16[16,4096]{1,0:T(8,128)(2,1)S(1)}, bf16[80,4096]{1,0:T(8,128)(2,1)S...) custom-call(s32[1]{0:T(128)} %bitcast.own_ref.refs_0_, bf16[64,4224]{1,0:T(8,128)(2,1)S(1)} %gather.3.refs_1_, ...), custom_call_target="tpu_custom_call" | custom-call | flops 4831838208 | bytes 4194304 | tf_op jit(solution)/shard_map/experts/pallas_call | solution.py:197
  33.5 1.3 %collective-permute-done.12.refs_2_ = bf16[32,4224]{1,0:T(8,128)(2,1)S(1)} collective-permute-done((bf16[32,4224]{1,0:T(8,128)(2,1)S(1)}, bf16[32,4224]{1,0:T(8,128)(2,1)S(1)}, u32[]{:S(2)}, u32[]{:S(2)}) %collective-permute-start.12) | collective-permute-done | bytes 270368 | tf_op jit(solution)/shard_map/ppermute | solution.py:284
  34.9 1.3 %collective-permute-done.13.refs_3_ = bf16[32,4224]{1,0:T(8,128)(2,1)S(1)} collective-permute-done((bf16[32,4224]{1,0:T(8,128)(2,1)S(1)}, bf16[32,4224]{1,0:T(8,128)(2,1)S(1)}, u32[]{:S(2)}, u32[]{:S(2)}) %collective-permute-start.13) | collective-permute-done | bytes 270368 | tf_op jit(solution)/shard_map/ppermute | solution.py:284
  37.2 1.1 %collective-permute-done.15 = bf16[80,4096]{1,0:T(8,128)(2,1)S(1)} collective-permute-done((bf16[80,4096]{1,0:T(8,128)(2,1)S(1)}, bf16[80,4096]{1,0:T(8,128)(2,1)S(1)}, u32[]{:S(2)}, u32[]{:S(2)}) %collective-permute-start.15) | collective-permute-done | bytes 655392 | tf_op jit(solution)/shard_map/ppermute | solution.py:284
  40.2 1.7 %collective-permute-start.24 = (bf16[32,4096]{1,0:T(8,128)(2,1)S(1)}, bf16[32,4096]{1,0:T(8,128)(2,1)S(1)}, u32[]{:S(2)}, u32[]{:S(2)}) collective-permute-start(bf16[32,4096]{1,0:T(8,128)(2,1)S(1)} %get-tuple-element.91), channel_id=1, source_target_pairs={{0,2},{1,3},{2,0},{3,1},{4,6},{5,7},{6,4},{7,5},{8,10},{9,11},{10,... | collective-permute-start | bytes 786440 | tf_op jit(solution)/shard_map/ppermute | solution.py:284
  41.9 5.1 %experts.3 = (bf16[16,4096]{1,0:T(8,128)(2,1)S(1)}, bf16[16,4096]{1,0:T(8,128)(2,1)S(1)}, bf16[32,4096]{1,0:T(8,128)(2,1)S(1)}, bf16[32,4096]{1,0:T(8,128)(2,1)S...) custom-call(s32[1]{0:T(128)} %bitcast.own_ref.refs_0_, ...), custom_call_target="tpu_custom_call" | custom-call | flops 4831838208 | bytes 4194304 | tf_op jit(solution)/shard_map/experts/pallas_call | solution.py:197
  47.1 1.3 %collective-permute-done.22 = bf16[16,4096]{1,0:T(8,128)(2,1)S(1)} collective-permute-done((bf16[16,4096]{1,0:T(8,128)(2,1)S(1)}, bf16[16,4096]{1,0:T(8,128)(2,1)S(1)}, u32[]{:S(2)}, u32[]{:S(2)}) %collective-permute-start.22) | collective-permute-done | bytes 131104 | tf_op jit(solution)/shard_map/ppermute | solution.py:289
  48.5 0.8 %collective-permute-done.25 = bf16[96,4096]{1,0:T(8,128)(2,1)S(1)} collective-permute-done((bf16[96,4096]{1,0:T(8,128)(2,1)S(1)}, bf16[96,4096]{1,0:T(8,128)(2,1)S(1)}, u32[]{:S(2)}, u32[]{:S(2)}) %collective-permute-start.25) | collective-permute-done | bytes 786464 | tf_op jit(solution)/shard_map/ppermute | solution.py:284
  50.4 1.3 %collective-permute-start.31 = (bf16[32,4096]{1,0:T(8,128)(2,1)S(1)}, bf16[32,4096]{1,0:T(8,128)(2,1)S(1)}, u32[]{:S(2)}, u32[]{:S(2)}) collective-permute-start(bf16[32,4096]{1,0:T(8,128)(2,1)S(1)} %get-tuple-element.125), channel_id=1, source_target_pairs={{0,2},{1,3},{2,0},{3,1},{4,6},{5,7},{6,4},{7,5},{8,10},{9,11},{10,... | collective-permute-start | bytes 786440 | tf_op jit(solution)/shard_map/ppermute | solution.py:284
  51.7 2.1 %collective-permute-start.26 = (bf16[16,4096]{1,0:T(8,128)(2,1)S(1)}, bf16[16,4096]{1,0:T(8,128)(2,1)S(1)}, u32[]{:S(2)}, u32[]{:S(2)}) collective-permute-start(bf16[16,4096]{1,0:T(8,128)(2,1)S(1)} %fusion.4), channel_id=1, source_target_pairs={{0,16},{8,24},{16,0},{24,8},{1,17},{9,25},{17,1},{25,9},{2,18},{10... | collective-permute-start | bytes 393224 | tf_op jit(solution)/shard_map/ppermute | solution.py:289
  53.9 0.7 collective-permute-start.28
  55.4 2.9 %collective-permute-done.32 = bf16[32,4096]{1,0:T(8,128)(2,1)S(1)} collective-permute-done((bf16[32,4096]{1,0:T(8,128)(2,1)S(1)}, bf16[32,4096]{1,0:T(8,128)(2,1)S(1)}, u32[]{:S(2)}, u32[]{:S(2)}) %collective-permute-start.32) | collective-permute-done | bytes 262176 | tf_op jit(solution)/shard_map/ppermute | solution.py:284
  58.9 2.0 %collective-permute-start.34 = (bf16[16,4096]{1,0:T(8,128)(2,1)S(1)}, bf16[16,4096]{1,0:T(8,128)(2,1)S(1)}, u32[]{:S(2)}, u32[]{:S(2)}) collective-permute-start(bf16[16,4096]{1,0:T(8,128)(2,1)S(1)} %get-tuple-element.128), channel_id=1, source_target_pairs={{0,24},{8,16},{16,8},{24,0},{1,25},{9,17},{17,9},{25,1},{2,26},{10... | collective-permute-start | bytes 393224 | tf_op jit(solution)/shard_map/ppermute | solution.py:289
  61.6 2.6 %collective-permute-done.26 = bf16[16,4096]{1,0:T(8,128)(2,1)S(1)} collective-permute-done((bf16[16,4096]{1,0:T(8,128)(2,1)S(1)}, bf16[16,4096]{1,0:T(8,128)(2,1)S(1)}, u32[]{:S(2)}, u32[]{:S(2)}) %collective-permute-start.26) | collective-permute-done | bytes 131104 | tf_op jit(solution)/shard_map/ppermute | solution.py:289
  64.2 4.9 %collective-permute-done.29 = bf16[16,4096]{1,0:T(8,128)(2,1)S(1)} collective-permute-done((bf16[16,4096]{1,0:T(8,128)(2,1)S(1)}, bf16[16,4096]{1,0:T(8,128)(2,1)S(1)}, u32[]{:S(2)}, u32[]{:S(2)}) %collective-permute-start.29) | collective-permute-done | bytes 131104 | tf_op jit(solution)/shard_map/ppermute | solution.py:289
  69.1 1.6 %collective-permute-start.30 = (bf16[16,4096]{1,0:T(8,128)(2,1)S(1)}, bf16[16,4096]{1,0:T(8,128)(2,1)S(1)}, u32[]{:S(2)}, u32[]{:S(2)}) collective-permute-start(bf16[16,4096]{1,0:T(8,128)(2,1)S(1)} %fusion.2), channel_id=1, source_target_pairs={{0,6},{1,7},{2,4},{3,5},{4,2},{5,3},{6,0},{7,1},{8,14},{9,15},{10,... | collective-permute-start | bytes 393224 | tf_op jit(solution)/shard_map/ppermute | solution.py:284
  70.7 4.4 %collective-permute-done.30 = bf16[16,4096]{1,0:T(8,128)(2,1)S(1)} collective-permute-done((bf16[16,4096]{1,0:T(8,128)(2,1)S(1)}, bf16[16,4096]{1,0:T(8,128)(2,1)S(1)}, u32[]{:S(2)}, u32[]{:S(2)}) %collective-permute-start.30) | collective-permute-done | bytes 131104 | tf_op jit(solution)/shard_map/ppermute | solution.py:284
  75.0 0.8 %fusion.9 = bf16[16,4096]{1,0:T(8,128)(2,1)} fusion(f32[48,4096]{1,0:T(8,128)S(1)} %convert_add_fusion, bf16[16,4096]{1,0:T(8,128)(2,1)S(1)} %collective-permute-done.34, bf16[16,4096]{1,0:T(8,128)(2,1)S(1)} %collective-permute-done.33, bf16[16,4096]{1,0:T(8,128)(2,1)S(1)} %collective-permute-done.30, bf16[16,4096]{1,0:T(8,128)(2,1)S(1)} %collective-permute-done.26, ...), kind=kLoop, calls=%fused_computation.17 | loop fusion | flops 851968 | bytes 1179648 | tf_op jit(solution)/shard_map/convert_element_type | solution.py:300
  (75 shorter events, 10.0 us)
Async XLA Ops:
  1.2 13.4 %collective-permute-start = (bf16[16,4224]{1,0:T(8,128)(2,1)S(1)}, bf16[16,4224]{1,0:T(8,128)(2,1)S(1)}, u32[]{:S(2)}, u32[]{:S(2)}) collective-permute-start(bf16[16,4224]{1,0:T(8,128)(2,1)S(1)} %pack.1.refs_0_), channel_id=1, source_target_pairs={{0,16},{8,24},{16,0},{24,8},{1,17},{9,25},{17,1},{25,9},{2,18},{10... | collective-permute-start | bytes 405512 | tf_op jit(solution)/shard_map/ppermute | solution.py:289
  5.3 9.3 %collective-permute-start.1 = (bf16[16,4224]{1,0:T(8,128)(2,1)S(1)}, bf16[16,4224]{1,0:T(8,128)(2,1)S(1)}, u32[]{:S(2)}, u32[]{:S(2)}) collective-permute-start(bf16[16,4224]{1,0:T(8,128)(2,1)S(1)} %pack.1.refs_0_), channel_id=1, source_target_pairs={{0,8},{8,0},{16,24},{24,16},{1,9},{9,1},{17,25},{25,17},{2,10},{10... | collective-permute-start | bytes 405512 | tf_op jit(solution)/shard_map/ppermute | solution.py:289
  6.9 7.7 %collective-permute-start.2 = (bf16[16,4224]{1,0:T(8,128)(2,1)S(1)}, bf16[16,4224]{1,0:T(8,128)(2,1)S(1)}, u32[]{:S(2)}, u32[]{:S(2)}) collective-permute-start(bf16[16,4224]{1,0:T(8,128)(2,1)S(1)} %pack.1.refs_0_), channel_id=1, source_target_pairs={{0,6},{1,7},{2,4},{3,5},{4,2},{5,3},{6,0},{7,1},{8,14},{9,15},{10,... | collective-permute-start | bytes 405512 | tf_op jit(solution)/shard_map/ppermute | solution.py:284
  9.4 6.1 %collective-permute-start.3 = (bf16[16,4224]{1,0:T(8,128)(2,1)S(1)}, bf16[16,4224]{1,0:T(8,128)(2,1)S(1)}, u32[]{:S(2)}, u32[]{:S(2)}) collective-permute-start(bf16[16,4224]{1,0:T(8,128)(2,1)S(1)} %pack.1.refs_0_), channel_id=1, source_target_pairs={{0,4},{1,5},{2,6},{3,7},{4,0},{5,1},{6,2},{7,3},{8,12},{9,13},{10,... | collective-permute-start | bytes 405512 | tf_op jit(solution)/shard_map/ppermute | solution.py:284
  9.9 5.7 %collective-permute-start.4 = (bf16[16,4224]{1,0:T(8,128)(2,1)S(1)}, bf16[16,4224]{1,0:T(8,128)(2,1)S(1)}, u32[]{:S(2)}, u32[]{:S(2)}) collective-permute-start(bf16[16,4224]{1,0:T(8,128)(2,1)S(1)} %pack.1.refs_0_), channel_id=1, source_target_pairs={{0,2},{1,3},{2,0},{3,1},{4,6},{5,7},{6,4},{7,5},{8,10},{9,11},{10,... | collective-permute-start | bytes 405512 | tf_op jit(solution)/shard_map/ppermute | solution.py:284
  15.5 6.3 %collective-permute-start.5 = (bf16[16,4224]{1,0:T(8,128)(2,1)S(1)}, bf16[16,4224]{1,0:T(8,128)(2,1)S(1)}, u32[]{:S(2)}, u32[]{:S(2)}) collective-permute-start(bf16[16,4224]{1,0:T(8,128)(2,1)S(1)} %collective-permute-done.refs_0_), channel_id=1, source_target_pairs={{0,2},{1,3},{2,0},{3,1},{4,6},{5,7},{6,4},{7,5},{8,10},{9,11},{10,... | collective-permute-start | bytes 405512 | tf_op jit(solution)/shard_map/ppermute | solution.py:284
  17.1 7.5 %collective-permute-start.6 = (bf16[16,4224]{1,0:T(8,128)(2,1)S(1)}, bf16[16,4224]{1,0:T(8,128)(2,1)S(1)}, u32[]{:S(2)}, u32[]{:S(2)}) collective-permute-start(bf16[16,4224]{1,0:T(8,128)(2,1)S(1)} %collective-permute-done.refs_0_), channel_id=1, source_target_pairs={{0,4},{1,5},{2,6},{3,7},{4,0},{5,1},{6,2},{7,3},{8,12},{9,13},{10,... | collective-permute-start | bytes 405512 | tf_op jit(solution)/shard_map/ppermute | solution.py:284
  17.8 6.8 %collective-permute-start.7 = (bf16[16,4224]{1,0:T(8,128)(2,1)S(1)}, bf16[16,4224]{1,0:T(8,128)(2,1)S(1)}, u32[]{:S(2)}, u32[]{:S(2)}) collective-permute-start(bf16[16,4224]{1,0:T(8,128)(2,1)S(1)} %collective-permute-done.refs_0_), channel_id=1, source_target_pairs={{0,6},{1,7},{2,4},{3,5},{4,2},{5,3},{6,0},{7,1},{8,14},{9,15},{10,... | collective-permute-start | bytes 405512 | tf_op jit(solution)/shard_map/ppermute | solution.py:284
  19.0 5.6 %collective-permute-start.8 = (bf16[16,4224]{1,0:T(8,128)(2,1)S(1)}, bf16[16,4224]{1,0:T(8,128)(2,1)S(1)}, u32[]{:S(2)}, u32[]{:S(2)}) collective-permute-start(bf16[16,4224]{1,0:T(8,128)(2,1)S(1)} %collective-permute-done.refs_0_), channel_id=1, source_target_pairs={{0,8},{8,0},{16,24},{24,16},{1,9},{9,1},{17,25},{25,17},{2,10},{10... | collective-permute-start | bytes 405512 | tf_op jit(solution)/shard_map/ppermute | solution.py:289
  19.5 6.4 %collective-permute-start.9 = (bf16[16,4224]{1,0:T(8,128)(2,1)S(1)}, bf16[16,4224]{1,0:T(8,128)(2,1)S(1)}, u32[]{:S(2)}, u32[]{:S(2)}) collective-permute-start(bf16[16,4224]{1,0:T(8,128)(2,1)S(1)} %collective-permute-done.2.refs_3_), channel_id=1, source_target_pairs={{0,8},{8,0},{16,24},{24,16},{1,9},{9,1},{17,25},{25,17},{2,10},{10... | collective-permute-start | bytes 405512 | tf_op jit(solution)/shard_map/ppermute | solution.py:289
  21.9 6.5 %collective-permute-start.10 = (bf16[64,4224]{1,0:T(8,128)(2,1)S(1)}, bf16[64,4224]{1,0:T(8,128)(2,1)S(1)}, u32[]{:S(2)}, u32[]{:S(2)}) collective-permute-start(bf16[64,4224]{1,0:T(8,128)(2,1)S(1)} %gather.3.refs_1_), channel_id=1, source_target_pairs={{0,1},{1,0},{2,3},{3,2},{4,5},{5,4},{6,7},{7,6},{8,9},{9,8},{10,11... | collective-permute-start | bytes 1622024 | tf_op jit(solution)/shard_map/ppermute | solution.py:284
  25.9 2.5 %collective-permute-start.11 = (bf16[64,4224]{1,0:T(8,128)(2,1)S(1)}, bf16[64,4224]{1,0:T(8,128)(2,1)S(1)}, u32[]{:S(2)}, u32[]{:S(2)}) collective-permute-start(bf16[64,4224]{1,0:T(8,128)(2,1)S(1)} %gather.4.refs_2_), channel_id=1, source_target_pairs={{0,1},{1,0},{2,3},{3,2},{4,5},{5,4},{6,7},{7,6},{8,9},{9,8},{10,11... | collective-permute-start | bytes 1622024 | tf_op jit(solution)/shard_map/ppermute | solution.py:284
  25.9 9.0 %collective-permute-start.12 = (bf16[32,4224]{1,0:T(8,128)(2,1)S(1)}, bf16[32,4224]{1,0:T(8,128)(2,1)S(1)}, u32[]{:S(2)}, u32[]{:S(2)}) collective-permute-start(bf16[32,4224]{1,0:T(8,128)(2,1)S(1)} %gather.5.refs_1_), channel_id=1, source_target_pairs={{0,2},{1,3},{2,0},{3,1},{4,6},{5,7},{6,4},{7,5},{8,10},{9,11},{10,... | collective-permute-start | bytes 811016 | tf_op jit(solution)/shard_map/ppermute | solution.py:284
  27.6 8.6 %collective-permute-start.13 = (bf16[32,4224]{1,0:T(8,128)(2,1)S(1)}, bf16[32,4224]{1,0:T(8,128)(2,1)S(1)}, u32[]{:S(2)}, u32[]{:S(2)}) collective-permute-start(bf16[32,4224]{1,0:T(8,128)(2,1)S(1)} %gather.5.refs_1_), channel_id=1, source_target_pairs={{0,4},{1,5},{2,6},{3,7},{4,0},{5,1},{6,2},{7,3},{8,12},{9,13},{10,... | collective-permute-start | bytes 811016 | tf_op jit(solution)/shard_map/ppermute | solution.py:284
  27.9 5.6 %collective-permute-start.14 = (bf16[16,4224]{1,0:T(8,128)(2,1)S(1)}, bf16[16,4224]{1,0:T(8,128)(2,1)S(1)}, u32[]{:S(2)}, u32[]{:S(2)}) collective-permute-start(bf16[16,4224]{1,0:T(8,128)(2,1)S(1)} %collective-permute-done.7.refs_3_), channel_id=1, source_target_pairs={{0,8},{8,0},{16,24},{24,16},{1,9},{9,1},{17,25},{25,17},{2,10},{10... | collective-permute-start | bytes 405512 | tf_op jit(solution)/shard_map/ppermute | solution.py:289
  36.2 2.9 %collective-permute-start.17 = (bf16[32,4224]{1,0:T(8,128)(2,1)S(1)}, bf16[32,4224]{1,0:T(8,128)(2,1)S(1)}, u32[]{:S(2)}, u32[]{:S(2)}) collective-permute-start(bf16[32,4224]{1,0:T(8,128)(2,1)S(1)} %gather.5.refs_1_), channel_id=1, source_target_pairs={{0,1},{1,0},{2,3},{3,2},{4,5},{5,4},{6,7},{7,6},{8,9},{9,8},{10,11... | collective-permute-start | bytes 811016 | tf_op jit(solution)/shard_map/ppermute | solution.py:284
  36.7 3.5 %collective-permute-start.18 = (bf16[32,4224]{1,0:T(8,128)(2,1)S(1)}, bf16[32,4224]{1,0:T(8,128)(2,1)S(1)}, u32[]{:S(2)}, u32[]{:S(2)}) collective-permute-start(bf16[32,4224]{1,0:T(8,128)(2,1)S(1)} %collective-permute-done.12.refs_2_), channel_id=1, source_target_pairs={{0,1},{1,0},{2,3},{3,2},{4,5},{5,4},{6,7},{7,6},{8,9},{9,8},{10,11... | collective-permute-start | bytes 811016 | tf_op jit(solution)/shard_map/ppermute | solution.py:284
  37.2 4.7 %collective-permute-start.19 = (bf16[32,4224]{1,0:T(8,128)(2,1)S(1)}, bf16[32,4224]{1,0:T(8,128)(2,1)S(1)}, u32[]{:S(2)}, u32[]{:S(2)}) collective-permute-start(bf16[32,4224]{1,0:T(8,128)(2,1)S(1)} %collective-permute-done.13.refs_3_), channel_id=1, source_target_pairs={{0,1},{1,0},{2,3},{3,2},{4,5},{5,4},{6,7},{7,6},{8,9},{9,8},{10,11... | collective-permute-start | bytes 811016 | tf_op jit(solution)/shard_map/ppermute | solution.py:284
  38.9 9.5 %collective-permute-start.16 = (bf16[48,4096]{1,0:T(8,128)(2,1)S(1)}, bf16[48,4096]{1,0:T(8,128)(2,1)S(1)}, u32[]{:S(2)}, u32[]{:S(2)}) collective-permute-start(bf16[48,4096]{1,0:T(8,128)(2,1)S(1)} %get-tuple-element.90), channel_id=1, source_target_pairs={{0,1},{1,0},{2,3},{3,2},{4,5},{5,4},{6,7},{7,6},{8,9},{9,8},{10,11... | collective-permute-start | bytes 1179656 | tf_op jit(solution)/shard_map/ppermute | solution.py:284
  39.1 9.3 %collective-permute-start.22 = (bf16[16,4096]{1,0:T(8,128)(2,1)S(1)}, bf16[16,4096]{1,0:T(8,128)(2,1)S(1)}, u32[]{:S(2)}, u32[]{:S(2)}) collective-permute-start(bf16[16,4096]{1,0:T(8,128)(2,1)S(1)} %add_convert_fusion.8), channel_id=1, source_target_pairs={{0,16},{8,24},{16,0},{24,8},{1,17},{9,25},{17,1},{25,9},{2,18},{10... | collective-permute-start | bytes 393224 | tf_op jit(solution)/shard_map/ppermute | solution.py:289
  39.9 8.5 %collective-permute-start.23 = (bf16[32,4096]{1,0:T(8,128)(2,1)S(1)}, bf16[32,4096]{1,0:T(8,128)(2,1)S(1)}, u32[]{:S(2)}, u32[]{:S(2)}) collective-permute-start(bf16[32,4096]{1,0:T(8,128)(2,1)S(1)} %get-tuple-element.92), channel_id=1, source_target_pairs={{0,4},{1,5},{2,6},{3,7},{4,0},{5,1},{6,2},{7,3},{8,12},{9,13},{10,... | collective-permute-start | bytes 786440 | tf_op jit(solution)/shard_map/ppermute | solution.py:284
  40.2 8.2 %collective-permute-start.24 = (bf16[32,4096]{1,0:T(8,128)(2,1)S(1)}, bf16[32,4096]{1,0:T(8,128)(2,1)S(1)}, u32[]{:S(2)}, u32[]{:S(2)}) collective-permute-start(bf16[32,4096]{1,0:T(8,128)(2,1)S(1)} %get-tuple-element.91), channel_id=1, source_target_pairs={{0,2},{1,3},{2,0},{3,1},{4,6},{5,7},{6,4},{7,5},{8,10},{9,11},{10,... | collective-permute-start | bytes 786440 | tf_op jit(solution)/shard_map/ppermute | solution.py:284
  47.0 2.4 %collective-permute-start.25 = (bf16[96,4096]{1,0:T(8,128)(2,1)S(1)}, bf16[96,4096]{1,0:T(8,128)(2,1)S(1)}, u32[]{:S(2)}, u32[]{:S(2)}) collective-permute-start(bf16[96,4096]{1,0:T(8,128)(2,1)S(1)} %get-tuple-element.111), channel_id=1, source_target_pairs={{0,1},{1,0},{2,3},{3,2},{4,5},{5,4},{6,7},{7,6},{8,9},{9,8},{10,11... | collective-permute-start | bytes 2359304 | tf_op jit(solution)/shard_map/ppermute | solution.py:284
  49.5 4.4 %collective-permute-start.27 = (bf16[32,4096]{1,0:T(8,128)(2,1)S(1)}, bf16[32,4096]{1,0:T(8,128)(2,1)S(1)}, u32[]{:S(2)}, u32[]{:S(2)}) collective-permute-start(bf16[32,4096]{1,0:T(8,128)(2,1)S(1)} %get-tuple-element.118), channel_id=1, source_target_pairs={{0,1},{1,0},{2,3},{3,2},{4,5},{5,4},{6,7},{7,6},{8,9},{9,8},{10,11... | collective-permute-start | bytes 786440 | tf_op jit(solution)/shard_map/ppermute | solution.py:284
  49.7 8.6 %collective-permute-start.32 = (bf16[32,4096]{1,0:T(8,128)(2,1)S(1)}, bf16[32,4096]{1,0:T(8,128)(2,1)S(1)}, u32[]{:S(2)}, u32[]{:S(2)}) collective-permute-start(bf16[32,4096]{1,0:T(8,128)(2,1)S(1)} %get-tuple-element.126), channel_id=1, source_target_pairs={{0,4},{1,5},{2,6},{3,7},{4,0},{5,1},{6,2},{7,3},{8,12},{9,13},{10,... | collective-permute-start | bytes 786440 | tf_op jit(solution)/shard_map/ppermute | solution.py:284
  50.4 8.4 %collective-permute-start.31 = (bf16[32,4096]{1,0:T(8,128)(2,1)S(1)}, bf16[32,4096]{1,0:T(8,128)(2,1)S(1)}, u32[]{:S(2)}, u32[]{:S(2)}) collective-permute-start(bf16[32,4096]{1,0:T(8,128)(2,1)S(1)} %get-tuple-element.125), channel_id=1, source_target_pairs={{0,2},{1,3},{2,0},{3,1},{4,6},{5,7},{6,4},{7,5},{8,10},{9,11},{10,... | collective-permute-start | bytes 786440 | tf_op jit(solution)/shard_map/ppermute | solution.py:284
  51.7 12.5 %collective-permute-start.26 = (bf16[16,4096]{1,0:T(8,128)(2,1)S(1)}, bf16[16,4096]{1,0:T(8,128)(2,1)S(1)}, u32[]{:S(2)}, u32[]{:S(2)}) collective-permute-start(bf16[16,4096]{1,0:T(8,128)(2,1)S(1)} %fusion.4), channel_id=1, source_target_pairs={{0,16},{8,24},{16,0},{24,8},{1,17},{9,25},{17,1},{25,9},{2,18},{10... | collective-permute-start | bytes 393224 | tf_op jit(solution)/shard_map/ppermute | solution.py:289
  53.9 10.2 %collective-permute-start.28 = (bf16[16,4096]{1,0:T(8,128)(2,1)S(1)}, bf16[16,4096]{1,0:T(8,128)(2,1)S(1)}, u32[]{:S(2)}, u32[]{:S(2)}) collective-permute-start(bf16[16,4096]{1,0:T(8,128)(2,1)S(1)} %get-tuple-element.134), channel_id=1, source_target_pairs={{0,24},{8,16},{16,8},{24,0},{1,25},{9,17},{17,9},{25,1},{2,26},{10... | collective-permute-start | bytes 393224 | tf_op jit(solution)/shard_map/ppermute | solution.py:289
  54.7 14.4 %collective-permute-start.29 = (bf16[16,4096]{1,0:T(8,128)(2,1)S(1)}, bf16[16,4096]{1,0:T(8,128)(2,1)S(1)}, u32[]{:S(2)}, u32[]{:S(2)}) collective-permute-start(bf16[16,4096]{1,0:T(8,128)(2,1)S(1)} %get-tuple-element.133), channel_id=1, source_target_pairs={{0,8},{8,0},{16,24},{24,16},{1,9},{9,1},{17,25},{25,17},{2,10},{10... | collective-permute-start | bytes 393224 | tf_op jit(solution)/shard_map/ppermute | solution.py:289
  58.9 11.8 %collective-permute-start.34 = (bf16[16,4096]{1,0:T(8,128)(2,1)S(1)}, bf16[16,4096]{1,0:T(8,128)(2,1)S(1)}, u32[]{:S(2)}, u32[]{:S(2)}) collective-permute-start(bf16[16,4096]{1,0:T(8,128)(2,1)S(1)} %get-tuple-element.128), channel_id=1, source_target_pairs={{0,24},{8,16},{16,8},{24,0},{1,25},{9,17},{17,9},{25,1},{2,26},{10... | collective-permute-start | bytes 393224 | tf_op jit(solution)/shard_map/ppermute | solution.py:289
  60.9 9.8 %collective-permute-start.33 = (bf16[16,4096]{1,0:T(8,128)(2,1)S(1)}, bf16[16,4096]{1,0:T(8,128)(2,1)S(1)}, u32[]{:S(2)}, u32[]{:S(2)}) collective-permute-start(bf16[16,4096]{1,0:T(8,128)(2,1)S(1)} %get-tuple-element.127), channel_id=1, source_target_pairs={{0,8},{8,0},{16,24},{24,16},{1,9},{9,1},{17,25},{25,17},{2,10},{10... | collective-permute-start | bytes 393224 | tf_op jit(solution)/shard_map/ppermute | solution.py:289
  69.1 5.9 %collective-permute-start.30 = (bf16[16,4096]{1,0:T(8,128)(2,1)S(1)}, bf16[16,4096]{1,0:T(8,128)(2,1)S(1)}, u32[]{:S(2)}, u32[]{:S(2)}) collective-permute-start(bf16[16,4096]{1,0:T(8,128)(2,1)S(1)} %fusion.2), channel_id=1, source_target_pairs={{0,6},{1,7},{2,4},{3,5},{4,2},{5,3},{6,0},{7,1},{8,14},{9,15},{10,... | collective-permute-start | bytes 393224 | tf_op jit(solution)/shard_map/ppermute | solution.py:284
  (11 other events, 60.9 us)

commit v15 on v13

--- a/solution.py
+++ b/solution.py
@@ -380,7 +380,7 @@
     from_far = swap_exp(to_far, 6)
     to_one = rounded(far_kept[:rows], back[4 * rows : 5 * rows], far_x[:rows], far_y[:rows])
     to_three = rounded(far_kept[rows:], back[5 * rows :], far_x[rows:], far_y[rows:])
-    arrived = [swap_rep(to_one, 1), swap_rep(to_three, 3)]
+    arrived = [swap_rep(to_three, 3), swap_rep(to_one, 1)]
     return rounded(own_sum, from_two, from_far, *arrived)
 
 

time: 70.3 us -> 71 us (level)
  starting transfers between devices: 31.1 us -> 30.2 us
  waiting for transfers between devices: 20.9 us -> 21.8 us
    ppermute x11, starting transfers between devices: 14 us -> 13.1 us  [swap_rep(): return lax.ppermute(value, 'rep', [(i, i ^ bits) for i in range(replicas)])]
    ppermute x11, waiting for transfers between devices: 7.48 us -> 8.37 us  [swap_rep(): return lax.ppermute(value, 'rep', [(i, i ^ bits) for i in range(replicas)])]
  transfers between devices with their start and end apart: 35 -> 35, of which waited for: 15 -> 16; matrix products, arithmetic and copies ran while one was open for 1% -> 1% of each run, Pallas kernels for 22% -> 22%
where the time goes in v15:
time: 71 us; the launch traced here: 70.2 us
  starting transfers between devices  30.2 us (43%)
  waiting for transfers between devices  21.8 us (31%)
  Pallas kernels  16 us (23%)
  other arithmetic  1.48 us (2%)
    ppermute x24, starting transfers between devices, swap_exp(): return lax.ppermute(value, 'exp', [(i, i ^ bits) for i in range(owners)])  17.1 us
    ppermute x24, waiting for transfers between devices, swap_exp(): return lax.ppermute(value, 'exp', [(i, i ^ bits) for i in range(owners)])  13.4 us
    ppermute x11, starting transfers between devices, swap_rep(): return lax.ppermute(value, 'rep', [(i, i ^ bits) for i in range(replicas)])  13.1 us
    pallas_call x2, Pallas kernels, experts_of(): pl.pallas_call(kernel, out_shape=[jax.ShapeDtypeStruct((count, model_widt...  10.2 us
    ppermute x11, waiting for transfers between devices, swap_rep(): return lax.ppermute(value, 'rep', [(i, i ^ bits) for i in range(replicas)])  8.37 us
    pallas_call x3, Pallas kernels, fetched(): pl.pallas_call(functools.partial(fetch_kernel, turn), out_shape=jax.Shape...  4.88 us
  transfers between devices with their start and end apart: 35, of which 16 were waited for; matrix products, arithmetic and copies ran while one was open for 1% of the time, Pallas kernels for 22%

profile of v15, /device:TPU:0, one launch (start us, length us, event | category | flops | bytes accessed | tf_op | source)
XLA Modules:
  0.0 70.2 jit_solution(11282062678926952209)
XLA Ops:
  1.2 4.1 %collective-permute-start.4 = (bf16[16,4224]{1,0:T(8,128)(2,1)S(1)}, bf16[16,4224]{1,0:T(8,128)(2,1)S(1)}, u32[]{:S(2)}, u32[]{:S(2)}) collective-permute-start(bf16[16,4224]{1,0:T(8,128)(2,1)S(1)} %pack.1.refs_0_), channel_id=1, source_target_pairs={{0,16},{8,24},{16,0},{24,8},{1,17},{9,25},{17,1},{25,9},{2,18},{10... | collective-permute-start | bytes 405512 | tf_op jit(solution)/shard_map/ppermute | solution.py:289
  5.3 1.6 %collective-permute-start.3 = (bf16[16,4224]{1,0:T(8,128)(2,1)S(1)}, bf16[16,4224]{1,0:T(8,128)(2,1)S(1)}, u32[]{:S(2)}, u32[]{:S(2)}) collective-permute-start(bf16[16,4224]{1,0:T(8,128)(2,1)S(1)} %pack.1.refs_0_), channel_id=1, source_target_pairs={{0,8},{8,0},{16,24},{24,16},{1,9},{9,1},{17,25},{25,17},{2,10},{10... | collective-permute-start | bytes 405512 | tf_op jit(solution)/shard_map/ppermute | solution.py:289
  6.9 2.4 %collective-permute-start.2 = (bf16[16,4224]{1,0:T(8,128)(2,1)S(1)}, bf16[16,4224]{1,0:T(8,128)(2,1)S(1)}, u32[]{:S(2)}, u32[]{:S(2)}) collective-permute-start(bf16[16,4224]{1,0:T(8,128)(2,1)S(1)} %pack.1.refs_0_), channel_id=1, source_target_pairs={{0,6},{1,7},{2,4},{3,5},{4,2},{5,3},{6,0},{7,1},{8,14},{9,15},{10,... | collective-permute-start | bytes 405512 | tf_op jit(solution)/shard_map/ppermute | solution.py:284
  10.4 2.1 %fetch_turned.2.refs_5_.refs_11_ = bf16[4096,768]{1,0:T(8,128)(2,1)S(1)} custom-call(bf16[768,4096]{1,0:T(8,128)(2,1)S(1)} %bitcast.7), custom_call_target="tpu_custom_call" | custom-call | bytes 12582912 | tf_op jit(solution)/shard_map/fetch_turned/pallas_call | solution.py:103
  12.5 2.1 %fetch_turned.3.refs_6_.refs_12_ = bf16[4096,768]{1,0:T(8,128)(2,1)S(1)} custom-call(bf16[768,4096]{1,0:T(8,128)(2,1)S(1)} %bitcast.11), custom_call_target="tpu_custom_call" | custom-call | bytes 12582912 | tf_op jit(solution)/shard_map/fetch_turned/pallas_call | solution.py:103
  14.6 0.8 %collective-permute-done.1.refs_2_ = bf16[16,4224]{1,0:T(8,128)(2,1)S(1)} collective-permute-done((bf16[16,4224]{1,0:T(8,128)(2,1)S(1)}, bf16[16,4224]{1,0:T(8,128)(2,1)S(1)}, u32[]{:S(2)}, u32[]{:S(2)}) %collective-permute-start.1) | collective-permute-done | bytes 135200 | tf_op jit(solution)/shard_map/ppermute | solution.py:284
  15.5 1.7 %collective-permute-start.7 = (bf16[16,4224]{1,0:T(8,128)(2,1)S(1)}, bf16[16,4224]{1,0:T(8,128)(2,1)S(1)}, u32[]{:S(2)}, u32[]{:S(2)}) collective-permute-start(bf16[16,4224]{1,0:T(8,128)(2,1)S(1)} %collective-permute-done.4.refs_0_), channel_id=1, source_target_pairs={{0,6},{1,7},{2,4},{3,5},{4,2},{5,3},{6,0},{7,1},{8,14},{9,15},{10,... | collective-permute-start | bytes 405512 | tf_op jit(solution)/shard_map/ppermute | solution.py:284
  17.2 1.3 %collective-permute-start.6 = (bf16[16,4224]{1,0:T(8,128)(2,1)S(1)}, bf16[16,4224]{1,0:T(8,128)(2,1)S(1)}, u32[]{:S(2)}, u32[]{:S(2)}) collective-permute-start(bf16[16,4224]{1,0:T(8,128)(2,1)S(1)} %collective-permute-done.4.refs_0_), channel_id=1, source_target_pairs={{0,4},{1,5},{2,6},{3,7},{4,0},{5,1},{6,2},{7,3},{8,12},{9,13},{10,... | collective-permute-start | bytes 405512 | tf_op jit(solution)/shard_map/ppermute | solution.py:284
  19.5 0.8 %fetch.1.refs_7_.refs_13_ = bf16[768,4096]{1,0:T(8,128)(2,1)S(1)} custom-call(bf16[768,4096]{1,0:T(8,128)(2,1)S(1)} %bitcast.15), custom_call_target="tpu_custom_call" | custom-call | bytes 12582912 | tf_op jit(solution)/shard_map/fetch/pallas_call | solution.py:103
  20.4 2.4 %collective-permute-done.7.refs_3_ = bf16[16,4224]{1,0:T(8,128)(2,1)S(1)} collective-permute-done((bf16[16,4224]{1,0:T(8,128)(2,1)S(1)}, bf16[16,4224]{1,0:T(8,128)(2,1)S(1)}, u32[]{:S(2)}, u32[]{:S(2)}) %collective-permute-start.7) | collective-permute-done | bytes 135200 | tf_op jit(solution)/shard_map/ppermute | solution.py:284
  22.7 1.4 %collective-permute-done.6.refs_2_ = bf16[16,4224]{1,0:T(8,128)(2,1)S(1)} collective-permute-done((bf16[16,4224]{1,0:T(8,128)(2,1)S(1)}, bf16[16,4224]{1,0:T(8,128)(2,1)S(1)}, u32[]{:S(2)}, u32[]{:S(2)}) %collective-permute-start.6) | collective-permute-done | bytes 135200 | tf_op jit(solution)/shard_map/ppermute | solution.py:284
  24.5 1.5 %collective-permute-start.12 = (bf16[32,4224]{1,0:T(8,128)(2,1)S(1)}, bf16[32,4224]{1,0:T(8,128)(2,1)S(1)}, u32[]{:S(2)}, u32[]{:S(2)}) collective-permute-start(bf16[32,4224]{1,0:T(8,128)(2,1)S(1)} %gather.5.refs_1_), channel_id=1, source_target_pairs={{0,4},{1,5},{2,6},{3,7},{4,0},{5,1},{6,2},{7,3},{8,12},{9,13},{10,... | collective-permute-start | bytes 811016 | tf_op jit(solution)/shard_map/ppermute | solution.py:284
  27.0 1.6 %collective-permute-start.14 = (bf16[16,4224]{1,0:T(8,128)(2,1)S(1)}, bf16[16,4224]{1,0:T(8,128)(2,1)S(1)}, u32[]{:S(2)}, u32[]{:S(2)}) collective-permute-start(bf16[16,4224]{1,0:T(8,128)(2,1)S(1)} %collective-permute-done.7.refs_3_), channel_id=1, source_target_pairs={{0,8},{8,0},{16,24},{24,16},{1,9},{9,1},{17,25},{25,17},{2,10},{10... | collective-permute-start | bytes 405512 | tf_op jit(solution)/shard_map/ppermute | solution.py:289
  28.6 5.1 %experts.2 = (bf16[32,4096]{1,0:T(8,128)(2,1)S(1)}, bf16[32,4096]{1,0:T(8,128)(2,1)S(1)}, bf16[16,4096]{1,0:T(8,128)(2,1)S(1)}, bf16[80,4096]{1,0:T(8,128)(2,1)S...) custom-call(s32[1]{0:T(128)} %bitcast.own_ref.refs_0_, bf16[64,4224]{1,0:T(8,128)(2,1)S(1)} %gather.3.refs_1_, ...), custom_call_target="tpu_custom_call" | custom-call | flops 4831838208 | bytes 4194304 | tf_op jit(solution)/shard_map/experts/pallas_call | solution.py:197
  33.7 1.2 %collective-permute-done.14.refs_5_ = bf16[16,4224]{1,0:T(8,128)(2,1)S(1)} collective-permute-done((bf16[16,4224]{1,0:T(8,128)(2,1)S(1)}, bf16[16,4224]{1,0:T(8,128)(2,1)S(1)}, u32[]{:S(2)}, u32[]{:S(2)}) %collective-permute-start.14) | collective-permute-done | bytes 135200 | tf_op jit(solution)/shard_map/ppermute | solution.py:289
  36.1 1.0 %collective-permute-done.15 = bf16[80,4096]{1,0:T(8,128)(2,1)S(1)} collective-permute-done((bf16[80,4096]{1,0:T(8,128)(2,1)S(1)}, bf16[80,4096]{1,0:T(8,128)(2,1)S(1)}, u32[]{:S(2)}, u32[]{:S(2)}) %collective-permute-start.15) | collective-permute-done | bytes 655392 | tf_op jit(solution)/shard_map/ppermute | solution.py:284
  37.9 1.4 %collective-permute-start.24 = (bf16[32,4096]{1,0:T(8,128)(2,1)S(1)}, bf16[32,4096]{1,0:T(8,128)(2,1)S(1)}, u32[]{:S(2)}, u32[]{:S(2)}) collective-permute-start(bf16[32,4096]{1,0:T(8,128)(2,1)S(1)} %get-tuple-element.95), channel_id=1, source_target_pairs={{0,2},{1,3},{2,0},{3,1},{4,6},{5,7},{6,4},{7,5},{8,10},{9,11},{10,... | collective-permute-start | bytes 786440 | tf_op jit(solution)/shard_map/ppermute | solution.py:284
  39.9 5.1 %experts.3 = (bf16[16,4096]{1,0:T(8,128)(2,1)S(1)}, bf16[16,4096]{1,0:T(8,128)(2,1)S(1)}, bf16[32,4096]{1,0:T(8,128)(2,1)S(1)}, bf16[32,4096]{1,0:T(8,128)(2,1)S...) custom-call(s32[1]{0:T(128)} %bitcast.own_ref.refs_0_, ...), custom_call_target="tpu_custom_call" | custom-call | flops 4831838208 | bytes 4194304 | tf_op jit(solution)/shard_map/experts/pallas_call | solution.py:197
  45.6 1.3 %collective-permute-done.22 = bf16[16,4096]{1,0:T(8,128)(2,1)S(1)} collective-permute-done((bf16[16,4096]{1,0:T(8,128)(2,1)S(1)}, bf16[16,4096]{1,0:T(8,128)(2,1)S(1)}, u32[]{:S(2)}, u32[]{:S(2)}) %collective-permute-start.22) | collective-permute-done | bytes 131104 | tf_op jit(solution)/shard_map/ppermute | solution.py:289
  48.1 2.5 %collective-permute-start.29 = (bf16[16,4096]{1,0:T(8,128)(2,1)S(1)}, bf16[16,4096]{1,0:T(8,128)(2,1)S(1)}, u32[]{:S(2)}, u32[]{:S(2)}) collective-permute-start(bf16[16,4096]{1,0:T(8,128)(2,1)S(1)} %fusion.4), channel_id=1, source_target_pairs={{0,16},{8,24},{16,0},{24,8},{1,17},{9,25},{17,1},{25,9},{2,18},{10... | collective-permute-start | bytes 393224 | tf_op jit(solution)/shard_map/ppermute | solution.py:289
  50.6 1.4 %collective-permute-start.31 = (bf16[32,4096]{1,0:T(8,128)(2,1)S(1)}, bf16[32,4096]{1,0:T(8,128)(2,1)S(1)}, u32[]{:S(2)}, u32[]{:S(2)}) collective-permute-start(bf16[32,4096]{1,0:T(8,128)(2,1)S(1)} %get-tuple-element.129), channel_id=1, source_target_pairs={{0,2},{1,3},{2,0},{3,1},{4,6},{5,7},{6,4},{7,5},{8,10},{9,11},{10,... | collective-permute-start | bytes 786440 | tf_op jit(solution)/shard_map/ppermute | solution.py:284
  52.0 0.6 collective-permute-start.32
  52.7 0.8 %collective-permute-start.28 = (bf16[16,4096]{1,0:T(8,128)(2,1)S(1)}, bf16[16,4096]{1,0:T(8,128)(2,1)S(1)}, u32[]{:S(2)}, u32[]{:S(2)}) collective-permute-start(bf16[16,4096]{1,0:T(8,128)(2,1)S(1)} %get-tuple-element.137), channel_id=1, source_target_pairs={{0,24},{8,16},{16,8},{24,0},{1,25},{9,17},{17,9},{25,1},{2,26},{10... | collective-permute-start | bytes 393224 | tf_op jit(solution)/shard_map/ppermute | solution.py:289
  53.7 4.9 %collective-permute-done.31 = bf16[32,4096]{1,0:T(8,128)(2,1)S(1)} collective-permute-done((bf16[32,4096]{1,0:T(8,128)(2,1)S(1)}, bf16[32,4096]{1,0:T(8,128)(2,1)S(1)}, u32[]{:S(2)}, u32[]{:S(2)}) %collective-permute-start.31) | collective-permute-done | bytes 262176 | tf_op jit(solution)/shard_map/ppermute | solution.py:284
  58.7 1.2 %collective-permute-done.32 = bf16[32,4096]{1,0:T(8,128)(2,1)S(1)} collective-permute-done((bf16[32,4096]{1,0:T(8,128)(2,1)S(1)}, bf16[32,4096]{1,0:T(8,128)(2,1)S(1)}, u32[]{:S(2)}, u32[]{:S(2)}) %collective-permute-start.32) | collective-permute-done | bytes 262176 | tf_op jit(solution)/shard_map/ppermute | solution.py:284
  60.0 0.6 collective-permute-start.33
  61.0 2.0 %collective-permute-done.27 = bf16[16,4096]{1,0:T(8,128)(2,1)S(1)} collective-permute-done((bf16[16,4096]{1,0:T(8,128)(2,1)S(1)}, bf16[16,4096]{1,0:T(8,128)(2,1)S(1)}, u32[]{:S(2)}, u32[]{:S(2)}) %collective-permute-start.27) | collective-permute-done | bytes 131104 | tf_op jit(solution)/shard_map/ppermute | solution.py:289
  63.1 1.5 %collective-permute-start.30 = (bf16[16,4096]{1,0:T(8,128)(2,1)S(1)}, bf16[16,4096]{1,0:T(8,128)(2,1)S(1)}, u32[]{:S(2)}, u32[]{:S(2)}) collective-permute-start(bf16[16,4096]{1,0:T(8,128)(2,1)S(1)} %fusion.2), channel_id=1, source_target_pairs={{0,6},{1,7},{2,4},{3,5},{4,2},{5,3},{6,0},{7,1},{8,14},{9,15},{10,... | collective-permute-start | bytes 393224 | tf_op jit(solution)/shard_map/ppermute | solution.py:284
  64.6 2.9 %collective-permute-done.33 = bf16[16,4096]{1,0:T(8,128)(2,1)S(1)} collective-permute-done((bf16[16,4096]{1,0:T(8,128)(2,1)S(1)}, bf16[16,4096]{1,0:T(8,128)(2,1)S(1)}, u32[]{:S(2)}, u32[]{:S(2)}) %collective-permute-start.33) | collective-permute-done | bytes 131104 | tf_op jit(solution)/shard_map/ppermute | solution.py:289
  67.5 1.0 %collective-permute-done.34 = bf16[16,4096]{1,0:T(8,128)(2,1)S(1)} collective-permute-done((bf16[16,4096]{1,0:T(8,128)(2,1)S(1)}, bf16[16,4096]{1,0:T(8,128)(2,1)S(1)}, u32[]{:S(2)}, u32[]{:S(2)}) %collective-permute-start.34) | collective-permute-done | bytes 131104 | tf_op jit(solution)/shard_map/ppermute | solution.py:289
  68.5 0.8 %collective-permute-done.30 = bf16[16,4096]{1,0:T(8,128)(2,1)S(1)} collective-permute-done((bf16[16,4096]{1,0:T(8,128)(2,1)S(1)}, bf16[16,4096]{1,0:T(8,128)(2,1)S(1)}, u32[]{:S(2)}, u32[]{:S(2)}) %collective-permute-start.30) | collective-permute-done | bytes 131104 | tf_op jit(solution)/shard_map/ppermute | solution.py:284
  69.4 0.8 %fusion.9 = bf16[16,4096]{1,0:T(8,128)(2,1)} fusion(f32[48,4096]{1,0:T(8,128)S(1)} %convert_add_fusion, bf16[16,4096]{1,0:T(8,128)(2,1)S(1)} %collective-permute-done.34, bf16[16,4096]{1,0:T(8,128)(2,1)S(1)} %collective-permute-done.33, bf16[16,4096]{1,0:T(8,128)(2,1)S(1)} %collective-permute-done.30, bf16[16,4096]{1,0:T(8,128)(2,1)S(1)} %collective-permute-done.29, ...), kind=kLoop, calls=%fused_computation.17 | loop fusion | flops 851968 | bytes 1179648 | tf_op jit(solution)/shard_map/convert_element_type | solution.py:300
  (75 shorter events, 9.9 us)
Async XLA Ops:
  1.2 13.4 %collective-permute-start.4 = (bf16[16,4224]{1,0:T(8,128)(2,1)S(1)}, bf16[16,4224]{1,0:T(8,128)(2,1)S(1)}, u32[]{:S(2)}, u32[]{:S(2)}) collective-permute-start(bf16[16,4224]{1,0:T(8,128)(2,1)S(1)} %pack.1.refs_0_), channel_id=1, source_target_pairs={{0,16},{8,24},{16,0},{24,8},{1,17},{9,25},{17,1},{25,9},{2,18},{10... | collective-permute-start | bytes 405512 | tf_op jit(solution)/shard_map/ppermute | solution.py:289
  5.3 9.3 %collective-permute-start.3 = (bf16[16,4224]{1,0:T(8,128)(2,1)S(1)}, bf16[16,4224]{1,0:T(8,128)(2,1)S(1)}, u32[]{:S(2)}, u32[]{:S(2)}) collective-permute-start(bf16[16,4224]{1,0:T(8,128)(2,1)S(1)} %pack.1.refs_0_), channel_id=1, source_target_pairs={{0,8},{8,0},{16,24},{24,16},{1,9},{9,1},{17,25},{25,17},{2,10},{10... | collective-permute-start | bytes 405512 | tf_op jit(solution)/shard_map/ppermute | solution.py:289
  6.9 7.7 %collective-permute-start.2 = (bf16[16,4224]{1,0:T(8,128)(2,1)S(1)}, bf16[16,4224]{1,0:T(8,128)(2,1)S(1)}, u32[]{:S(2)}, u32[]{:S(2)}) collective-permute-start(bf16[16,4224]{1,0:T(8,128)(2,1)S(1)} %pack.1.refs_0_), channel_id=1, source_target_pairs={{0,6},{1,7},{2,4},{3,5},{4,2},{5,3},{6,0},{7,1},{8,14},{9,15},{10,... | collective-permute-start | bytes 405512 | tf_op jit(solution)/shard_map/ppermute | solution.py:284
  9.4 6.1 %collective-permute-start.1 = (bf16[16,4224]{1,0:T(8,128)(2,1)S(1)}, bf16[16,4224]{1,0:T(8,128)(2,1)S(1)}, u32[]{:S(2)}, u32[]{:S(2)}) collective-permute-start(bf16[16,4224]{1,0:T(8,128)(2,1)S(1)} %pack.1.refs_0_), channel_id=1, source_target_pairs={{0,4},{1,5},{2,6},{3,7},{4,0},{5,1},{6,2},{7,3},{8,12},{9,13},{10,... | collective-permute-start | bytes 405512 | tf_op jit(solution)/shard_map/ppermute | solution.py:284
  9.9 5.7 %collective-permute-start = (bf16[16,4224]{1,0:T(8,128)(2,1)S(1)}, bf16[16,4224]{1,0:T(8,128)(2,1)S(1)}, u32[]{:S(2)}, u32[]{:S(2)}) collective-permute-start(bf16[16,4224]{1,0:T(8,128)(2,1)S(1)} %pack.1.refs_0_), channel_id=1, source_target_pairs={{0,2},{1,3},{2,0},{3,1},{4,6},{5,7},{6,4},{7,5},{8,10},{9,11},{10,... | collective-permute-start | bytes 405512 | tf_op jit(solution)/shard_map/ppermute | solution.py:284
  15.5 7.2 %collective-permute-start.7 = (bf16[16,4224]{1,0:T(8,128)(2,1)S(1)}, bf16[16,4224]{1,0:T(8,128)(2,1)S(1)}, u32[]{:S(2)}, u32[]{:S(2)}) collective-permute-start(bf16[16,4224]{1,0:T(8,128)(2,1)S(1)} %collective-permute-done.4.refs_0_), channel_id=1, source_target_pairs={{0,6},{1,7},{2,4},{3,5},{4,2},{5,3},{6,0},{7,1},{8,14},{9,15},{10,... | collective-permute-start | bytes 405512 | tf_op jit(solution)/shard_map/ppermute | solution.py:284
  17.2 6.9 %collective-permute-start.6 = (bf16[16,4224]{1,0:T(8,128)(2,1)S(1)}, bf16[16,4224]{1,0:T(8,128)(2,1)S(1)}, u32[]{:S(2)}, u32[]{:S(2)}) collective-permute-start(bf16[16,4224]{1,0:T(8,128)(2,1)S(1)} %collective-permute-done.4.refs_0_), channel_id=1, source_target_pairs={{0,4},{1,5},{2,6},{3,7},{4,0},{5,1},{6,2},{7,3},{8,12},{9,13},{10,... | collective-permute-start | bytes 405512 | tf_op jit(solution)/shard_map/ppermute | solution.py:284
  18.5 5.8 %collective-permute-start.5 = (bf16[16,4224]{1,0:T(8,128)(2,1)S(1)}, bf16[16,4224]{1,0:T(8,128)(2,1)S(1)}, u32[]{:S(2)}, u32[]{:S(2)}) collective-permute-start(bf16[16,4224]{1,0:T(8,128)(2,1)S(1)} %collective-permute-done.4.refs_0_), channel_id=1, source_target_pairs={{0,2},{1,3},{2,0},{3,1},{4,6},{5,7},{6,4},{7,5},{8,10},{9,11},{10,... | collective-permute-start | bytes 405512 | tf_op jit(solution)/shard_map/ppermute | solution.py:284
  19.0 5.3 %collective-permute-start.8 = (bf16[16,4224]{1,0:T(8,128)(2,1)S(1)}, bf16[16,4224]{1,0:T(8,128)(2,1)S(1)}, u32[]{:S(2)}, u32[]{:S(2)}) collective-permute-start(bf16[16,4224]{1,0:T(8,128)(2,1)S(1)} %collective-permute-done.4.refs_0_), channel_id=1, source_target_pairs={{0,8},{8,0},{16,24},{24,16},{1,9},{9,1},{17,25},{25,17},{2,10},{10... | collective-permute-start | bytes 405512 | tf_op jit(solution)/shard_map/ppermute | solution.py:289
  20.3 6.8 %collective-permute-start.9 = (bf16[64,4224]{1,0:T(8,128)(2,1)S(1)}, bf16[64,4224]{1,0:T(8,128)(2,1)S(1)}, u32[]{:S(2)}, u32[]{:S(2)}) collective-permute-start(bf16[64,4224]{1,0:T(8,128)(2,1)S(1)} %gather.3.refs_1_), channel_id=1, source_target_pairs={{0,1},{1,0},{2,3},{3,2},{4,5},{5,4},{6,7},{7,6},{8,9},{9,8},{10,11... | collective-permute-start | bytes 1622024 | tf_op jit(solution)/shard_map/ppermute | solution.py:284
  24.4 4.3 %collective-permute-start.10 = (bf16[64,4224]{1,0:T(8,128)(2,1)S(1)}, bf16[64,4224]{1,0:T(8,128)(2,1)S(1)}, u32[]{:S(2)}, u32[]{:S(2)}) collective-permute-start(bf16[64,4224]{1,0:T(8,128)(2,1)S(1)} %gather.4.refs_2_), channel_id=1, source_target_pairs={{0,1},{1,0},{2,3},{3,2},{4,5},{5,4},{6,7},{7,6},{8,9},{9,8},{10,11... | collective-permute-start | bytes 1622024 | tf_op jit(solution)/shard_map/ppermute | solution.py:284
  24.5 10.4 %collective-permute-start.12 = (bf16[32,4224]{1,0:T(8,128)(2,1)S(1)}, bf16[32,4224]{1,0:T(8,128)(2,1)S(1)}, u32[]{:S(2)}, u32[]{:S(2)}) collective-permute-start(bf16[32,4224]{1,0:T(8,128)(2,1)S(1)} %gather.5.refs_1_), channel_id=1, source_target_pairs={{0,4},{1,5},{2,6},{3,7},{4,0},{5,1},{6,2},{7,3},{8,12},{9,13},{10,... | collective-permute-start | bytes 811016 | tf_op jit(solution)/shard_map/ppermute | solution.py:284
  26.0 8.9 %collective-permute-start.11 = (bf16[32,4224]{1,0:T(8,128)(2,1)S(1)}, bf16[32,4224]{1,0:T(8,128)(2,1)S(1)}, u32[]{:S(2)}, u32[]{:S(2)}) collective-permute-start(bf16[32,4224]{1,0:T(8,128)(2,1)S(1)} %gather.5.refs_1_), channel_id=1, source_target_pairs={{0,2},{1,3},{2,0},{3,1},{4,6},{5,7},{6,4},{7,5},{8,10},{9,11},{10,... | collective-permute-start | bytes 811016 | tf_op jit(solution)/shard_map/ppermute | solution.py:284
  26.6 8.3 %collective-permute-start.13 = (bf16[16,4224]{1,0:T(8,128)(2,1)S(1)}, bf16[16,4224]{1,0:T(8,128)(2,1)S(1)}, u32[]{:S(2)}, u32[]{:S(2)}) collective-permute-start(bf16[16,4224]{1,0:T(8,128)(2,1)S(1)} %collective-permute-done.2.refs_3_), channel_id=1, source_target_pairs={{0,8},{8,0},{16,24},{24,16},{1,9},{9,1},{17,25},{25,17},{2,10},{10... | collective-permute-start | bytes 405512 | tf_op jit(solution)/shard_map/ppermute | solution.py:289
  27.0 7.9 %collective-permute-start.14 = (bf16[16,4224]{1,0:T(8,128)(2,1)S(1)}, bf16[16,4224]{1,0:T(8,128)(2,1)S(1)}, u32[]{:S(2)}, u32[]{:S(2)}) collective-permute-start(bf16[16,4224]{1,0:T(8,128)(2,1)S(1)} %collective-permute-done.7.refs_3_), channel_id=1, source_target_pairs={{0,8},{8,0},{16,24},{24,16},{1,9},{9,1},{17,25},{25,17},{2,10},{10... | collective-permute-start | bytes 405512 | tf_op jit(solution)/shard_map/ppermute | solution.py:289
  35.0 2.5 %collective-permute-start.17 = (bf16[32,4224]{1,0:T(8,128)(2,1)S(1)}, bf16[32,4224]{1,0:T(8,128)(2,1)S(1)}, u32[]{:S(2)}, u32[]{:S(2)}) collective-permute-start(bf16[32,4224]{1,0:T(8,128)(2,1)S(1)} %gather.5.refs_1_), channel_id=1, source_target_pairs={{0,1},{1,0},{2,3},{3,2},{4,5},{5,4},{6,7},{7,6},{8,9},{9,8},{10,11... | collective-permute-start | bytes 811016 | tf_op jit(solution)/shard_map/ppermute | solution.py:284
  35.6 3.7 %collective-permute-start.21 = (bf16[16,4224]{1,0:T(8,128)(2,1)S(1)}, bf16[16,4224]{1,0:T(8,128)(2,1)S(1)}, u32[]{:S(2)}, u32[]{:S(2)}) collective-permute-start(bf16[16,4224]{1,0:T(8,128)(2,1)S(1)} %collective-permute-done.14.refs_5_), channel_id=1, source_target_pairs={{0,1},{1,0},{2,3},{3,2},{4,5},{5,4},{6,7},{7,6},{8,9},{9,8},{10,11... | collective-permute-start | bytes 405512 | tf_op jit(solution)/shard_map/ppermute | solution.py:284
  36.0 3.9 %collective-permute-start.18 = (bf16[32,4224]{1,0:T(8,128)(2,1)S(1)}, bf16[32,4224]{1,0:T(8,128)(2,1)S(1)}, u32[]{:S(2)}, u32[]{:S(2)}) collective-permute-start(bf16[32,4224]{1,0:T(8,128)(2,1)S(1)} %collective-permute-done.11.refs_2_), channel_id=1, source_target_pairs={{0,1},{1,0},{2,3},{3,2},{4,5},{5,4},{6,7},{7,6},{8,9},{9,8},{10,11... | collective-permute-start | bytes 811016 | tf_op jit(solution)/shard_map/ppermute | solution.py:284
  37.1 2.8 %collective-permute-start.19 = (bf16[32,4224]{1,0:T(8,128)(2,1)S(1)}, bf16[32,4224]{1,0:T(8,128)(2,1)S(1)}, u32[]{:S(2)}, u32[]{:S(2)}) collective-permute-start(bf16[32,4224]{1,0:T(8,128)(2,1)S(1)} %collective-permute-done.12.refs_3_), channel_id=1, source_target_pairs={{0,1},{1,0},{2,3},{3,2},{4,5},{5,4},{6,7},{7,6},{8,9},{9,8},{10,11... | collective-permute-start | bytes 811016 | tf_op jit(solution)/shard_map/ppermute | solution.py:284
  37.5 9.4 %collective-permute-start.22 = (bf16[16,4096]{1,0:T(8,128)(2,1)S(1)}, bf16[16,4096]{1,0:T(8,128)(2,1)S(1)}, u32[]{:S(2)}, u32[]{:S(2)}) collective-permute-start(bf16[16,4096]{1,0:T(8,128)(2,1)S(1)} %add_convert_fusion.8), channel_id=1, source_target_pairs={{0,16},{8,24},{16,0},{24,8},{1,17},{9,25},{17,1},{25,9},{2,18},{10... | collective-permute-start | bytes 393224 | tf_op jit(solution)/shard_map/ppermute | solution.py:289
  37.9 9.0 %collective-permute-start.24 = (bf16[32,4096]{1,0:T(8,128)(2,1)S(1)}, bf16[32,4096]{1,0:T(8,128)(2,1)S(1)}, u32[]{:S(2)}, u32[]{:S(2)}) collective-permute-start(bf16[32,4096]{1,0:T(8,128)(2,1)S(1)} %get-tuple-element.95), channel_id=1, source_target_pairs={{0,2},{1,3},{2,0},{3,1},{4,6},{5,7},{6,4},{7,5},{8,10},{9,11},{10,... | collective-permute-start | bytes 786440 | tf_op jit(solution)/shard_map/ppermute | solution.py:284
  39.3 8.0 %collective-permute-start.23 = (bf16[32,4096]{1,0:T(8,128)(2,1)S(1)}, bf16[32,4096]{1,0:T(8,128)(2,1)S(1)}, u32[]{:S(2)}, u32[]{:S(2)}) collective-permute-start(bf16[32,4096]{1,0:T(8,128)(2,1)S(1)} %get-tuple-element.96), channel_id=1, source_target_pairs={{0,4},{1,5},{2,6},{3,7},{4,0},{5,1},{6,2},{7,3},{8,12},{9,13},{10,... | collective-permute-start | bytes 786440 | tf_op jit(solution)/shard_map/ppermute | solution.py:284
  39.9 7.4 %collective-permute-start.16 = (bf16[48,4096]{1,0:T(8,128)(2,1)S(1)}, bf16[48,4096]{1,0:T(8,128)(2,1)S(1)}, u32[]{:S(2)}, u32[]{:S(2)}) collective-permute-start(bf16[48,4096]{1,0:T(8,128)(2,1)S(1)} %get-tuple-element.94), channel_id=1, source_target_pairs={{0,1},{1,0},{2,3},{3,2},{4,5},{5,4},{6,7},{7,6},{8,9},{9,8},{10,11... | collective-permute-start | bytes 1179656 | tf_op jit(solution)/shard_map/ppermute | solution.py:284
  47.6 5.0 %collective-permute-start.26 = (bf16[32,4096]{1,0:T(8,128)(2,1)S(1)}, bf16[32,4096]{1,0:T(8,128)(2,1)S(1)}, u32[]{:S(2)}, u32[]{:S(2)}) collective-permute-start(bf16[32,4096]{1,0:T(8,128)(2,1)S(1)} %get-tuple-element.121), channel_id=1, source_target_pairs={{0,1},{1,0},{2,3},{3,2},{4,5},{5,4},{6,7},{7,6},{8,9},{9,8},{10,11... | collective-permute-start | bytes 786440 | tf_op jit(solution)/shard_map/ppermute | solution.py:284
  48.1 12.9 %collective-permute-start.29 = (bf16[16,4096]{1,0:T(8,128)(2,1)S(1)}, bf16[16,4096]{1,0:T(8,128)(2,1)S(1)}, u32[]{:S(2)}, u32[]{:S(2)}) collective-permute-start(bf16[16,4096]{1,0:T(8,128)(2,1)S(1)} %fusion.4), channel_id=1, source_target_pairs={{0,16},{8,24},{16,0},{24,8},{1,17},{9,25},{17,1},{25,9},{2,18},{10... | collective-permute-start | bytes 393224 | tf_op jit(solution)/shard_map/ppermute | solution.py:289
  50.6 8.1 %collective-permute-start.31 = (bf16[32,4096]{1,0:T(8,128)(2,1)S(1)}, bf16[32,4096]{1,0:T(8,128)(2,1)S(1)}, u32[]{:S(2)}, u32[]{:S(2)}) collective-permute-start(bf16[32,4096]{1,0:T(8,128)(2,1)S(1)} %get-tuple-element.129), channel_id=1, source_target_pairs={{0,2},{1,3},{2,0},{3,1},{4,6},{5,7},{6,4},{7,5},{8,10},{9,11},{10,... | collective-permute-start | bytes 786440 | tf_op jit(solution)/shard_map/ppermute | solution.py:284
  52.0 7.8 %collective-permute-start.32 = (bf16[32,4096]{1,0:T(8,128)(2,1)S(1)}, bf16[32,4096]{1,0:T(8,128)(2,1)S(1)}, u32[]{:S(2)}, u32[]{:S(2)}) collective-permute-start(bf16[32,4096]{1,0:T(8,128)(2,1)S(1)} %get-tuple-element.130), channel_id=1, source_target_pairs={{0,4},{1,5},{2,6},{3,7},{4,0},{5,1},{6,2},{7,3},{8,12},{9,13},{10,... | collective-permute-start | bytes 786440 | tf_op jit(solution)/shard_map/ppermute | solution.py:284
  52.7 8.3 %collective-permute-start.28 = (bf16[16,4096]{1,0:T(8,128)(2,1)S(1)}, bf16[16,4096]{1,0:T(8,128)(2,1)S(1)}, u32[]{:S(2)}, u32[]{:S(2)}) collective-permute-start(bf16[16,4096]{1,0:T(8,128)(2,1)S(1)} %get-tuple-element.137), channel_id=1, source_target_pairs={{0,24},{8,16},{16,8},{24,0},{1,25},{9,17},{17,9},{25,1},{2,26},{10... | collective-permute-start | bytes 393224 | tf_op jit(solution)/shard_map/ppermute | solution.py:289
  53.5 9.5 %collective-permute-start.27 = (bf16[16,4096]{1,0:T(8,128)(2,1)S(1)}, bf16[16,4096]{1,0:T(8,128)(2,1)S(1)}, u32[]{:S(2)}, u32[]{:S(2)}) collective-permute-start(bf16[16,4096]{1,0:T(8,128)(2,1)S(1)} %get-tuple-element.138), channel_id=1, source_target_pairs={{0,8},{8,0},{16,24},{24,16},{1,9},{9,1},{17,25},{25,17},{2,10},{10... | collective-permute-start | bytes 393224 | tf_op jit(solution)/shard_map/ppermute | solution.py:289
  60.0 7.5 %collective-permute-start.33 = (bf16[16,4096]{1,0:T(8,128)(2,1)S(1)}, bf16[16,4096]{1,0:T(8,128)(2,1)S(1)}, u32[]{:S(2)}, u32[]{:S(2)}) collective-permute-start(bf16[16,4096]{1,0:T(8,128)(2,1)S(1)} %get-tuple-element.131), channel_id=1, source_target_pairs={{0,24},{8,16},{16,8},{24,0},{1,25},{9,17},{17,9},{25,1},{2,26},{10... | collective-permute-start | bytes 393224 | tf_op jit(solution)/shard_map/ppermute | solution.py:289
  60.6 7.9 %collective-permute-start.34 = (bf16[16,4096]{1,0:T(8,128)(2,1)S(1)}, bf16[16,4096]{1,0:T(8,128)(2,1)S(1)}, u32[]{:S(2)}, u32[]{:S(2)}) collective-permute-start(bf16[16,4096]{1,0:T(8,128)(2,1)S(1)} %get-tuple-element.132), channel_id=1, source_target_pairs={{0,8},{8,0},{16,24},{24,16},{1,9},{9,1},{17,25},{25,17},{2,10},{10... | collective-permute-start | bytes 393224 | tf_op jit(solution)/shard_map/ppermute | solution.py:289
  63.1 6.3 %collective-permute-start.30 = (bf16[16,4096]{1,0:T(8,128)(2,1)S(1)}, bf16[16,4096]{1,0:T(8,128)(2,1)S(1)}, u32[]{:S(2)}, u32[]{:S(2)}) collective-permute-start(bf16[16,4096]{1,0:T(8,128)(2,1)S(1)} %fusion.2), channel_id=1, source_target_pairs={{0,6},{1,7},{2,4},{3,5},{4,2},{5,3},{6,0},{7,1},{8,14},{9,15},{10,... | collective-permute-start | bytes 393224 | tf_op jit(solution)/shard_map/ppermute | solution.py:284
  (11 other events, 59.0 us)
